TPU v7x, 32 devices: a whole 2x2x4 slice. The times are simulated.
32 devices in a mesh: fsdp: 8 (over z, y), context: 2 (over x), tensor: 2 (over core).
Axes of the slice: x: 2, y: 2, z: 4, core: 2. Of those that a mesh axis runs over, the one named last changes fastest.
Arguments:
- tokens: bfloat16 [2, 8, 1024, 2048], P(None, 'fsdp', 'context'), may hold values from -6 to 6
- lengths: int32 [2, 8, 2], P(None, 'fsdp'), may hold values from 128 to 896, as said below
- block_order: int32 [2, 8, 8], P(None, 'fsdp'), may hold values from 0 to 7, each once within a row
- cotangent: bfloat16 [2, 8, 1024, 2048], P(None, 'fsdp', 'context'), may hold values from -6 to 6
- norm_gain: float32 [2048], replicated, may hold values from 0.1 to 1.9
- in_weight: bfloat16 [2048, 2, 4096], P('fsdp', None, 'tensor'), may hold values from -0.125 to 0.125
- coupling_weight: bfloat16 [2048, 256], P('fsdp'), may hold values from -0.125 to 0.125
- step_weight: bfloat16 [2048, 64], P('fsdp', 'tensor'), may hold values from -0.125 to 0.125
- out_weight: bfloat16 [4096, 2048], P('tensor', 'fsdp'), may hold values from -0.09375 to 0.09375
- conv_weight: float32 [4, 4096], P(None, 'tensor'), may hold values from -3 to 3
- conv_bias: float32 [4096], P('tensor'), may hold values from -3 to 3
- coupling_conv: float32 [4, 256], replicated, may hold values from -3 to 3
- coupling_bias: float32 [256], replicated, may hold values from -3 to 3
- step_bias: float32 [64], P('tensor'), may hold values from -1 to 1
- decay_rate: float32 [64], P('tensor'), may hold values from 0.00012207031 to 0.041666667
- skip_gain: float32 [64], P('tensor'), may hold values from 0.5 to 1.5
- inner_gain: float32 [4096], P('tensor'), may hold values from 0.1 to 1.9
Outputs:
- block_out: bfloat16 [2, 8, 1024, 2048], P(None, 'fsdp', 'context')
- input_grad: bfloat16 [2, 8, 1024, 2048], P(None, 'fsdp', 'context')
- norm_gain_grad: float32 [2048], replicated
- in_weight_grad: float32 [2048, 2, 4096], P('fsdp', None, 'tensor')
- coupling_weight_grad: float32 [2048, 256], P('fsdp')
- step_weight_grad: float32 [2048, 64], P('fsdp', 'tensor')
- out_weight_grad: float32 [4096, 2048], P('tensor', 'fsdp')
- conv_weight_grad: float32 [4, 4096], P(None, 'tensor')
- conv_bias_grad: float32 [4096], P('tensor')
- coupling_conv_grad: float32 [4, 256], replicated
- coupling_bias_grad: float32 [256], replicated
- step_bias_grad: float32 [64], P('tensor')
- decay_rate_grad: float32 [64], P('tensor')
- skip_gain_grad: float32 [64], P('tensor')
- inner_gain_grad: float32 [4096], P('tensor')
Inputs may be any that keep to these rules, and one draw needn't show every extreme that they name: Each row of 1024 positions holds two packed sequences of these lengths, in this order, then padding; the longer one covers all but fewer than half of 512 positions of the row. `block_order`: each row's entries are a permutation of its 8 blocks.
All inputs are finite; a program needn't handle non-finite values.
Results may differ from a plain program's by a relative error of at most 0.00225.
The roundings to bfloat16 on the way count: a program that leaves them out, or rounds other values in their place, can miss the bound.
Values may be sent and summed in bfloat16 or wider, within the bound.
A program may use at most 768 MiB of HBM per device.

v0:
```python
import jax
import jax.numpy as jnp
from jax import lax
from jax.sharding import PartitionSpec as P

SPAN = 256


epsilon = 1e-05


def passed_along(value, axis, steps):
    count = lax.axis_size(axis)
    initial, last = (max(0, -steps), min(count, count - steps))
    return lax.ppermute(value, axis, [(source, source + steps) for source in range(initial, last)])


def segment_of(position, seq_lens):
    first_part = (position >= seq_lens[0]).astype(jnp.int32)
    second_part = (position >= seq_lens[0] + seq_lens[1]).astype(jnp.int32)
    return jnp.where(position < 0, -1, first_part + second_part)


def conv_apply(padded, weights, biases, same_masks):
    width_conv = weights.shape[0]
    rim_rows = width_conv - 1
    length_rows = padded.shape[0] - rim_rows
    summed = biases
    for lag_index in range(width_conv):
        start_row = rim_rows - lag_index
        summed = (
            summed
            + weights[lag_index]
            * padded[start_row : start_row + length_rows]
            * same_masks[lag_index][:, None]
        )
    return jax.nn.silu(summed)


def span_step(state_now, span_parts):
    value_part, input_part, output_part, step_part, log_part, segment_part, segment_prior = (
        span_parts
    )
    highest = lax.Precision.HIGHEST
    cumulative = jnp.cumsum(log_part, axis=0)
    places = jnp.arange(segment_part.shape[0])
    joined = (segment_part[:, None] == segment_part[None, :]) & (places[:, None] >= places[None, :])
    spread = jnp.where(joined[:, :, None], cumulative[:, None, :] - cumulative[None, :, :], 0.0)
    decays = jnp.where(joined[:, :, None], jnp.exp(spread), 0.0)
    gram_mat = jnp.dot(output_part, input_part.T, precision=highest)
    inside = jnp.einsum(
        "ijh,jhp->ihp",
        gram_mat[:, :, None] * decays,
        step_part[:, :, None] * value_part,
        precision=highest,
    )
    carried_in = jnp.exp(cumulative) * (segment_part == segment_prior)[:, None]
    from_state = carried_in[:, :, None] * jnp.einsum(
        "in,hpn->ihp", output_part, state_now, precision=highest
    )
    tail_decay = (
        jnp.exp(cumulative[-1][None, :] - cumulative) * (segment_part == segment_part[-1])[:, None]
    )
    fresh_state = jnp.einsum(
        "jh,jhp,jn->hpn", tail_decay * step_part, value_part, input_part, precision=highest
    )
    through = jnp.exp(cumulative[-1]) * (segment_part[-1] == segment_prior)
    return (through[:, None, None] * state_now + fresh_state, inside + from_state)


def ssd_part(
    seg_ids,
    seg_before,
    value_heads,
    input_map,
    output_map,
    step_raw,
    step_bias,
    decay_rates,
    skip_gains,
    state_start,
):
    step_size = jax.nn.softplus(step_raw + step_bias)
    log_decay = -step_size * decay_rates
    tok_count, heads_local, head_size = value_heads.shape
    state_size = input_map.shape[1]
    span_count = tok_count // SPAN
    segment_prior = jnp.concatenate(
        [jnp.reshape(seg_before, (1,)), seg_ids.reshape(span_count, SPAN)[:-1, -1]]
    )
    span_parts = (
        value_heads.reshape(span_count, SPAN, heads_local, head_size),
        input_map.reshape(span_count, SPAN, state_size),
        output_map.reshape(span_count, SPAN, state_size),
        step_size.reshape(span_count, SPAN, heads_local),
        log_decay.reshape(span_count, SPAN, heads_local),
        seg_ids.reshape(span_count, SPAN),
        segment_prior,
    )
    state_final, span_out = lax.scan(span_step, state_start, span_parts)
    mixer_out = (
        span_out.reshape(tok_count, heads_local, head_size)
        + skip_gains[None, :, None] * value_heads
    )
    return (mixer_out, state_final)


def pass_state(factor, values, shift_by):

    def hand_on(step_index, inbound):
        return passed_along(factor[:, None, None] * inbound + values, "context", shift_by)

    return lax.fori_loop(0, lax.axis_size("context") - 1, hand_on, jnp.zeros_like(values))


def pass_rim(value_rows, coupling_rows, shift_by):
    return passed_along((value_rows, coupling_rows), "context", shift_by)


def contract_rows(left, right):
    return lax.dot_general(
        left, right, (((0,), (0,)), ((), ())), preferred_element_type=jnp.float32
    )


def contract_cols(left, right):
    return lax.dot_general(
        left, right, (((1,), (1,)), ((), ())), preferred_element_type=jnp.float32
    )


def shards(
    tokens,
    lengths,
    block_order,
    cotangent,
    norm_gain,
    in_weight,
    coupling_weight,
    step_weight,
    out_weight,
    conv_weight,
    conv_bias,
    coupling_conv,
    coupling_bias,
    step_bias,
    decay_rate,
    skip_gain,
    inner_gain,
):
    highest = lax.Precision.HIGHEST
    micro_count = tokens.shape[0]
    tok_count = tokens.shape[2]
    model_width = tokens.shape[3]
    inner_local = inner_gain.shape[0]
    heads_local = step_bias.shape[0]
    head_size = inner_local // heads_local
    state_size = coupling_weight.shape[1] // 2
    rim_rows = conv_weight.shape[0] - 1
    blocks_row = block_order.shape[2]
    block_len = tok_count * lax.axis_size("context") // blocks_row
    inner_total = inner_local * lax.axis_size("tensor")
    base_pos = lax.axis_index("context") * tok_count
    positions = base_pos + jnp.arange(tok_count, dtype=jnp.int32)
    slot_ids = jnp.arange(blocks_row, dtype=jnp.int32)
    in_total = jnp.zeros((model_width, 2 * inner_local), jnp.float32)
    coupling_total = jnp.zeros((model_width, 2 * state_size), jnp.float32)
    step_total = jnp.zeros((model_width, heads_local), jnp.float32)
    out_total = jnp.zeros((inner_local, model_width), jnp.float32)
    gain_total = jnp.zeros_like(norm_gain)
    convw_total = jnp.zeros_like(conv_weight)
    convb_total = jnp.zeros_like(conv_bias)
    couplingw_total = jnp.zeros_like(coupling_conv)
    couplingb_total = jnp.zeros_like(coupling_bias)
    stepb_total = jnp.zeros_like(step_bias)
    rate_total = jnp.zeros_like(decay_rate)
    skip_total = jnp.zeros_like(skip_gain)
    inner_total_grad = jnp.zeros_like(inner_gain)
    block_outs = []
    input_grads = []
    for micro_index in range(micro_count):
        seq_lens = lengths[micro_index, 0]
        order_row = block_order[micro_index, 0]
        own_block = positions // block_len
        source_slot = jnp.sum(
            jnp.where(order_row[None, :] == own_block[:, None], slot_ids[None, :], 0), axis=1
        )
        source_pos = source_slot * block_len + positions % block_len

        def place_rows(current, piece_rows, piece_start, source_pos=source_pos):
            inside = (source_pos >= 0) & (source_pos < piece_rows.shape[0])
            picked = jnp.take(piece_rows, jnp.clip(source_pos, 0, piece_rows.shape[0] - 1), axis=0)
            return jnp.where(inside[:, None], picked, current)

        x_input = place_rows(
            jnp.zeros((tok_count, model_width), jnp.bfloat16),
            lax.all_gather(tokens[micro_index, 0], "context", axis=0, tiled=True),
            jnp.int32(0),
        )
        in_full, coupling_full, step_full, out_full = (
            lax.all_gather(in_weight, "fsdp", axis=0, tiled=True),
            lax.all_gather(coupling_weight, "fsdp", axis=0, tiled=True),
            lax.all_gather(step_weight, "fsdp", axis=0, tiled=True),
            lax.all_gather(out_weight, "fsdp", axis=1, tiled=True),
        )
        in_full = in_full.reshape(model_width, 2 * inner_local)
        x_float = x_input.astype(jnp.float32)
        inv_rms = lax.rsqrt(jnp.mean(x_float * x_float, axis=-1, keepdims=True) + epsilon)
        x_hat = x_float * inv_rms
        normed = (x_hat * norm_gain).astype(jnp.bfloat16)
        both_proj = jnp.dot(normed, in_full, preferred_element_type=jnp.float32)
        gate_in = both_proj[:, :inner_local]
        value_raw = both_proj[:, inner_local:]
        coupling_raw = jnp.dot(normed, coupling_full, preferred_element_type=jnp.float32)
        step_raw = jnp.dot(normed, step_full, preferred_element_type=jnp.float32)
        value_rim, coupling_rim = pass_rim(
            value_raw[tok_count - rim_rows :], coupling_raw[tok_count - rim_rows :], 1
        )
        seg_ids = segment_of(positions, seq_lens)
        seg_before = segment_of(base_pos - 1, seq_lens)
        same_masks = jnp.stack(
            [
                (segment_of(positions - lag_index, seq_lens) == seg_ids).astype(jnp.float32)
                for lag_index in range(rim_rows + 1)
            ]
        )

        def conv_both(
            value_values,
            coupling_values,
            value_edge,
            coupling_edge,
            weight_value,
            bias_value,
            weight_coupling,
            bias_coupling,
            same_masks=same_masks,
        ):
            value_conv = conv_apply(
                jnp.concatenate([value_edge, value_values]), weight_value, bias_value, same_masks
            )
            coupling_out = conv_apply(
                jnp.concatenate([coupling_edge, coupling_values]),
                weight_coupling,
                bias_coupling,
                same_masks,
            )
            return (value_conv, coupling_out)

        (value_conv, coupling_out), conv_back = jax.vjp(
            conv_both,
            value_raw,
            coupling_raw,
            value_rim,
            coupling_rim,
            conv_weight,
            conv_bias,
            coupling_conv,
            coupling_bias,
        )
        value_heads = value_conv.reshape(tok_count, heads_local, head_size)
        input_map = coupling_out[:, :state_size]
        output_map = coupling_out[:, state_size:]
        step_size = jax.nn.softplus(step_raw + step_bias)
        cumulative = jnp.cumsum(-step_size * decay_rate, axis=0)
        tail_decay = (
            jnp.exp(cumulative[-1][None, :] - cumulative) * (seg_ids == seg_ids[-1])[:, None]
        )
        own_state = jnp.einsum(
            "th,thp,tn->hpn", tail_decay * step_size, value_heads, input_map, precision=highest
        )
        through = jnp.exp(cumulative[-1]) * (seg_ids[-1] == seg_before)
        state_in = pass_state(through, own_state, 1)

        def ssd_local(
            value_values,
            input_values,
            output_values,
            step_values,
            bias_step,
            decay_rates,
            skip_gains,
            state_start,
            seg_ids=seg_ids,
            seg_before=seg_before,
        ):
            return ssd_part(
                seg_ids,
                seg_before,
                value_values,
                input_values,
                output_values,
                step_values,
                bias_step,
                decay_rates,
                skip_gains,
                state_start,
            )

        (mixer_out, state_final), ssd_back = jax.vjp(
            ssd_local,
            value_heads,
            input_map,
            output_map,
            step_raw,
            step_bias,
            decay_rate,
            skip_gain,
            state_in,
        )
        mixer_flat = mixer_out.reshape(tok_count, inner_local)
        gate_act = jax.nn.silu(gate_in)
        gated_value = mixer_flat * gate_act
        square_sum = lax.psum(jnp.sum(gated_value * gated_value, axis=-1), "tensor")
        inv_norm = lax.rsqrt(square_sum / inner_total + epsilon)[:, None]
        gated_norm = (gated_value * inv_norm * inner_gain).astype(jnp.bfloat16)
        branch_out = lax.psum(
            jnp.dot(gated_norm, out_full, preferred_element_type=jnp.float32), "tensor"
        )
        keep_mask = (seg_ids < 2).astype(jnp.float32)[:, None]
        block_outs.append((x_float + keep_mask * branch_out).astype(jnp.bfloat16))
        cot_row = cotangent[micro_index, 0]
        out_grad = cot_row * keep_mask.astype(jnp.bfloat16)
        out_total = out_total + contract_rows(gated_norm, out_grad)
        norm_grad = contract_cols(out_grad, out_full)
        inner_total_grad = inner_total_grad + jnp.sum(norm_grad * gated_value * inv_norm, axis=0)
        scaled_grad = norm_grad * inner_gain
        inner_dot = lax.psum(jnp.sum(scaled_grad * gated_value, axis=-1), "tensor")
        gated_grad = scaled_grad * inv_norm - gated_value * (
            inner_dot[:, None] * inv_norm**3 / inner_total
        )
        sigmoid_gate = jax.nn.sigmoid(gate_in)
        gate_grad = gated_grad * mixer_flat * sigmoid_gate * (1.0 + gate_in * (1.0 - sigmoid_gate))
        mixer_grad = (gated_grad * gate_act).reshape(tok_count, heads_local, head_size)
        carried_in = jnp.exp(cumulative) * (seg_ids == seg_before)[:, None]
        own_pull = jnp.einsum(
            "th,thp,tn->hpn", carried_in, mixer_grad, output_map, precision=highest
        )
        state_grad = pass_state(through, own_pull, -1)
        (
            value_heads_grad,
            input_grad_map,
            output_grad_map,
            step_raw_grad,
            stepb_grad,
            rate_grad,
            skip_grad,
            _,
        ) = ssd_back((mixer_grad, state_grad))
        (
            value_raw_grad,
            coupling_raw_grad,
            value_rim_grad,
            coupling_rim_grad,
            convw_grad,
            convb_grad,
            couplingw_grad,
            couplingb_grad,
        ) = conv_back(
            (
                value_heads_grad.reshape(tok_count, inner_local),
                jnp.concatenate([input_grad_map, output_grad_map], axis=1),
            )
        )
        value_back, coupling_back = pass_rim(value_rim_grad, coupling_rim_grad, -1)
        value_raw_grad = value_raw_grad + jnp.concatenate(
            [jnp.zeros((tok_count - rim_rows, inner_local), jnp.float32), value_back]
        )
        coupling_raw_grad = coupling_raw_grad + jnp.concatenate(
            [jnp.zeros((tok_count - rim_rows, 2 * state_size), jnp.float32), coupling_back]
        )
        proj_grad = jnp.concatenate([gate_grad, value_raw_grad], axis=1).astype(jnp.bfloat16)
        step_grad_low = step_raw_grad.astype(jnp.bfloat16)
        in_total = in_total + contract_rows(normed, proj_grad)
        step_total = step_total + contract_rows(normed, step_grad_low)
        normed_part = contract_cols(proj_grad, in_full) + contract_cols(step_grad_low, step_full)
        normed_sum, coupling_sum, couplingw_sum, couplingb_sum = lax.psum(
            (normed_part, coupling_raw_grad, couplingw_grad, couplingb_grad), "tensor"
        )
        coupling_grad_low = coupling_sum.astype(jnp.bfloat16)
        coupling_total = coupling_total + contract_rows(normed, coupling_grad_low)
        normed_grad = normed_sum + contract_cols(coupling_grad_low, coupling_full)
        gain_total = gain_total + jnp.sum(normed_grad * x_hat, axis=0)
        hat_grad = normed_grad * norm_gain
        input_grads.append(
            (
                cot_row.astype(jnp.float32)
                + inv_rms * (hat_grad - x_hat * jnp.mean(hat_grad * x_hat, axis=-1, keepdims=True))
            ).astype(jnp.bfloat16)
        )
        convw_total = convw_total + convw_grad
        convb_total = convb_total + convb_grad
        couplingw_total = couplingw_total + couplingw_sum
        couplingb_total = couplingb_total + couplingb_sum
        stepb_total = stepb_total + stepb_grad
        rate_total = rate_total + rate_grad
        skip_total = skip_total + skip_grad
    in_grid = in_total.reshape(model_width, 2, inner_local)
    in_shard, coupling_shard, step_shard, out_shard = (
        lax.psum_scatter(in_grid, "fsdp", scatter_dimension=0, tiled=True),
        lax.psum_scatter(coupling_total, "fsdp", scatter_dimension=0, tiled=True),
        lax.psum_scatter(step_total, "fsdp", scatter_dimension=0, tiled=True),
        lax.psum_scatter(out_total, "fsdp", scatter_dimension=1, tiled=True),
    )
    in_grad, coupling_grad, step_grad, out_grad_w = lax.psum(
        (in_shard, coupling_shard, step_shard, out_shard), "context"
    )
    (
        gain_grad,
        convw_all,
        convb_all,
        couplingw_all,
        couplingb_all,
        stepb_all,
        rate_all,
        skip_all,
        inner_all,
    ) = lax.psum(
        (
            gain_total,
            convw_total,
            convb_total,
            couplingw_total,
            couplingb_total,
            stepb_total,
            rate_total,
            skip_total,
            inner_total_grad,
        ),
        ("fsdp", "context"),
    )
    return (
        jnp.stack(block_outs)[:, None],
        jnp.stack(input_grads)[:, None],
        gain_grad,
        in_grad,
        coupling_grad,
        step_grad,
        out_grad_w,
        convw_all,
        convb_all,
        couplingw_all,
        couplingb_all,
        stepb_all,
        rate_all,
        skip_all,
        inner_all,
    )


def solution(mesh):
    return jax.shard_map(
        shards,
        mesh=mesh,
        in_specs=(
            P(None, "fsdp", "context", None),
            P(None, "fsdp", None),
            P(None, "fsdp", None),
            P(None, "fsdp", "context", None),
            P(),
            P("fsdp", None, "tensor"),
            P("fsdp", None),
            P("fsdp", "tensor"),
            P("tensor", "fsdp"),
            P(None, "tensor"),
            P("tensor"),
            P(),
            P(),
            P("tensor"),
            P("tensor"),
            P("tensor"),
            P("tensor"),
        ),
        out_specs=(
            P(None, "fsdp", "context", None),
            P(None, "fsdp", "context", None),
            P(),
            P("fsdp", None, "tensor"),
            P("fsdp", None),
            P("fsdp", "tensor"),
            P("tensor", "fsdp"),
            P(None, "tensor"),
            P("tensor"),
            P(),
            P(),
            P("tensor"),
            P("tensor"),
            P("tensor"),
            P("tensor"),
        ),
        check_vma=False,
    )
```

profile of v0, /device:TPU:0, one launch (start us, length us, event | category | flops | bytes accessed | tf_op | source)
XLA Modules:
  0.0 3640.1 jit_solution(4257997559496266867)
XLA Ops:
  27.9 32.3 all_gather.23
  83.3 47.3 %all-gather.16.cloned.1.call-done = bf16[1,1,1024,2048]{3,2,1,0:T(8,128)(2,1)} async-done(((bf16[1,1,512,2048]{3,2,1,0:T(8,128)(2,1)}), bf16[1,1,1024,2048]{3,2,1,0:T(8,128)(2,1)}) %all-gather.16.cloned.1.call-update) | async-done | bytes 4194320 | tf_op jit(solution)/shard_map/all_gather | solution.py:197
  148.2 24.8 all-gather.10.cloned.1.call-done
  201.5 97.6 %all-gather.12.cloned.1.call-done = bf16[2048,2048]{1,0:T(8,128)(2,1)} async-done(((bf16[2048,256]{1,0:T(8,128)(2,1)}), bf16[2048,2048]{1,0:T(8,128)(2,1)}) %all-gather.12.cloned.1.call-update) | async-done | bytes 8388624 | tf_op jit(solution)/shard_map/all_gather | solution.py:204
  309.7 217.2 %all-gather.8.cloned.1.call-done = bf16[2048,2,2048]{2,1,0:T(2,128)(2,1)} async-done(((bf16[256,2,2048]{2,1,0:T(2,128)(2,1)}), bf16[2048,2,2048]{2,1,0:T(2,128)(2,1)}) %all-gather.8.cloned.1.call-update) | async-done | bytes 16777232 | tf_op jit(solution)/shard_map/all_gather | solution.py:201
  526.9 17.4 copy.504
  577.1 15.5 collective-permute-start
  696.9 322.6 %while.187 = (s32[]{:T(128)}, f32[32,64,128]{2,1,0:T(8,128)S(1)}, f32[2,256,32,64]{1,3,2,0:T(8,128)}, pred[2,256,256,32]{2,1,3,0:T(32,128)(4,1)}, f32[2,256,256,...) while((s32[]{:T(128)}, f32[32,64,128]{2,1,0:T(8,128)S(1)}, ...), condition=%wide.region_18.21_spmd.clone, body=%wide.region_15.20_spmd.clone.sunk | while | flops 3343632640 | bytes 243146160 | solution.py:100
  706.8 31.5 broadcast_multiply_fusion.11
  738.3 22.3 copy.613
  760.6 22.2 copy.614
  794.1 22.3 copy.612
  867.9 31.5 broadcast_multiply_fusion.11
  899.4 22.3 copy.613
  921.7 22.2 copy.614
  955.0 22.3 copy.612
  1081.2 306.8 %while.186 = (s32[]{:T(128)}, f32[32,64,128]{2,1,0:T(8,128)}, f32[2,256,32,64]{1,3,2,0:T(8,128)}, pred[2,256,256,32]{2,1,3,0:T(32,128)(4,1)}, f32[2,256,256,32]{...) while((s32[]{:T(128)}, f32[32,64,128]{2,1,0:T(8,128)}, ...), condition=%wide.region_7.10_spmd.clone, body=%wide.region_4.9_spmd.clone.sunk | while | flops 3343632640 | bytes 239088688 | solution.py:100
  1086.1 31.4 broadcast_multiply_fusion.10
  1117.5 22.1 copy.606
  1139.6 22.2 copy.607
  1173.0 22.2 copy.605
  1239.3 31.4 broadcast_multiply_fusion.10
  1270.6 22.1 copy.606
  1292.7 22.2 copy.607
  1326.2 22.2 copy.605
  1421.7 14.7 multiply_reduce_fusion.3
  1438.8 20.3 multiply_reduce_fusion.4
  1522.9 127.5 %while.185 = (s32[]{:T(128)}, f32[32,64,128]{2,1,0:T(8,128)S(1)}, f32[2,256,32,64]{1,3,2,0:T(8,128)}, f32[2,256,128]{2,1,0:T(8,128)}, f32[2,256,128]{2,1,0:T(8,1...) while((s32[]{:T(128)}, f32[32,64,128]{2,1,0:T(8,128)S(1)}, ...), condition=%wide.region_50.53_spmd, body=%wide.region_40.52_spmd.sunk | while | flops 6668500992 | bytes 139778672 | solution.py:100
  1546.0 15.5 fusion.580
  1609.6 15.5 fusion.580
  1655.6 162.0 %while.184 = (s32[]{:T(128)}, f32[32,64,128]{2,1,0:T(8,128)S(1)}, f32[2,256,32,64]{1,3,2,0:T(8,128)}, f32[2,256,128]{2,1,0:T(8,128)}, f32[2,256,128]{2,1,0:T(8,1...) while((s32[]{:T(128)}, f32[32,64,128]{2,1,0:T(8,128)S(1)}, ...), condition=%wide.region_34.37_spmd, body=%wide.region_24.36_spmd.sunk | while | flops 6668500992 | bytes 141351632 | solution.py:100
  1698.9 16.2 fusion.556
  1766.1 16.2 fusion.556
  1851.7 14.8 multiply_reduce_fusion.13
  1910.7 17.6 fusion.272
  1930.2 29.0 convolution_add_fusion.4
  1959.2 42.6 %reshape.1094 = f32[2048,2,2048]{2,1,0:T(2,128)} reshape(f32[2048,4096]{1,0:T(8,128)} %convolution_add_fusion.4) | data formatting | bytes 67108864 | tf_op jit(solution)/shard_map/reshape | solution.py:398
  2025.3 13.6 fusion.283
  2081.4 15.9 convolution_add_fusion.7
  2097.3 15.1 convolution_add_fusion.6
  2114.2 861.2 %all-reduce.52.cloned.1.call-done = f32[2048,2,2048]{2,1,0:T(2,128)} async-done(((f32[2048,2,2048]{2,1,0:T(2,128)}), f32[2048,2,2048]{2,1,0:T(2,128)}) %all-reduce.52.cloned.1.call-update) | async-done | bytes 33554448
  2981.8 64.2 %reduce-scatter.4.cloned.1.call-done = f32[256,256]{1,0:T(8,128)} async-done(((f32[2048,256]{1,0:T(8,128)}), f32[256,256]{1,0:T(8,128)}) %reduce-scatter.4.cloned.1.call-update) | async-done | bytes 262160 | tf_op jit(solution)/shard_map/reduce_scatter | solution.py:401
  3046.0 285.5 %reduce-scatter.8.cloned.1.call-done = f32[2048,256]{1,0:T(8,128)} async-done(((f32[2048,2048]{1,0:T(8,128)}), f32[2048,256]{1,0:T(8,128)}) %reduce-scatter.8.cloned.1.call-update) | async-done | bytes 2097168 | tf_op jit(solution)/shard_map/reduce_scatter | solution.py:403
  3341.9 54.0 %reduce-scatter.6.cloned.1.call-done = f32[256,32]{0,1:T(8,128)} async-done(((f32[2048,32]{0,1:T(8,128)}), f32[256,32]{0,1:T(8,128)}) %reduce-scatter.6.cloned.1.call-update) | async-done | bytes 32784 | tf_op jit(solution)/shard_map/reduce_scatter | solution.py:402
  3405.7 53.1 %all-reduce.54.cloned.1.call-done = (f32[512,2048]{1,0:T(8,128)}, f32[512,2048]{1,0:T(8,128)}, f32[512,2048]{1,0:T(8,128)}, f32[512,2048]{1,0:T(8,128)}) async-done(((f32[512,2048]{1,0:T(8,128)}, f32[512,2048]{1,0:T(8,128)}, f32[512,2048]{1,0:T(8,128)}, f32[512,2048]{1,0:T(8,128)}), (f32[512,2048]{1,0:T(8,128)}, f32[512,2048]{1,0:T(8,128)}, f32[512,2048]{1,0:T(8,128)}, ...) | async-done | bytes 16777232 | tf_op jit(solution)/shard_map/psum | solution.py:317
  3467.2 79.1 %all-reduce.41 = (f32[2048]{0:T(1024)}, f32[4,2048]{1,0:T(4,128)}, f32[2048]{0:T(1024)}, f32[4,256]{1,0:T(4,128)}, f32[256]{0:T(256)}, /*index=5*/f32[32]{0:T(128)}, f32[32]{0:T(128)}, f32[32]{0:T(128)}, f32[2048]{0:T(1024)}) all-reduce(f32[2048]{0:T(1024)S(1)} %add.819, ...), channel_id=1, replica_groups=mesh['fsdp'=8,'context'=2,'tensor'=2] {'fsdp','context'}, use_global_device_ids=true, to_apply=%region_56.59 | all-reduce | flops 15712 | bytes 125696 | tf_op jit(solution)/shard_map/psum | solution.py:418
  3546.3 15.1 fusion.276
  3567.8 57.1 %all-reduce.56.cloned.1.call-done = (f32[256,2,2048]{2,1,0:T(2,128)}, f32[256,256]{1,0:T(8,128)}, f32[2048,256]{1,0:T(8,128)}) async-done(((f32[256,2,2048]{2,1,0:T(2,128)}, f32[256,256]{1,0:T(8,128)}, f32[2048,256]{1,0:T(8,128)}), (f32[256,2,2048]{2,1,0:T(2,128)}, f32[256,256]{1,0:T(8,128)}, f32[2048,256]{1,0:T(8,128)})) %all-reduce.56.cloned.1.call-update) | async-done | bytes 6553616 | tf_op jit(solution)/shard_map/psum | solution.py:405
  (1048 shorter events, 1022.4 us)
Async XLA Ops:
  7.2 69.0 %all-gather.14.cloned.1.call-start = ((), (), s32[]{:S(2)}) async-start(), calls=%async_computation.9 | async-start | bytes 6291456 | tf_op jit(solution)/shard_map/all_gather | solution.py:197
  12.1 118.5 %all-gather.16.cloned.1.call-start = ((), (), s32[]{:S(2)}) async-start(), calls=%async_computation.10 | async-start | bytes 6291456 | tf_op jit(solution)/shard_map/all_gather | solution.py:197
  12.9 160.1 %all-gather.10.cloned.1.call-start = ((), (), s32[]{:S(2)}) async-start(), calls=%async_computation.4 | async-start | bytes 1179648 | tf_op jit(solution)/shard_map/all_gather | solution.py:202
  13.6 285.5 %all-gather.12.cloned.1.call-start = ((), (), s32[]{:S(2)}) async-start(), calls=%async_computation.5 | async-start | bytes 9437184 | tf_op jit(solution)/shard_map/all_gather | solution.py:204
  14.2 512.7 %all-gather.8.cloned.1.call-start = ((), (), s32[]{:S(2)}) async-start(), calls=%async_computation.3 | async-start | bytes 18874368 | tf_op jit(solution)/shard_map/all_gather | solution.py:201
  14.8 2960.7 %all-reduce.52.cloned.1.call-start = ((), (), s32[]{:S(2)}) async-start(), calls=%async_computation.11 | async-start | bytes 67108864
  60.2 85.7 %copy-start.72 = (bf16[2048,32]{0,1:T(8,128)(2,1)}, bf16[2048,32]{0,1:T(8,128)(2,1)S(1)}, u32[]{:S(2)}) copy-start(bf16[2048,32]{0,1:T(8,128)(2,1)S(1)} %all_gather.23) | copy-start | bytes 393220
  74.8 67.2 %copy-start.170 = (pred[512]{0:T(512)(128)(4,1)}, pred[512]{0:T(512)(128)(4,1)S(1)}, u32[]{:S(2)}) copy-start(pred[512]{0:T(512)(128)(4,1)S(1)} %get-tuple-element.3627) | copy-start | bytes 1540
  76.1 545.4 %copy-start.109 = (f32[1,2048]{1,0:T(1,128)}, f32[1,2048]{1,0:T(1,128)S(1)}, u32[]{:S(2)}) copy-start(f32[1,2048]{1,0:T(1,128)S(1)} %get-tuple-element.3729) | copy-start | bytes 24580
  177.1 16.2 collective-permute-start.4
  187.3 9.8 collective-permute-start.1
  196.3 407.3 %copy-start.59 = (f32[512,256]{1,0:T(8,128)}, f32[512,256]{1,0:T(8,128)S(1)}, u32[]{:S(2)}) copy-start(f32[512,256]{1,0:T(8,128)S(1)} %get-tuple-element.3631) | copy-start | bytes 1572868
  200.6 438.6 %copy-start.57 = (f32[512,256]{1,0:T(8,128)}, f32[512,256]{1,0:T(8,128)S(1)}, u32[]{:S(2)}) copy-start(f32[512,256]{1,0:T(8,128)S(1)} %get-tuple-element.3623) | copy-start | bytes 1572868
  556.2 36.4 collective-permute-start.3
  577.1 44.4 %collective-permute-start = (f32[3,2048]{1,0:T(4,128)}, f32[3,2048]{1,0:T(4,128)}, u32[]{:S(2)}, u32[]{:S(2)}) collective-permute-start(f32[3,2048]{1,0:T(4,128)} %slice.383), channel_id=1, source_target_pairs={{0,2},{1,3},{4,6},{5,7},{8,10},{9,11},{12,14},{13,15},{16,18},{17,... | collective-permute-start | bytes 73736 | tf_op jit(solution)/shard_map/ppermute | solution.py:15
  615.1 35.8 collective-permute-start.5
  646.0 391.4 %collective-permute-start.2 = (f32[32,64,128]{2,1,0:T(8,128)}, f32[32,64,128]{2,1,0:T(8,128)}, u32[]{:S(2)}, u32[]{:S(2)}) collective-permute-start(f32[32,64,128]{2,1,0:T(8,128)} %fusion.292), channel_id=1, source_target_pairs={{0,2},{1,3},{4,6},{5,7},{8,10},{9,11},{12,14},{13,15},{16,18},{17,... | collective-permute-start | bytes 3145736 | tf_op jit(solution)/shard_map/while/body/eval_jaxpr/ppermute | solution.py:15
  1471.3 46.4 %collective-permute-start.9 = (f32[32,64,128]{2,1,0:T(8,128)}, f32[32,64,128]{2,1,0:T(8,128)S(1)}, u32[]{:S(2)}, u32[]{:S(2)}) collective-permute-start(f32[32,64,128]{2,1,0:T(8,128)} %fusion.301), channel_id=1, source_target_pairs={{2,0},{3,1},{6,4},{7,5},{10,8},{11,9},{14,12},{15,13},{18,16},{19,... | collective-permute-start | bytes 3145736 | tf_op jit(solution)/shard_map/while/body/eval_jaxpr/ppermute | solution.py:15
  1516.4 134.0 %collective-permute-start.6 = (f32[32,64,128]{2,1,0:T(8,128)}, f32[32,64,128]{2,1,0:T(8,128)S(1)}, u32[]{:S(2)}, u32[]{:S(2)}) collective-permute-start(f32[32,64,128]{2,1,0:T(8,128)} %fusion.298), channel_id=1, source_target_pairs={{2,0},{3,1},{6,4},{7,5},{10,8},{11,9},{14,12},{15,13},{18,16},{19,... | collective-permute-start | bytes 3145736 | tf_op jit(solution)/shard_map/while/body/eval_jaxpr/ppermute | solution.py:15
  1897.7 11.0 collective-permute-start.7
  1906.8 21.5 collective-permute-start.10
  2001.9 1044.1 %reduce-scatter.4.cloned.1.call-start = ((), (), s32[]{:S(2)}) async-start(), calls=%async_computation.6 | async-start | bytes 2359296 | tf_op jit(solution)/shard_map/reduce_scatter | solution.py:401
  2006.8 5.6 collective-permute-start.8
  2008.1 5.6 collective-permute-start.11
  2025.2 1306.3 %reduce-scatter.8.cloned.1.call-start = ((), (), s32[]{:S(2)}) async-start(), calls=%async_computation.8 | async-start | bytes 18874368 | tf_op jit(solution)/shard_map/reduce_scatter | solution.py:403
  2051.5 1344.4 %reduce-scatter.6.cloned.1.call-start = ((), (), s32[]{:S(2)}) async-start(), calls=%async_computation.7 | async-start | bytes 294912 | tf_op jit(solution)/shard_map/reduce_scatter | solution.py:402
  2081.1 1377.7 %all-reduce.54.cloned.1.call-start = ((), (), s32[]{:S(2)}) async-start(), calls=%async_computation.12 | async-start | bytes 33554432 | tf_op jit(solution)/shard_map/psum | solution.py:317
  2112.4 1512.5 %all-reduce.56.cloned.1.call-start = ((), (), s32[]{:S(2)}) async-start(), calls=%async_computation.13 | async-start | bytes 13107200 | tf_op jit(solution)/shard_map/psum | solution.py:405
  2981.7 352.4 %copy-start.141 = (f32[2048]{0:T(1024)S(1)}, f32[2048]{0:T(1024)}, u32[]{:S(2)}) copy-start(f32[2048]{0:T(1024)} %get-tuple-element.3734) | copy-start | bytes 24580
  2981.7 352.5 %copy-start.140 = (f32[2048]{0:T(1024)S(1)}, f32[2048]{0:T(1024)}, u32[]{:S(2)}) copy-start(f32[2048]{0:T(1024)} %get-tuple-element.3609) | copy-start | bytes 24580
  2981.7 352.6 %copy-start.178 = (f32[2048]{0:T(1024)S(1)}, f32[2048]{0:T(1024)}, u32[]{:S(2)}) copy-start(f32[2048]{0:T(1024)} %get-tuple-element.3293) | copy-start | bytes 24580
  2981.7 356.4 %copy-start.146 = (f32[2048]{0:T(1024)S(1)}, f32[2048]{0:T(1024)}, u32[]{:S(2)}) copy-start(f32[2048]{0:T(1024)} %get-tuple-element.3296) | copy-start | bytes 24580
  2981.7 356.4 %copy-start.151 = (f32[2048]{0:T(1024)S(1)}, f32[2048]{0:T(1024)}, u32[]{:S(2)}) copy-start(f32[2048]{0:T(1024)} %get-tuple-element.3295) | copy-start | bytes 24580
  2981.7 356.4 %copy-start.142 = (f32[2048]{0:T(1024)S(1)}, f32[2048]{0:T(1024)}, u32[]{:S(2)}) copy-start(f32[2048]{0:T(1024)} %get-tuple-element.3285) | copy-start | bytes 24580
  2981.7 356.4 %copy-start.143 = (f32[2048]{0:T(1024)S(1)}, f32[2048]{0:T(1024)}, u32[]{:S(2)}) copy-start(f32[2048]{0:T(1024)} %get-tuple-element.3286) | copy-start | bytes 24580
  2981.7 356.4 %copy-start.144 = (f32[2048]{0:T(1024)S(1)}, f32[2048]{0:T(1024)}, u32[]{:S(2)}) copy-start(f32[2048]{0:T(1024)} %get-tuple-element.3287) | copy-start | bytes 24580
  2981.7 356.4 %copy-start.145 = (f32[2048]{0:T(1024)S(1)}, f32[2048]{0:T(1024)}, u32[]{:S(2)}) copy-start(f32[2048]{0:T(1024)} %get-tuple-element.3297) | copy-start | bytes 24580
  2981.7 356.4 %copy-start.147 = (f32[2048]{0:T(1024)S(1)}, f32[2048]{0:T(1024)}, u32[]{:S(2)}) copy-start(f32[2048]{0:T(1024)} %get-tuple-element.3288) | copy-start | bytes 24580
  2981.7 356.4 %copy-start.148 = (f32[2048]{0:T(1024)S(1)}, f32[2048]{0:T(1024)}, u32[]{:S(2)}) copy-start(f32[2048]{0:T(1024)} %get-tuple-element.3289) | copy-start | bytes 24580
  2981.8 356.4 %copy-start.149 = (f32[2048]{0:T(1024)S(1)}, f32[2048]{0:T(1024)}, u32[]{:S(2)}) copy-start(f32[2048]{0:T(1024)} %get-tuple-element.3290) | copy-start | bytes 24580
  2981.8 356.4 %copy-start.150 = (f32[2048]{0:T(1024)S(1)}, f32[2048]{0:T(1024)}, u32[]{:S(2)}) copy-start(f32[2048]{0:T(1024)} %get-tuple-element.3298) | copy-start | bytes 24580
  2981.8 356.5 %copy-start.66 = (bf16[2048,256]{1,0:T(8,128)(2,1)S(1)}, bf16[2048,256]{1,0:T(8,128)(2,1)}, u32[]{:S(2)}) copy-start(bf16[2048,256]{1,0:T(8,128)(2,1)} %all-gather.10.cloned.1.call-done) | copy-start | bytes 3145732
  3331.5 127.3 %copy-start.16 = (bf16[512,2048]{1,0:T(8,128)(2,1)S(1)}, bf16[512,2048]{1,0:T(8,128)(2,1)}, u32[]{:S(2)}) copy-start(bf16[512,2048]{1,0:T(8,128)(2,1)} %copy-done.15) | copy-start | bytes 6291460
  3331.6 127.3 %copy-start.139 = (f32[512]{0:T(512)S(1)}, f32[512]{0:T(512)}, u32[]{:S(2)}) copy-start(f32[512]{0:T(512)} %copy-done.138) | copy-start | bytes 6148
  3458.9 87.5 %copy-start.171 = (pred[512]{0:T(512)(128)(4,1)S(1)}, pred[512]{0:T(512)(128)(4,1)}, u32[]{:S(2)}) copy-start(pred[512]{0:T(512)(128)(4,1)} %copy-done.170) | copy-start | bytes 1540
  3458.9 87.5 %copy-start.173 = (pred[512]{0:T(512)(128)(4,1)S(1)}, pred[512]{0:T(512)(128)(4,1)}, u32[]{:S(2)}) copy-start(pred[512]{0:T(512)(128)(4,1)} %copy-done.172) | copy-start | bytes 1540
  3458.9 87.4 %copy-start.174 = (f32[512]{0:T(512)S(1)}, f32[512]{0:T(512)}, u32[]{:S(2)}) copy-start(f32[512]{0:T(512)} %compare_convert_fusion.15) | copy-start | bytes 6148
  3458.9 87.4 %copy-start.175 = (f32[512]{0:T(512)S(1)}, f32[512]{0:T(512)}, u32[]{:S(2)}) copy-start(f32[512]{0:T(512)} %compare_convert_fusion.17) | copy-start | bytes 6148
  (240 other events, 2693.5 us)
Sparse Core Ops, SparseCore 0:
  12.2 59.4 all-gather.13
  73.8 56.7 all-gather.15
  132.7 40.1 all-gather.9
  174.9 124.1 all-gather.11
  301.0 225.7 all-gather.7
  2002.0 973.4 all-reduce.51
  2979.0 66.9 reduce-scatter.3
  3049.8 281.6 reduce-scatter.7
  3335.2 60.6 reduce-scatter.5
  3399.4 59.3 all-reduce.53
  3461.4 163.3 all-reduce.55
where the time goes:
time: 3660 us; the launch traced here: 3640 us
  waiting for transfers between devices  1770 us (48%)
  local copies, waits for them, and re-layouts  791 us (22%)
  matrix products  484 us (13%)
  other arithmetic  369 us (10%)
  blocking collectives  133 us (4%)
  starting transfers between devices  37.4 us (1%)
    unnamed x12, waiting for transfers between devices  864 us
    dynamic_update_slice x60, local copies, waits for them, and re-layouts, ssd_part(): state_final, span_out = lax.scan(span_step, state_start, span_parts)  381 us
    reduce_scatter x1, waiting for transfers between devices, shards(): lax.psum_scatter(out_total, 'fsdp', scatter_dimension=1, tiled=True)  286 us
    all_gather x1, waiting for transfers between devices, shards(): lax.all_gather(in_weight, 'fsdp', axis=0, tiled=True)  217 us
    dot_general x12, matrix products, span_step(): jnp.einsum('ijh,jhp->ihp', gram_mat[:, :, None] * decays, step_part[:, :,...  150 us
    mul x4, other arithmetic, span_step(): gram_mat[:, :, None] * decays  126 us
    another operation x80, local copies, waits for them, and re-layouts  101 us
    all_gather x1, waiting for transfers between devices, shards(): lax.all_gather(out_weight, 'fsdp', axis=1, tiled=True)  97.6 us
  transfers between devices with their start and end apart: 23, of which 12 were waited for; matrix products, arithmetic and copies ran while one was open for 24% of the time, Pallas kernels for 0%

commit v1 on v0

v1 whole, which is shorter than its diff:
```python
import functools

import jax
import jax.numpy as jnp
import numpy as np
from jax import lax
from jax.experimental import pallas as pl
from jax.experimental.pallas import tpu as pltpu
from jax.sharding import PartitionSpec as P

CHUNK = 128
LANES = 128
f32 = jnp.float32
bf16 = jnp.bfloat16
epsilon = 1e-05


def split_two(value):
    high = value.astype(bf16)
    return high, (value - high.astype(f32)).astype(bf16)


def split_three(value):
    high = value.astype(bf16)
    rest = value - high.astype(f32)
    middle = rest.astype(bf16)
    return high, middle, (rest - middle.astype(f32)).astype(bf16)


def mm(left, right):
    return jnp.dot(left, right, preferred_element_type=f32)


def mm_nt(left, right):
    return lax.dot_general(left, right, (((1,), (1,)), ((), ())), preferred_element_type=f32)


def mm_three(left, right):
    wide = mm(left[0], jnp.concatenate([right[0], right[1]], axis=1))
    count = right[0].shape[1]
    return wide[:, :count] + wide[:, count:] + mm(left[1], right[0])


def mm_three_nt(left, right):
    return mm_nt(left[0], right[0]) + mm_nt(left[0], right[1]) + mm_nt(left[1], right[0])


def packed_parts(value, heads):
    high, middle, lowest = split_three(value)
    joined = (
        high.astype(f32)
        + pltpu.roll(middle.astype(f32), heads, 1)
        + pltpu.roll(lowest.astype(f32), 2 * heads, 1)
    )
    return joined.astype(bf16)


def segment_at(position, first_end, second_end):
    first_part = (position >= first_end).astype(jnp.int32)
    second_part = (position >= second_end).astype(jnp.int32)
    return jnp.where(position < 0, -1, first_part + second_part)


def chunk_frame(marks, chunk, step_raw, step_bias, rate, heads):
    first_end, second_end, base = marks[0], marks[1], marks[2]
    start = base + chunk * CHUNK
    rows = start + lax.broadcasted_iota(jnp.int32, (CHUNK, LANES), 0)
    columns = start + lax.broadcasted_iota(jnp.int32, (CHUNK, CHUNK), 1)
    seg_rows = segment_at(rows, first_end, second_end)
    seg_columns = segment_at(columns, first_end, second_end)
    seg_prior = segment_at(start - 1, first_end, second_end)
    seg_last = segment_at(start + CHUNK - 1, first_end, second_end)
    same = [
        (segment_at(rows - lag, first_end, second_end) == seg_rows).astype(f32) for lag in range(4)
    ]
    shifted = step_raw + step_bias
    step = jnp.maximum(shifted, 0.0) + jnp.log1p(jnp.exp(-jnp.abs(shifted)))
    lanes = lax.broadcasted_iota(jnp.int32, (CHUNK, LANES), 1)
    step = jnp.where(lanes < heads, step, 0.0)
    log_decay = -step * rate
    row_ids = lax.broadcasted_iota(jnp.int32, (CHUNK, CHUNK), 0)
    column_ids = lax.broadcasted_iota(jnp.int32, (CHUNK, CHUNK), 1)
    lower = (row_ids >= column_ids).astype(bf16)
    parts = split_three(log_decay)
    cumulative = mm(lower, parts[0]) + mm(lower, parts[1]) + mm(lower, parts[2])
    last = cumulative[CHUNK - 1 :, :]
    carry = jnp.exp(cumulative) * (seg_rows == seg_prior).astype(f32)
    tail = jnp.exp(last - cumulative) * (seg_rows == seg_last).astype(f32)
    live = lanes < heads
    carry = jnp.where(live, carry, 0.0)
    tail = jnp.where(live, tail, 0.0)
    return dict(
        seg_rows=seg_rows,
        seg_columns=seg_columns,
        row_ids=row_ids,
        column_ids=column_ids,
        same=same,
        step=step,
        shifted=shifted,
        cumulative=cumulative,
        carry=carry,
        tail=tail,
    )


def conv_sum(current, halo, weights, biases, same):
    full = jnp.concatenate([halo, current], axis=0)
    total = biases + weights(0) * current
    for lag in range(1, 4):
        total = total + weights(lag) * (pltpu.roll(full, lag, 0)[8:] * same[lag])
    return total


def logistic(value):
    return 1.0 / (1.0 + jnp.exp(-value))


def forward_kernel(
    heads,
    marks,
    vraw,
    vprev,
    vrim,
    craw,
    cprev,
    crim,
    sraw,
    cw,
    cb,
    ccw,
    ccb,
    sbias,
    rate,
    skip,
    sel,
    selcol,
    y_out,
    st_out,
    fin_out,
    bc_out,
    carry_out,
    cd_out,
    state,
    cumt,
    stack,
    cumpack,
    halo,
    same_s,
    bias_s,
    gram_s,
    cd_s,
    cparts,
    btparts,
):
    chunk = pl.program_id(0)
    chunks = pl.num_programs(0)
    width = state.shape[0]

    @pl.when(chunk == 0)
    def _():
        state[...] = jnp.zeros_like(state)
        cd_s[...] = jnp.ones_like(cd_s)
        cd_out[...] = jnp.zeros_like(cd_out)
        halo[...] = vrim[...]

    @pl.when(chunk > 0)
    def _():
        halo[...] = vprev[...]

    frame = chunk_frame(marks, chunk, sraw[...], sbias[...], rate[...], heads)
    same = frame["same"]
    for lag in range(1, 4):
        same_s[lag - 1] = same[lag]
    joined = (frame["seg_rows"] == frame["seg_columns"]) & (frame["row_ids"] >= frame["column_ids"])
    bias_s[...] = jnp.where(joined, 0.0, -1e30)
    stack[0:CHUNK, :] = packed_parts(frame["step"], heads)
    stack[CHUNK : 2 * CHUNK, :] = packed_parts(frame["carry"], heads)
    stack[2 * CHUNK : 3 * CHUNK, :] = packed_parts(frame["tail"], heads)
    cumpack[...] = packed_parts(frame["cumulative"], heads)
    cumt[...] = jnp.transpose(frame["cumulative"])
    coupling_halo = jnp.where(chunk == 0, crim[...], cprev[...])
    wide_same = [None] + [jnp.concatenate([same[lag], same[lag]], axis=1) for lag in range(1, 4)]
    pre = conv_sum(
        craw[...], coupling_halo, lambda lag: ccw[lag : lag + 1, :], ccb[...], wide_same
    )
    coupled = pre * logistic(pre)
    bc_out[...] = coupled
    b_part = split_two(coupled[:, :width])
    c_part = split_two(coupled[:, width:])
    gram_s[...] = mm_three_nt(c_part, b_part)
    cparts[0] = c_part[0]
    cparts[1] = c_part[1]
    turned = jnp.transpose(coupled[:, :width])
    bt_part = split_two(turned)
    btparts[0] = bt_part[0]
    btparts[1] = bt_part[1]
    lane = lax.broadcasted_iota(jnp.int32, (CHUNK, LANES), 1)
    low_half = (lane < LANES // 2).astype(f32)
    high_half = 1.0 - low_half

    def pair(index, carried):
        cols = pl.ds(pl.multiple_of(index * LANES, LANES), LANES)
        wide = pl.ds(pl.multiple_of(index * 2 * LANES, 2 * LANES), 2 * LANES)
        pre_value = conv_sum(
            vraw[:, cols],
            halo[:, cols],
            lambda lag: cw[lag : lag + 1, cols],
            cb[:, cols],
            [None] + [same_s[lag - 1] for lag in range(1, 4)],
        )
        value = pre_value * logistic(pre_value)
        spread = mm(stack[...], sel[:, cols])
        step_e = spread[:CHUNK]
        carry_e = spread[CHUNK : 2 * CHUNK]
        tail_e = spread[2 * CHUNK :]
        inputs = step_e * value
        column = mm(cumpack[...], selcol[:, wide])
        row_pair = jnp.concatenate(
            [cumt[pl.ds(2 * index, 1), :], cumt[pl.ds(2 * index + 1, 1), :]], axis=1
        )
        bias = bias_s[...]
        gram = gram_s[...]
        mixing = jnp.concatenate([gram, gram], axis=1) * jnp.exp(
            column - row_pair + jnp.concatenate([bias, bias], axis=1)
        )
        mix_high, mix_low = split_two(mixing)
        in_low = split_two(inputs * low_half)
        in_high = split_two(inputs * high_half)
        diag_high = jnp.concatenate([in_low[0], in_high[0]], axis=0)
        diag_low = jnp.concatenate([in_low[1], in_high[1]], axis=0)
        both = mm(mix_high, jnp.concatenate([diag_high, diag_low], axis=1))
        inside = both[:, :LANES] + both[:, LANES:] + mm(mix_low, diag_high)
        held = state[:, cols]
        from_state = mm_three((cparts[0], cparts[1]), split_two(held))
        y_out[:, cols] = inside + carry_e * from_state + skip[:, cols] * value
        fresh = mm_three((btparts[0], btparts[1]), split_two(tail_e * inputs))
        through = carry_e[CHUNK - 1 :, :]
        st_out[0, :, cols] = held
        renewed = through * held + fresh
        state[:, cols] = renewed
        fin_out[:, cols] = renewed
        reach = cd_s[0:1, cols]
        carry_out[:, cols] = carry_e * reach
        cd_s[0:1, cols] = reach * through
        return carried

    eight_rows = lax.broadcasted_iota(jnp.int32, cd_out.shape, 0)
    cd_out[...] = jnp.where(eight_rows == chunk, cd_s[0:1, :], cd_out[...])
    lax.fori_loop(0, heads // 2, pair, 0, unroll=4)
    cd_out[...] = jnp.where(eight_rows == chunk + 1, cd_s[0:1, :], cd_out[...])


def selectors(heads, head_size):
    inner = heads * head_size
    head_of_lane = np.arange(inner) // head_size
    narrow = np.zeros((LANES, inner), np.float32)
    wide = np.zeros((LANES, heads * LANES), np.float32)
    head_of_wide = np.arange(heads * LANES) // LANES
    for part in range(3):
        narrow[part * heads + head_of_lane, np.arange(inner)] = 1.0
        wide[part * heads + head_of_wide, np.arange(heads * LANES)] = 1.0
    return narrow, wide


def whole(shape):
    return pl.BlockSpec(shape, lambda index, *_: (0,) * len(shape))


def forward_ssd(
    marks, micro, raw, rim, inner, twice, tokens, cw, cb, ccw, ccb, sbias, rate, skip, sel, selcol
):
    width = twice // 2
    chunks = tokens // CHUNK
    heads = inner // (LANES // 2)
    eighth = CHUNK // 8
    initial = micro * chunks

    def rows(count):
        return pl.BlockSpec((CHUNK, count), lambda chunk, *_: (chunk, 0))

    def part(count, start):
        return pl.BlockSpec((CHUNK, count), lambda chunk, *_: (initial + chunk, start // count))

    def before(count, start):
        return pl.BlockSpec(
            (8, count),
            lambda chunk, *_: (jnp.maximum((initial + chunk) * eighth - 1, 0), start // count),
        )

    def edge(count, start):
        return pl.BlockSpec((8, count), lambda *_: (0, start // count))

    return pl.pallas_call(
        functools.partial(forward_kernel, heads),
        grid_spec=pltpu.PrefetchScalarGridSpec(
            num_scalar_prefetch=1,
            grid=(chunks,),
            in_specs=[
                part(inner, 0),
                before(inner, 0),
                edge(inner, 0),
                part(twice, inner),
                before(twice, inner),
                edge(twice, inner),
                part(LANES, inner + twice),
                whole(cw.shape),
                whole(cb.shape),
                whole(ccw.shape),
                whole(ccb.shape),
                whole(sbias.shape),
                whole(rate.shape),
                whole(skip.shape),
                whole(sel.shape),
                whole(selcol.shape),
            ],
            out_specs=[
                rows(inner),
                pl.BlockSpec((1, width, inner), lambda chunk, *_: (chunk, 0, 0)),
                whole((width, inner)),
                rows(twice),
                rows(inner),
                whole((8, inner)),
            ],
            scratch_shapes=[
                pltpu.VMEM((width, inner), f32),
                pltpu.VMEM((LANES, CHUNK), f32),
                pltpu.VMEM((3 * CHUNK, LANES), bf16),
                pltpu.VMEM((CHUNK, LANES), bf16),
                pltpu.VMEM((8, inner), f32),
                pltpu.VMEM((3, CHUNK, LANES), f32),
                pltpu.VMEM((CHUNK, CHUNK), f32),
                pltpu.VMEM((CHUNK, CHUNK), f32),
                pltpu.VMEM((8, inner), f32),
                pltpu.VMEM((2, CHUNK, width), bf16),
                pltpu.VMEM((2, width, CHUNK), bf16),
            ],
        ),
        out_shape=[
            jax.ShapeDtypeStruct((tokens, inner), f32),
            jax.ShapeDtypeStruct((chunks, width, inner), f32),
            jax.ShapeDtypeStruct((width, inner), f32),
            jax.ShapeDtypeStruct((tokens, twice), f32),
            jax.ShapeDtypeStruct((tokens, inner), f32),
            jax.ShapeDtypeStruct((8, inner), f32),
        ],
        compiler_params=pltpu.CompilerParams(vmem_limit_bytes=40 * 1024 * 1024),
        cost_estimate=pl.CostEstimate(
            flops=20 * tokens * inner * 128 * 2, bytes_accessed=24 * tokens * inner, transcendentals=0
        ),
    )(marks, raw, raw, rim, raw, raw, rim, raw, cw, cb, ccw, ccb, sbias, rate, skip, sel, selcol)


def backward_kernel(
    heads,
    marks,
    vraw,
    vprev,
    vrim,
    craw,
    cprev,
    crim,
    sraw,
    grad,
    mixer,
    st_now,
    st_next,
    fin,
    entering,
    cd,
    pulled,
    cw,
    cb,
    ccw,
    ccb,
    sbias,
    rate,
    skip,
    sel,
    selcol,
    selt,
    vraw_g,
    vrim_g,
    craw_g,
    crim_g,
    sraw_g,
    cw_g,
    ccw_g,
    small_g,
    skip_g,
    state,
    cumt,
    stack,
    cumpack,
    halo,
    same_s,
    bias_s,
    gram_s,
    cparts,
    bparts,
    ctparts,
    rim_s,
    crim_s,
    dgram,
    dcoup,
    dhead,
    cd_s,
):
    step_id = pl.program_id(0)
    chunks = pl.num_programs(0)
    chunk = chunks - 1 - step_id
    width = state.shape[0]

    @pl.when(step_id == 0)
    def _():
        state[...] = pulled[...]
        rim_s[...] = jnp.zeros_like(rim_s)
        crim_s[...] = jnp.zeros_like(crim_s)
        cw_g[...] = jnp.zeros_like(cw_g)
        ccw_g[...] = jnp.zeros_like(ccw_g)
        small_g[...] = jnp.zeros_like(small_g)
        skip_g[...] = jnp.zeros_like(skip_g)

    @pl.when(chunk == 0)
    def _():
        halo[...] = vrim[...]

    @pl.when(chunk > 0)
    def _():
        halo[...] = vprev[...]

    frame = chunk_frame(marks, chunk, sraw[...], sbias[...], rate[...], heads)
    same = frame["same"]
    for lag in range(1, 4):
        same_s[lag - 1] = same[lag]
    joined = (frame["seg_rows"] == frame["seg_columns"]) & (frame["row_ids"] <= frame["column_ids"])
    bias_s[...] = jnp.where(joined, 0.0, -1e30)
    stack[0:CHUNK, :] = packed_parts(frame["step"], heads)
    stack[CHUNK : 2 * CHUNK, :] = packed_parts(frame["carry"], heads)
    stack[2 * CHUNK : 3 * CHUNK, :] = packed_parts(frame["tail"], heads)
    cumpack[...] = packed_parts(frame["cumulative"], heads)
    cumt[...] = jnp.transpose(frame["cumulative"])
    coupling_halo = jnp.where(chunk == 0, crim[...], cprev[...])
    wide_same = [None] + [jnp.concatenate([same[lag], same[lag]], axis=1) for lag in range(1, 4)]
    craw_now = craw[...]
    pre = conv_sum(craw_now, coupling_halo, lambda lag: ccw[lag : lag + 1, :], ccb[...], wide_same)
    csig = logistic(pre)
    coupled = pre * csig
    b_value = coupled[:, :width]
    c_value = coupled[:, width:]
    b_part = split_two(b_value)
    c_part = split_two(c_value)
    gram_s[...] = mm_three_nt(b_part, c_part)
    cparts[0] = c_part[0]
    cparts[1] = c_part[1]
    bparts[0] = b_part[0]
    bparts[1] = b_part[1]
    ct_part = split_two(jnp.transpose(c_value))
    ctparts[0] = ct_part[0]
    ctparts[1] = ct_part[1]
    dgram[...] = jnp.zeros_like(dgram)
    dcoup[...] = jnp.zeros_like(dcoup)
    dhead[...] = jnp.zeros_like(dhead)
    lane = lax.broadcasted_iota(jnp.int32, (CHUNK, LANES), 1)
    row = lax.broadcasted_iota(jnp.int32, (CHUNK, LANES), 0)
    low_half = (lane < LANES // 2).astype(f32)
    high_half = 1.0 - low_half
    last_row = (row == CHUNK - 1).astype(f32)
    is_end = step_id == 0
    eight_rows = lax.broadcasted_iota(jnp.int32, cd.shape, 0)
    for place in range(2):
        chosen = jnp.where(eight_rows == chunk + place, cd[...], 0.0)
        cd_s[place : place + 1, :] = jnp.sum(chosen, axis=0, keepdims=True)

    def pair(index, carried):
        cols = pl.ds(pl.multiple_of(index * LANES, LANES), LANES)
        wide = pl.ds(pl.multiple_of(index * 2 * LANES, 2 * LANES), 2 * LANES)
        raw = vraw[:, cols]
        full = jnp.concatenate([halo[:, cols], raw], axis=0)
        lagged = [raw] + [pltpu.roll(full, lag, 0)[8:] * same_s[lag - 1] for lag in range(1, 4)]
        pre_value = cb[:, cols]
        for lag in range(4):
            pre_value = pre_value + cw[lag : lag + 1, cols] * lagged[lag]
        sig = logistic(pre_value)
        value = pre_value * sig
        spread = mm(stack[...], sel[:, cols])
        step_e = spread[:CHUNK]
        carry_e = spread[CHUNK : 2 * CHUNK]
        tail_e = spread[2 * CHUNK :]
        inputs = step_e * value
        grads = grad[:, cols]
        column = mm(cumpack[...], selcol[:, wide])
        row_pair = jnp.concatenate(
            [cumt[pl.ds(2 * index, 1), :], cumt[pl.ds(2 * index + 1, 1), :]], axis=1
        )
        bias = bias_s[...]
        gram = gram_s[...]
        decays = jnp.exp(row_pair - column + jnp.concatenate([bias, bias], axis=1))
        mixing = jnp.concatenate([gram, gram], axis=1) * decays
        mix_high, mix_low = split_two(mixing)
        g_low = split_two(grads * low_half)
        g_high = split_two(grads * high_half)
        diag_high = jnp.concatenate([g_low[0], g_high[0]], axis=0)
        diag_low = jnp.concatenate([g_low[1], g_high[1]], axis=0)
        both = mm(mix_high, jnp.concatenate([diag_high, diag_low], axis=1))
        input_g = both[:, :LANES] + both[:, LANES:] + mm(mix_low, diag_high)
        held_g = state[:, cols]
        held_parts = split_two(held_g)
        input_g = input_g + tail_e * mm_three((bparts[0], bparts[1]), held_parts)
        in_parts = split_two(inputs)
        outer = mm_three_nt(in_parts, (diag_high, diag_low)) * decays
        dgram[...] += outer[:, :CHUNK] + outer[:, CHUNK:]
        reach_now = cd_s[0:1, cols]
        reach_next = cd_s[1:2, cols]
        arriving = entering[:, cols]
        held = st_now[0, :, cols] + reach_now * arriving
        next_own = jnp.where(is_end, fin[:, cols], st_next[0, :, cols])
        following = next_own + reach_next * arriving
        carried_g = split_two(carry_e * grads)
        state[:, cols] = carry_e[CHUNK - 1 :, :] * held_g + mm_three(
            (ctparts[0], ctparts[1]), carried_g
        )
        dcoup[1] += mm_three_nt(carried_g, split_two(held))
        dcoup[0] += mm_three_nt(split_two(tail_e * inputs), held_parts)
        value_g = input_g * step_e + skip[:, cols] * grads
        kept = jnp.sum(held_g * following, axis=0, keepdims=True)
        balance = grads * (mixer[:, cols] - skip[:, cols] * value) - inputs * input_g
        balance = balance + last_row * kept
        sums = jnp.concatenate([balance, input_g * value], axis=0)
        sums_parts = split_three(sums)
        pick = selt[cols, :]
        dhead[...] += mm(sums_parts[0], pick) + mm(sums_parts[1], pick) + mm(sums_parts[2], pick)
        skip_g[0:1, cols] += jnp.sum(grads * value, axis=0, keepdims=True)
        pre_g = value_g * (sig * (1.0 + pre_value * (1.0 - sig)))
        cw_g[4:5, cols] += jnp.sum(pre_g, axis=0, keepdims=True)
        raw_g = cw[0:1, cols] * pre_g
        cw_g[0:1, cols] += jnp.sum(pre_g * raw, axis=0, keepdims=True)
        none = jnp.zeros((8, LANES), f32)
        edge = none
        for lag in range(1, 4):
            cw_g[lag : lag + 1, cols] += jnp.sum(pre_g * lagged[lag], axis=0, keepdims=True)
            weighted = cw[lag : lag + 1, cols] * (pre_g * same_s[lag - 1])
            padded = jnp.concatenate([none, weighted, none], axis=0)
            turned = pltpu.roll(padded, CHUNK + 16 - lag, 0)
            raw_g = raw_g + turned[8 : 8 + CHUNK]
            edge = edge + turned[:8]
        vraw_g[:, cols] = raw_g
        vraw_g[CHUNK - 8 :, cols] += rim_s[:, cols]
        rim_s[:, cols] = edge
        vrim_g[:, cols] = edge
        return carried

    lax.fori_loop(0, heads // 2, pair, 0, unroll=4)

    total = dgram[...]
    total_parts = split_two(total)
    turned_parts = split_two(jnp.transpose(total))
    b_grad = dcoup[0] + mm_three(total_parts, (cparts[0], cparts[1]))
    c_grad = dcoup[1] + mm_three(turned_parts, (bparts[0], bparts[1]))
    coupled_g = jnp.concatenate([b_grad, c_grad], axis=1)
    pre_g = coupled_g * (csig * (1.0 + pre * (1.0 - csig)))
    ccw_g[4:5, :] += jnp.sum(pre_g, axis=0, keepdims=True)
    ccw_g[0:1, :] += jnp.sum(pre_g * craw_now, axis=0, keepdims=True)
    raw_g = ccw[0:1, :] * pre_g
    full = jnp.concatenate([coupling_halo, craw_now], axis=0)
    none = jnp.zeros((8, 2 * width), f32)
    edge = none
    for lag in range(1, 4):
        masked = pre_g * wide_same[lag]
        ccw_g[lag : lag + 1, :] += jnp.sum(
            masked * pltpu.roll(full, lag, 0)[8:], axis=0, keepdims=True
        )
        padded = jnp.concatenate([none, ccw[lag : lag + 1, :] * masked, none], axis=0)
        turned = pltpu.roll(padded, CHUNK + 16 - lag, 0)
        raw_g = raw_g + turned[8 : 8 + CHUNK]
        edge = edge + turned[:8]
    craw_g[...] = raw_g
    craw_g[CHUNK - 8 :, :] += crim_s[...]
    crim_s[...] = edge
    crim_g[...] = edge

    upper = (frame["row_ids"] <= frame["column_ids"]).astype(bf16)
    parts = split_three(dhead[:CHUNK])
    decay_g = mm(upper, parts[0]) + mm(upper, parts[1]) + mm(upper, parts[2])
    step_g = (dhead[CHUNK:] - rate[...] * decay_g) * logistic(frame["shifted"])
    sraw_g[...] = step_g
    small_g[0:1, :] += jnp.sum(step_g, axis=0, keepdims=True)
    small_g[1:2, :] += jnp.sum(-frame["step"] * decay_g, axis=0, keepdims=True)


def backward_ssd(
    marks, micro, raw, rim, inner, twice, tokens, grad, mixer, states, fin, entering, cd, pulled,
    cw, cb, ccw, ccb, sbias, rate, skip, sel, selcol, selt,
):
    width = twice // 2
    chunks = tokens // CHUNK
    heads = inner // (LANES // 2)
    eighth = CHUNK // 8
    final = (micro + 1) * chunks - 1

    def rows(count):
        return pl.BlockSpec((CHUNK, count), lambda step, *_: (chunks - 1 - step, 0))

    def part(count, start):
        return pl.BlockSpec((CHUNK, count), lambda step, *_: (final - step, start // count))

    def before(count, start):
        return pl.BlockSpec(
            (8, count),
            lambda step, *_: (jnp.maximum((final - step) * eighth - 1, 0), start // count),
        )

    def edge(count, start):
        return pl.BlockSpec((8, count), lambda *_: (0, start // count))

    def held(offset):
        return pl.BlockSpec(
            (1, width, inner),
            lambda step, *_: (jnp.minimum(chunks - 1 - step + offset, chunks - 1), 0, 0),
        )

    return pl.pallas_call(
        functools.partial(backward_kernel, heads),
        grid_spec=pltpu.PrefetchScalarGridSpec(
            num_scalar_prefetch=1,
            grid=(chunks,),
            in_specs=[
                part(inner, 0),
                before(inner, 0),
                edge(inner, 0),
                part(twice, inner),
                before(twice, inner),
                edge(twice, inner),
                part(LANES, inner + twice),
                part(inner, 0),
                part(inner, 0),
                held(0),
                held(1),
                whole((width, inner)),
                whole((width, inner)),
                whole((8, inner)),
                whole((width, inner)),
                whole(cw.shape),
                whole(cb.shape),
                whole(ccw.shape),
                whole(ccb.shape),
                whole(sbias.shape),
                whole(rate.shape),
                whole(skip.shape),
                whole(sel.shape),
                whole(selcol.shape),
                whole(selt.shape),
            ],
            out_specs=[
                rows(inner),
                whole((8, inner)),
                rows(twice),
                whole((8, twice)),
                rows(LANES),
                whole((8, inner)),
                whole((8, twice)),
                whole((8, LANES)),
                whole((8, inner)),
            ],
            scratch_shapes=[
                pltpu.VMEM((width, inner), f32),
                pltpu.VMEM((LANES, CHUNK), f32),
                pltpu.VMEM((3 * CHUNK, LANES), bf16),
                pltpu.VMEM((CHUNK, LANES), bf16),
                pltpu.VMEM((8, inner), f32),
                pltpu.VMEM((3, CHUNK, LANES), f32),
                pltpu.VMEM((CHUNK, CHUNK), f32),
                pltpu.VMEM((CHUNK, CHUNK), f32),
                pltpu.VMEM((2, CHUNK, width), bf16),
                pltpu.VMEM((2, CHUNK, width), bf16),
                pltpu.VMEM((2, width, CHUNK), bf16),
                pltpu.VMEM((8, inner), f32),
                pltpu.VMEM((8, twice), f32),
                pltpu.VMEM((CHUNK, CHUNK), f32),
                pltpu.VMEM((2, CHUNK, width), f32),
                pltpu.VMEM((2 * CHUNK, LANES), f32),
                pltpu.VMEM((8, inner), f32),
            ],
        ),
        out_shape=[
            jax.ShapeDtypeStruct((tokens, inner), f32),
            jax.ShapeDtypeStruct((8, inner), f32),
            jax.ShapeDtypeStruct((tokens, twice), f32),
            jax.ShapeDtypeStruct((8, twice), f32),
            jax.ShapeDtypeStruct((tokens, LANES), f32),
            jax.ShapeDtypeStruct((8, inner), f32),
            jax.ShapeDtypeStruct((8, twice), f32),
            jax.ShapeDtypeStruct((8, LANES), f32),
            jax.ShapeDtypeStruct((8, inner), f32),
        ],
        compiler_params=pltpu.CompilerParams(vmem_limit_bytes=48 * 1024 * 1024),
        cost_estimate=pl.CostEstimate(
            flops=60 * tokens * inner * 128 * 2, bytes_accessed=32 * tokens * inner, transcendentals=0
        ),
    )(
        marks, raw, raw, rim, raw, raw, rim, raw, grad, mixer, states, states, fin, entering,
        cd, pulled, cw, cb, ccw, ccb, sbias, rate, skip, sel, selcol, selt,
    )


def passed_along(value, axis, steps):
    count = lax.axis_size(axis)
    initial, last = (max(0, -steps), min(count, count - steps))
    return lax.ppermute(value, axis, [(source, source + steps) for source in range(initial, last)])


def paired(value, axis):
    count = lax.axis_size(axis)
    return lax.ppermute(value, axis, [(source, source ^ 1) for source in range(count)])


def ring_shift(value, axis, steps):
    count = lax.axis_size(axis)
    return lax.ppermute(
        value, axis, [(source, (source + 2 * steps) % count) for source in range(count)]
    )


def gathered(shard, dim):
    pairs = lax.axis_size("fsdp") // 2
    own = lax.axis_index("fsdp")
    size = shard.shape[dim]
    shape = list(shard.shape)
    shape[dim] = size * 2 * pairs
    full = jnp.zeros(shape, shard.dtype)
    blocks = [shard]
    for _ in range(pairs - 1):
        blocks.append(ring_shift(blocks[-1], "fsdp", 1))
    for offset, block in enumerate(blocks):
        place = lax.rem(own + 2 * (pairs - offset), 2 * pairs)
        full = lax.dynamic_update_slice_in_dim(full, block, place * size, dim)
        other = paired(block, "fsdp")
        full = lax.dynamic_update_slice_in_dim(full, other, (place ^ 1) * size, dim)
    return full


def scattered(block_of):
    pairs = lax.axis_size("fsdp") // 2
    own = lax.axis_index("fsdp")
    order = list(range(1, pairs)) + [0]
    arrived = {}
    for offset in order:
        place = lax.rem(own + 2 * offset, 2 * pairs)
        arrived[offset] = paired(block_of(place ^ 1).astype(bf16), "fsdp")
    total = None
    for offset in order:
        place = lax.rem(own + 2 * offset, 2 * pairs)
        partial = block_of(place) + arrived[offset].astype(f32)
        if offset:
            partial = ring_shift(partial.astype(bf16), "fsdp", offset).astype(f32)
        total = partial if total is None else total + partial
    return total + lax.ppermute(
        total, "context", [(source, source ^ 1) for source in range(lax.axis_size("context"))]
    )


def summed_everywhere(values):
    sizes = [value.size for value in values]
    shapes = [value.shape for value in values]
    flat = jnp.concatenate([value.reshape(-1) for value in values])
    count = flat.shape[0]
    flat = jnp.pad(flat, (0, -count % 1024)).reshape(-1, 128)
    for axis in ("context", "fsdp"):
        members = lax.axis_size(axis)
        reach = 1
        while reach < members:
            flat = flat + lax.ppermute(
                flat, axis, [(source, source ^ reach) for source in range(members)]
            )
            reach *= 2
    flat = flat.reshape(-1)
    results, start = [], 0
    for size, shape in zip(sizes, shapes):
        results.append(flat[start : start + size].reshape(shape))
        start += size
    return results


def chained(own, factor, steps):
    arriving = passed_along(own, "context", steps)
    for _ in range(lax.axis_size("context") - 2):
        arriving = passed_along(factor * arriving + own, "context", steps)
    return arriving


def shards(
    tokens,
    lengths,
    block_order,
    cotangent,
    norm_gain,
    in_weight,
    coupling_weight,
    step_weight,
    out_weight,
    conv_weight,
    conv_bias,
    coupling_conv,
    coupling_bias,
    step_bias,
    decay_rate,
    skip_gain,
    inner_gain,
):
    highest = lax.Precision.HIGHEST
    micros = tokens.shape[0]
    count = tokens.shape[2]
    model = tokens.shape[3]
    inner = inner_gain.shape[0]
    heads = step_bias.shape[0]
    head_size = inner // heads
    twice = coupling_weight.shape[1]
    width = twice // 2
    blocks_row = block_order.shape[2]
    block_len = count * lax.axis_size("context") // blocks_row
    own_blocks = count // block_len
    inner_total = inner * lax.axis_size("tensor")
    side = lax.axis_index("tensor")
    place = lax.axis_index("context")
    base = place * count
    shard_rows = in_weight.shape[0]
    half = model // 2

    narrow, wide_columns = selectors(heads, head_size)
    sel = jnp.asarray(narrow, bf16)
    selcol = jnp.asarray(wide_columns, bf16)
    selt = jnp.asarray(narrow[:heads].T, bf16)
    selt = jnp.pad(selt, ((0, 0), (0, LANES - heads)))

    lead = jnp.concatenate(
        [
            in_weight[:, 1, :],
            coupling_weight,
            jnp.pad(step_weight, ((0, 0), (0, LANES - heads))),
        ],
        axis=1,
    )
    lead_full = gathered(lead, 0)
    gate_full = gathered(in_weight[:, 0, :], 0)
    out_full = gathered(out_weight, 1)

    mine = lax.dynamic_slice_in_dim(tokens[:, 0], side * half, half, 2)
    far_half = lax.ppermute(
        mine, "context", [(source, source ^ 1) for source in range(lax.axis_size("context"))]
    )
    far_other = paired(far_half, "tensor")
    far = jnp.where(
        side == 0,
        jnp.concatenate([far_half, far_other], axis=2),
        jnp.concatenate([far_other, far_half], axis=2),
    )
    near = tokens[:, 0].reshape(micros, own_blocks, block_len, model)
    far = far.reshape(micros, own_blocks, block_len, model)
    everything = jnp.where(
        place == 0, jnp.concatenate([near, far], 1), jnp.concatenate([far, near], 1)
    )
    slots = jnp.arange(blocks_row, dtype=jnp.int32)
    picked = []
    for micro in range(micros):
        for own in range(own_blocks):
            wanted = place * own_blocks + own
            slot = jnp.sum(jnp.where(block_order[micro, 0] == wanted, slots, 0))
            picked.append(
                lax.dynamic_slice(
                    everything, (micro, slot, 0, 0), (1, 1, block_len, model)
                ).reshape(block_len, model)
            )
    x_input = jnp.concatenate(picked, axis=0)
    x_float = x_input.astype(f32)
    inv_rms = lax.rsqrt(jnp.mean(x_float * x_float, axis=-1, keepdims=True) + epsilon)
    normed = (x_float * inv_rms * norm_gain).astype(bf16)

    first_end = lengths[:, 0, 0]
    second_end = first_end + lengths[:, 0, 1]
    marks = [
        jnp.stack([first_end[micro], second_end[micro], base]).astype(jnp.int32)
        for micro in range(micros)
    ]
    positions = base + jnp.arange(count, dtype=jnp.int32)
    keep = jnp.concatenate([(positions < second_end[micro]) for micro in range(micros)])
    keep = keep.astype(f32)[:, None]

    cw, cb = conv_weight, conv_bias.reshape(1, inner)
    ccw, ccb = coupling_conv, coupling_bias.reshape(1, twice)
    sbias = jnp.pad(step_bias, (0, LANES - heads)).reshape(1, LANES)
    rate = jnp.pad(decay_rate, (0, LANES - heads)).reshape(1, LANES)
    skip = jnp.repeat(skip_gain, head_size).reshape(1, inner)

    raw = jnp.dot(normed, lead_full, preferred_element_type=f32)
    rims = passed_along(
        jnp.stack([raw[(micro + 1) * count - 8 : (micro + 1) * count] for micro in range(micros)]),
        "context",
        1,
    )
    forwards = []
    for micro in range(micros):
        forwards.append(
            forward_ssd(
                marks[micro], micro, raw, rims[micro], inner, twice, count,
                cw, cb, ccw, ccb, sbias, rate, skip, sel, selcol,
            )
        )
    entering = [
        chained(forwards[micro][2], forwards[micro][5][count // CHUNK], 1)
        for micro in range(micros)
    ]
    gate_in = jnp.dot(normed, gate_full, preferred_element_type=f32)
    cot = cotangent[:, 0].reshape(micros * count, model)
    out_grad = cot * keep.astype(bf16)
    norm_grad = contract_cols(out_grad, out_full)

    mixers = []
    for micro in range(micros):
        y_own, _, _, coupled, carry, _ = forwards[micro]
        mixers.append(
            y_own + carry * jnp.dot(coupled[:, width:], entering[micro], precision=highest)
        )
    mixer = jnp.concatenate(mixers, axis=0)
    gate_sig = jax.nn.sigmoid(gate_in)
    gate_act = gate_in * gate_sig
    gated = mixer * gate_act
    scaled_grad = norm_grad * inner_gain
    row_sums = jnp.stack([jnp.sum(gated * gated, axis=-1), jnp.sum(scaled_grad * gated, axis=-1)])
    row_sums = row_sums + paired(row_sums, "tensor")
    inv_norm = lax.rsqrt(row_sums[0] / inner_total + epsilon)[:, None]
    inner_dot = row_sums[1][:, None]
    gated_norm = (gated * inv_norm * inner_gain).astype(bf16)
    inner_gain_grad = jnp.sum(norm_grad * gated * inv_norm, axis=0)
    gated_grad = scaled_grad * inv_norm - gated * (inner_dot * inv_norm**3 / inner_total)
    gate_grad = (gated_grad * mixer * gate_sig * (1.0 + gate_in * (1.0 - gate_sig))).astype(bf16)
    mixer_grad = gated_grad * gate_act

    pulled = []
    for micro in range(micros):
        part = slice(micro * count, (micro + 1) * count)
        own_pull = lax.dot_general(
            forwards[micro][3][:, width:],
            forwards[micro][4] * mixer_grad[part],
            (((0,), (0,)), ((), ())),
            precision=highest,
        )
        pulled.append(chained(own_pull, forwards[micro][5][count // CHUNK], -1))

    branch = jnp.dot(gated_norm, out_full, preferred_element_type=f32)
    branch = branch + paired(branch, "tensor")
    block_out = (x_float + keep * branch).astype(bf16)

    def out_block(index):
        columns = lax.dynamic_slice_in_dim(out_grad, index * shard_rows, shard_rows, 1)
        return contract_rows(gated_norm, columns)

    out_shard = scattered(out_block)

    def in_block(grads):
        def block(index):
            columns = lax.dynamic_slice_in_dim(normed, index * shard_rows, shard_rows, 1)
            return contract_rows(columns, grads)

        return block

    gate_shard = scattered(in_block(gate_grad))

    backs = []
    for micro in range(micros):
        y_own, states, final, coupled, carry, reach = forwards[micro]
        backs.append(
            backward_ssd(
                marks[micro], micro, raw, rims[micro], inner, twice, count, mixer_grad, mixer,
                states, final, entering[micro], reach, pulled[micro],
                cw, cb, ccw, ccb, sbias, rate, skip, sel, selcol, selt,
            )
        )
    edges = passed_along(
        jnp.stack([jnp.concatenate([back[1], back[3]], axis=1) for back in backs]), "context", -1
    )
    tail_pad = ((count - 8, 0), (0, 0))
    coupling_raw_grad = jnp.stack(
        [back[2] + jnp.pad(edges[micro][:, inner:], tail_pad) for micro, back in enumerate(backs)]
    )
    coupling_raw_grad = coupling_raw_grad + paired(coupling_raw_grad, "tensor")
    lane_ids = jnp.arange(twice, dtype=jnp.int32)
    own_lanes = ((lane_ids // width) == side).astype(bf16)
    coupling_low = coupling_raw_grad.astype(bf16) * own_lanes
    lead_grad = jnp.concatenate(
        [
            jnp.concatenate(
                [
                    (back[0] + jnp.pad(edges[micro][:, :inner], tail_pad)).astype(bf16),
                    coupling_low[micro],
                    back[4].astype(bf16),
                ],
                axis=1,
            )
            for micro, back in enumerate(backs)
        ],
        axis=0,
    )
    lead_shard = scattered(in_block(lead_grad))
    normed_part = contract_cols(gate_grad, gate_full) + contract_cols(lead_grad, lead_full)
    normed_grad = normed_part + paired(normed_part, "tensor")
    x_hat = x_float * inv_rms
    hat_grad = normed_grad * norm_gain
    input_grad = (
        cot.astype(f32)
        + inv_rms * (hat_grad - x_hat * jnp.mean(hat_grad * x_hat, axis=-1, keepdims=True))
    ).astype(bf16)
    norm_gain_grad = jnp.sum(normed_grad * x_hat, axis=0)

    value_sums = sum(back[5] for back in backs)
    coupling_sums = sum(back[6] for back in backs)
    small_sums = sum(back[7] for back in backs)
    skip_sums = sum(back[8] for back in backs)[0].reshape(heads, head_size).sum(axis=1)
    coupling_sums = coupling_sums + paired(coupling_sums, "tensor")
    (value_all, coupling_all, small_all, skip_all, inner_all, norm_all) = summed_everywhere(
        [value_sums[:5], coupling_sums[:5], small_sums[:2], skip_sums, inner_gain_grad, norm_gain_grad]
    )
    coupling_shard = lead_shard[:, inner : inner + twice]
    coupling_shard = coupling_shard + paired(coupling_shard, "tensor")
    return (
        block_out.reshape(micros, 1, count, model),
        input_grad.reshape(micros, 1, count, model),
        norm_all,
        jnp.stack([gate_shard, lead_shard[:, :inner]], axis=1),
        coupling_shard,
        lead_shard[:, inner + twice : inner + twice + heads],
        out_shard,
        value_all[:4],
        value_all[4],
        coupling_all[:4],
        coupling_all[4],
        small_all[0, :heads],
        small_all[1, :heads],
        skip_all,
        inner_all,
    )


def contract_rows(left, right):
    return lax.dot_general(
        left, right, (((0,), (0,)), ((), ())), preferred_element_type=jnp.float32
    )


def contract_cols(left, right):
    return lax.dot_general(
        left, right, (((1,), (1,)), ((), ())), preferred_element_type=jnp.float32
    )


def solution(mesh):
    return jax.shard_map(
        shards,
        mesh=mesh,
        in_specs=(
            P(None, "fsdp", "context", None),
            P(None, "fsdp", None),
            P(None, "fsdp", None),
            P(None, "fsdp", "context", None),
            P(),
            P("fsdp", None, "tensor"),
            P("fsdp", None),
            P("fsdp", "tensor"),
            P("tensor", "fsdp"),
            P(None, "tensor"),
            P("tensor"),
            P(),
            P(),
            P("tensor"),
            P("tensor"),
            P("tensor"),
            P("tensor"),
        ),
        out_specs=(
            P(None, "fsdp", "context", None),
            P(None, "fsdp", "context", None),
            P(),
            P("fsdp", None, "tensor"),
            P("fsdp", None),
            P("fsdp", "tensor"),
            P("tensor", "fsdp"),
            P(None, "tensor"),
            P("tensor"),
            P(),
            P(),
            P("tensor"),
            P("tensor"),
            P("tensor"),
            P("tensor"),
        ),
        check_vma=False,
    )
```

time: 3660 us -> 1160 us (0.32)
  waiting for transfers between devices: 1770 us -> 512 us
  local copies, waits for them, and re-layouts: 791 us -> 67.8 us
  matrix products: 484 us -> 173 us
  other arithmetic: 369 us -> 112 us
  Pallas kernels: 0 us -> 147 us
  blocking collectives: 133 us -> 0 us
  starting transfers between devices: 37.4 us -> 120 us
    unnamed x12 -> x0, waiting for transfers between devices: 864 us -> none
    ppermute x0 -> x57, waiting for transfers between devices: none -> 489 us  [the longest x31 180 us: paired(): lax.ppermute(value, axis, [(source, source ^ 1) for source in range(count)])]
    reduce_scatter x3 -> x0, waiting for transfers between devices: 404 us -> none  [the longest x1 286 us: shards(): lax.psum_scatter(out_total, 'fsdp', scatter_dimension=1, tiled=True)]
    all_gather x5 -> x0, waiting for transfers between devices: 387 us -> none  [the longest x1 217 us: shards(): lax.all_gather(in_weight, 'fsdp', axis=0, tiled=True)]
    dynamic_update_slice x60 -> x23, local copies, waits for them, and re-layouts: 381 us -> 32 us  [the longest x12 16.8 us: gathered(): full = lax.dynamic_update_slice_in_dim(full, other, (place ^ 1) * size, dim)]
    dot_general x60 -> x7, matrix products: 331 us -> 52.5 us  [the longest x1 14.2 us: shards(): raw = jnp.dot(normed, lead_full, preferred_element_type=f32)]
    mul x30 -> x2, other arithmetic: 168 us -> 2.98 us  [the longest x1 2.81 us: shards(): out_grad = cot * keep.astype(bf16)]
    pallas_call x0 -> x4, Pallas kernels: none -> 147 us  [the longest x2 94.6 us: backward_ssd(): pl.pallas_call(functools.partial(backward_kernel, heads), grid_spec=pltpu...]
  transfers between devices with their start and end apart: 23 -> 63, of which waited for: 12 -> 33; matrix products, arithmetic and copies ran while one was open for 24% -> 22% of each run, Pallas kernels for 0% -> 13%
where the time goes in v1:
time: 1160 us; the launch traced here: 1150 us
  waiting for transfers between devices  512 us (44%)
  matrix products  173 us (15%)
  Pallas kernels  147 us (13%)
  starting transfers between devices  120 us (10%)
  other arithmetic  112 us (10%)
  local copies, waits for them, and re-layouts  67.8 us (6%)
  between operations  17.9 us (2%)
    ppermute x31, waiting for transfers between devices, paired(): lax.ppermute(value, axis, [(source, source ^ 1) for source in range(count)])  180 us
    ppermute x18, waiting for transfers between devices, ring_shift(): lax.ppermute(value, axis, [(source, (source + 2 * steps) % count) for sou...  169 us
    ppermute x3, waiting for transfers between devices, scattered(): lax.ppermute(total, 'context', [(source, source ^ 1) for source in range(...  134 us
    pallas_call x2, Pallas kernels, backward_ssd(): pl.pallas_call(functools.partial(backward_kernel, heads), grid_spec=pltpu...  94.6 us
    dot_general x24, matrix products, contract_rows(): lax.dot_general(left, right, (((0,), (0,)), ((), ())), preferred_element_...  69.2 us
    pallas_call x2, Pallas kernels, forward_ssd(): pl.pallas_call(functools.partial(forward_kernel, heads), grid_spec=pltpu....  52.1 us
    dot_general x3, matrix products, contract_cols(): lax.dot_general(left, right, (((1,), (1,)), ((), ())), preferred_element_...  51.4 us
    ppermute x18, starting transfers between devices, ring_shift(): lax.ppermute(value, axis, [(source, (source + 2 * steps) % count) for sou...  41.9 us
  transfers between devices with their start and end apart: 63, of which 33 were waited for; matrix products, arithmetic and copies ran while one was open for 22% of the time, Pallas kernels for 13%

profile of v1, /device:TPU:0, one launch (start us, length us, event | category | flops | bytes accessed | tf_op | source)
XLA Modules:
  0.0 1149.9 jit_solution(11497418280437800564)
XLA Ops:
  0.7 5.5 fusion.126
  53.6 13.3 %collective-permute-done.12 = bf16[256,2048]{1,0:T(8,128)(2,1)} collective-permute-done((bf16[256,2048]{1,0:T(8,128)(2,1)S(1)}, bf16[256,2048]{1,0:T(8,128)(2,1)}, u32[]{:S(2)}, u32[]{:S(2)}) %collective-permute-start.12) | collective-permute-done | bytes 1048608 | tf_op jit(solution)/shard_map/ppermute | solution.py:713
  78.1 11.4 collective-permute-done.19
  100.2 11.6 %collective-permute-done.14 = bf16[256,2048]{1,0:T(8,128)(2,1)S(1)} collective-permute-done((bf16[256,2048]{1,0:T(8,128)(2,1)}, bf16[256,2048]{1,0:T(8,128)(2,1)S(1)}, u32[]{:S(2)}, u32[]{:S(2)}) %collective-permute-start.14) | collective-permute-done | bytes 1048608 | tf_op jit(solution)/shard_map/ppermute | solution.py:713
  121.7 12.6 %collective-permute-done.21 = bf16[2048,256]{1,0:T(8,128)(2,1)S(1)} collective-permute-done((bf16[2048,256]{1,0:T(8,128)(2,1)S(1)}, bf16[2048,256]{1,0:T(8,128)(2,1)S(1)}, u32[]{:S(2)}, u32[]{:S(2)}) %collective-permute-start.21) | collective-permute-done | bytes 1048608 | tf_op jit(solution)/shard_map/ppermute | solution.py:713
  136.3 6.7 collective-permute-done.22
  146.0 15.0 %collective-permute-done.4 = bf16[256,2432]{1,0:T(8,128)(2,1)S(1)} collective-permute-done((bf16[256,2432]{1,0:T(8,128)(2,1)}, bf16[256,2432]{1,0:T(8,128)(2,1)S(1)}, u32[]{:S(2)}, u32[]{:S(2)}) %collective-permute-start.4) | collective-permute-done | bytes 1245216 | tf_op jit(solution)/shard_map/ppermute | solution.py:713
  164.2 5.6 collective-permute-done.5
  169.8 13.7 %collective-permute-done.16 = bf16[256,2048]{1,0:T(8,128)(2,1)S(1)} collective-permute-done((bf16[256,2048]{1,0:T(8,128)(2,1)S(1)}, bf16[256,2048]{1,0:T(8,128)(2,1)S(1)}, u32[]{:S(2)}, u32[]{:S(2)}) %collective-permute-start.16) | collective-permute-done | bytes 1048608 | tf_op jit(solution)/shard_map/ppermute | solution.py:713
  185.5 6.8 collective-permute-done.17
  197.3 8.6 collective-permute-done.23
  208.0 6.8 collective-permute-done.24
  217.8 19.8 %collective-permute-done.7 = bf16[256,2432]{1,0:T(8,128)(2,1)S(1)} collective-permute-done((bf16[256,2432]{1,0:T(8,128)(2,1)S(1)}, bf16[256,2432]{1,0:T(8,128)(2,1)S(1)}, u32[]{:S(2)}, u32[]{:S(2)}) %collective-permute-start.7) | collective-permute-done | bytes 1245216 | tf_op jit(solution)/shard_map/ppermute | solution.py:718
  247.0 56.4 %collective-permute-done.8 = bf16[256,2432]{1,0:T(8,128)(2,1)S(1)} collective-permute-done((bf16[256,2432]{1,0:T(8,128)(2,1)S(1)}, bf16[256,2432]{1,0:T(8,128)(2,1)S(1)}, u32[]{:S(2)}, u32[]{:S(2)}) %collective-permute-start.8) | collective-permute-done | bytes 1245216 | tf_op jit(solution)/shard_map/ppermute | solution.py:713
  304.6 14.2 %fusion.131.vraw.vprev.craw.cprev.sraw = f32[1024,2432]{1,0:T(8,128)S(1)} fusion(bf16[1024,2048]{1,0:T(8,128)(2,1)S(1)} %fusion.4, bf16[2048,2432]{1,0:T(8,128)(2,1)} %constant_dynamic-update-slice_fusion.16), kind=kOutput, calls=%fused_computation.246 | convolution fusion | flops 10200547328 | bytes 24117248 | tf_op jit(solution)/shard_map/dot_general | solution.py:893
  325.3 26.1 %shard_map.307 = (f32[512,2048]{1,0:T(8,128)S(1)}, f32[4,128,2048]{2,1,0:T(8,128)S(1)}, f32[128,2048]{1,0:T(8,128)S(1)}, f32[512,256]{1,0:T(8,128)S(1)}, f32[512,2048]{1,0:T(8,128)}, /*index=5*/f32[8,2048]{1,0:T(8,128)S(1)}) custom-call(s32[3]{0:T(128)S(1)} %get-tuple-element.152.marks, f32[1024,2432]{1,0:T(8,128)} %copy-done.15, f32[1024,2432]{1,0:T(8,128)} %copy-done.15, ...), custom_call_target="tpu_custom_call" | custom-call | flops 5368709120 | bytes 25165824 | tf_op jit(solution)/shard_map/pallas_call | solution.py:293
  351.4 4.6 collective-permute-start.10
  356.0 13.2 %fusion.132 = f32[1024,2048]{1,0:T(8,128)} fusion(bf16[1024,2048]{1,0:T(8,128)(2,1)S(1)} %fusion.4, bf16[2048,2048]{1,0:T(8,128)(2,1)} %constant_dynamic-update-slice_fusion.8), kind=kOutput, calls=%fused_computation.247 | convolution fusion | flops 8589934592 | bytes 20971520 | tf_op jit(solution)/shard_map/dot_general | solution.py:911
  371.6 26.0 %shard_map.308 = (f32[512,2048]{1,0:T(8,128)S(1)}, f32[4,128,2048]{2,1,0:T(8,128)S(1)}, f32[128,2048]{1,0:T(8,128)S(1)}, f32[512,256]{1,0:T(8,128)S(1)}, f32[512,2048]{1,0:T(8,128)}, /*index=5*/f32[8,2048]{1,0:T(8,128)S(1)}) custom-call(s32[3]{0:T(128)S(1)} %get-tuple-element.153.marks, f32[1024,2432]{1,0:T(8,128)} %copy-done.15, f32[1024,2432]{1,0:T(8,128)} %copy-done.15, ...), custom_call_target="tpu_custom_call" | custom-call | flops 5368709120 | bytes 25165824 | tf_op jit(solution)/shard_map/pallas_call | solution.py:293
  399.1 4.9 fusion.81
  404.1 6.8 multiply_add_fusion.1
  410.9 8.6 collective-permute-done.11.entering
  426.5 20.3 %multiply_reduce_fusion.2 = (f32[1024]{0:T(1024)S(1)}, f32[1024]{0:T(1024)S(1)}, f32[1024,2048]{1,0:T(8,128)}, f32[1024,2048]{1,0:T(8,128)}) fusion(f32[2048]{0:T(1024)S(1)} %copy-done.52, f32[1024,2048]{1,0:T(8,128)} %fusion.132, f32[512,2048]{1,0:T(8,128)} %multiply_add_fusion, f32[512,2048]{1,0:T(8,128)} %multiply_add_fusion.1, ...), kind=kOutput, calls=%fused_computation.23 | convolution fusion | flops 8613001216 | bytes 46153728 | tf_op jit(solution)/shard_map/dot_general | solution.py:1049
  448.0 16.2 %multiply_convert_fusion = (bf16[1024,2048]{1,0:T(8,128)(2,1)S(1)}, f32[1024,2048]{1,0:T(8,128)S(1)}, f32[2048]{0:T(1024)}, bf16[1024,2048]{1,0:T(8,128)(2,1)S(1)}, f32[1024,2048]{1,0:T(8,128)}) fusion(f32[1024,2048]{1,0:T(8,128)} %fusion.132, f32[1024,2048]{1,0:T(8,128)} %get-tuple-element.117, f32[1024]{0:T(1024)S(1)} %fusion.109, f32[1024]{0:T(1024)S(1)} %bitcast.187, ...), kind=kLoop, calls=%fused_computation.19 | loop fusion | flops 48232448 | bytes 58744832 | tf_op jit(solution)/shard_map/convert_element_type | solution.py:934
  478.4 4.6 convolution_convert_fusion.10
  483.0 4.6 convolution_convert_fusion.9
  487.7 11.4 fusion.133
  530.1 11.1 collective-permute-done.28.pulled
  541.7 47.5 %shard_map.309 = (f32[512,2048]{1,0:T(8,128)}, f32[8,2048]{1,0:T(8,128)S(1)}, f32[512,256]{1,0:T(8,128)S(1)}, f32[8,256]{1,0:T(8,128)S(1)}, f32[512,128]{1,0:T(8...) custom-call(s32[3]{0:T(128)S(1)} %get-tuple-element.152.marks, ...), custom_call_target="tpu_custom_call" | custom-call | flops 16106127360 | bytes 33554432 | tf_op jit(solution)/shard_map/pallas_call | solution.py:621
  590.8 47.1 %shard_map.310 = (f32[512,2048]{1,0:T(8,128)}, f32[8,2048]{1,0:T(8,128)S(1)}, f32[512,256]{1,0:T(8,128)S(1)}, f32[8,256]{1,0:T(8,128)S(1)}, f32[512,128]{1,0:T(8...) custom-call(s32[3]{0:T(128)S(1)} %get-tuple-element.153.marks, ...), custom_call_target="tpu_custom_call" | custom-call | flops 16106127360 | bytes 33554432 | tf_op jit(solution)/shard_map/pallas_call | solution.py:621
  638.5 4.8 add_convert_fusion.10
  666.6 23.5 %maximum_maximum_fusion = bf16[1024,2432]{1,0:T(8,128)(2,1)S(1)} fusion(bf16[512,128]{1,0:T(8,128)(2,1)S(1)} %convert_element_type.215, bf16[512,256]{1,0:T(8,128)(2,1)S(1)} %get-tuple-element.134, bf16[512,2048]{1,0:T(8,128)(2,1)S(1)} %add_convert_fusion, bf16[512,128]{1,0:T(8,128)(2,1)S(1)} %convert_element_type.213, ...), kind=kLoop, calls=%fused_computation.26 | loop fusion | flops 29884416 | bytes 9961472 | tf_op jit(solution)/shard_map/concatenate | solution.py:988
  690.1 16.0 %fusion.134 = f32[1024,2048]{1,0:T(8,128)} fusion(bf16[1024,2432]{1,0:T(8,128)(2,1)S(1)} %maximum_maximum_fusion, bf16[2048,2432]{1,0:T(8,128)(2,1)} %constant_dynamic-update-slice_fusion.16), kind=kOutput, calls=%fused_computation.249 | convolution fusion | flops 10200547328 | bytes 23330816 | tf_op jit(solution)/shard_map/dot_general | solution.py:1049
  706.1 15.2 %convolution_add_fusion = f32[1024,2048]{1,0:T(8,128)} fusion(f32[1024,2048]{1,0:T(8,128)} %fusion.134, bf16[1024,2048]{1,0:T(8,128)(2,1)S(1)} %copy-done.34, bf16[2048,2048]{1,0:T(8,128)(2,1)} %constant_dynamic-update-slice_fusion.8), kind=kOutput, calls=%fused_computation.43 | convolution fusion | flops 8592031744 | bytes 29360128 | tf_op jit(solution)/shard_map/dot_general | solution.py:1049
  730.1 38.8 %collective-permute-done.60 = bf16[2048,256]{1,0:T(8,128)(2,1)S(1)} collective-permute-done((bf16[2048,256]{1,0:T(8,128)(2,1)}, bf16[2048,256]{1,0:T(8,128)(2,1)S(1)}, u32[]{:S(2)}, u32[]{:S(2)}) %collective-permute-start.60) | collective-permute-done | bytes 1048608 | tf_op jit(solution)/shard_map/ppermute | solution.py:718
  774.3 9.1 collective-permute-done.48
  785.9 24.2 %collective-permute-done.50 = bf16[256,2432]{1,0:T(8,128)(2,1)S(1)} collective-permute-done((bf16[256,2432]{1,0:T(8,128)(2,1)S(1)}, bf16[256,2432]{1,0:T(8,128)(2,1)S(1)}, u32[]{:S(2)}, u32[]{:S(2)}) %collective-permute-start.50) | collective-permute-done | bytes 1245216 | tf_op jit(solution)/shard_map/ppermute | solution.py:713
  813.3 4.8 collective-permute-done.41
  818.1 22.1 %collective-permute-start.47 = (bf16[256,2432]{1,0:T(8,128)(2,1)S(1)}, bf16[256,2432]{1,0:T(8,128)(2,1)S(1)}, u32[]{:S(2)}, u32[]{:S(2)}) collective-permute-start(bf16[256,2432]{1,0:T(8,128)(2,1)S(1)} %add_convert_fusion.4), channel_id=1, source_target_pairs={{0,8},{4,12},{8,16},{12,20},{16,24},{20,28},{24,0},{28,4},{1,9},{5... | collective-permute-start | bytes 3735560 | tf_op jit(solution)/shard_map/ppermute | solution.py:718
  849.5 21.8 %collective-permute-done.47 = bf16[256,2432]{1,0:T(8,128)(2,1)S(1)} collective-permute-done((bf16[256,2432]{1,0:T(8,128)(2,1)S(1)}, bf16[256,2432]{1,0:T(8,128)(2,1)S(1)}, u32[]{:S(2)}, u32[]{:S(2)}) %collective-permute-start.47) | collective-permute-done | bytes 1245216 | tf_op jit(solution)/shard_map/ppermute | solution.py:718
  871.4 52.7 %collective-permute-done.49 = bf16[256,2432]{1,0:T(8,128)(2,1)S(1)} collective-permute-done((bf16[256,2432]{1,0:T(8,128)(2,1)S(1)}, bf16[256,2432]{1,0:T(8,128)(2,1)S(1)}, u32[]{:S(2)}, u32[]{:S(2)}) %collective-permute-start.49) | collective-permute-done | bytes 1245216 | tf_op jit(solution)/shard_map/ppermute | solution.py:718
  928.4 44.5 %collective-permute-done.62 = f32[2048,256]{1,0:T(8,128)} collective-permute-done((f32[2048,256]{1,0:T(8,128)}, f32[2048,256]{1,0:T(8,128)}, u32[]{:S(2)}, u32[]{:S(2)}) %collective-permute-start.62) | collective-permute-done | bytes 2097184 | tf_op jit(solution)/shard_map/ppermute | solution.py:756
  976.7 41.1 %collective-permute-done.45 = f32[256,2048]{1,0:T(8,128)} collective-permute-done((f32[256,2048]{1,0:T(8,128)}, f32[256,2048]{1,0:T(8,128)}, u32[]{:S(2)}, u32[]{:S(2)}) %collective-permute-start.45) | collective-permute-done | bytes 2097184 | tf_op jit(solution)/shard_map/ppermute | solution.py:756
  1021.7 48.5 %collective-permute-done.53 = f32[256,2432]{1,0:T(8,128)} collective-permute-done((f32[256,2432]{1,0:T(8,128)S(1)}, f32[256,2432]{1,0:T(8,128)}, u32[]{:S(2)}, u32[]{:S(2)}) %collective-permute-start.53) | collective-permute-done | bytes 2490400 | tf_op jit(solution)/shard_map/ppermute | solution.py:756
  1076.8 7.7 fusion.10
  1087.4 5.2 copy.45
  1097.7 22.9 %collective-permute-start.36 = (f32[128,128]{1,0:T(8,128)S(1)}, f32[128,128]{1,0:T(8,128)S(1)}, u32[]{:S(2)}, u32[]{:S(2)}) collective-permute-start(f32[128,128]{1,0:T(8,128)S(1)} %fusion.173), channel_id=1, source_target_pairs={{0,8},{4,12},{8,0},{12,4},{16,24},{20,28},{24,16},{28,20},{1,9},{5... | collective-permute-start | bytes 196616 | tf_op jit(solution)/shard_map/ppermute | solution.py:771
  1126.7 18.6 %fusion.9 = (bf16[1024,2048]{1,0:T(8,128)(2,1)}, bf16[1024,2048]{1,0:T(8,128)(2,1)}) fusion(bf16[1024,2048]{1,0:T(8,128)(2,1)} %copy-done.17, bf16[2,1,512,2048]{3,2,1,0:T(8,128)(2,1)} %param.23, f32[1024]{0:T(1024)S(1)} %broadcast_multiply_fusion, f32[2048]{0:T(1024)S(1)} %copy-done.45, f32[1024]{0:T(1024)S(1)} %copy-done.47, ...), kind=kLoop, calls=%fused_computation.12 | loop fusion | flops 29360128 | bytes 50352128 | tf_op jit(solution)/shard_map/convert_element_type | solution.py:1010
  (366 shorter events, 249.4 us)
Async XLA Ops:
  13.0 81.4 %collective-permute-start.2 = (bf16[256,2432]{1,0:T(8,128)(2,1)}, bf16[256,2432]{1,0:T(8,128)(2,1)}, u32[]{:S(2)}, u32[]{:S(2)}) collective-permute-start(bf16[256,2432]{1,0:T(8,128)(2,1)} %get-tuple-element.131), channel_id=1, source_target_pairs={{0,4},{4,0},{8,12},{12,8},{16,20},{20,16},{24,28},{28,24},{1,5},{5... | collective-permute-start | bytes 3735560 | tf_op jit(solution)/shard_map/ppermute | solution.py:713
  16.0 80.0 %collective-permute-start.3 = (bf16[256,2432]{1,0:T(8,128)(2,1)}, bf16[256,2432]{1,0:T(8,128)(2,1)}, u32[]{:S(2)}, u32[]{:S(2)}) collective-permute-start(bf16[256,2432]{1,0:T(8,128)(2,1)} %get-tuple-element.131), channel_id=1, source_target_pairs={{0,8},{4,12},{8,16},{12,20},{16,24},{20,28},{24,0},{28,4},{1,9},{5... | collective-permute-start | bytes 3735560 | tf_op jit(solution)/shard_map/ppermute | solution.py:718
  23.5 43.5 %collective-permute-start.12 = (bf16[256,2048]{1,0:T(8,128)(2,1)S(1)}, bf16[256,2048]{1,0:T(8,128)(2,1)}, u32[]{:S(2)}, u32[]{:S(2)}) collective-permute-start(bf16[256,2048]{1,0:T(8,128)(2,1)S(1)} %get-tuple-element.119), channel_id=1, source_target_pairs={{0,4},{4,0},{8,12},{12,8},{16,20},{20,16},{24,28},{28,24},{1,5},{5... | collective-permute-start | bytes 3145736 | tf_op jit(solution)/shard_map/ppermute | solution.py:713
  24.0 47.9 %collective-permute-start.13 = (bf16[256,2048]{1,0:T(8,128)(2,1)S(1)}, bf16[256,2048]{1,0:T(8,128)(2,1)}, u32[]{:S(2)}, u32[]{:S(2)}) collective-permute-start(bf16[256,2048]{1,0:T(8,128)(2,1)S(1)} %get-tuple-element.119), channel_id=1, source_target_pairs={{0,8},{4,12},{8,16},{12,20},{16,24},{20,28},{24,0},{28,4},{1,9},{5... | collective-permute-start | bytes 3145736 | tf_op jit(solution)/shard_map/ppermute | solution.py:718
  25.6 63.8 %collective-permute-start.19 = (bf16[2048,256]{1,0:T(8,128)(2,1)}, bf16[2048,256]{1,0:T(8,128)(2,1)}, u32[]{:S(2)}, u32[]{:S(2)}) collective-permute-start(bf16[2048,256]{1,0:T(8,128)(2,1)} %param.28), channel_id=1, source_target_pairs={{0,4},{4,0},{8,12},{12,8},{16,20},{20,16},{24,28},{28,24},{1,5},{5... | collective-permute-start | bytes 3145736 | tf_op jit(solution)/shard_map/ppermute | solution.py:713
  71.9 40.0 %collective-permute-start.14 = (bf16[256,2048]{1,0:T(8,128)(2,1)}, bf16[256,2048]{1,0:T(8,128)(2,1)S(1)}, u32[]{:S(2)}, u32[]{:S(2)}) collective-permute-start(bf16[256,2048]{1,0:T(8,128)(2,1)} %collective-permute-done.13), channel_id=1, source_target_pairs={{0,4},{4,0},{8,12},{12,8},{16,20},{20,16},{24,28},{28,24},{1,5},{5... | collective-permute-start | bytes 3145736 | tf_op jit(solution)/shard_map/ppermute | solution.py:713
  89.5 55.0 %collective-permute-start = (bf16[2,512,1024]{2,1,0:T(8,128)(2,1)S(1)}, bf16[2,512,1024]{2,1,0:T(8,128)(2,1)S(1)}, u32[]{:S(2)}, u32[]{:S(2)}) collective-permute-start(bf16[2,512,1024]{2,1,0:T(8,128)(2,1)S(1)} %dynamic-slice_bitcast_fusion), channel_id=1, source_target_pairs={{0,2},{2,0},{1,3},{3,1},{4,6},{6,4},{5,7},{7,5},{8,10},{10,8},{9,1... | collective-permute-start | bytes 6291464 | tf_op jit(solution)/shard_map/ppermute | solution.py:847
  96.0 47.1 %collective-permute-start.22 = (bf16[2048,256]{1,0:T(8,128)(2,1)S(1)}, bf16[2048,256]{1,0:T(8,128)(2,1)S(1)}, u32[]{:S(2)}, u32[]{:S(2)}) collective-permute-start(bf16[2048,256]{1,0:T(8,128)(2,1)S(1)} %collective-permute-done.20), channel_id=1, source_target_pairs={{0,8},{4,12},{8,16},{12,20},{16,24},{20,28},{24,0},{28,4},{1,9},{5... | collective-permute-start | bytes 3145736 | tf_op jit(solution)/shard_map/ppermute | solution.py:718
  111.8 49.2 %collective-permute-start.4 = (bf16[256,2432]{1,0:T(8,128)(2,1)}, bf16[256,2432]{1,0:T(8,128)(2,1)S(1)}, u32[]{:S(2)}, u32[]{:S(2)}) collective-permute-start(bf16[256,2432]{1,0:T(8,128)(2,1)} %collective-permute-done.3), channel_id=1, source_target_pairs={{0,4},{4,0},{8,12},{12,8},{16,20},{20,16},{24,28},{28,24},{1,5},{5... | collective-permute-start | bytes 3735560 | tf_op jit(solution)/shard_map/ppermute | solution.py:713
  120.6 49.2 %collective-permute-start.5 = (bf16[256,2432]{1,0:T(8,128)(2,1)}, bf16[256,2432]{1,0:T(8,128)(2,1)S(1)}, u32[]{:S(2)}, u32[]{:S(2)}) collective-permute-start(bf16[256,2432]{1,0:T(8,128)(2,1)} %collective-permute-done.3), channel_id=1, source_target_pairs={{0,8},{4,12},{8,16},{12,20},{16,24},{20,28},{24,0},{28,4},{1,9},{5... | collective-permute-start | bytes 3735560 | tf_op jit(solution)/shard_map/ppermute | solution.py:718
  134.3 49.2 %collective-permute-start.16 = (bf16[256,2048]{1,0:T(8,128)(2,1)S(1)}, bf16[256,2048]{1,0:T(8,128)(2,1)S(1)}, u32[]{:S(2)}, u32[]{:S(2)}) collective-permute-start(bf16[256,2048]{1,0:T(8,128)(2,1)S(1)} %collective-permute-done.15), channel_id=1, source_target_pairs={{0,4},{4,0},{8,12},{12,8},{16,20},{20,16},{24,28},{28,24},{1,5},{5... | collective-permute-start | bytes 3145736 | tf_op jit(solution)/shard_map/ppermute | solution.py:713
  143.1 49.3 %collective-permute-start.17 = (bf16[256,2048]{1,0:T(8,128)(2,1)S(1)}, bf16[256,2048]{1,0:T(8,128)(2,1)}, u32[]{:S(2)}, u32[]{:S(2)}) collective-permute-start(bf16[256,2048]{1,0:T(8,128)(2,1)S(1)} %collective-permute-done.15), channel_id=1, source_target_pairs={{0,8},{4,12},{8,16},{12,20},{16,24},{20,28},{24,0},{28,4},{1,9},{5... | collective-permute-start | bytes 3145736 | tf_op jit(solution)/shard_map/ppermute | solution.py:718
  144.5 61.4 %collective-permute-start.23 = (bf16[2048,256]{1,0:T(8,128)(2,1)S(1)}, bf16[2048,256]{1,0:T(8,128)(2,1)S(1)}, u32[]{:S(2)}, u32[]{:S(2)}) collective-permute-start(bf16[2048,256]{1,0:T(8,128)(2,1)S(1)} %collective-permute-done.22), channel_id=1, source_target_pairs={{0,4},{4,0},{8,12},{12,8},{16,20},{20,16},{24,28},{28,24},{1,5},{5... | collective-permute-start | bytes 3145736 | tf_op jit(solution)/shard_map/ppermute | solution.py:713
  161.0 53.8 %collective-permute-start.24 = (bf16[2048,256]{1,0:T(8,128)(2,1)S(1)}, bf16[2048,256]{1,0:T(8,128)(2,1)}, u32[]{:S(2)}, u32[]{:S(2)}) collective-permute-start(bf16[2048,256]{1,0:T(8,128)(2,1)S(1)} %collective-permute-done.22), channel_id=1, source_target_pairs={{0,8},{4,12},{8,16},{12,20},{16,24},{20,28},{24,0},{28,4},{1,9},{5... | collective-permute-start | bytes 3145736 | tf_op jit(solution)/shard_map/ppermute | solution.py:718
  169.8 71.2 %collective-permute-start.1 = (bf16[2,512,1024]{2,1,0:T(8,128)(2,1)S(1)}, bf16[2,512,1024]{2,1,0:T(8,128)(2,1)S(1)}, u32[]{:S(2)}, u32[]{:S(2)}) collective-permute-start(bf16[2,512,1024]{2,1,0:T(8,128)(2,1)S(1)} %collective-permute-done), channel_id=1, source_target_pairs={{0,1},{1,0},{2,3},{3,2},{4,5},{5,4},{6,7},{7,6},{8,9},{9,8},{10,11... | collective-permute-start | bytes 6291464 | tf_op jit(solution)/shard_map/ppermute | solution.py:713
  183.4 55.3 %collective-permute-start.6 = (bf16[256,2432]{1,0:T(8,128)(2,1)S(1)}, bf16[256,2432]{1,0:T(8,128)(2,1)S(1)}, u32[]{:S(2)}, u32[]{:S(2)}) collective-permute-start(bf16[256,2432]{1,0:T(8,128)(2,1)S(1)} %collective-permute-done.5), channel_id=1, source_target_pairs={{0,4},{4,0},{8,12},{12,8},{16,20},{20,16},{24,28},{28,24},{1,5},{5... | collective-permute-start | bytes 3735560 | tf_op jit(solution)/shard_map/ppermute | solution.py:713
  192.3 45.3 %collective-permute-start.7 = (bf16[256,2432]{1,0:T(8,128)(2,1)S(1)}, bf16[256,2432]{1,0:T(8,128)(2,1)S(1)}, u32[]{:S(2)}, u32[]{:S(2)}) collective-permute-start(bf16[256,2432]{1,0:T(8,128)(2,1)S(1)} %collective-permute-done.5), channel_id=1, source_target_pairs={{0,8},{4,12},{8,16},{12,20},{16,24},{20,28},{24,0},{28,4},{1,9},{5... | collective-permute-start | bytes 3735560 | tf_op jit(solution)/shard_map/ppermute | solution.py:718
  205.9 116.6 %collective-permute-start.18 = (bf16[256,2048]{1,0:T(8,128)(2,1)}, bf16[256,2048]{1,0:T(8,128)(2,1)}, u32[]{:S(2)}, u32[]{:S(2)}) collective-permute-start(bf16[256,2048]{1,0:T(8,128)(2,1)} %collective-permute-done.17), channel_id=1, source_target_pairs={{0,4},{4,0},{8,12},{12,8},{16,20},{20,16},{24,28},{28,24},{1,5},{5... | collective-permute-start | bytes 3145736 | tf_op jit(solution)/shard_map/ppermute | solution.py:713
  214.8 154.5 %collective-permute-start.25 = (bf16[2048,256]{1,0:T(8,128)(2,1)}, bf16[2048,256]{1,0:T(8,128)(2,1)}, u32[]{:S(2)}, u32[]{:S(2)}) collective-permute-start(bf16[2048,256]{1,0:T(8,128)(2,1)} %collective-permute-done.24), channel_id=1, source_target_pairs={{0,4},{4,0},{8,12},{12,8},{16,20},{20,16},{24,28},{28,24},{1,5},{5... | collective-permute-start | bytes 3145736 | tf_op jit(solution)/shard_map/ppermute | solution.py:713
  237.6 65.8 %collective-permute-start.8 = (bf16[256,2432]{1,0:T(8,128)(2,1)S(1)}, bf16[256,2432]{1,0:T(8,128)(2,1)S(1)}, u32[]{:S(2)}, u32[]{:S(2)}) collective-permute-start(bf16[256,2432]{1,0:T(8,128)(2,1)S(1)} %collective-permute-done.7), channel_id=1, source_target_pairs={{0,4},{4,0},{8,12},{12,8},{16,20},{20,16},{24,28},{28,24},{1,5},{5... | collective-permute-start | bytes 3735560 | tf_op jit(solution)/shard_map/ppermute | solution.py:713
  351.4 47.7 %collective-permute-start.10 = (f32[128,2048]{1,0:T(8,128)S(1)}, f32[128,2048]{1,0:T(8,128)S(1)}, u32[]{:S(2)}, u32[]{:S(2)}) collective-permute-start(f32[128,2048]{1,0:T(8,128)S(1)} %get-tuple-element.48.fin), channel_id=1, source_target_pairs={{0,2},{1,3},{4,6},{5,7},{8,10},{9,11},{12,14},{13,15},{16,18},{17,... | collective-permute-start | bytes 3145736 | tf_op jit(solution)/shard_map/ppermute | solution.py:708
  517.0 126.3 %collective-permute-start.57 = (bf16[2048,256]{1,0:T(8,128)(2,1)}, bf16[2048,256]{1,0:T(8,128)(2,1)}, u32[]{:S(2)}, u32[]{:S(2)}) collective-permute-start(bf16[2048,256]{1,0:T(8,128)(2,1)} %convolution_convert_fusion.6), channel_id=1, source_target_pairs={{0,4},{4,0},{8,12},{12,8},{16,20},{20,16},{24,28},{28,24},{1,5},{5... | collective-permute-start | bytes 3145736 | tf_op jit(solution)/shard_map/ppermute | solution.py:713
  517.5 130.8 %collective-permute-start.59 = (bf16[2048,256]{1,0:T(8,128)(2,1)}, bf16[2048,256]{1,0:T(8,128)(2,1)}, u32[]{:S(2)}, u32[]{:S(2)}) collective-permute-start(bf16[2048,256]{1,0:T(8,128)(2,1)} %convolution_convert_fusion.5), channel_id=1, source_target_pairs={{0,4},{4,0},{8,12},{12,8},{16,20},{20,16},{24,28},{28,24},{1,5},{5... | collective-permute-start | bytes 3145736 | tf_op jit(solution)/shard_map/ppermute | solution.py:713
  519.0 202.2 %collective-permute-start.61 = (bf16[2048,256]{1,0:T(8,128)(2,1)}, bf16[2048,256]{1,0:T(8,128)(2,1)}, u32[]{:S(2)}, u32[]{:S(2)}) collective-permute-start(bf16[2048,256]{1,0:T(8,128)(2,1)} %convolution_convert_fusion.4), channel_id=1, source_target_pairs={{0,4},{4,0},{8,12},{12,8},{16,20},{20,16},{24,28},{28,24},{1,5},{5... | collective-permute-start | bytes 3145736 | tf_op jit(solution)/shard_map/ppermute | solution.py:713
  525.3 63.9 %collective-permute-start.29 = (f32[128,2048]{1,0:T(8,128)S(1)}, f32[128,2048]{1,0:T(8,128)S(1)}, u32[]{:S(2)}, u32[]{:S(2)}) collective-permute-start(f32[128,2048]{1,0:T(8,128)S(1)} %fusion.14), channel_id=1, source_target_pairs={{2,0},{3,1},{6,4},{7,5},{10,8},{11,9},{14,12},{15,13},{18,16},{19,... | collective-permute-start | bytes 3145736 | tf_op jit(solution)/shard_map/ppermute | solution.py:708
  541.2 96.7 %collective-permute-start.38 = (bf16[256,2048]{1,0:T(8,128)(2,1)S(1)}, bf16[256,2048]{1,0:T(8,128)(2,1)S(1)}, u32[]{:S(2)}, u32[]{:S(2)}) collective-permute-start(bf16[256,2048]{1,0:T(8,128)(2,1)S(1)} %copy-done.59), channel_id=1, source_target_pairs={{0,4},{4,0},{8,12},{12,8},{16,20},{20,16},{24,28},{28,24},{1,5},{5... | collective-permute-start | bytes 3145736 | tf_op jit(solution)/shard_map/ppermute | solution.py:713
  589.2 64.6 %collective-permute-start.40 = (bf16[256,2048]{1,0:T(8,128)(2,1)}, bf16[256,2048]{1,0:T(8,128)(2,1)S(1)}, u32[]{:S(2)}, u32[]{:S(2)}) collective-permute-start(bf16[256,2048]{1,0:T(8,128)(2,1)} %convolution_convert_fusion.10), channel_id=1, source_target_pairs={{0,4},{4,0},{8,12},{12,8},{16,20},{20,16},{24,28},{28,24},{1,5},{5... | collective-permute-start | bytes 3145736 | tf_op jit(solution)/shard_map/ppermute | solution.py:713
  637.9 84.8 %collective-permute-start.42 = (bf16[256,2048]{1,0:T(8,128)(2,1)}, bf16[256,2048]{1,0:T(8,128)(2,1)}, u32[]{:S(2)}, u32[]{:S(2)}) collective-permute-start(bf16[256,2048]{1,0:T(8,128)(2,1)} %convolution_convert_fusion.9), channel_id=1, source_target_pairs={{0,4},{4,0},{8,12},{12,8},{16,20},{20,16},{24,28},{28,24},{1,5},{5... | collective-permute-start | bytes 3145736 | tf_op jit(solution)/shard_map/ppermute | solution.py:713
  643.3 82.5 %collective-permute-start.44 = (bf16[256,2048]{1,0:T(8,128)(2,1)}, bf16[256,2048]{1,0:T(8,128)(2,1)S(1)}, u32[]{:S(2)}, u32[]{:S(2)}) collective-permute-start(bf16[256,2048]{1,0:T(8,128)(2,1)} %convolution_convert_fusion.8), channel_id=1, source_target_pairs={{0,4},{4,0},{8,12},{12,8},{16,20},{20,16},{24,28},{28,24},{1,5},{5... | collective-permute-start | bytes 3145736 | tf_op jit(solution)/shard_map/ppermute | solution.py:713
  648.4 78.1 %collective-permute-start.56 = (bf16[2048,256]{1,0:T(8,128)(2,1)}, bf16[2048,256]{1,0:T(8,128)(2,1)}, u32[]{:S(2)}, u32[]{:S(2)}) collective-permute-start(bf16[2048,256]{1,0:T(8,128)(2,1)} %add_convert_fusion.7), channel_id=1, source_target_pairs={{0,8},{4,12},{8,16},{12,20},{16,24},{20,28},{24,0},{28,4},{1,9},{5... | collective-permute-start | bytes 3145736 | tf_op jit(solution)/shard_map/ppermute | solution.py:718
  663.8 63.6 %collective-permute-start.58 = (bf16[2048,256]{1,0:T(8,128)(2,1)}, bf16[2048,256]{1,0:T(8,128)(2,1)}, u32[]{:S(2)}, u32[]{:S(2)}) collective-permute-start(bf16[2048,256]{1,0:T(8,128)(2,1)} %add_convert_fusion.6), channel_id=1, source_target_pairs={{0,16},{4,20},{8,24},{12,28},{16,0},{20,4},{24,8},{28,12},{1,17},{... | collective-permute-start | bytes 3145736 | tf_op jit(solution)/shard_map/ppermute | solution.py:718
  721.3 47.6 %collective-permute-start.60 = (bf16[2048,256]{1,0:T(8,128)(2,1)}, bf16[2048,256]{1,0:T(8,128)(2,1)S(1)}, u32[]{:S(2)}, u32[]{:S(2)}) collective-permute-start(bf16[2048,256]{1,0:T(8,128)(2,1)} %add_convert_fusion.5), channel_id=1, source_target_pairs={{0,24},{4,28},{8,0},{12,4},{16,8},{20,12},{24,16},{28,20},{1,25},{... | collective-permute-start | bytes 3145736 | tf_op jit(solution)/shard_map/ppermute | solution.py:718
  722.7 352.0 %collective-permute-start.32 = (f32[1024,2048]{1,0:T(8,128)}, f32[1024,2048]{1,0:T(8,128)}, u32[]{:S(2)}, u32[]{:S(2)}) collective-permute-start(f32[1024,2048]{1,0:T(8,128)} %convolution_add_fusion), channel_id=1, source_target_pairs={{0,1},{1,0},{2,3},{3,2},{4,5},{5,4},{6,7},{7,6},{8,9},{9,8},{10,11... | collective-permute-start | bytes 25165832 | tf_op jit(solution)/shard_map/ppermute | solution.py:713
  725.8 48.0 %collective-permute-start.39 = (bf16[256,2048]{1,0:T(8,128)(2,1)S(1)}, bf16[256,2048]{1,0:T(8,128)(2,1)S(1)}, u32[]{:S(2)}, u32[]{:S(2)}) collective-permute-start(bf16[256,2048]{1,0:T(8,128)(2,1)S(1)} %copy-done.57), channel_id=1, source_target_pairs={{0,8},{4,12},{8,16},{12,20},{16,24},{20,28},{24,0},{28,4},{1,9},{5... | collective-permute-start | bytes 3145736 | tf_op jit(solution)/shard_map/ppermute | solution.py:718
  726.5 47.5 %collective-permute-start.46 = (bf16[256,2432]{1,0:T(8,128)(2,1)S(1)}, bf16[256,2432]{1,0:T(8,128)(2,1)S(1)}, u32[]{:S(2)}, u32[]{:S(2)}) collective-permute-start(bf16[256,2432]{1,0:T(8,128)(2,1)S(1)} %convolution_convert_fusion.3), channel_id=1, source_target_pairs={{0,4},{4,0},{8,12},{12,8},{16,20},{20,16},{24,28},{28,24},{1,5},{5... | collective-permute-start | bytes 3735560 | tf_op jit(solution)/shard_map/ppermute | solution.py:713
  727.4 56.0 %collective-permute-start.48 = (bf16[256,2432]{1,0:T(8,128)(2,1)S(1)}, bf16[256,2432]{1,0:T(8,128)(2,1)S(1)}, u32[]{:S(2)}, u32[]{:S(2)}) collective-permute-start(bf16[256,2432]{1,0:T(8,128)(2,1)S(1)} %convolution_convert_fusion.2), channel_id=1, source_target_pairs={{0,4},{4,0},{8,12},{12,8},{16,20},{20,16},{24,28},{28,24},{1,5},{5... | collective-permute-start | bytes 3735560 | tf_op jit(solution)/shard_map/ppermute | solution.py:713
  768.9 41.2 %collective-permute-start.50 = (bf16[256,2432]{1,0:T(8,128)(2,1)S(1)}, bf16[256,2432]{1,0:T(8,128)(2,1)S(1)}, u32[]{:S(2)}, u32[]{:S(2)}) collective-permute-start(bf16[256,2432]{1,0:T(8,128)(2,1)S(1)} %convolution_convert_fusion.1), channel_id=1, source_target_pairs={{0,4},{4,0},{8,12},{12,8},{16,20},{20,16},{24,28},{28,24},{1,5},{5... | collective-permute-start | bytes 3735560 | tf_op jit(solution)/shard_map/ppermute | solution.py:713
  773.9 44.2 %collective-permute-start.41 = (bf16[256,2048]{1,0:T(8,128)(2,1)S(1)}, bf16[256,2048]{1,0:T(8,128)(2,1)S(1)}, u32[]{:S(2)}, u32[]{:S(2)}) collective-permute-start(bf16[256,2048]{1,0:T(8,128)(2,1)S(1)} %copy-done.58), channel_id=1, source_target_pairs={{0,16},{4,20},{8,24},{12,28},{16,0},{20,4},{24,8},{28,12},{1,17},{... | collective-permute-start | bytes 3145736 | tf_op jit(solution)/shard_map/ppermute | solution.py:718
  774.0 66.2 %collective-permute-start.43 = (bf16[256,2048]{1,0:T(8,128)(2,1)S(1)}, bf16[256,2048]{1,0:T(8,128)(2,1)S(1)}, u32[]{:S(2)}, u32[]{:S(2)}) collective-permute-start(bf16[256,2048]{1,0:T(8,128)(2,1)S(1)} %add_convert_fusion.8), channel_id=1, source_target_pairs={{0,24},{4,28},{8,0},{12,4},{16,8},{20,12},{24,16},{28,20},{1,25},{... | collective-permute-start | bytes 3145736 | tf_op jit(solution)/shard_map/ppermute | solution.py:718
  783.4 60.2 %collective-permute-start.52 = (bf16[256,2432]{1,0:T(8,128)(2,1)S(1)}, bf16[256,2432]{1,0:T(8,128)(2,1)S(1)}, u32[]{:S(2)}, u32[]{:S(2)}) collective-permute-start(bf16[256,2432]{1,0:T(8,128)(2,1)S(1)} %convolution_convert_fusion), channel_id=1, source_target_pairs={{0,4},{4,0},{8,12},{12,8},{16,20},{20,16},{24,28},{28,24},{1,5},{5... | collective-permute-start | bytes 3735560 | tf_op jit(solution)/shard_map/ppermute | solution.py:713
  810.1 316.6 %collective-permute-start.27 = (f32[1024,2048]{1,0:T(8,128)}, f32[1024,2048]{1,0:T(8,128)}, u32[]{:S(2)}, u32[]{:S(2)}) collective-permute-start(f32[1024,2048]{1,0:T(8,128)} %fusion.133), channel_id=1, source_target_pairs={{0,1},{1,0},{2,3},{3,2},{4,5},{5,4},{6,7},{7,6},{8,9},{9,8},{10,11... | collective-permute-start | bytes 25165832 | tf_op jit(solution)/shard_map/ppermute | solution.py:713
  818.1 53.2 %collective-permute-start.47 = (bf16[256,2432]{1,0:T(8,128)(2,1)S(1)}, bf16[256,2432]{1,0:T(8,128)(2,1)S(1)}, u32[]{:S(2)}, u32[]{:S(2)}) collective-permute-start(bf16[256,2432]{1,0:T(8,128)(2,1)S(1)} %add_convert_fusion.4), channel_id=1, source_target_pairs={{0,8},{4,12},{8,16},{12,20},{16,24},{20,28},{24,0},{28,4},{1,9},{5... | collective-permute-start | bytes 3735560 | tf_op jit(solution)/shard_map/ppermute | solution.py:718
  840.2 83.9 %collective-permute-start.49 = (bf16[256,2432]{1,0:T(8,128)(2,1)S(1)}, bf16[256,2432]{1,0:T(8,128)(2,1)S(1)}, u32[]{:S(2)}, u32[]{:S(2)}) collective-permute-start(bf16[256,2432]{1,0:T(8,128)(2,1)S(1)} %add_convert_fusion.3), channel_id=1, source_target_pairs={{0,16},{4,20},{8,24},{12,28},{16,0},{20,4},{24,8},{28,12},{1,17},{... | collective-permute-start | bytes 3735560 | tf_op jit(solution)/shard_map/ppermute | solution.py:718
  843.6 80.5 %collective-permute-start.51 = (bf16[256,2432]{1,0:T(8,128)(2,1)S(1)}, bf16[256,2432]{1,0:T(8,128)(2,1)S(1)}, u32[]{:S(2)}, u32[]{:S(2)}) collective-permute-start(bf16[256,2432]{1,0:T(8,128)(2,1)S(1)} %add_convert_fusion.2), channel_id=1, source_target_pairs={{0,24},{4,28},{8,0},{12,4},{16,8},{20,12},{24,16},{28,20},{1,25},{... | collective-permute-start | bytes 3735560 | tf_op jit(solution)/shard_map/ppermute | solution.py:718
  871.4 56.7 %collective-permute-start.33 = (f32[8,256]{1,0:T(8,128)S(1)}, f32[8,256]{1,0:T(8,128)S(1)}, u32[]{:S(2)}, u32[]{:S(2)}) collective-permute-start(f32[8,256]{1,0:T(8,128)S(1)} %add.401), channel_id=1, source_target_pairs={{0,1},{1,0},{2,3},{3,2},{4,5},{5,4},{6,7},{7,6},{8,9},{9,8},{10,11... | collective-permute-start | bytes 24584 | tf_op jit(solution)/shard_map/ppermute | solution.py:713
  924.1 48.8 %collective-permute-start.62 = (f32[2048,256]{1,0:T(8,128)}, f32[2048,256]{1,0:T(8,128)}, u32[]{:S(2)}, u32[]{:S(2)}) collective-permute-start(f32[2048,256]{1,0:T(8,128)} %add_add_fusion.1), channel_id=1, source_target_pairs={{0,2},{2,0},{1,3},{3,1},{4,6},{6,4},{5,7},{7,5},{8,10},{10,8},{9,1... | collective-permute-start | bytes 6291464 | tf_op jit(solution)/shard_map/ppermute | solution.py:756
  924.1 93.8 %collective-permute-start.45 = (f32[256,2048]{1,0:T(8,128)}, f32[256,2048]{1,0:T(8,128)}, u32[]{:S(2)}, u32[]{:S(2)}) collective-permute-start(f32[256,2048]{1,0:T(8,128)} %add_add_fusion.2), channel_id=1, source_target_pairs={{0,2},{2,0},{1,3},{3,1},{4,6},{6,4},{5,7},{7,5},{8,10},{10,8},{9,1... | collective-permute-start | bytes 6291464 | tf_op jit(solution)/shard_map/ppermute | solution.py:756
  928.1 142.1 %collective-permute-start.53 = (f32[256,2432]{1,0:T(8,128)S(1)}, f32[256,2432]{1,0:T(8,128)}, u32[]{:S(2)}, u32[]{:S(2)}) collective-permute-start(f32[256,2432]{1,0:T(8,128)S(1)} %add_add_fusion), channel_id=1, source_target_pairs={{0,2},{2,0},{1,3},{3,1},{4,6},{6,4},{5,7},{7,5},{8,10},{10,8},{9,1... | collective-permute-start | bytes 7471112 | tf_op jit(solution)/shard_map/ppermute | solution.py:756
  (78 other events, 1346.9 us)

commit v2 on v1

--- a/solution.py
+++ b/solution.py
@@ -10,6 +10,7 @@
 
 CHUNK = 128
 LANES = 128
+MESH = pl.DeviceIdType.MESH
 f32 = jnp.float32
 bf16 = jnp.bfloat16
 epsilon = 1e-05
@@ -702,6 +703,478 @@
     )
 
 
+def gather_kernel(arrays, shared, *refs):
+    weights, tokens = refs[:arrays], refs[arrays]
+    fulls, far = refs[arrays + 1 : 2 * arrays + 1], refs[2 * arrays + 1]
+    refs = refs[2 * arrays + 2 :]
+    ring_send, ring_recv, pair_send, pair_recv, cross_send, cross_recv, extra_send, extra_recv, local_sem = refs
+    count = lax.axis_size("fsdp")
+    pairs = count // 2
+    own, place, side = lax.axis_index("fsdp"), lax.axis_index("context"), lax.axis_index("tensor")
+    pair, member = own // 2, lax.rem(own, 2)
+    rows = weights[0].shape[0]
+    moved = rows - shared
+
+    def at(offset, which):
+        there = lax.rem(pair + pairs - offset, pairs)
+        return 2 * there + (member if which == 0 else 1 - member)
+
+    ahead = (2 * lax.rem(pair + 1, pairs) + member, place, side)
+    behind = (2 * lax.rem(pair + pairs - 1, pairs) + member, place, side)
+    partner = (2 * pair + 1 - member, place, side)
+    across = (own, 1 - place, side)
+    beside = (own, place, 1 - side)
+    barrier = pltpu.get_barrier_semaphore()
+    greeted = [ahead, behind, partner, across, beside]
+    for device in greeted:
+        pl.semaphore_signal(barrier, inc=1, device_id=device, device_id_type=MESH)
+    pl.semaphore_wait(barrier, len(greeted))
+
+    def part(index, j, start, size):
+        return fulls[j].at[pl.ds(pl.multiple_of(index * rows + start, 16), size), :]
+
+    moved_start = pl.multiple_of(place * shared, 16)
+    shared_start = pl.multiple_of(place * moved, 16)
+
+    started = []
+
+    def send(src, dst, send_sem, recv_sem, device):
+        copy = pltpu.make_async_remote_copy(
+            src_ref=src, dst_ref=dst, send_sem=send_sem, recv_sem=recv_sem,
+            device_id=device, device_id_type=MESH,
+        )
+        copy.start()
+        started.append(copy)
+        return copy
+
+    kept = []
+    for j in range(arrays):
+        kept.append(
+            pltpu.make_async_copy(
+                weights[j], fulls[j].at[pl.ds(pl.multiple_of(own * rows, 16), rows), :], local_sem.at[j]
+            )
+        )
+        kept[-1].start()
+
+    def from_own(j):
+        return weights[j].at[pl.ds(moved_start, moved), :]
+
+    ring, within, crossed = {}, {}, []
+
+    def start_ring(j, k):
+        dst = part(at(k, 0), j, moved_start, moved)
+        ring[j, k] = send(
+            from_own(j) if k == 0 else dst, dst, ring_send.at[j, k], ring_recv.at[j, k], ahead
+        )
+
+    def start_pair(j, k):
+        dst = part(at(k, 0), j, moved_start, moved)
+        within[j, k] = send(
+            from_own(j) if k == 0 else dst, dst, pair_send.at[j, k], pair_recv.at[j, k], partner
+        )
+
+    def start_cross(j, k, which):
+        here = part(at(k, which), j, shared_start, shared)
+        slot = 2 * k + which
+        crossed.append(
+            send(here, here, cross_send.at[j, slot], cross_recv.at[j, slot], across)
+        )
+
+    half = tokens.shape[2] // 2
+    lanes = pl.ds(pl.multiple_of(side * half, 128), half)
+    token_copy = send(
+        tokens.at[:, :, lanes], far.at[:, :, lanes], extra_send.at[0], extra_recv.at[0], across
+    )
+    steps = [(j, k) for j in range(arrays) for k in range(pairs)]
+    waiting = []
+    forwarded = None
+    for number, (j, k) in enumerate(steps):
+        if k > 0:
+            ring[j, k - 1].wait_recv()
+        if k < pairs - 1:
+            start_ring(j, k)
+        start_pair(j, k)
+        if k > 0:
+            start_cross(j, k, 0)
+        waiting.append((j, k))
+        if len(waiting) > 2:
+            wj, wk = waiting.pop(0)
+            within[wj, wk].wait_recv()
+            start_cross(wj, wk, 1)
+        if number == min(pairs, len(steps) - 1):
+            token_copy.wait_recv()
+            forwarded = send(
+                far.at[:, :, lanes], far.at[:, :, lanes], extra_send.at[1], extra_recv.at[1], beside
+            )
+    for wj, wk in waiting:
+        within[wj, wk].wait_recv()
+        start_cross(wj, wk, 1)
+    forwarded.wait_recv()
+    for copy in crossed:
+        copy.wait_recv()
+    for copy in started:
+        copy.wait_send()
+    for copy in kept:
+        copy.wait()
+
+
+def gather_weights(shards, tokens, shared, collective_id):
+    rows = shards[0].shape[0]
+    pairs = lax.axis_size("fsdp") // 2
+    count = len(shards)
+    hbm = pl.BlockSpec(memory_space=pl.ANY)
+    dma = pltpu.SemaphoreType.DMA
+    return pl.pallas_call(
+        functools.partial(gather_kernel, count, shared),
+        out_shape=[
+            jax.ShapeDtypeStruct((2 * pairs * rows, shard.shape[1]), shard.dtype) for shard in shards
+        ]
+        + [jax.ShapeDtypeStruct(tokens.shape, tokens.dtype)],
+        in_specs=[hbm] * (count + 1),
+        out_specs=[hbm] * (count + 1),
+        scratch_shapes=[
+            dma((count, max(pairs - 1, 1))),
+            dma((count, max(pairs - 1, 1))),
+            dma((count, pairs)),
+            dma((count, pairs)),
+            dma((count, 2 * pairs)),
+            dma((count, 2 * pairs)),
+            dma((2,)),
+            dma((2,)),
+            dma((count,)),
+        ],
+        compiler_params=pltpu.CompilerParams(collective_id=collective_id, has_side_effects=True),
+    )(*shards, tokens)
+
+
+class Reduction:
+    def __init__(self, rows, pairs, columns, lag):
+        self.rows, self.pairs, self.columns, self.lag = rows, pairs, columns, lag
+        self.shared = rows // 4
+        self.moved = rows - self.shared
+        self.counts = [count // LANES for count in columns]
+        self.count = sum(self.counts)
+        self.steps = self.count + 4 * lag
+
+    def scratch(self):
+        shared, moved, pairs, count = self.shared, self.moved, self.pairs, self.count
+        cross, pair, ring = 2 * pairs * shared + 16, pairs * moved + 16, moved + 16
+        i16, dma = jnp.int16, pltpu.SemaphoreType.DMA
+        return [
+            pltpu.VMEM((count, cross, LANES), i16),
+            pltpu.VMEM((count, pair, LANES), i16),
+            pltpu.VMEM((count, pairs - 1, ring, LANES), i16),
+            pltpu.VMEM((count, ring, LANES), i16),
+            pltpu.VMEM((2, cross, LANES), i16),
+            pltpu.VMEM((2, pair, LANES), i16),
+            pltpu.VMEM((2, pairs - 1, ring, LANES), i16),
+            pltpu.VMEM((2, ring, LANES), i16),
+            pltpu.VMEM((2, pairs, 2, shared, LANES), f32),
+            pltpu.VMEM((2, pairs, moved, LANES), f32),
+            pltpu.VMEM((2, pairs, moved, LANES), f32),
+            pltpu.VMEM((2 * self.lag, moved, LANES), f32),
+            pltpu.VMEM((2 * self.lag, moved, LANES), f32),
+            pltpu.VMEM((2, self.rows, LANES), f32),
+            dma((count,)),
+            dma((count,)),
+            dma((pairs - 1, count)),
+            dma((count,)),
+            dma((2,)),
+            dma((2,)),
+            dma((pairs - 1, 2)),
+            dma((2,)),
+            dma((3, 2)),
+            dma((2,)),
+        ]
+
+    def bind(self, terms, outs, scratch):
+        self.terms, self.outs = terms, outs
+        (
+            self.cross_in, self.pair_in, self.ring_in, self.last_in,
+            self.cross_out, self.pair_out, self.ring_out, self.last_out,
+            self.cross_term, self.pair_term, self.ring_term,
+            self.kept, self.held, self.result,
+            self.cross_recv, self.pair_recv, self.ring_recv, self.last_recv,
+            self.cross_sent, self.pair_sent, self.ring_sent, self.last_sent,
+            self.loaded, self.stored,
+        ) = scratch
+        self.own, self.place = lax.axis_index("fsdp"), lax.axis_index("context")
+        self.side = lax.axis_index("tensor")
+        self.pair, self.member = self.own // 2, lax.rem(self.own, 2)
+        self.across = (self.own, 1 - self.place, self.side)
+        self.partner = (2 * self.pair + 1 - self.member, self.place, self.side)
+        self.inset = pl.multiple_of(self.place * (self.moved - self.shared), 16)
+        self.start = pl.multiple_of(self.place * self.shared, 16)
+
+    def peer(self, offset):
+        there = lax.rem(self.pair + offset, self.pairs)
+        return (2 * there + self.member, self.place, self.side)
+
+    def greet(self):
+        barrier = pltpu.get_barrier_semaphore()
+        devices = [self.across, self.partner] + [self.peer(k) for k in range(1, self.pairs)]
+        for device in devices:
+            pl.semaphore_signal(barrier, inc=1, device_id=device, device_id_type=MESH)
+        pl.semaphore_wait(barrier, len(devices))
+
+    def cross_copy(self, chunk):
+        slot = lax.rem(chunk, 2)
+        return pltpu.make_async_remote_copy(
+            src_ref=self.cross_out.at[slot], dst_ref=self.cross_in.at[chunk],
+            send_sem=self.cross_sent.at[slot], recv_sem=self.cross_recv.at[chunk],
+            device_id=self.across, device_id_type=MESH,
+        )
+
+    def pair_copy(self, chunk):
+        slot = lax.rem(chunk, 2)
+        return pltpu.make_async_remote_copy(
+            src_ref=self.pair_out.at[slot], dst_ref=self.pair_in.at[chunk],
+            send_sem=self.pair_sent.at[slot], recv_sem=self.pair_recv.at[chunk],
+            device_id=self.partner, device_id_type=MESH,
+        )
+
+    def ring_copy(self, chunk, offset):
+        slot = lax.rem(chunk, 2)
+        return pltpu.make_async_remote_copy(
+            src_ref=self.ring_out.at[slot, offset - 1], dst_ref=self.ring_in.at[chunk, offset - 1],
+            send_sem=self.ring_sent.at[offset - 1, slot],
+            recv_sem=self.ring_recv.at[offset - 1, chunk],
+            device_id=self.peer(offset), device_id_type=MESH,
+        )
+
+    def last_copy(self, chunk):
+        slot = lax.rem(chunk, 2)
+        return pltpu.make_async_remote_copy(
+            src_ref=self.last_out.at[slot], dst_ref=self.last_in.at[chunk],
+            send_sem=self.last_sent.at[slot], recv_sem=self.last_recv.at[chunk],
+            device_id=self.across, device_id_type=MESH,
+        )
+
+    def load_copy(self, stage, term, cols, slot):
+        if stage == 0:
+            rows = pl.ds(pl.multiple_of((1 - self.place) * self.moved, 16), self.shared)
+            src, dst = term.at[:, :, rows, cols], self.cross_term.at[slot]
+        elif stage == 1:
+            src = term.at[:, 1 - self.member, pl.ds(self.start, self.moved), cols]
+            dst = self.pair_term.at[slot]
+        else:
+            src = term.at[:, self.member, pl.ds(self.start, self.moved), cols]
+            dst = self.ring_term.at[slot]
+        return pltpu.make_async_copy(src, dst, self.loaded.at[stage, slot])
+
+    def each_array(self, chunk, act):
+        first = 0
+        for number, count in enumerate(self.counts):
+            inside = (chunk >= first) & (chunk < first + count)
+            offset = first
+
+            @pl.when(inside)
+            def _(number=number, offset=offset):
+                act(number, pl.ds(pl.multiple_of((chunk - offset) * LANES, LANES), LANES))
+
+            first += count
+
+    def load(self, stage, chunk):
+        @pl.when((chunk >= 0) & (chunk < self.count))
+        def _():
+            self.each_array(
+                chunk,
+                lambda number, cols: self.load_copy(
+                    stage, self.terms[number], cols, lax.rem(chunk, 2)
+                ).start(),
+            )
+
+    def loaded_now(self, stage, chunk):
+        self.load_copy(stage, self.terms[0], pl.ds(0, LANES), lax.rem(chunk, 2)).wait()
+
+    @staticmethod
+    def encode(value, out, place):
+        count = value.shape[0]
+        peak = jnp.maximum(jnp.max(jnp.abs(value), axis=0, keepdims=True), 1e-30)
+        exponent = jnp.ceil(jnp.log(peak) * 1.4426950408889634)
+        factor = jnp.exp(exponent * -0.6931471805599453) * 32000.0
+        out[place + (pl.ds(0, count), slice(None))] = (
+            jnp.round(value * factor).astype(jnp.int32).astype(jnp.int16)
+        )
+        out[place + (pl.ds(count, 16), slice(None))] = (
+            jnp.broadcast_to(exponent, (16, LANES)).astype(jnp.int32).astype(jnp.int16)
+        )
+
+    @staticmethod
+    def unit(ref, place, count):
+        exponents = ref[place + (pl.ds(count, 16), slice(None))].astype(jnp.int32).astype(f32)
+        return jnp.exp(exponents[:1] * 0.6931471805599453) * (1.0 / 32000.0)
+
+    @staticmethod
+    def decode(ref, place, first, count, unit):
+        first = pl.multiple_of(first, 16) if not isinstance(first, int) else first
+        return ref[place + (pl.ds(first, count), slice(None))].astype(jnp.int32).astype(f32) * unit
+
+    def step(self, number):
+        lag, pairs, shared, moved = self.lag, self.pairs, self.shared, self.moved
+
+        @pl.when(number == 0)
+        def _():
+            self.load(0, number)
+
+        self.load(0, number + 1)
+        self.load(1, number + 1 - lag)
+        self.load(2, number + 1 - 2 * lag)
+
+        def stage(index, act):
+            chunk = number - index * lag
+
+            @pl.when((chunk >= 0) & (chunk < self.count))
+            def _():
+                act(chunk, lax.rem(chunk, 2))
+
+        def cross(chunk, slot):
+            self.loaded_now(0, chunk)
+
+            @pl.when(chunk >= 2)
+            def _():
+                self.cross_copy(chunk - 2).wait_send()
+
+            value = self.cross_term[slot].reshape(2 * pairs * shared, LANES)
+            self.encode(value, self.cross_out, (slot,))
+            self.cross_copy(chunk).start()
+
+        def pair(chunk, slot):
+            self.loaded_now(1, chunk)
+            self.cross_copy(chunk).wait_recv()
+
+            @pl.when(chunk >= 2)
+            def _():
+                self.pair_copy(chunk - 2).wait_send()
+
+            unit = self.unit(self.cross_in, (chunk,), 2 * pairs * shared)
+            for there in range(pairs):
+                first = (2 * there + 1 - self.member) * shared
+                self.pair_term[slot, there, pl.ds(self.inset, shared), :] += self.decode(
+                    self.cross_in, (chunk,), first, shared, unit
+                )
+            value = self.pair_term[slot].reshape(pairs * moved, LANES)
+            self.encode(value, self.pair_out, (slot,))
+            self.pair_copy(chunk).start()
+
+        def ring(chunk, slot):
+            self.loaded_now(2, chunk)
+            self.pair_copy(chunk).wait_recv()
+
+            @pl.when(chunk >= 2)
+            def _():
+                for offset in range(1, pairs):
+                    self.ring_copy(chunk - 2, offset).wait_send()
+
+            cross_unit = self.unit(self.cross_in, (chunk,), 2 * pairs * shared)
+            pair_unit = self.unit(self.pair_in, (chunk,), pairs * moved)
+            for offset in list(range(1, pairs)) + [0]:
+                there = lax.rem(self.pair + offset, pairs)
+                first = (2 * there + self.member) * shared
+                self.ring_term[slot, there, pl.ds(self.inset, shared), :] += self.decode(
+                    self.cross_in, (chunk,), first, shared, cross_unit
+                )
+                value = self.ring_term[slot, there] + self.decode(
+                    self.pair_in, (chunk,), there * moved, moved, pair_unit
+                )
+                if offset:
+                    self.encode(value, self.ring_out, (slot, offset - 1))
+                    self.ring_copy(chunk, offset).start()
+                else:
+                    self.kept[lax.rem(chunk, 2 * lag)] = value
+
+        def last(chunk, slot):
+            for offset in range(1, pairs):
+                self.ring_copy(chunk, offset).wait_recv()
+
+            @pl.when(chunk >= 2)
+            def _():
+                self.last_copy(chunk - 2).wait_send()
+
+            total = self.kept[lax.rem(chunk, 2 * lag)]
+            for offset in range(1, pairs):
+                place = (chunk, offset - 1)
+                total = total + self.decode(
+                    self.ring_in, place, 0, moved, self.unit(self.ring_in, place, moved)
+                )
+            self.encode(total, self.last_out, (slot,))
+            self.held[lax.rem(chunk, 2 * lag)] = self.decode(
+                self.last_out, (slot,), 0, moved, self.unit(self.last_out, (slot,), moved)
+            )
+            self.last_copy(chunk).start()
+
+        def write_copy(number, cols, slot):
+            return pltpu.make_async_copy(
+                self.result.at[slot], self.outs[number].at[:, cols], self.stored.at[slot]
+            )
+
+        def write(chunk, slot):
+            self.last_copy(chunk).wait_recv()
+
+            @pl.when(chunk >= 2)
+            def _():
+                write_copy(0, pl.ds(0, LANES), slot).wait()
+
+            mine = self.held[lax.rem(chunk, 2 * lag)]
+            other = self.decode(
+                self.last_in, (chunk,), 0, moved, self.unit(self.last_in, (chunk,), moved)
+            )
+            low = jnp.where(self.place == 0, mine, other)
+            high = jnp.where(self.place == 0, other, mine)
+            self.result[slot, pl.ds(0, shared), :] = low[:shared]
+            self.result[slot, pl.ds(shared, moved - shared), :] = (
+                low[shared:] + high[: moved - shared]
+            )
+            self.result[slot, pl.ds(moved, shared), :] = high[moved - shared :]
+            self.each_array(chunk, lambda which, cols: write_copy(which, cols, slot).start())
+
+        stage(4, write)
+        stage(3, last)
+        stage(2, ring)
+        stage(1, pair)
+        stage(0, cross)
+
+        @pl.when(number == self.steps - 1)
+        def _():
+            for slot in range(2):
+                write_copy(0, pl.ds(0, LANES), slot).wait()
+                self.cross_copy(jnp.int32(self.count - 2 + slot)).wait_send()
+                self.pair_copy(jnp.int32(self.count - 2 + slot)).wait_send()
+                self.last_copy(jnp.int32(self.count - 2 + slot)).wait_send()
+                for offset in range(1, pairs):
+                    self.ring_copy(jnp.int32(self.count - 2 + slot), offset).wait_send()
+
+
+def reduce_kernel(plan, arrays, *refs):
+    plan.bind(refs[:arrays], refs[arrays : 2 * arrays], refs[2 * arrays :])
+    plan.greet()
+
+    def body(number, carried):
+        plan.step(number)
+        return carried
+
+    lax.fori_loop(0, plan.steps, body, 0)
+
+
+def reduce_terms(terms, lag, collective_id):
+    pairs = lax.axis_size("fsdp") // 2
+    rows = terms[0].shape[0] // (2 * pairs)
+    columns = [term.shape[1] for term in terms]
+    plan = Reduction(rows, pairs, columns, lag)
+    hbm = pl.BlockSpec(memory_space=pl.ANY)
+    arrays = len(terms)
+    return pl.pallas_call(
+        functools.partial(reduce_kernel, plan, arrays),
+        out_shape=[jax.ShapeDtypeStruct((rows, count), f32) for count in columns],
+        in_specs=[hbm] * arrays,
+        out_specs=[hbm] * arrays,
+        scratch_shapes=plan.scratch(),
+        compiler_params=pltpu.CompilerParams(
+            collective_id=collective_id, has_side_effects=True, vmem_limit_bytes=58 * 1024 * 1024
+        ),
+    )(*[term.reshape(pairs, 2, rows, -1) for term in terms])
+
+
 def passed_along(value, axis, steps):
     count = lax.axis_size(axis)
     initial, last = (max(0, -steps), min(count, count - steps))
@@ -717,44 +1190,6 @@
     count = lax.axis_size(axis)
     return lax.ppermute(
         value, axis, [(source, (source + 2 * steps) % count) for source in range(count)]
-    )
-
-
-def gathered(shard, dim):
-    pairs = lax.axis_size("fsdp") // 2
-    own = lax.axis_index("fsdp")
-    size = shard.shape[dim]
-    shape = list(shard.shape)
-    shape[dim] = size * 2 * pairs
-    full = jnp.zeros(shape, shard.dtype)
-    blocks = [shard]
-    for _ in range(pairs - 1):
-        blocks.append(ring_shift(blocks[-1], "fsdp", 1))
-    for offset, block in enumerate(blocks):
-        place = lax.rem(own + 2 * (pairs - offset), 2 * pairs)
-        full = lax.dynamic_update_slice_in_dim(full, block, place * size, dim)
-        other = paired(block, "fsdp")
-        full = lax.dynamic_update_slice_in_dim(full, other, (place ^ 1) * size, dim)
-    return full
-
-
-def scattered(block_of):
-    pairs = lax.axis_size("fsdp") // 2
-    own = lax.axis_index("fsdp")
-    order = list(range(1, pairs)) + [0]
-    arrived = {}
-    for offset in order:
-        place = lax.rem(own + 2 * offset, 2 * pairs)
-        arrived[offset] = paired(block_of(place ^ 1).astype(bf16), "fsdp")
-    total = None
-    for offset in order:
-        place = lax.rem(own + 2 * offset, 2 * pairs)
-        partial = block_of(place) + arrived[offset].astype(f32)
-        if offset:
-            partial = ring_shift(partial.astype(bf16), "fsdp", offset).astype(f32)
-        total = partial if total is None else total + partial
-    return total + lax.ppermute(
-        total, "context", [(source, source ^ 1) for source in range(lax.axis_size("context"))]
     )
 
 
@@ -823,7 +1258,6 @@
     place = lax.axis_index("context")
     base = place * count
     shard_rows = in_weight.shape[0]
-    half = model // 2
 
     narrow, wide_columns = selectors(heads, head_size)
     sel = jnp.asarray(narrow, bf16)
@@ -839,20 +1273,11 @@
         ],
         axis=1,
     )
-    lead_full = gathered(lead, 0)
-    gate_full = gathered(in_weight[:, 0, :], 0)
-    out_full = gathered(out_weight, 1)
-
-    mine = lax.dynamic_slice_in_dim(tokens[:, 0], side * half, half, 2)
-    far_half = lax.ppermute(
-        mine, "context", [(source, source ^ 1) for source in range(lax.axis_size("context"))]
-    )
-    far_other = paired(far_half, "tensor")
-    far = jnp.where(
-        side == 0,
-        jnp.concatenate([far_half, far_other], axis=2),
-        jnp.concatenate([far_other, far_half], axis=2),
-    )
+    shared_rows = max(shard_rows * 5 // 16 // 16 * 16, 16)
+    lead_full, gate_full, out_full, far = gather_weights(
+        [lead, in_weight[:, 0, :], jnp.transpose(out_weight)], tokens[:, 0], shared_rows, 1
+    )
+
     near = tokens[:, 0].reshape(micros, own_blocks, block_len, model)
     far = far.reshape(micros, own_blocks, block_len, model)
     everything = jnp.where(
@@ -911,7 +1336,7 @@
     gate_in = jnp.dot(normed, gate_full, preferred_element_type=f32)
     cot = cotangent[:, 0].reshape(micros * count, model)
     out_grad = cot * keep.astype(bf16)
-    norm_grad = contract_cols(out_grad, out_full)
+    norm_grad = jnp.dot(out_grad, out_full, preferred_element_type=f32)
 
     mixers = []
     for micro in range(micros):
@@ -945,24 +1370,12 @@
         )
         pulled.append(chained(own_pull, forwards[micro][5][count // CHUNK], -1))
 
-    branch = jnp.dot(gated_norm, out_full, preferred_element_type=f32)
+    branch = contract_cols(gated_norm, out_full)
     branch = branch + paired(branch, "tensor")
     block_out = (x_float + keep * branch).astype(bf16)
 
-    def out_block(index):
-        columns = lax.dynamic_slice_in_dim(out_grad, index * shard_rows, shard_rows, 1)
-        return contract_rows(gated_norm, columns)
-
-    out_shard = scattered(out_block)
-
-    def in_block(grads):
-        def block(index):
-            columns = lax.dynamic_slice_in_dim(normed, index * shard_rows, shard_rows, 1)
-            return contract_rows(columns, grads)
-
-        return block
-
-    gate_shard = scattered(in_block(gate_grad))
+    out_term = contract_rows(out_grad, gated_norm)
+    gate_term = contract_rows(normed, gate_grad)
 
     backs = []
     for micro in range(micros):
@@ -999,7 +1412,9 @@
         ],
         axis=0,
     )
-    lead_shard = scattered(in_block(lead_grad))
+    out_shard, gate_shard, lead_shard = reduce_terms(
+        [out_term, gate_term, contract_rows(normed, lead_grad)], 2, 2
+    )
     normed_part = contract_cols(gate_grad, gate_full) + contract_cols(lead_grad, lead_full)
     normed_grad = normed_part + paired(normed_part, "tensor")
     x_hat = x_float * inv_rms
@@ -1027,7 +1442,7 @@
         jnp.stack([gate_shard, lead_shard[:, :inner]], axis=1),
         coupling_shard,
         lead_shard[:, inner + twice : inner + twice + heads],
-        out_shard,
+        jnp.transpose(out_shard),
         value_all[:4],
         value_all[4],
         coupling_all[:4],

time: 1160 us -> 997 us (0.86)
  waiting for transfers between devices: 512 us -> 25.1 us
  Pallas kernels: 147 us -> 616 us
  starting transfers between devices: 120 us -> 16.4 us
  other arithmetic: 112 us -> 81.1 us
  local copies, waits for them, and re-layouts: 67.8 us -> 48.1 us
  matrix products: 173 us -> 185 us
    pallas_call x0 -> x2, Pallas kernels: none -> 470 us  [the longest x1 255 us: reduce_terms(): pl.pallas_call(functools.partial(reduce_kernel, plan, arrays), out_shape=...]
    ppermute x22 -> x0, waiting for transfers between devices: 303 us -> none  [the longest x18 169 us: ring_shift(): lax.ppermute(value, axis, [(source, (source + 2 * steps) % count) for sou...]
    ppermute x31 -> x6, waiting for transfers between devices: 180 us -> 1.17 us  [paired(): lax.ppermute(value, axis, [(source, source ^ 1) for source in range(count)])]
    ppermute x22 -> x0, starting transfers between devices: 46 us -> none  [the longest x18 41.9 us: ring_shift(): lax.ppermute(value, axis, [(source, (source + 2 * steps) % count) for sou...]
    dynamic_update_slice x23 -> x0, local copies, waits for them, and re-layouts: 32 us -> none  [the longest x12 16.8 us: gathered(): full = lax.dynamic_update_slice_in_dim(full, other, (place ^ 1) * size, dim)]
    ppermute x31 -> x6, starting transfers between devices: 32.6 us -> 0.73 us  [paired(): lax.ppermute(value, axis, [(source, source ^ 1) for source in range(count)])]
    concatenate x1 -> x0, other arithmetic: 23.5 us -> none  [shards(): jnp.concatenate([jnp.concatenate([(back[0] + jnp.pad(edges[micro][:, :inn...]
    ppermute x4, starting transfers between devices: 27.8 us -> 6.03 us  [summed_everywhere(): lax.ppermute(flat, axis, [(source, source ^ reach) for source in range(me...]
  transfers between devices with their start and end apart: 63 -> 16, of which waited for: 33 -> 5; matrix products, arithmetic and copies ran while one was open for 22% -> 18% of each run, Pallas kernels for 13% -> 33%
where the time goes in v2:
time: 997 us; the launch traced here: 989 us
  Pallas kernels  616 us (62%)
  matrix products  185 us (19%)
  other arithmetic  81.1 us (8%)
  local copies, waits for them, and re-layouts  48.1 us (5%)
  waiting for transfers between devices  25.1 us (3%)
  between operations  17.6 us (2%)
  starting transfers between devices  16.4 us (2%)
    pallas_call x1, Pallas kernels, reduce_terms(): pl.pallas_call(functools.partial(reduce_kernel, plan, arrays), out_shape=...  255 us
    pallas_call x1, Pallas kernels, gather_weights(): pl.pallas_call(functools.partial(gather_kernel, count, shared), out_shape...  214 us
    pallas_call x2, Pallas kernels, backward_ssd(): pl.pallas_call(functools.partial(backward_kernel, heads), grid_spec=pltpu...  94.4 us
    dot_general x3, matrix products, contract_cols(): lax.dot_general(left, right, (((1,), (1,)), ((), ())), preferred_element_...  64.7 us
    dot_general x3, matrix products, contract_rows(): lax.dot_general(left, right, (((0,), (0,)), ((), ())), preferred_element_...  52.9 us
    pallas_call x2, Pallas kernels, forward_ssd(): pl.pallas_call(functools.partial(forward_kernel, heads), grid_spec=pltpu....  51.7 us
    unnamed x124, local copies, waits for them, and re-layouts  20.7 us
    ppermute x6, waiting for transfers between devices, passed_along(): lax.ppermute(value, axis, [(source, source + steps) for source in range(i...  20.2 us
  transfers between devices with their start and end apart: 16, of which 5 were waited for; matrix products, arithmetic and copies ran while one was open for 18% of the time, Pallas kernels for 33%

profile of v2, /device:TPU:0, one launch (start us, length us, event | category | flops | bytes accessed | tf_op | source)
XLA Modules:
  0.0 988.9 jit_solution(12649230233624069220)
XLA Ops:
  0.7 1.4 fusion.44
  13.3 2.3 copy.38
  15.6 6.4 fusion.57
  27.2 3.8 copy_bitcast_fusion
  32.2 214.3 %shard_map.307 = (bf16[2048,2432]{1,0:T(8,128)(2,1)}, bf16[2048,2048]{1,0:T(8,128)(2,1)}, bf16[2048,2048]{1,0:T(8,128)(2,1)}, bf16[2,512,2048]{2,1,0:T(8,128)(2,1)}) custom-call(bf16[256,2432]{1,0:T(8,128)(2,1)} %fusion.21.refs_0_, bf16[256,2048]{1,0:T(8,128)(2,1)} %get-tuple-element.146.refs_1_, bf16[256,2048]{1,0:T(8,128)(2,1)} %bitcast.164, ...), custom_call_target="tpu_custom_call" | custom-call | tf_op jit(solution)/shard_map/pallas_call | solution.py:827
  246.5 6.8 maximum_select_fusion
  254.6 14.7 %fusion.54.vraw.vprev.craw.cprev.sraw = f32[1024,2432]{1,0:T(8,128)S(1)} fusion(bf16[2048,2432]{1,0:T(8,128)(2,1)} %get-tuple-element.53, bf16[1024,2048]{1,0:T(8,128)(2,1)S(1)} %bitcast_dynamic-update-slice_fusion, f32[2048]{0:T(1024)S(1)} %copy-done.46, f32[1024]{0:T(1024)S(1)} %add_rsqrt_fusion), kind=kOutput, calls=%fused_computation.136 | convolution fusion | flops 10208935936 | bytes 24129536 | tf_op jit(solution)/shard_map/dot_general | solution.py:1318
  269.4 3.7 copy-done.27
  273.1 2.7 collective-permute-start
  277.0 14.7 %fusion.52 = f32[1024,2048]{1,0:T(8,128)} fusion(bf16[2048,2048]{1,0:T(8,128)(2,1)} %get-tuple-element.62, bf16[1024,2048]{1,0:T(8,128)(2,1)} %copy-done.29, f32[2048]{0:T(1024)S(1)} %copy-done.46, f32[1024]{0:T(1024)S(1)} %add_rsqrt_fusion), kind=kOutput, calls=%fused_computation.135 | convolution fusion | flops 8598323200 | bytes 20983808 | tf_op jit(solution)/shard_map/dot_general | solution.py:1336
  293.0 2.7 add_add_fusion
  296.5 26.1 %shard_map.308 = (f32[512,2048]{1,0:T(8,128)S(1)}, f32[4,128,2048]{2,1,0:T(8,128)S(1)}, f32[128,2048]{1,0:T(8,128)S(1)}, f32[512,256]{1,0:T(8,128)S(1)}, f32[512,2048]{1,0:T(8,128)}, /*index=5*/f32[8,2048]{1,0:T(8,128)S(1)}) custom-call(s32[3]{0:T(128)S(1)} %get-tuple-element.148.marks, f32[1024,2432]{1,0:T(8,128)} %copy-done.27, f32[1024,2432]{1,0:T(8,128)} %copy-done.27, ...), custom_call_target="tpu_custom_call" | custom-call | flops 5368709120 | bytes 25165824 | tf_op jit(solution)/shard_map/pallas_call | solution.py:294
  324.1 2.8 bitcast_multiply_fusion
  326.8 25.6 %shard_map.309 = (f32[512,2048]{1,0:T(8,128)S(1)}, f32[4,128,2048]{2,1,0:T(8,128)S(1)}, f32[128,2048]{1,0:T(8,128)S(1)}, f32[512,256]{1,0:T(8,128)S(1)}, f32[512,2048]{1,0:T(8,128)}, /*index=5*/f32[8,2048]{1,0:T(8,128)S(1)}) custom-call(s32[3]{0:T(128)S(1)} %get-tuple-element.149.marks, f32[1024,2432]{1,0:T(8,128)} %copy-done.27, f32[1024,2432]{1,0:T(8,128)} %copy-done.27, ...), custom_call_target="tpu_custom_call" | custom-call | flops 5368709120 | bytes 25165824 | tf_op jit(solution)/shard_map/pallas_call | solution.py:294
  352.5 1.8 collective-permute-start.2
  354.2 4.9 fusion.27
  359.2 7.0 multiply_add_fusion.1
  366.2 7.2 collective-permute-done.2.entering
  373.4 3.5 fusion.24
  377.0 3.3 multiply_add_fusion
  380.3 19.8 %multiply_reduce_fusion.2 = (f32[1024]{0:T(1024)S(1)}, f32[1024]{0:T(1024)S(1)}, f32[1024,2048]{1,0:T(8,128)}, f32[1024,2048]{1,0:T(8,128)}) fusion(f32[2048]{0:T(1024)S(1)} %copy-done.51, f32[1024,2048]{1,0:T(8,128)} %fusion.52, f32[512,2048]{1,0:T(8,128)} %multiply_add_fusion, f32[512,2048]{1,0:T(8,128)} %multiply_add_fusion.1, ...), kind=kOutput, calls=%fused_computation.23 | convolution fusion | flops 8613001216 | bytes 46153728 | tf_op jit(solution)/shard_map/dot_general | solution.py:1339
  401.4 17.0 %fusion.18 = (f32[1024,2048]{1,0:T(8,128)S(1)}, bf16[1024,2048]{1,0:T(8,128)(2,1)}, f32[2048]{0:T(1024)}, f32[1024,2048]{1,0:T(8,128)}) fusion(f32[1024,2048]{1,0:T(8,128)} %get-tuple-element.116, f32[1024]{0:T(1024)S(1)} %fusion.31, f32[1024]{0:T(1024)S(1)} %bitcast.171, f32[1024,2048]{1,0:T(8,128)} %get-tuple-element.145, f32[2048]{0:T(1024)S(1)} %copy-done.51, ...), kind=kLoop, calls=%fused_computation.37 | loop fusion | flops 41940992 | bytes 54550528 | tf_op jit(solution)/shard_map/mul | solution.py:1360
  418.4 3.7 fusion.15
  423.4 6.5 copy.46
  429.9 6.1 fusion.14
  437.4 12.9 %collective-permute-done.5.pulled = f32[128,2048]{1,0:T(8,128)} collective-permute-done((f32[128,2048]{1,0:T(8,128)}, f32[128,2048]{1,0:T(8,128)}, u32[]{:S(2)}, u32[]{:S(2)}) %collective-permute-start.5) | collective-permute-done | bytes 1048608 | tf_op jit(solution)/shard_map/ppermute | solution.py:1181
  450.4 47.3 %shard_map.310 = (f32[512,2048]{1,0:T(8,128)}, f32[8,2048]{1,0:T(8,128)S(1)}, f32[512,256]{1,0:T(8,128)S(1)}, f32[8,256]{1,0:T(8,128)S(1)}, f32[512,128]{1,0:T(8...) custom-call(s32[3]{0:T(128)S(1)} %copy-done.23, ...), custom_call_target="tpu_custom_call" | custom-call | flops 16106127360 | bytes 33554432 | tf_op jit(solution)/shard_map/pallas_call | solution.py:622
  498.3 47.1 %shard_map.311 = (f32[512,2048]{1,0:T(8,128)}, f32[8,2048]{1,0:T(8,128)S(1)}, f32[512,256]{1,0:T(8,128)S(1)}, f32[8,256]{1,0:T(8,128)S(1)}, f32[512,128]{1,0:T(8...) custom-call(s32[3]{0:T(128)S(1)} %copy-done.21, ...), custom_call_target="tpu_custom_call" | custom-call | flops 16106127360 | bytes 33554432 | tf_op jit(solution)/shard_map/pallas_call | solution.py:622
  546.8 13.3 %fusion.62 = f32[1024,2048]{1,0:T(8,128)} fusion(bf16[1024,2048]{1,0:T(8,128)(2,1)S(1)} %copy-done.38, bf16[2048,2048]{1,0:T(8,128)(2,1)} %get-tuple-element.62), kind=kOutput, calls=%fused_computation.142 | convolution fusion | flops 8589934592 | bytes 20971520 | tf_op jit(solution)/shard_map/dot_general | solution.py:1464
  560.5 1.8 copy-done.35
  563.6 1.6 add_convert_fusion
  565.4 35.3 %convolution_add_fusion = f32[1024,2048]{1,0:T(8,128)} fusion(f32[1024,2048]{1,0:T(8,128)} %fusion.62, bf16[2048,2432]{1,0:T(8,128)(2,1)} %get-tuple-element.53, bf16[512,128]{1,0:T(8,128)(2,1)S(1)} %convert_element_type.89, bf16[512,256]{1,0:T(8,128)(2,1)S(1)} %get-tuple-element.128, bf16[512,2048]{1,0:T(8,128)(2,1)} %add_convert_fusion, ...), kind=kOutput, calls=%fused_computation.40 | convolution fusion | flops 10232528896 | bytes 31719424 | tf_op jit(solution)/shard_map/dot_general | solution.py:1464
  600.8 16.0 %fusion.47 = f32[1024,2048]{1,0:T(8,128)} fusion(bf16[2048,2048]{1,0:T(8,128)(2,1)} %get-tuple-element.63, f32[1024,2048]{1,0:T(8,128)} %get-tuple-element.116, f32[1024]{0:T(1024)S(1)} %bitcast.172, f32[2048]{0:T(1024)S(1)} %copy-done.52), kind=kOutput, calls=%fused_computation.132 | convolution fusion | flops 8596226048 | bytes 25178112 | tf_op jit(solution)/shard_map/dot_general | solution.py:1464
  617.2 15.5 %fusion.16.refs_0_ = f32[4,2,256,2048]{3,2,1,0:T(8,128)} fusion(bf16[4,2,256,1024]{3,2,1,0:T(8,128)(2,1)S(1)} %bitcast.165, f32[1024,2048]{1,0:T(8,128)} %get-tuple-element.116, f32[1024]{0:T(1024)S(1)} %bitcast.173, f32[2048]{0:T(1024)S(1)} %copy-done.52), kind=kOutput, calls=%fused_computation.32 | convolution fusion | flops 8596226048 | bytes 29372416 | tf_op jit(solution)/shard_map/dot_general | solution.py:1458
  632.7 12.5 %fusion.50 = f32[2048,2048]{1,0:T(8,128)} fusion(bf16[1024,2048]{1,0:T(8,128)(2,1)S(1)} %copy-done.39, bf16[1024,2048]{1,0:T(8,128)(2,1)S(1)} %copy-done.30, f32[2048]{0:T(1024)S(1)} %copy-done.47, f32[1024]{0:T(1024)S(1)} %copy-done.43), kind=kOutput, calls=%fused_computation.134 | convolution fusion | flops 8598323200 | bytes 25178112 | tf_op jit(solution)/shard_map/dot_general | solution.py:1458
  646.5 24.9 %fusion.48 = f32[2048,2432]{1,0:T(8,128)} fusion(bf16[512,128]{1,0:T(8,128)(2,1)S(1)} %convert_element_type.89, bf16[512,256]{1,0:T(8,128)(2,1)S(1)} %get-tuple-element.128, bf16[512,2048]{1,0:T(8,128)(2,1)} %add_convert_fusion, bf16[512,128]{1,0:T(8,128)(2,1)S(1)} %convert_element_type.87, bf16[512,256]{1,0:T(8,128)(2,1)S(1)} %get-tuple-element.127, ...), kind=kOutput, calls=%fused_computation.133 | convolution fusion | flops 10238820352 | bytes 29110272 | tf_op jit(solution)/shard_map/dot_general | solution.py:1458
  671.4 255.3 %shard_map.312 = (f32[256,2048]{1,0:T(8,128)}, f32[256,2048]{1,0:T(8,128)}, f32[256,2432]{1,0:T(8,128)}) custom-call(f32[4,2,256,2048]{3,2,1,0:T(8,128)} %fusion.16.refs_0_, f32[4,2,256,2048]{3,2,1,0:T(8,128)} %bitcast.157, f32[4,2,256,2432]{3,2,1,0:T(8,128)} %bitcast.156), custom_call_target="tpu_custom_call" | custom-call | tf_op jit(solution)/shard_map/pallas_call | solution.py:1166
  927.7 3.1 slice_bitcast_fusion
  930.9 7.5 fusion.10
  939.7 4.7 pad_maximum_fusion.1
  945.3 1.8 copy.44
  947.8 7.4 copy.42
  955.3 1.7 collective-permute-start.12
  957.0 1.7 slice_add_fusion.4
  959.6 1.5 collective-permute-start.13
  961.1 2.9 collective-permute-done.13
  964.0 1.7 collective-permute-start.14
  965.7 18.7 %fusion.9 = (bf16[1024,2048]{1,0:T(8,128)(2,1)}, bf16[1024,2048]{1,0:T(8,128)(2,1)}) fusion(bf16[1024,2048]{1,0:T(8,128)(2,1)} %copy-done.29, bf16[2,1,512,2048]{3,2,1,0:T(8,128)(2,1)} %param.23, f32[1024]{0:T(1024)S(1)} %broadcast_multiply_fusion, f32[2048]{0:T(1024)S(1)} %copy-done.47, f32[1024]{0:T(1024)S(1)} %copy-done.43, ...), kind=kLoop, calls=%fused_computation.12 | loop fusion | flops 29360128 | bytes 50352128 | tf_op jit(solution)/shard_map/convert_element_type | solution.py:1425
  (207 shorter events, 26.2 us)
Async XLA Ops:
  13.3 17.8 %copy-start.41 = (bf16[256,256]{1,0:T(8,128)(2,1)S(1)}, bf16[256,256]{1,0:T(8,128)(2,1)}, u32[]{:S(2)}) copy-start(bf16[256,256]{1,0:T(8,128)(2,1)} %param.26) | copy-start | bytes 393220
  254.6 22.3 %copy-start.42 = (f32[1024]{0:T(1024)}, f32[1024]{0:T(1024)S(1)}, u32[]{:S(2)}) copy-start(f32[1024]{0:T(1024)S(1)} %add_rsqrt_fusion) | copy-start | bytes 12292
  254.6 21.2 %copy-start.50 = (s32[2,1,2]{2,1,0:T(1,128)S(1)}, s32[2,1,2]{2,1,0:T(1,128)}, u32[]{:S(2)}) copy-start(s32[2,1,2]{2,1,0:T(1,128)} %param.21) | copy-start | bytes 52
  273.1 23.4 %collective-permute-start = (f32[2,8,2432]{2,1,0:T(8,128)S(1)}, f32[2,8,2432]{2,1,0:T(8,128)S(1)}, u32[]{:S(2)}, u32[]{:S(2)}) collective-permute-start(f32[2,8,2432]{2,1,0:T(8,128)S(1)} %pad_maximum_fusion.3), channel_id=1, source_target_pairs={{0,2},{1,3},{4,6},{5,7},{8,10},{9,11},{12,14},{13,15},{16,18},{17,... | collective-permute-start | bytes 466952 | tf_op jit(solution)/shard_map/ppermute | solution.py:1181
  276.9 18.8 %copy-start.53 = (f32[32]{0:T(128)S(1)}, f32[32]{0:T(128)}, u32[]{:S(2)}) copy-start(f32[32]{0:T(128)} %param.35) | copy-start | bytes 388
  276.9 19.6 %copy-start = (bf16[128,4096]{1,0:T(8,128)(2,1)S(1)}, bf16[128,4096]{1,0:T(8,128)(2,1)}, u32[]{:S(2)}) copy-start(bf16[128,4096]{1,0:T(8,128)(2,1)} %constant.62.clone.selcol) | copy-start | bytes 3145732
  276.9 19.6 %copy-start.3 = (bf16[128,2048]{1,0:T(8,128)(2,1)S(1)}, bf16[128,2048]{1,0:T(8,128)(2,1)}, u32[]{:S(2)}) copy-start(bf16[128,2048]{1,0:T(8,128)(2,1)} %constant.61.clone.sel) | copy-start | bytes 1572868
  276.9 19.6 %copy-start.9 = (f32[4,2048]{1,0:T(4,128)S(1)}, f32[4,2048]{1,0:T(4,128)}, u32[]{:S(2)}) copy-start(f32[4,2048]{1,0:T(4,128)} %cw.7) | copy-start | bytes 98308
  277.0 19.6 %copy-start.11 = (f32[2048]{0:T(1024)S(1)}, f32[2048]{0:T(1024)}, u32[]{:S(2)}) copy-start(f32[2048]{0:T(1024)} %param.30) | copy-start | bytes 24580
  277.0 19.6 %copy-start.12 = (f32[4,256]{1,0:T(4,128)S(1)}, f32[4,256]{1,0:T(4,128)}, u32[]{:S(2)}) copy-start(f32[4,256]{1,0:T(4,128)} %ccw.7) | copy-start | bytes 12292
  277.0 19.5 %copy-start.13 = (f32[256]{0:T(256)S(1)}, f32[256]{0:T(256)}, u32[]{:S(2)}) copy-start(f32[256]{0:T(256)} %param.32) | copy-start | bytes 3076
  291.7 35.1 %copy-start.14 = (f32[1,128]{1,0:T(1,128)}, f32[1,128]{1,0:T(1,128)S(1)}, u32[]{:S(2)}) copy-start(f32[1,128]{1,0:T(1,128)S(1)} %get-tuple-element.152.rate) | copy-start | bytes 1540
  291.7 35.1 %copy-start.16 = (f32[1,128]{1,0:T(1,128)}, f32[1,128]{1,0:T(1,128)S(1)}, u32[]{:S(2)}) copy-start(f32[1,128]{1,0:T(1,128)S(1)} %get-tuple-element.153.sbias) | copy-start | bytes 1540
  295.7 27.0 %copy-start.22 = (s32[3]{0:T(128)}, s32[3]{0:T(128)S(1)}, u32[]{:S(2)}) copy-start(s32[3]{0:T(128)S(1)} %get-tuple-element.148.marks) | copy-start | bytes 40
  295.7 31.1 %copy-start.20 = (s32[3]{0:T(128)}, s32[3]{0:T(128)S(1)}, u32[]{:S(2)}) copy-start(s32[3]{0:T(128)S(1)} %get-tuple-element.149.marks) | copy-start | bytes 40
  296.5 27.5 %copy-start.32 = (bf16[2,1,512,2048]{3,2,1,0:T(8,128)(2,1)S(1)}, bf16[2,1,512,2048]{3,2,1,0:T(8,128)(2,1)}, u32[]{:S(2)}) copy-start(bf16[2,1,512,2048]{3,2,1,0:T(8,128)(2,1)} %param.23) | copy-start | bytes 12582916
  322.7 29.8 %copy-start.7 = (f32[128,2048]{1,0:T(8,128)}, f32[128,2048]{1,0:T(8,128)S(1)}, u32[]{:S(2)}) copy-start(f32[128,2048]{1,0:T(8,128)S(1)} %get-tuple-element.57.fin) | copy-start | bytes 3145732
  322.7 31.6 %collective-permute-start.1 = (f32[128,2048]{1,0:T(8,128)S(1)}, f32[128,2048]{1,0:T(8,128)S(1)}, u32[]{:S(2)}, u32[]{:S(2)}) collective-permute-start(f32[128,2048]{1,0:T(8,128)S(1)} %get-tuple-element.57.fin), channel_id=1, source_target_pairs={{0,2},{1,3},{4,6},{5,7},{8,10},{9,11},{12,14},{13,15},{16,18},{17,... | collective-permute-start | bytes 3145736 | tf_op jit(solution)/shard_map/ppermute | solution.py:1181
  352.5 20.9 %copy-start.10 = (f32[512,256]{1,0:T(8,128)}, f32[512,256]{1,0:T(8,128)S(1)}, u32[]{:S(2)}) copy-start(f32[512,256]{1,0:T(8,128)S(1)} %get-tuple-element.60) | copy-start | bytes 1572868
  352.5 20.9 %collective-permute-start.2 = (f32[128,2048]{1,0:T(8,128)S(1)}, f32[128,2048]{1,0:T(8,128)S(1)}, u32[]{:S(2)}, u32[]{:S(2)}) collective-permute-start(f32[128,2048]{1,0:T(8,128)S(1)} %get-tuple-element.61.fin), channel_id=1, source_target_pairs={{0,2},{1,3},{4,6},{5,7},{8,10},{9,11},{12,14},{13,15},{16,18},{17,... | collective-permute-start | bytes 3145736 | tf_op jit(solution)/shard_map/ppermute | solution.py:1181
  359.2 17.8 %copy-start.33 = (f32[512,2048]{1,0:T(8,128)S(1)}, f32[512,2048]{1,0:T(8,128)}, u32[]{:S(2)}) copy-start(f32[512,2048]{1,0:T(8,128)} %get-tuple-element.59) | copy-start | bytes 12582916
  400.1 1.2 collective-permute-start.3
  422.1 28.2 %collective-permute-start.5 = (f32[128,2048]{1,0:T(8,128)}, f32[128,2048]{1,0:T(8,128)}, u32[]{:S(2)}, u32[]{:S(2)}) collective-permute-start(f32[128,2048]{1,0:T(8,128)} %fusion.15), channel_id=1, source_target_pairs={{2,0},{3,1},{6,4},{7,5},{10,8},{11,9},{14,12},{15,13},{18,16},{19,... | collective-permute-start | bytes 3145736 | tf_op jit(solution)/shard_map/ppermute | solution.py:1181
  423.4 26.9 %copy-start.4 = (bf16[2048,128]{1,0:T(8,128)(2,1)S(1)}, bf16[2048,128]{1,0:T(8,128)(2,1)}, u32[]{:S(2)}) copy-start(bf16[2048,128]{1,0:T(8,128)(2,1)} %constant.86.selt) | copy-start | bytes 1572868
  429.9 20.4 %copy-start.8 = (f32[128,2048]{1,0:T(8,128)S(1)}, f32[128,2048]{1,0:T(8,128)}, u32[]{:S(2)}) copy-start(f32[128,2048]{1,0:T(8,128)} %copy-done.7) | copy-start | bytes 3145732
  429.9 20.4 %copy-start.15 = (f32[1,128]{1,0:T(1,128)S(1)}, f32[1,128]{1,0:T(1,128)}, u32[]{:S(2)}) copy-start(f32[1,128]{1,0:T(1,128)} %copy-done.14) | copy-start | bytes 1540
  429.9 20.4 %copy-start.17 = (f32[1,128]{1,0:T(1,128)S(1)}, f32[1,128]{1,0:T(1,128)}, u32[]{:S(2)}) copy-start(f32[1,128]{1,0:T(1,128)} %copy-done.16) | copy-start | bytes 1540
  429.9 20.4 %copy-start.23 = (s32[3]{0:T(128)S(1)}, s32[3]{0:T(128)}, u32[]{:S(2)}) copy-start(s32[3]{0:T(128)} %copy-done.22) | copy-start | bytes 40
  436.1 61.6 %collective-permute-start.6 = (f32[128,2048]{1,0:T(8,128)S(1)}, f32[128,2048]{1,0:T(8,128)S(1)}, u32[]{:S(2)}, u32[]{:S(2)}) collective-permute-start(f32[128,2048]{1,0:T(8,128)S(1)} %fusion.14), channel_id=1, source_target_pairs={{2,0},{3,1},{6,4},{7,5},{10,8},{11,9},{14,12},{15,13},{18,16},{19,... | collective-permute-start | bytes 3145736 | tf_op jit(solution)/shard_map/ppermute | solution.py:1181
  450.4 47.9 %copy-start.6 = (f32[128,2048]{1,0:T(8,128)S(1)}, f32[128,2048]{1,0:T(8,128)}, u32[]{:S(2)}) copy-start(f32[128,2048]{1,0:T(8,128)} %copy-done.5) | copy-start | bytes 3145732
  450.4 47.9 %copy-start.21 = (s32[3]{0:T(128)S(1)}, s32[3]{0:T(128)}, u32[]{:S(2)}) copy-start(s32[3]{0:T(128)} %copy-done.20) | copy-start | bytes 40
  497.7 47.7 %copy-start.18 = (f32[8,256]{1,0:T(8,128)}, f32[8,256]{1,0:T(8,128)S(1)}, u32[]{:S(2)}) copy-start(f32[8,256]{1,0:T(8,128)S(1)} %get-tuple-element.80) | copy-start | bytes 24580
  497.7 47.7 %copy-start.24 = (f32[8,128]{1,0:T(8,128)}, f32[8,128]{1,0:T(8,128)S(1)}, u32[]{:S(2)}) copy-start(f32[8,128]{1,0:T(8,128)S(1)} %get-tuple-element.82) | copy-start | bytes 12292
  498.3 48.5 %copy-start.38 = (bf16[1024,2048]{1,0:T(8,128)(2,1)S(1)}, bf16[1024,2048]{1,0:T(8,128)(2,1)}, u32[]{:S(2)}) copy-start(bf16[1024,2048]{1,0:T(8,128)(2,1)} %get-tuple-element.118) | copy-start | bytes 12582916
  545.5 14.7 %collective-permute-start.7 = (f32[2,8,2304]{2,1,0:T(8,128)S(1)}, f32[2,8,2304]{2,1,0:T(8,128)S(1)}, u32[]{:S(2)}, u32[]{:S(2)}) collective-permute-start(f32[2,8,2304]{2,1,0:T(8,128)S(1)} %pad_maximum_fusion.4), channel_id=1, source_target_pairs={{2,0},{3,1},{6,4},{7,5},{10,8},{11,9},{14,12},{15,13},{18,16},{19,... | collective-permute-start | bytes 442376 | tf_op jit(solution)/shard_map/ppermute | solution.py:1181
  560.4 4.8 collective-permute-start.8
  565.4 35.4 %copy-start.45 = (f32[1,1024]{1,0:T(1,128)S(1)}, f32[1,1024]{1,0:T(1,128)}, u32[]{:S(2)}) copy-start(f32[1,1024]{1,0:T(1,128)} %copy-done.44) | copy-start | bytes 12292
  565.4 35.4 %copy-start.52 = (f32[2048]{0:T(1024)S(1)}, f32[2048]{0:T(1024)}, u32[]{:S(2)}) copy-start(f32[2048]{0:T(1024)} %param.36) | copy-start | bytes 24580
  600.8 330.1 %collective-permute-start.9 = (f32[1024,2048]{1,0:T(8,128)}, f32[1024,2048]{1,0:T(8,128)}, u32[]{:S(2)}, u32[]{:S(2)}) collective-permute-start(f32[1024,2048]{1,0:T(8,128)} %convolution_add_fusion), channel_id=1, source_target_pairs={{0,1},{1,0},{2,3},{3,2},{4,5},{5,4},{6,7},{7,6},{8,9},{9,8},{10,11... | collective-permute-start | bytes 25165832 | tf_op jit(solution)/shard_map/ppermute | solution.py:1186
  616.8 348.9 %collective-permute-start.4 = (f32[1024,2048]{1,0:T(8,128)}, f32[1024,2048]{1,0:T(8,128)}, u32[]{:S(2)}, u32[]{:S(2)}) collective-permute-start(f32[1024,2048]{1,0:T(8,128)} %fusion.47), channel_id=1, source_target_pairs={{0,1},{1,0},{2,3},{3,2},{4,5},{5,4},{6,7},{7,6},{8,9},{9,8},{10,11... | collective-permute-start | bytes 25165832 | tf_op jit(solution)/shard_map/ppermute | solution.py:1186
  645.2 1.3 collective-permute-start.10
  671.4 259.5 %copy-start.31 = (bf16[1024,2048]{1,0:T(8,128)(2,1)S(1)}, bf16[1024,2048]{1,0:T(8,128)(2,1)}, u32[]{:S(2)}) copy-start(bf16[1024,2048]{1,0:T(8,128)(2,1)} %copy-done.29) | copy-start | bytes 12582916
  927.7 29.3 %collective-permute-start.15 = (f32[256,256]{1,0:T(8,128)S(1)}, f32[256,256]{1,0:T(8,128)S(1)}, u32[]{:S(2)}, u32[]{:S(2)}) collective-permute-start(f32[256,256]{1,0:T(8,128)S(1)} %slice.218), channel_id=1, source_target_pairs={{0,1},{1,0},{2,3},{3,2},{4,5},{5,4},{6,7},{7,6},{8,9},{9,8},{10,11... | collective-permute-start | bytes 786440 | tf_op jit(solution)/shard_map/ppermute | solution.py:1186
  938.5 16.8 %collective-permute-start.11 = (f32[128,128]{1,0:T(8,128)S(1)}, f32[128,128]{1,0:T(8,128)S(1)}, u32[]{:S(2)}, u32[]{:S(2)}) collective-permute-start(f32[128,128]{1,0:T(8,128)S(1)} %pad_bitcast_fusion), channel_id=1, source_target_pairs={{0,2},{2,0},{1,3},{3,1},{4,6},{6,4},{5,7},{7,5},{8,10},{10,8},{9,1... | collective-permute-start | bytes 196616 | tf_op jit(solution)/shard_map/ppermute | solution.py:1206
  944.4 21.3 %copy-start.49 = (f32[1024]{0:T(1024)S(1)}, f32[1024]{0:T(1024)}, u32[]{:S(2)}) copy-start(f32[1024]{0:T(1024)} %get-tuple-element.139) | copy-start | bytes 12292
  955.3 4.3 collective-permute-start.12
  959.6 4.3 collective-permute-start.13
  964.0 20.5 %collective-permute-start.14 = (f32[128,128]{1,0:T(8,128)S(1)}, f32[128,128]{1,0:T(8,128)S(1)}, u32[]{:S(2)}, u32[]{:S(2)}) collective-permute-start(f32[128,128]{1,0:T(8,128)S(1)} %add.213), channel_id=1, source_target_pairs={{0,16},{4,20},{8,24},{12,28},{16,0},{20,4},{24,8},{28,12},{1,17},{... | collective-permute-start | bytes 196616 | tf_op jit(solution)/shard_map/ppermute | solution.py:1206
  (24 other events, 247.5 us)

commit v3 on v2

--- a/solution.py
+++ b/solution.py
@@ -118,6 +118,7 @@
 
 def forward_kernel(
     heads,
+    extra,
     marks,
     vraw,
     vprev,
@@ -135,24 +136,12 @@
     skip,
     sel,
     selcol,
-    y_out,
-    st_out,
-    fin_out,
-    bc_out,
-    carry_out,
-    cd_out,
-    state,
-    cumt,
-    stack,
-    cumpack,
-    halo,
-    same_s,
-    bias_s,
-    gram_s,
-    cd_s,
-    cparts,
-    btparts,
+    *refs,
 ):
+    y_out, st_out, fin_out, bc_out, carry_out, cd_out = refs[extra : extra + 6]
+    (state, cumt, stack, cumpack, halo, same_s, bias_s, gram_s, cd_s, cparts, btparts) = refs[
+        extra + 6 :
+    ]
     chunk = pl.program_id(0)
     chunks = pl.num_programs(0)
     width = state.shape[0]
@@ -268,7 +257,8 @@
 
 
 def forward_ssd(
-    marks, micro, raw, rim, inner, twice, tokens, cw, cb, ccw, ccb, sbias, rate, skip, sel, selcol
+    marks, micro, micros, before_this, raw, rim, inner, twice, tokens,
+    cw, cb, ccw, ccb, sbias, rate, skip, sel, selcol,
 ):
     width = twice // 2
     chunks = tokens // CHUNK
@@ -276,9 +266,6 @@
     eighth = CHUNK // 8
     initial = micro * chunks
 
-    def rows(count):
-        return pl.BlockSpec((CHUNK, count), lambda chunk, *_: (chunk, 0))
-
     def part(count, start):
         return pl.BlockSpec((CHUNK, count), lambda chunk, *_: (initial + chunk, start // count))
 
@@ -292,7 +279,7 @@
         return pl.BlockSpec((8, count), lambda *_: (0, start // count))
 
     return pl.pallas_call(
-        functools.partial(forward_kernel, heads),
+        functools.partial(forward_kernel, heads, len(before_this)),
         grid_spec=pltpu.PrefetchScalarGridSpec(
             num_scalar_prefetch=1,
             grid=(chunks,),
@@ -313,14 +300,15 @@
                 whole(skip.shape),
                 whole(sel.shape),
                 whole(selcol.shape),
-            ],
+            ]
+            + [pl.BlockSpec(memory_space=pl.ANY)] * len(before_this),
             out_specs=[
-                rows(inner),
-                pl.BlockSpec((1, width, inner), lambda chunk, *_: (chunk, 0, 0)),
+                part(inner, 0),
+                pl.BlockSpec((1, width, inner), lambda chunk, *_: (initial + chunk, 0, 0)),
                 whole((width, inner)),
-                rows(twice),
-                rows(inner),
-                whole((8, inner)),
+                part(twice, 0),
+                part(inner, 0),
+                pl.BlockSpec((None, 8, inner), lambda *_: (micro, 0, 0)),
             ],
             scratch_shapes=[
                 pltpu.VMEM((width, inner), f32),
@@ -337,89 +325,72 @@
             ],
         ),
         out_shape=[
-            jax.ShapeDtypeStruct((tokens, inner), f32),
-            jax.ShapeDtypeStruct((chunks, width, inner), f32),
+            jax.ShapeDtypeStruct((micros * tokens, inner), f32),
+            jax.ShapeDtypeStruct((micros * chunks, width, inner), f32),
             jax.ShapeDtypeStruct((width, inner), f32),
-            jax.ShapeDtypeStruct((tokens, twice), f32),
-            jax.ShapeDtypeStruct((tokens, inner), f32),
-            jax.ShapeDtypeStruct((8, inner), f32),
+            jax.ShapeDtypeStruct((micros * tokens, twice), f32),
+            jax.ShapeDtypeStruct((micros * tokens, inner), f32),
+            jax.ShapeDtypeStruct((micros, 8, inner), f32),
         ],
+        input_output_aliases={
+            17 + number: where for number, where in enumerate([0, 1, 3, 4, 5][: len(before_this)])
+        },
         compiler_params=pltpu.CompilerParams(vmem_limit_bytes=40 * 1024 * 1024),
         cost_estimate=pl.CostEstimate(
             flops=20 * tokens * inner * 128 * 2, bytes_accessed=24 * tokens * inner, transcendentals=0
         ),
-    )(marks, raw, raw, rim, raw, raw, rim, raw, cw, cb, ccw, ccb, sbias, rate, skip, sel, selcol)
-
-
-def backward_kernel(
-    heads,
-    marks,
-    vraw,
-    vprev,
-    vrim,
-    craw,
-    cprev,
-    crim,
-    sraw,
-    grad,
-    mixer,
-    st_now,
-    st_next,
-    fin,
-    entering,
-    cd,
-    pulled,
-    cw,
-    cb,
-    ccw,
-    ccb,
-    sbias,
-    rate,
-    skip,
-    sel,
-    selcol,
-    selt,
-    vraw_g,
-    vrim_g,
-    craw_g,
-    crim_g,
-    sraw_g,
-    cw_g,
-    ccw_g,
-    small_g,
-    skip_g,
-    state,
-    cumt,
-    stack,
-    cumpack,
-    halo,
-    same_s,
-    bias_s,
-    gram_s,
-    cparts,
-    bparts,
-    ctparts,
-    rim_s,
-    crim_s,
-    dgram,
-    dcoup,
-    dhead,
-    cd_s,
-):
-    step_id = pl.program_id(0)
-    chunks = pl.num_programs(0)
+    )(
+        marks, raw, raw, rim, raw, raw, rim, raw, cw, cb, ccw, ccb, sbias, rate, skip, sel, selcol,
+        *before_this,
+    )
+
+
+def backward_kernel(heads, chunks, plan, *refs):
+    (
+        marks, vraw, vprev, vrim, craw, cprev, crim, sraw, grad, mixer, st_now, st_next, fin,
+        entering, cd, pulled, cw, cb, ccw, ccb, sbias, rate, skip, sel, selcol, selt,
+    ) = refs[:26]
+    arrays = len(plan.counts)
+    refs = refs[26:]
+    terms, refs = refs[:arrays], refs[arrays:]
+    (
+        lead_g, vtail_g, vrim_g, craw_g, crim_g, cw_g, ccw_g, small_g, skip_g,
+    ) = refs[:9]
+    outs, refs = refs[9 : 9 + arrays], refs[9 + arrays :]
+    (
+        state, cumt, stack, cumpack, halo, same_s, bias_s, gram_s, cparts, bparts, ctparts,
+        rim_s, crim_s, dgram, dcoup, dhead, cd_s,
+    ) = refs[:17]
+    plan.bind(terms, outs, refs[17:])
+    grid_step = pl.program_id(0)
+    step_id = lax.rem(grid_step, chunks)
+    micro = grid_step // chunks
     chunk = chunks - 1 - step_id
     width = state.shape[0]
+    inner = state.shape[1]
+    per_step = -(-plan.steps // pl.num_programs(0))
+
+    @pl.when(grid_step == 0)
+    def _():
+        plan.greet()
+        cw_g[...] = jnp.zeros_like(cw_g)
+        ccw_g[...] = jnp.zeros_like(ccw_g)
+        small_g[...] = jnp.zeros_like(small_g)
+        skip_g[...] = jnp.zeros_like(skip_g)
+
+    def reduce_steps(first, count):
+        def one(number, carried):
+            plan.step(number)
+            return carried
+
+        start = grid_step * per_step + first
+        lax.fori_loop(start, jnp.minimum(start + count, plan.steps), one, 0)
 
     @pl.when(step_id == 0)
     def _():
         state[...] = pulled[...]
         rim_s[...] = jnp.zeros_like(rim_s)
         crim_s[...] = jnp.zeros_like(crim_s)
-        cw_g[...] = jnp.zeros_like(cw_g)
-        ccw_g[...] = jnp.zeros_like(ccw_g)
-        small_g[...] = jnp.zeros_like(small_g)
-        skip_g[...] = jnp.zeros_like(skip_g)
 
     @pl.when(chunk == 0)
     def _():
@@ -429,7 +400,7 @@
     def _():
         halo[...] = vprev[...]
 
-    frame = chunk_frame(marks, chunk, sraw[...], sbias[...], rate[...], heads)
+    frame = chunk_frame([marks[micro, place] for place in range(3)], chunk, sraw[...], sbias[...], rate[...], heads)
     same = frame["same"]
     for lag in range(1, 4):
         same_s[lag - 1] = same[lag]
@@ -472,7 +443,7 @@
         chosen = jnp.where(eight_rows == chunk + place, cd[...], 0.0)
         cd_s[place : place + 1, :] = jnp.sum(chosen, axis=0, keepdims=True)
 
-    def pair(index, carried):
+    def pair(index):
         cols = pl.ds(pl.multiple_of(index * LANES, LANES), LANES)
         wide = pl.ds(pl.multiple_of(index * 2 * LANES, 2 * LANES), 2 * LANES)
         raw = vraw[:, cols]
@@ -544,13 +515,29 @@
             turned = pltpu.roll(padded, CHUNK + 16 - lag, 0)
             raw_g = raw_g + turned[8 : 8 + CHUNK]
             edge = edge + turned[:8]
-        vraw_g[:, cols] = raw_g
-        vraw_g[CHUNK - 8 :, cols] += rim_s[:, cols]
+        last_rows = raw_g[CHUNK - 8 :] + rim_s[:, cols]
+        lead_g[:, cols] = jnp.concatenate([raw_g[: CHUNK - 8], last_rows], axis=0).astype(bf16)
+
+        @pl.when(step_id == 0)
+        def _():
+            vtail_g[:, cols] = last_rows
+
         rim_s[:, cols] = edge
         vrim_g[:, cols] = edge
+
+    groups = 4
+    per_group = heads // 2 // groups
+
+    def group(number, carried):
+        for inside in range(per_group):
+            pair(number * per_group + inside)
+        share = per_step // (groups + 1)
+        reduce_steps(number * share, share)
         return carried
 
-    lax.fori_loop(0, heads // 2, pair, 0, unroll=4)
+    lax.fori_loop(0, groups, group, 0)
+    used = groups * (per_step // (groups + 1))
+    reduce_steps(used, per_step - used)
 
     total = dgram[...]
     total_parts = split_two(total)
@@ -583,123 +570,136 @@
     parts = split_three(dhead[:CHUNK])
     decay_g = mm(upper, parts[0]) + mm(upper, parts[1]) + mm(upper, parts[2])
     step_g = (dhead[CHUNK:] - rate[...] * decay_g) * logistic(frame["shifted"])
-    sraw_g[...] = step_g
+    lead_g[:, inner : inner + 2 * width] = jnp.zeros((CHUNK, 2 * width), bf16)
+    lead_g[:, inner + 2 * width :] = step_g.astype(bf16)
     small_g[0:1, :] += jnp.sum(step_g, axis=0, keepdims=True)
     small_g[1:2, :] += jnp.sum(-frame["step"] * decay_g, axis=0, keepdims=True)
 
 
 def backward_ssd(
-    marks, micro, raw, rim, inner, twice, tokens, grad, mixer, states, fin, entering, cd, pulled,
-    cw, cb, ccw, ccb, sbias, rate, skip, sel, selcol, selt,
+    marks, micros, raw, rims, inner, twice, tokens, grad, mixer, states, fin, entering, cd, pulled,
+    cw, cb, ccw, ccb, sbias, rate, skip, sel, selcol, selt, terms, collective_id,
 ):
     width = twice // 2
     chunks = tokens // CHUNK
     heads = inner // (LANES // 2)
     eighth = CHUNK // 8
-    final = (micro + 1) * chunks - 1
-
-    def rows(count):
-        return pl.BlockSpec((CHUNK, count), lambda step, *_: (chunks - 1 - step, 0))
+    pairs = lax.axis_size("fsdp") // 2
+    shard_rows = terms[0].shape[0] // (2 * pairs)
+    plan = Reduction(shard_rows, pairs, [term.shape[1] for term in terms], 2)
+    lead = inner + twice + LANES
+
+    def row(step):
+        return step // chunks * chunks + chunks - 1 - lax.rem(step, chunks)
 
     def part(count, start):
-        return pl.BlockSpec((CHUNK, count), lambda step, *_: (final - step, start // count))
+        return pl.BlockSpec((CHUNK, count), lambda step: (row(step), start // count))
 
     def before(count, start):
         return pl.BlockSpec(
-            (8, count),
-            lambda step, *_: (jnp.maximum((final - step) * eighth - 1, 0), start // count),
+            (8, count), lambda step: (jnp.maximum(row(step) * eighth - 1, 0), start // count)
         )
 
     def edge(count, start):
-        return pl.BlockSpec((8, count), lambda *_: (0, start // count))
+        return pl.BlockSpec(
+            (None, 8, count), lambda step: (step // chunks, 0, start // count)
+        )
 
     def held(offset):
         return pl.BlockSpec(
             (1, width, inner),
-            lambda step, *_: (jnp.minimum(chunks - 1 - step + offset, chunks - 1), 0, 0),
-        )
-
+            lambda step: (
+                jnp.minimum(row(step) + offset, (step // chunks + 1) * chunks - 1), 0, 0,
+            ),
+        )
+
+    def each(*shape):
+        return pl.BlockSpec((None, *shape), lambda step: (step // chunks, 0, 0))
+
+    hbm = pl.BlockSpec(memory_space=pl.ANY)
     return pl.pallas_call(
-        functools.partial(backward_kernel, heads),
-        grid_spec=pltpu.PrefetchScalarGridSpec(
-            num_scalar_prefetch=1,
-            grid=(chunks,),
-            in_specs=[
-                part(inner, 0),
-                before(inner, 0),
-                edge(inner, 0),
-                part(twice, inner),
-                before(twice, inner),
-                edge(twice, inner),
-                part(LANES, inner + twice),
-                part(inner, 0),
-                part(inner, 0),
-                held(0),
-                held(1),
-                whole((width, inner)),
-                whole((width, inner)),
-                whole((8, inner)),
-                whole((width, inner)),
-                whole(cw.shape),
-                whole(cb.shape),
-                whole(ccw.shape),
-                whole(ccb.shape),
-                whole(sbias.shape),
-                whole(rate.shape),
-                whole(skip.shape),
-                whole(sel.shape),
-                whole(selcol.shape),
-                whole(selt.shape),
-            ],
-            out_specs=[
-                rows(inner),
-                whole((8, inner)),
-                rows(twice),
-                whole((8, twice)),
-                rows(LANES),
-                whole((8, inner)),
-                whole((8, twice)),
-                whole((8, LANES)),
-                whole((8, inner)),
-            ],
-            scratch_shapes=[
-                pltpu.VMEM((width, inner), f32),
-                pltpu.VMEM((LANES, CHUNK), f32),
-                pltpu.VMEM((3 * CHUNK, LANES), bf16),
-                pltpu.VMEM((CHUNK, LANES), bf16),
-                pltpu.VMEM((8, inner), f32),
-                pltpu.VMEM((3, CHUNK, LANES), f32),
-                pltpu.VMEM((CHUNK, CHUNK), f32),
-                pltpu.VMEM((CHUNK, CHUNK), f32),
-                pltpu.VMEM((2, CHUNK, width), bf16),
-                pltpu.VMEM((2, CHUNK, width), bf16),
-                pltpu.VMEM((2, width, CHUNK), bf16),
-                pltpu.VMEM((8, inner), f32),
-                pltpu.VMEM((8, twice), f32),
-                pltpu.VMEM((CHUNK, CHUNK), f32),
-                pltpu.VMEM((2, CHUNK, width), f32),
-                pltpu.VMEM((2 * CHUNK, LANES), f32),
-                pltpu.VMEM((8, inner), f32),
-            ],
-        ),
+        functools.partial(backward_kernel, heads, chunks, plan),
+        grid=(micros * chunks,),
+        in_specs=[
+            pl.BlockSpec(memory_space=pltpu.SMEM),
+            part(inner, 0),
+            before(inner, 0),
+            edge(inner, 0),
+            part(twice, inner),
+            before(twice, inner),
+            edge(twice, inner),
+            part(LANES, inner + twice),
+            part(inner, 0),
+            part(inner, 0),
+            held(0),
+            held(1),
+            each(width, inner),
+            each(width, inner),
+            each(8, inner),
+            each(width, inner),
+            whole(cw.shape),
+            whole(cb.shape),
+            whole(ccw.shape),
+            whole(ccb.shape),
+            whole(sbias.shape),
+            whole(rate.shape),
+            whole(skip.shape),
+            whole(sel.shape),
+            whole(selcol.shape),
+            whole(selt.shape),
+        ]
+        + [hbm] * len(terms),
+        out_specs=[
+            part(lead, 0),
+            each(8, inner),
+            each(8, inner),
+            part(twice, 0),
+            each(8, twice),
+            whole((8, inner)),
+            whole((8, twice)),
+            whole((8, LANES)),
+            whole((8, inner)),
+        ]
+        + [hbm] * len(terms),
+        scratch_shapes=[
+            pltpu.VMEM((width, inner), f32),
+            pltpu.VMEM((LANES, CHUNK), f32),
+            pltpu.VMEM((3 * CHUNK, LANES), bf16),
+            pltpu.VMEM((CHUNK, LANES), bf16),
+            pltpu.VMEM((8, inner), f32),
+            pltpu.VMEM((3, CHUNK, LANES), f32),
+            pltpu.VMEM((CHUNK, CHUNK), f32),
+            pltpu.VMEM((CHUNK, CHUNK), f32),
+            pltpu.VMEM((2, CHUNK, width), bf16),
+            pltpu.VMEM((2, CHUNK, width), bf16),
+            pltpu.VMEM((2, width, CHUNK), bf16),
+            pltpu.VMEM((8, inner), f32),
+            pltpu.VMEM((8, twice), f32),
+            pltpu.VMEM((CHUNK, CHUNK), f32),
+            pltpu.VMEM((2, CHUNK, width), f32),
+            pltpu.VMEM((2 * CHUNK, LANES), f32),
+            pltpu.VMEM((8, inner), f32),
+        ]
+        + plan.scratch(),
         out_shape=[
-            jax.ShapeDtypeStruct((tokens, inner), f32),
-            jax.ShapeDtypeStruct((8, inner), f32),
-            jax.ShapeDtypeStruct((tokens, twice), f32),
-            jax.ShapeDtypeStruct((8, twice), f32),
-            jax.ShapeDtypeStruct((tokens, LANES), f32),
+            jax.ShapeDtypeStruct((micros * tokens, lead), bf16),
+            jax.ShapeDtypeStruct((micros, 8, inner), f32),
+            jax.ShapeDtypeStruct((micros, 8, inner), f32),
+            jax.ShapeDtypeStruct((micros * tokens, twice), f32),
+            jax.ShapeDtypeStruct((micros, 8, twice), f32),
             jax.ShapeDtypeStruct((8, inner), f32),
             jax.ShapeDtypeStruct((8, twice), f32),
             jax.ShapeDtypeStruct((8, LANES), f32),
             jax.ShapeDtypeStruct((8, inner), f32),
-        ],
-        compiler_params=pltpu.CompilerParams(vmem_limit_bytes=48 * 1024 * 1024),
-        cost_estimate=pl.CostEstimate(
-            flops=60 * tokens * inner * 128 * 2, bytes_accessed=32 * tokens * inner, transcendentals=0
+        ]
+        + [jax.ShapeDtypeStruct((shard_rows, term.shape[1]), f32) for term in terms],
+        compiler_params=pltpu.CompilerParams(
+            collective_id=collective_id, has_side_effects=True, vmem_limit_bytes=60 * 1024 * 1024
         ),
     )(
-        marks, raw, raw, rim, raw, raw, rim, raw, grad, mixer, states, states, fin, entering,
+        marks, raw, raw, rims, raw, raw, rims, raw, grad, mixer, states, states, fin, entering,
         cd, pulled, cw, cb, ccw, ccb, sbias, rate, skip, sel, selcol, selt,
+        *[term.reshape(pairs, 2, shard_rows, -1) for term in terms],
     )
 
 
@@ -1321,30 +1321,28 @@
         "context",
         1,
     )
-    forwards = []
+    chunk_count = count // CHUNK
+    written, finals, entering = (), [], []
     for micro in range(micros):
-        forwards.append(
-            forward_ssd(
-                marks[micro], micro, raw, rims[micro], inner, twice, count,
-                cw, cb, ccw, ccb, sbias, rate, skip, sel, selcol,
-            )
-        )
-    entering = [
-        chained(forwards[micro][2], forwards[micro][5][count // CHUNK], 1)
-        for micro in range(micros)
-    ]
+        y_own, states, final, coupled, carry, reach = forward_ssd(
+            marks[micro], micro, micros, written, raw, rims[micro], inner, twice, count,
+            cw, cb, ccw, ccb, sbias, rate, skip, sel, selcol,
+        )
+        written = (y_own, states, coupled, carry, reach)
+        finals.append(final)
+        entering.append(chained(final, reach[micro, chunk_count], 1))
+    entering = jnp.stack(entering)
+    coupled_c = coupled[:, width:].reshape(micros, count, width)
     gate_in = jnp.dot(normed, gate_full, preferred_element_type=f32)
     cot = cotangent[:, 0].reshape(micros * count, model)
     out_grad = cot * keep.astype(bf16)
     norm_grad = jnp.dot(out_grad, out_full, preferred_element_type=f32)
 
-    mixers = []
-    for micro in range(micros):
-        y_own, _, _, coupled, carry, _ = forwards[micro]
-        mixers.append(
-            y_own + carry * jnp.dot(coupled[:, width:], entering[micro], precision=highest)
-        )
-    mixer = jnp.concatenate(mixers, axis=0)
+    arrived = jnp.concatenate(
+        [jnp.dot(coupled_c[micro], entering[micro], precision=highest) for micro in range(micros)],
+        axis=0,
+    )
+    mixer = y_own + carry * arrived
     gate_sig = jax.nn.sigmoid(gate_in)
     gate_act = gate_in * gate_sig
     gated = mixer * gate_act
@@ -1359,62 +1357,46 @@
     gate_grad = (gated_grad * mixer * gate_sig * (1.0 + gate_in * (1.0 - gate_sig))).astype(bf16)
     mixer_grad = gated_grad * gate_act
 
+    out_term = contract_rows(out_grad, gated_norm)
+    gate_term = contract_rows(normed, gate_grad)
     pulled = []
     for micro in range(micros):
         part = slice(micro * count, (micro + 1) * count)
         own_pull = lax.dot_general(
-            forwards[micro][3][:, width:],
-            forwards[micro][4] * mixer_grad[part],
+            coupled_c[micro],
+            carry[part] * mixer_grad[part],
             (((0,), (0,)), ((), ())),
             precision=highest,
         )
-        pulled.append(chained(own_pull, forwards[micro][5][count // CHUNK], -1))
+        pulled.append(chained(own_pull, reach[micro, chunk_count], -1))
 
     branch = contract_cols(gated_norm, out_full)
     branch = branch + paired(branch, "tensor")
     block_out = (x_float + keep * branch).astype(bf16)
 
-    out_term = contract_rows(out_grad, gated_norm)
-    gate_term = contract_rows(normed, gate_grad)
-
-    backs = []
-    for micro in range(micros):
-        y_own, states, final, coupled, carry, reach = forwards[micro]
-        backs.append(
-            backward_ssd(
-                marks[micro], micro, raw, rims[micro], inner, twice, count, mixer_grad, mixer,
-                states, final, entering[micro], reach, pulled[micro],
-                cw, cb, ccw, ccb, sbias, rate, skip, sel, selcol, selt,
-            )
-        )
-    edges = passed_along(
-        jnp.stack([jnp.concatenate([back[1], back[3]], axis=1) for back in backs]), "context", -1
-    )
-    tail_pad = ((count - 8, 0), (0, 0))
-    coupling_raw_grad = jnp.stack(
-        [back[2] + jnp.pad(edges[micro][:, inner:], tail_pad) for micro, back in enumerate(backs)]
+    (
+        lead_grad, tails, rims_grad, coupling_raw_grad, coupling_rims_grad,
+        value_sums, coupling_sums, small_sums, skip_sums, out_shard, gate_shard,
+    ) = backward_ssd(
+        jnp.stack(marks), micros, raw, rims, inner, twice, count, mixer_grad, mixer, states,
+        jnp.stack(finals), entering, reach, jnp.stack(pulled),
+        cw, cb, ccw, ccb, sbias, rate, skip, sel, selcol, selt, [out_term, gate_term], 2,
+    )
+    edges = passed_along(jnp.concatenate([rims_grad, coupling_rims_grad], axis=2), "context", -1)
+    coupling_raw_grad = coupling_raw_grad.reshape(micros, count, twice) + jnp.pad(
+        edges[:, :, inner:], ((0, 0), (count - 8, 0), (0, 0))
     )
     coupling_raw_grad = coupling_raw_grad + paired(coupling_raw_grad, "tensor")
     lane_ids = jnp.arange(twice, dtype=jnp.int32)
     own_lanes = ((lane_ids // width) == side).astype(bf16)
-    coupling_low = coupling_raw_grad.astype(bf16) * own_lanes
-    lead_grad = jnp.concatenate(
-        [
-            jnp.concatenate(
-                [
-                    (back[0] + jnp.pad(edges[micro][:, :inner], tail_pad)).astype(bf16),
-                    coupling_low[micro],
-                    back[4].astype(bf16),
-                ],
-                axis=1,
-            )
-            for micro, back in enumerate(backs)
-        ],
-        axis=0,
-    )
-    out_shard, gate_shard, lead_shard = reduce_terms(
-        [out_term, gate_term, contract_rows(normed, lead_grad)], 2, 2
-    )
+    coupling_low = (coupling_raw_grad.astype(bf16) * own_lanes).reshape(micros * count, twice)
+    lead_grad = lax.dynamic_update_slice(lead_grad, coupling_low, (0, inner))
+    tails = (tails + edges[:, :, :inner]).astype(bf16)
+    for micro in range(micros):
+        lead_grad = lax.dynamic_update_slice(
+            lead_grad, tails[micro], ((micro + 1) * count - 8, 0)
+        )
+    (lead_shard,) = reduce_terms([contract_rows(normed, lead_grad)], 2, 3)
     normed_part = contract_cols(gate_grad, gate_full) + contract_cols(lead_grad, lead_full)
     normed_grad = normed_part + paired(normed_part, "tensor")
     x_hat = x_float * inv_rms
@@ -1425,10 +1407,7 @@
     ).astype(bf16)
     norm_gain_grad = jnp.sum(normed_grad * x_hat, axis=0)
 
-    value_sums = sum(back[5] for back in backs)
-    coupling_sums = sum(back[6] for back in backs)
-    small_sums = sum(back[7] for back in backs)
-    skip_sums = sum(back[8] for back in backs)[0].reshape(heads, head_size).sum(axis=1)
+    skip_sums = skip_sums[0].reshape(heads, head_size).sum(axis=1)
     coupling_sums = coupling_sums + paired(coupling_sums, "tensor")
     (value_all, coupling_all, small_all, skip_all, inner_all, norm_all) = summed_everywhere(
         [value_sums[:5], coupling_sums[:5], small_sums[:2], skip_sums, inner_gain_grad, norm_gain_grad]

time: 997 us -> 931 us (0.934)
  Pallas kernels: 616 us -> 553 us
  matrix products: 185 us -> 148 us
  waiting for transfers between devices: 25.1 us -> 46.7 us
  other arithmetic: 81.1 us -> 92.2 us
    pallas_call x1, Pallas kernels: 255 us -> 109 us  [reduce_terms(): pl.pallas_call(functools.partial(reduce_kernel, plan, arrays), out_shape=...]
    pallas_call x4 -> x3, Pallas kernels: 146 us -> 230 us  [the longest x1 176 us: backward_ssd(): pl.pallas_call(functools.partial(backward_kernel, heads, chunks, plan), g...]
    ppermute x6, waiting for transfers between devices: 20.2 us -> 39.1 us  [passed_along(): lax.ppermute(value, axis, [(source, source + steps) for source in range(i...]
    dot_general x3, matrix products: 64.7 us -> 47.3 us  [contract_cols(): lax.dot_general(left, right, (((1,), (1,)), ((), ())), preferred_element_...]
    reduce_sum x1 -> x2, other arithmetic: 0.12 us -> 14.6 us  [the longest x1 14.5 us: shards(): jnp.sum(gated * gated, axis=-1)]
    unnamed x124 -> x98, local copies, waits for them, and re-layouts: 20.7 us -> 18 us
  transfers between devices with their start and end apart: 16 -> 16, of which waited for: 5 -> 6; matrix products, arithmetic and copies ran while one was open for 18% -> 20% of each run, Pallas kernels for 33% -> 12%
where the time goes in v3:
time: 931 us; the launch traced here: 922 us
  Pallas kernels  553 us (59%)
  matrix products  148 us (16%)
  other arithmetic  92.2 us (10%)
  local copies, waits for them, and re-layouts  48 us (5%)
  waiting for transfers between devices  46.7 us (5%)
  between operations  17.2 us (2%)
  starting transfers between devices  15.6 us (2%)
    pallas_call x1, Pallas kernels, gather_weights(): pl.pallas_call(functools.partial(gather_kernel, count, shared), out_shape...  214 us
    pallas_call x1, Pallas kernels, backward_ssd(): pl.pallas_call(functools.partial(backward_kernel, heads, chunks, plan), g...  176 us
    pallas_call x1, Pallas kernels, reduce_terms(): pl.pallas_call(functools.partial(reduce_kernel, plan, arrays), out_shape=...  109 us
    pallas_call x2, Pallas kernels, forward_ssd(): pl.pallas_call(functools.partial(forward_kernel, heads, len(before_this))...  53.4 us
    dot_general x3, matrix products, contract_rows(): lax.dot_general(left, right, (((0,), (0,)), ((), ())), preferred_element_...  48.5 us
    dot_general x3, matrix products, contract_cols(): lax.dot_general(left, right, (((1,), (1,)), ((), ())), preferred_element_...  47.3 us
    ppermute x6, waiting for transfers between devices, passed_along(): lax.ppermute(value, axis, [(source, source + steps) for source in range(i...  39.1 us
    convert_element_type x1, other arithmetic, shards(): input_grad = (cot.astype(f32) + inv_rms * (hat_grad - x_hat * jnp.mean(ha...  18.7 us
  transfers between devices with their start and end apart: 16, of which 6 were waited for; matrix products, arithmetic and copies ran while one was open for 20% of the time, Pallas kernels for 12%

profile of v3, /device:TPU:0, one launch (start us, length us, event | category | flops | bytes accessed | tf_op | source)
XLA Modules:
  0.0 921.6 jit_solution(3336291264681536720)
XLA Ops:
  0.7 1.4 fusion.49
  13.3 2.3 copy.43
  15.6 6.5 fusion.63
  27.3 3.8 copy_bitcast_fusion
  32.3 214.3 %shard_map.307 = (bf16[2048,2432]{1,0:T(8,128)(2,1)}, bf16[2048,2048]{1,0:T(8,128)(2,1)}, bf16[2048,2048]{1,0:T(8,128)(2,1)}, bf16[2,512,2048]{2,1,0:T(8,128)(2,1)}) custom-call(bf16[256,2432]{1,0:T(8,128)(2,1)} %fusion.24.refs_0_, bf16[256,2048]{1,0:T(8,128)(2,1)} %get-tuple-element.121.refs_1_, bf16[256,2048]{1,0:T(8,128)(2,1)} %bitcast.175, ...), custom_call_target="tpu_custom_call" | custom-call | tf_op jit(solution)/shard_map/pallas_call | solution.py:827
  246.6 7.3 maximum_select_fusion
  256.0 11.0 %fusion.59.vraw.vprev.craw.cprev.sraw.refs_1_.refs_2_.refs_4_.refs_5_.refs_7_ = f32[1024,2432]{1,0:T(8,128)S(1)} fusion(bf16[2048,2432]{1,0:T(8,128)(2,1)S(1)} %bitcast.197, bf16[1024,2048]{1,0:T(8,128)(2,1)S(1)} %bitcast_dynamic-update-slice_fusion, f32[2048]{0:T(1024)S(1)} %copy-done.26, f32[1024]{0:T(1024)S(1)} %add_rsqrt_fusion), kind=kOutput, calls=%fused_computation.135 | convolution fusion | flops 10208935936 | bytes 24129536 | tf_op jit(solution)/shard_map/dot_general | solution.py:1318
  267.0 3.7 copy-done.11
  270.8 2.7 collective-permute-start
  274.6 14.8 %fusion.57 = f32[1024,2048]{1,0:T(8,128)} fusion(bf16[2048,2048]{1,0:T(8,128)(2,1)} %get-tuple-element.54, bf16[1024,2048]{1,0:T(8,128)(2,1)} %copy-done.13, f32[2048]{0:T(1024)S(1)} %copy-done.26, f32[1024]{0:T(1024)S(1)} %add_rsqrt_fusion), kind=kOutput, calls=%fused_computation.134 | convolution fusion | flops 8598323200 | bytes 20983808 | tf_op jit(solution)/shard_map/dot_general | solution.py:1336
  289.5 1.4 fusion.39
  291.5 2.8 bitcast_multiply_fusion
  294.5 2.7 add_add_fusion
  297.3 26.5 %shard_map.308 = (f32[1024,2048]{1,0:T(8,128)S(1)}, f32[8,128,2048]{2,1,0:T(8,128)}, f32[128,2048]{1,0:T(8,128)}, f32[1024,256]{1,0:T(8,128)S(1)}, f32[1024,2048]{1,0:T(8,128)}, /*index=5*/f32[2,8,2048]{2,1,0:T(8,128)S(1)}) custom-call(s32[3]{0:T(128)S(1)} %get-tuple-element.124.marks, f32[1024,2432]{1,0:T(8,128)} %copy-done.11, f32[1024,2432]{1,0:T(8,128)} %copy-done.11, ...), custom_call_target="tpu_custom_call" | custom-call | flops 5368709120 | bytes 25165824 | tf_op jit(solution)/shard_map/pallas_call | solution.py:281
  323.8 26.9 %shard_map.309 = (f32[1024,2048]{1,0:T(8,128)S(1)}, f32[8,128,2048]{2,1,0:T(8,128)}, f32[128,2048]{1,0:T(8,128)}, f32[1024,256]{1,0:T(8,128)S(1)}, f32[1024,2048]{1,0:T(8,128)}, /*index=5*/f32[2,8,2048]{2,1,0:T(8,128)S(1)}) custom-call(s32[3]{0:T(128)S(1)} %get-tuple-element.123.marks, ...), custom_call_target="tpu_custom_call", output_to_operand_aliasing={{0}: (17, {}), {1}: (18, {}), {3}: (19, {}), {4}: (20, {}),... | custom-call | flops 5368709120 | bytes 25165824 | tf_op jit(solution)/shard_map/pallas_call | solution.py:281
  352.1 2.7 collective-permute-start.1
  354.8 13.4 %fusion.68 = f32[1024,2048]{1,0:T(8,128)} fusion(bf16[1024,2048]{1,0:T(8,128)(2,1)S(1)} %copy-done.17, bf16[2048,2048]{1,0:T(8,128)(2,1)} %get-tuple-element.55), kind=kOutput, calls=%fused_computation.141 | convolution fusion | flops 8589934592 | bytes 20971520 | tf_op jit(solution)/shard_map/dot_general | solution.py:1339
  368.2 6.4 copy.51
  375.1 3.4 pad_maximum_fusion.1.refs_12_
  378.5 16.0 %collective-permute-done.1 = f32[128,2048]{1,0:T(8,128)} collective-permute-done((f32[128,2048]{1,0:T(8,128)}, f32[128,2048]{1,0:T(8,128)}, u32[]{:S(2)}, u32[]{:S(2)}) %collective-permute-start.1) | collective-permute-done | bytes 1048608 | tf_op jit(solution)/shard_map/ppermute | solution.py:1181
  394.5 4.9 fusion.30
  399.4 3.5 fusion.27
  403.0 14.5 %multiply_reduce_fusion.2 = (f32[1024]{0:T(1024)S(1)}, f32[1024]{0:T(1024)S(1)}, f32[1024,2048]{1,0:T(8,128)}, f32[1024,2048]{1,0:T(8,128)}) fusion(f32[1024,2048]{1,0:T(8,128)} %fusion.68, f32[2048]{0:T(1024)S(1)} %copy-done.25, f32[1024,2048]{1,0:T(8,128)} %fusion.57, f32[1024,2048]{1,0:T(8,128)S(1)} %bitcast.154, f32[1024,2048]{1,0:T(8,128)} %get-tuple-element.50, ...), kind=kLoop, calls=%fused_computation.24 | loop fusion | flops 27260928 | bytes 58736640 | tf_op jit(solution)/shard_map/reduce_sum | solution.py:1350
  417.6 2.9 pad_maximum_fusion.2.refs_13_
  420.6 16.3 %fusion.21 = (f32[1024,2048]{1,0:T(8,128)S(1)}, bf16[1024,2048]{1,0:T(8,128)(2,1)}, f32[2048]{0:T(1024)}) fusion(f32[1024,2048]{1,0:T(8,128)} %get-tuple-element.96, f32[1024]{0:T(1024)S(1)} %fusion.36, f32[1024]{0:T(1024)S(1)} %bitcast.188, f32[1024,2048]{1,0:T(8,128)} %fusion.68, f32[2048]{0:T(1024)S(1)} %copy-done.25, f32[1024,2048]{1,0:T(8,128)} %fusion.57, ...), kind=kLoop, calls=%fused_computation.37 | loop fusion | flops 39843840 | bytes 46161920 | tf_op jit(solution)/shard_map/mul | solution.py:1358
  437.0 2.5 fusion.15
  439.5 2.5 fusion.16
  444.7 14.9 %fusion.55 = f32[2048,2048]{1,0:T(8,128)} fusion(bf16[1024,2048]{1,0:T(8,128)(2,1)} %get-tuple-element.99, bf16[1024,2048]{1,0:T(8,128)(2,1)S(1)} %copy-done.14, f32[2048]{0:T(1024)S(1)} %copy-done.26, f32[1024]{0:T(1024)S(1)} %add_rsqrt_fusion), kind=kOutput, calls=%fused_computation.133 | convolution fusion | flops 8598323200 | bytes 25178112 | tf_op jit(solution)/shard_map/dot_general | solution.py:1437
  459.6 15.1 %fusion.17.refs_26_ = f32[4,2,256,2048]{3,2,1,0:T(8,128)} fusion(bf16[4,2,256,1024]{3,2,1,0:T(8,128)(2,1)S(1)} %bitcast.176, f32[1024,2048]{1,0:T(8,128)} %get-tuple-element.96, f32[1024]{0:T(1024)S(1)} %bitcast.189, f32[2048]{0:T(1024)S(1)} %copy-done.25), kind=kOutput, calls=%fused_computation.32 | convolution fusion | flops 8596226048 | bytes 29372416 | tf_op jit(solution)/shard_map/dot_general | solution.py:1437
  474.7 17.4 %collective-permute-done.6 = f32[128,2048]{1,0:T(8,128)S(1)} collective-permute-done((f32[128,2048]{1,0:T(8,128)S(1)}, f32[128,2048]{1,0:T(8,128)S(1)}, u32[]{:S(2)}, u32[]{:S(2)}) %collective-permute-start.6) | collective-permute-done | bytes 1048608 | tf_op jit(solution)/shard_map/ppermute | solution.py:1181
  492.1 1.5 pad_maximum_fusion.3.refs_15_
  493.6 176.4 %shard_map.310 = (bf16[1024,2432]{1,0:T(8,128)(2,1)}, f32[2,8,2048]{2,1,0:T(8,128)}, f32[2,8,2048]{2,1,0:T(8,128)}, f32[1024,256]{1,0:T(8,128)}, f32[2,8,256]{2,...) custom-call(s32[2,3]{1,0:T(2,128)} %pad_add_fusion.1.refs_0_, ...), custom_call_target="tpu_custom_call" | custom-call | tf_op jit(solution)/shard_map/pallas_call | solution.py:620
  672.3 5.7 collective-permute-done.7
  679.4 15.3 %fusion.69 = f32[1024,2048]{1,0:T(8,128)} fusion(bf16[1024,2048]{1,0:T(8,128)(2,1)} %get-tuple-element.99, bf16[2048,2048]{1,0:T(8,128)(2,1)} %get-tuple-element.54), kind=kOutput, calls=%fused_computation.142 | convolution fusion | flops 8589934592 | bytes 20971520 | tf_op jit(solution)/shard_map/dot_general | solution.py:1443
  697.0 18.5 %convolution_add_fusion = f32[1024,2048]{1,0:T(8,128)} fusion(f32[1024,2048]{1,0:T(8,128)} %fusion.69, bf16[1024,2432]{1,0:T(8,128)(2,1)} %fusion.33, bf16[2048,2432]{1,0:T(8,128)(2,1)} %get-tuple-element.43), kind=kOutput, calls=%fused_computation.38 | convolution fusion | flops 10202644480 | bytes 31719424 | tf_op jit(solution)/shard_map/dot_general | solution.py:1443
  716.0 13.4 %fusion.52 = f32[1024,2048]{1,0:T(8,128)} fusion(bf16[2048,2048]{1,0:T(8,128)(2,1)} %get-tuple-element.55, f32[1024,2048]{1,0:T(8,128)S(1)} %bitcast.166, f32[1024]{0:T(1024)S(1)} %bitcast.190, f32[2048]{0:T(1024)S(1)} %copy-done.25), kind=kOutput, calls=%fused_computation.131 | convolution fusion | flops 8596226048 | bytes 25178112 | tf_op jit(solution)/shard_map/dot_general | solution.py:1443
  731.6 1.8 copy.49
  733.6 1.4 collective-permute-done.10
  735.0 18.5 %fusion.53 = f32[2048,2432]{1,0:T(8,128)} fusion(bf16[1024,2432]{1,0:T(8,128)(2,1)} %fusion.33, bf16[1024,2048]{1,0:T(8,128)(2,1)} %copy-done.13, f32[2048]{0:T(1024)S(1)} %copy-done.26, f32[1024]{0:T(1024)S(1)} %add_rsqrt_fusion), kind=kOutput, calls=%fused_computation.132 | convolution fusion | flops 10208935936 | bytes 29110272 | tf_op jit(solution)/shard_map/dot_general | solution.py:1437
  753.5 109.2 %shard_map.311 = f32[256,2432]{1,0:T(8,128)} custom-call(f32[4,2,256,2432]{3,2,1,0:T(8,128)} %bitcast.167), custom_call_target="tpu_custom_call" | custom-call | tf_op jit(solution)/shard_map/pallas_call | solution.py:1166
  863.8 3.1 slice_bitcast_fusion
  866.9 7.6 fusion.10
  874.8 4.9 pad_maximum_fusion
  880.4 7.4 copy.47
  889.3 3.1 collective-permute-done.12
  893.6 3.1 collective-permute-done.13
  896.7 1.8 collective-permute-start.14
  898.5 18.7 %fusion.9 = (bf16[1024,2048]{1,0:T(8,128)(2,1)}, bf16[1024,2048]{1,0:T(8,128)(2,1)}) fusion(bf16[1024,2048]{1,0:T(8,128)(2,1)} %copy-done.13, bf16[2,1,512,2048]{3,2,1,0:T(8,128)(2,1)} %param.23, f32[1024]{0:T(1024)S(1)} %broadcast_multiply_fusion, f32[2048]{0:T(1024)S(1)} %copy-done.26, f32[1024]{0:T(1024)S(1)} %add_rsqrt_fusion, ...), kind=kLoop, calls=%fused_computation.12 | loop fusion | flops 29360128 | bytes 50352128 | tf_op jit(solution)/shard_map/convert_element_type | solution.py:1407
  (176 shorter events, 28.0 us)
Async XLA Ops:
  13.3 17.9 %copy-start.22 = (bf16[256,256]{1,0:T(8,128)(2,1)S(1)}, bf16[256,256]{1,0:T(8,128)(2,1)}, u32[]{:S(2)}) copy-start(bf16[256,256]{1,0:T(8,128)(2,1)} %param.26) | copy-start | bytes 393220
  246.5 8.7 slice-start.7
  246.6 8.7 slice-start.8
  254.3 12.6 %copy-start.13 = (bf16[1024,2048]{1,0:T(8,128)(2,1)}, bf16[1024,2048]{1,0:T(8,128)(2,1)S(1)}, u32[]{:S(2)}) copy-start(bf16[1024,2048]{1,0:T(8,128)(2,1)S(1)} %bitcast_dynamic-update-slice_fusion) | copy-start | bytes 12582916
  256.0 17.5 %copy-start.29 = (s32[2,1,2]{2,1,0:T(1,128)S(1)}, s32[2,1,2]{2,1,0:T(1,128)}, u32[]{:S(2)}) copy-start(s32[2,1,2]{2,1,0:T(1,128)} %param.21) | copy-start | bytes 52
  270.8 26.4 %collective-permute-start = (f32[2,8,2432]{2,1,0:T(8,128)S(1)}, f32[2,8,2432]{2,1,0:T(8,128)S(1)}, u32[]{:S(2)}, u32[]{:S(2)}) collective-permute-start(f32[2,8,2432]{2,1,0:T(8,128)S(1)} %pad_maximum_fusion.4), channel_id=1, source_target_pairs={{0,2},{1,3},{4,6},{5,7},{8,10},{9,11},{12,14},{13,15},{16,18},{17,... | collective-permute-start | bytes 466952 | tf_op jit(solution)/shard_map/ppermute | solution.py:1181
  274.6 16.9 %copy-start.16 = (bf16[2,1,512,2048]{3,2,1,0:T(8,128)(2,1)S(1)}, bf16[2,1,512,2048]{3,2,1,0:T(8,128)(2,1)}, u32[]{:S(2)}) copy-start(bf16[2,1,512,2048]{3,2,1,0:T(8,128)(2,1)} %param.23) | copy-start | bytes 12582916
  289.4 7.8 copy-start.1
  289.4 7.8 copy-start.2
  289.4 7.8 copy-start.4
  289.4 7.8 copy-start.6
  294.3 29.5 %copy-start.9 = (f32[1,128]{1,0:T(1,128)}, f32[1,128]{1,0:T(1,128)S(1)}, u32[]{:S(2)}) copy-start(f32[1,128]{1,0:T(1,128)S(1)} %get-tuple-element.127.rate.refs_21_) | copy-start | bytes 1540
  294.3 29.5 %copy-start.10 = (f32[1,128]{1,0:T(1,128)}, f32[1,128]{1,0:T(1,128)S(1)}, u32[]{:S(2)}) copy-start(f32[1,128]{1,0:T(1,128)S(1)} %get-tuple-element.128.sbias.refs_20_) | copy-start | bytes 1540
  294.5 29.3 %copy-start.5 = (f32[1,2048]{1,0:T(1,128)}, f32[1,2048]{1,0:T(1,128)S(1)}, u32[]{:S(2)}) copy-start(f32[1,2048]{1,0:T(1,128)S(1)} %reshape_reshape.3.skip.refs_22_) | copy-start | bytes 24580
  297.2 26.6 %copy-start.21 = (f32[2,8,2432]{2,1,0:T(8,128)}, f32[2,8,2432]{2,1,0:T(8,128)S(1)}, u32[]{:S(2)}) copy-start(f32[2,8,2432]{2,1,0:T(8,128)S(1)} %collective-permute-done.refs_3_.refs_6_) | copy-start | bytes 466948
  323.8 30.9 %copy-start.17 = (bf16[1024,2048]{1,0:T(8,128)(2,1)S(1)}, bf16[1024,2048]{1,0:T(8,128)(2,1)}, u32[]{:S(2)}) copy-start(bf16[1024,2048]{1,0:T(8,128)(2,1)} %bitcast_multiply_fusion) | copy-start | bytes 12582916
  350.7 17.4 %copy-start = (f32[1024,2048]{1,0:T(8,128)}, f32[1024,2048]{1,0:T(8,128)S(1)}, u32[]{:S(2)}) copy-start(f32[1024,2048]{1,0:T(8,128)S(1)} %get-tuple-element.49) | copy-start | bytes 25165828
  350.7 17.4 %copy-start.3 = (f32[2,8,2048]{2,1,0:T(8,128)}, f32[2,8,2048]{2,1,0:T(8,128)S(1)}, u32[]{:S(2)}) copy-start(f32[2,8,2048]{2,1,0:T(8,128)S(1)} %get-tuple-element.57.refs_14_) | copy-start | bytes 393220
  350.7 48.7 %collective-permute-start.2 = (f32[128,2048]{1,0:T(8,128)}, f32[128,2048]{1,0:T(8,128)S(1)}, u32[]{:S(2)}, u32[]{:S(2)}) collective-permute-start(f32[128,2048]{1,0:T(8,128)} %get-tuple-element.53), channel_id=1, source_target_pairs={{0,2},{1,3},{4,6},{5,7},{8,10},{9,11},{12,14},{13,15},{16,18},{17,... | collective-permute-start | bytes 3145736 | tf_op jit(solution)/shard_map/ppermute | solution.py:1181
  352.1 42.4 %collective-permute-start.1 = (f32[128,2048]{1,0:T(8,128)}, f32[128,2048]{1,0:T(8,128)}, u32[]{:S(2)}, u32[]{:S(2)}) collective-permute-start(f32[128,2048]{1,0:T(8,128)} %get-tuple-element.52), channel_id=1, source_target_pairs={{0,2},{1,3},{4,6},{5,7},{8,10},{9,11},{12,14},{13,15},{16,18},{17,... | collective-permute-start | bytes 3145736 | tf_op jit(solution)/shard_map/ppermute | solution.py:1181
  374.6 28.4 %slice-start = ((s8[8388608]{0:T(1024)(128)(4,1)}), s8[4194304]{0:T(1024)(128)(4,1)S(1)}, s32[]{:S(2)}) async-start(s8[8388608]{0:T(1024)(128)(4,1)} %bitcast.153), calls=%async_computation | async-start | bytes 8388608
  374.6 28.4 %copy-start.25 = (f32[2048]{0:T(1024)S(1)}, f32[2048]{0:T(1024)}, u32[]{:S(2)}) copy-start(f32[2048]{0:T(1024)} %param.36) | copy-start | bytes 24580
  394.5 8.5 slice-start.1
  417.5 3.0 collective-permute-start.3
  417.6 19.3 %slice-start.2 = ((s8[8388608]{0:T(1024)(128)(4,1)}), s8[4194304]{0:T(1024)(128)(4,1)S(1)}, s32[]{:S(2)}) async-start(s8[8388608]{0:T(1024)(128)(4,1)} %bitcast.163), calls=%async_computation.2 | async-start | bytes 8388608
  420.6 16.3 %slice-start.3 = ((s8[8388608]{0:T(1024)(128)(4,1)}), s8[4194304]{0:T(1024)(128)(4,1)S(1)}, s32[]{:S(2)}) async-start(s8[8388608]{0:T(1024)(128)(4,1)} %bitcast.163), calls=%async_computation.3 | async-start | bytes 8388608
  442.0 32.7 %collective-permute-start.5 = (f32[128,2048]{1,0:T(8,128)S(1)}, f32[128,2048]{1,0:T(8,128)S(1)}, u32[]{:S(2)}, u32[]{:S(2)}) collective-permute-start(f32[128,2048]{1,0:T(8,128)S(1)} %fusion.16), channel_id=1, source_target_pairs={{2,0},{3,1},{6,4},{7,5},{10,8},{11,9},{14,12},{15,13},{18,16},{19,... | collective-permute-start | bytes 3145736 | tf_op jit(solution)/shard_map/ppermute | solution.py:1181
  443.3 48.7 %collective-permute-start.6 = (f32[128,2048]{1,0:T(8,128)S(1)}, f32[128,2048]{1,0:T(8,128)S(1)}, u32[]{:S(2)}, u32[]{:S(2)}) collective-permute-start(f32[128,2048]{1,0:T(8,128)S(1)} %fusion.15), channel_id=1, source_target_pairs={{2,0},{3,1},{6,4},{7,5},{10,8},{11,9},{14,12},{15,13},{18,16},{19,... | collective-permute-start | bytes 3145736 | tf_op jit(solution)/shard_map/ppermute | solution.py:1181
  444.6 14.9 %copy-start.19 = (bf16[2048,1024]{1,0:T(8,128)(2,1)S(1)}, bf16[2048,1024]{1,0:T(8,128)(2,1)}, u32[]{:S(2)}) copy-start(bf16[2048,1024]{1,0:T(8,128)(2,1)} %copy.51) | copy-start | bytes 12582916
  671.0 7.0 collective-permute-start.7
  679.3 15.4 %copy-start.23 = (f32[2,8,2048]{2,1,0:T(8,128)S(1)}, f32[2,8,2048]{2,1,0:T(8,128)}, u32[]{:S(2)}) copy-start(f32[2,8,2048]{2,1,0:T(8,128)} %get-tuple-element.62) | copy-start | bytes 393220
  679.3 15.4 %collective-permute-start.8 = (f32[2,512,256]{2,1,0:T(8,128)S(1)}, f32[2,512,256]{2,1,0:T(8,128)S(1)}, u32[]{:S(2)}, u32[]{:S(2)}) collective-permute-start(f32[2,512,256]{2,1,0:T(8,128)S(1)} %pad_add_fusion), channel_id=1, source_target_pairs={{0,1},{1,0},{2,3},{3,2},{4,5},{5,4},{6,7},{7,6},{8,9},{9,8},{10,11... | collective-permute-start | bytes 3145736 | tf_op jit(solution)/shard_map/ppermute | solution.py:1186
  679.4 36.6 %slice-start.4 = ((s8[8388608]{0:T(1024)(128)(4,1)}), s8[4194304]{0:T(1024)(128)(4,1)S(1)}, s32[]{:S(2)}) async-start(s8[8388608]{0:T(1024)(128)(4,1)} %bitcast.165), calls=%async_computation.4 | async-start | bytes 8388608
  697.0 19.0 %slice-start.5 = ((s8[8388608]{0:T(1024)(128)(4,1)}), s8[4194304]{0:T(1024)(128)(4,1)S(1)}, s32[]{:S(2)}) async-start(s8[8388608]{0:T(1024)(128)(4,1)} %bitcast.165), calls=%async_computation.5 | async-start | bytes 8388608
  715.5 14.0 %copy-start.30 = (f32[8,256]{1,0:T(8,128)S(1)}, f32[8,256]{1,0:T(8,128)}, u32[]{:S(2)}) copy-start(f32[8,256]{1,0:T(8,128)} %get-tuple-element.64) | copy-start | bytes 24580
  715.5 16.1 %copy-start.24 = (f32[8,2048]{1,0:T(8,128)S(1)}, f32[8,2048]{1,0:T(8,128)}, u32[]{:S(2)}) copy-start(f32[8,2048]{1,0:T(8,128)} %get-tuple-element.63) | copy-start | bytes 196612
  715.5 16.1 %copy-start.20 = (f32[256,2048]{1,0:T(8,128)S(1)}, f32[256,2048]{1,0:T(8,128)}, u32[]{:S(2)}) copy-start(f32[256,2048]{1,0:T(8,128)} %get-tuple-element.68) | copy-start | bytes 6291460
  715.5 151.4 %collective-permute-start.9 = (f32[1024,2048]{1,0:T(8,128)}, f32[1024,2048]{1,0:T(8,128)}, u32[]{:S(2)}, u32[]{:S(2)}) collective-permute-start(f32[1024,2048]{1,0:T(8,128)} %convolution_add_fusion), channel_id=1, source_target_pairs={{0,1},{1,0},{2,3},{3,2},{4,5},{5,4},{6,7},{7,6},{8,9},{9,8},{10,11... | collective-permute-start | bytes 25165832 | tf_op jit(solution)/shard_map/ppermute | solution.py:1186
  729.5 169.0 %collective-permute-start.4 = (f32[1024,2048]{1,0:T(8,128)}, f32[1024,2048]{1,0:T(8,128)}, u32[]{:S(2)}, u32[]{:S(2)}) collective-permute-start(f32[1024,2048]{1,0:T(8,128)} %fusion.52), channel_id=1, source_target_pairs={{0,1},{1,0},{2,3},{3,2},{4,5},{5,4},{6,7},{7,6},{8,9},{9,8},{10,11... | collective-permute-start | bytes 25165832 | tf_op jit(solution)/shard_map/ppermute | solution.py:1186
  729.5 5.4 collective-permute-start.10
  753.5 113.4 %copy-start.15 = (bf16[1024,2048]{1,0:T(8,128)(2,1)S(1)}, bf16[1024,2048]{1,0:T(8,128)(2,1)}, u32[]{:S(2)}) copy-start(bf16[1024,2048]{1,0:T(8,128)(2,1)} %copy-done.13) | copy-start | bytes 12582916
  863.7 24.9 %collective-permute-start.15 = (f32[256,256]{1,0:T(8,128)S(1)}, f32[256,256]{1,0:T(8,128)S(1)}, u32[]{:S(2)}, u32[]{:S(2)}) collective-permute-start(f32[256,256]{1,0:T(8,128)S(1)} %slice.211), channel_id=1, source_target_pairs={{0,1},{1,0},{2,3},{3,2},{4,5},{5,4},{6,7},{7,6},{8,9},{9,8},{10,11... | collective-permute-start | bytes 786440 | tf_op jit(solution)/shard_map/ppermute | solution.py:1186
  874.7 13.1 %collective-permute-start.11 = (f32[128,128]{1,0:T(8,128)S(1)}, f32[128,128]{1,0:T(8,128)S(1)}, u32[]{:S(2)}, u32[]{:S(2)}) collective-permute-start(f32[128,128]{1,0:T(8,128)S(1)} %pad_bitcast_fusion), channel_id=1, source_target_pairs={{0,2},{2,0},{1,3},{3,1},{4,6},{6,4},{5,7},{7,5},{8,10},{10,8},{9,1... | collective-permute-start | bytes 196616 | tf_op jit(solution)/shard_map/ppermute | solution.py:1206
  874.8 13.8 %copy-start.18 = (f32[256,2432]{1,0:T(8,128)S(1)}, f32[256,2432]{1,0:T(8,128)}, u32[]{:S(2)}) copy-start(f32[256,2432]{1,0:T(8,128)} %shard_map.311) | copy-start | bytes 7471108
  874.8 23.7 %copy-start.28 = (f32[1024]{0:T(1024)S(1)}, f32[1024]{0:T(1024)}, u32[]{:S(2)}) copy-start(f32[1024]{0:T(1024)} %get-tuple-element.115) | copy-start | bytes 12292
  887.8 4.6 collective-permute-start.12
  892.4 4.3 collective-permute-start.13
  896.7 20.5 %collective-permute-start.14 = (f32[128,128]{1,0:T(8,128)S(1)}, f32[128,128]{1,0:T(8,128)S(1)}, u32[]{:S(2)}, u32[]{:S(2)}) collective-permute-start(f32[128,128]{1,0:T(8,128)S(1)} %add.179), channel_id=1, source_target_pairs={{0,16},{4,20},{8,24},{12,28},{16,0},{20,4},{24,8},{28,12},{1,17},{... | collective-permute-start | bytes 196616 | tf_op jit(solution)/shard_map/ppermute | solution.py:1206
  (12 other events, 63.1 us)

commit v4 on v3

--- a/solution.py
+++ b/solution.py
@@ -116,35 +116,43 @@
     return 1.0 / (1.0 + jnp.exp(-value))
 
 
-def forward_kernel(
-    heads,
-    extra,
-    marks,
-    vraw,
-    vprev,
-    vrim,
-    craw,
-    cprev,
-    crim,
-    sraw,
-    cw,
-    cb,
-    ccw,
-    ccb,
-    sbias,
-    rate,
-    skip,
-    sel,
-    selcol,
-    *refs,
-):
-    y_out, st_out, fin_out, bc_out, carry_out, cd_out = refs[extra : extra + 6]
-    (state, cumt, stack, cumpack, halo, same_s, bias_s, gram_s, cd_s, cparts, btparts) = refs[
-        extra + 6 :
-    ]
-    chunk = pl.program_id(0)
-    chunks = pl.num_programs(0)
+def forward_kernel(heads, chunks, plan, *refs):
+    (
+        marks, vraw, vprev, vrim, craw, cprev, crim, sraw, cw, cb, ccw, ccb, sbias, rate, skip,
+        sel, selcol,
+    ) = refs[:17]
+    arrays = plan.arrays
+    weights, refs = refs[17 : 17 + arrays], refs[17 + arrays :]
+    y_out, st_out, fin_out, bc_out, carry_out, cd_out, entering = refs[:7]
+    fulls, refs = refs[7 : 7 + arrays], refs[7 + arrays :]
+    (
+        state, cumt, stack, cumpack, halo, same_s, bias_s, gram_s, cd_s, cparts, btparts,
+        leaving, leave_send, leave_recv,
+    ) = refs[:14]
+    plan.bind(weights, fulls, refs[14:])
+    grid_step = pl.program_id(0)
+    steps = pl.num_programs(0)
+    chunk = lax.rem(grid_step, chunks)
+    micro = grid_step // chunks
     width = state.shape[0]
+    early = {0: range(0, arrays), 3: range(arrays, arrays + 1), 5: range(arrays + 1, arrays + 2)}
+    placed = max(early[5])
+
+    def leave_copy(which):
+        return pltpu.make_async_remote_copy(
+            src_ref=leaving.at[which], dst_ref=entering.at[which],
+            send_sem=leave_send.at[which], recv_sem=leave_recv.at[which],
+            device_id=plan.across, device_id_type=MESH,
+        )
+
+    for when, numbers in early.items():
+
+        @pl.when(grid_step == when)
+        def _(when=when, numbers=numbers):
+            if when == 0:
+                plan.greet()
+            for number in numbers:
+                plan.event(number)
 
     @pl.when(chunk == 0)
     def _():
@@ -157,7 +165,7 @@
     def _():
         halo[...] = vprev[...]
 
-    frame = chunk_frame(marks, chunk, sraw[...], sbias[...], rate[...], heads)
+    frame = chunk_frame([marks[micro, place] for place in range(3)], chunk, sraw[...], sbias[...], rate[...], heads)
     same = frame["same"]
     for lag in range(1, 4):
         same_s[lag - 1] = same[lag]
@@ -239,6 +247,19 @@
     lax.fori_loop(0, heads // 2, pair, 0, unroll=4)
     cd_out[...] = jnp.where(eight_rows == chunk + 1, cd_s[0:1, :], cd_out[...])
 
+    @pl.when(chunk == chunks - 1)
+    def _():
+        leaving[micro] = state[...]
+        leave_copy(micro).start()
+
+    @pl.when(grid_step == steps - 1)
+    def _():
+        for number in range(placed + 1, len(plan.order)):
+            plan.event(number)
+        plan.finish()
+        for which in range(leaving.shape[0]):
+            leave_copy(which).wait()
+
 
 def selectors(heads, head_size):
     inner = heads * head_size
@@ -257,102 +278,113 @@
 
 
 def forward_ssd(
-    marks, micro, micros, before_this, raw, rim, inner, twice, tokens,
-    cw, cb, ccw, ccb, sbias, rate, skip, sel, selcol,
+    marks, micros, raw, rims, inner, twice, tokens,
+    cw, cb, ccw, ccb, sbias, rate, skip, sel, selcol, shards, shared, collective_id,
 ):
     width = twice // 2
     chunks = tokens // CHUNK
     heads = inner // (LANES // 2)
     eighth = CHUNK // 8
-    initial = micro * chunks
+    pairs = lax.axis_size("fsdp") // 2
+    shard_rows = shards[0].shape[0]
+    plan = Gathering(shard_rows, pairs, len(shards), shared)
 
     def part(count, start):
-        return pl.BlockSpec((CHUNK, count), lambda chunk, *_: (initial + chunk, start // count))
+        return pl.BlockSpec((CHUNK, count), lambda step: (step, start // count))
 
     def before(count, start):
         return pl.BlockSpec(
-            (8, count),
-            lambda chunk, *_: (jnp.maximum((initial + chunk) * eighth - 1, 0), start // count),
+            (8, count), lambda step: (jnp.maximum(step * eighth - 1, 0), start // count)
         )
 
     def edge(count, start):
-        return pl.BlockSpec((8, count), lambda *_: (0, start // count))
-
+        return pl.BlockSpec((None, 8, count), lambda step: (step // chunks, 0, start // count))
+
+    def each(*shape):
+        return pl.BlockSpec((None, *shape), lambda step: (step // chunks, 0, 0))
+
+    hbm = pl.BlockSpec(memory_space=pl.ANY)
+    dma = pltpu.SemaphoreType.DMA
     return pl.pallas_call(
-        functools.partial(forward_kernel, heads, len(before_this)),
-        grid_spec=pltpu.PrefetchScalarGridSpec(
-            num_scalar_prefetch=1,
-            grid=(chunks,),
-            in_specs=[
-                part(inner, 0),
-                before(inner, 0),
-                edge(inner, 0),
-                part(twice, inner),
-                before(twice, inner),
-                edge(twice, inner),
-                part(LANES, inner + twice),
-                whole(cw.shape),
-                whole(cb.shape),
-                whole(ccw.shape),
-                whole(ccb.shape),
-                whole(sbias.shape),
-                whole(rate.shape),
-                whole(skip.shape),
-                whole(sel.shape),
-                whole(selcol.shape),
-            ]
-            + [pl.BlockSpec(memory_space=pl.ANY)] * len(before_this),
-            out_specs=[
-                part(inner, 0),
-                pl.BlockSpec((1, width, inner), lambda chunk, *_: (initial + chunk, 0, 0)),
-                whole((width, inner)),
-                part(twice, 0),
-                part(inner, 0),
-                pl.BlockSpec((None, 8, inner), lambda *_: (micro, 0, 0)),
-            ],
-            scratch_shapes=[
-                pltpu.VMEM((width, inner), f32),
-                pltpu.VMEM((LANES, CHUNK), f32),
-                pltpu.VMEM((3 * CHUNK, LANES), bf16),
-                pltpu.VMEM((CHUNK, LANES), bf16),
-                pltpu.VMEM((8, inner), f32),
-                pltpu.VMEM((3, CHUNK, LANES), f32),
-                pltpu.VMEM((CHUNK, CHUNK), f32),
-                pltpu.VMEM((CHUNK, CHUNK), f32),
-                pltpu.VMEM((8, inner), f32),
-                pltpu.VMEM((2, CHUNK, width), bf16),
-                pltpu.VMEM((2, width, CHUNK), bf16),
-            ],
-        ),
+        functools.partial(forward_kernel, heads, chunks, plan),
+        grid=(micros * chunks,),
+        in_specs=[
+            pl.BlockSpec(memory_space=pltpu.SMEM),
+            part(inner, 0),
+            before(inner, 0),
+            edge(inner, 0),
+            part(twice, inner),
+            before(twice, inner),
+            edge(twice, inner),
+            part(LANES, inner + twice),
+            whole(cw.shape),
+            whole(cb.shape),
+            whole(ccw.shape),
+            whole(ccb.shape),
+            whole(sbias.shape),
+            whole(rate.shape),
+            whole(skip.shape),
+            whole(sel.shape),
+            whole(selcol.shape),
+        ]
+        + [hbm] * len(shards),
+        out_specs=[
+            part(inner, 0),
+            pl.BlockSpec((1, width, inner), lambda step: (step, 0, 0)),
+            each(width, inner),
+            part(twice, 0),
+            part(inner, 0),
+            each(8, inner),
+            hbm,
+        ]
+        + [hbm] * len(shards),
+        scratch_shapes=[
+            pltpu.VMEM((width, inner), f32),
+            pltpu.VMEM((LANES, CHUNK), f32),
+            pltpu.VMEM((3 * CHUNK, LANES), bf16),
+            pltpu.VMEM((CHUNK, LANES), bf16),
+            pltpu.VMEM((8, inner), f32),
+            pltpu.VMEM((3, CHUNK, LANES), f32),
+            pltpu.VMEM((CHUNK, CHUNK), f32),
+            pltpu.VMEM((CHUNK, CHUNK), f32),
+            pltpu.VMEM((8, inner), f32),
+            pltpu.VMEM((2, CHUNK, width), bf16),
+            pltpu.VMEM((2, width, CHUNK), bf16),
+            pltpu.VMEM((micros, width, inner), f32),
+            dma((micros,)),
+            dma((micros,)),
+        ]
+        + plan.scratch(),
         out_shape=[
             jax.ShapeDtypeStruct((micros * tokens, inner), f32),
             jax.ShapeDtypeStruct((micros * chunks, width, inner), f32),
-            jax.ShapeDtypeStruct((width, inner), f32),
+            jax.ShapeDtypeStruct((micros, width, inner), f32),
             jax.ShapeDtypeStruct((micros * tokens, twice), f32),
             jax.ShapeDtypeStruct((micros * tokens, inner), f32),
             jax.ShapeDtypeStruct((micros, 8, inner), f32),
+            jax.ShapeDtypeStruct((micros, width, inner), f32),
+        ]
+        + [
+            jax.ShapeDtypeStruct((2 * pairs * shard_rows, shard.shape[1]), shard.dtype)
+            for shard in shards
         ],
-        input_output_aliases={
-            17 + number: where for number, where in enumerate([0, 1, 3, 4, 5][: len(before_this)])
-        },
-        compiler_params=pltpu.CompilerParams(vmem_limit_bytes=40 * 1024 * 1024),
-        cost_estimate=pl.CostEstimate(
-            flops=20 * tokens * inner * 128 * 2, bytes_accessed=24 * tokens * inner, transcendentals=0
+        compiler_params=pltpu.CompilerParams(
+            collective_id=collective_id, has_side_effects=True, vmem_limit_bytes=48 * 1024 * 1024
         ),
     )(
-        marks, raw, raw, rim, raw, raw, rim, raw, cw, cb, ccw, ccb, sbias, rate, skip, sel, selcol,
-        *before_this,
-    )
-
-
-def backward_kernel(heads, chunks, plan, *refs):
+        marks, raw, raw, rims, raw, raw, rims, raw, cw, cb, ccw, ccb, sbias, rate, skip, sel, selcol,
+        *shards,
+    )
+
+
+def backward_kernel(heads, chunks, plan, waited, *refs):
     (
         marks, vraw, vprev, vrim, craw, cprev, crim, sraw, grad, mixer, st_now, st_next, fin,
         entering, cd, pulled, cw, cb, ccw, ccb, sbias, rate, skip, sel, selcol, selt,
     ) = refs[:26]
     arrays = len(plan.counts)
     refs = refs[26:]
-    terms, refs = refs[:arrays], refs[arrays:]
+    terms, refs = refs[:arrays], refs[arrays + waited :]
     (
         lead_g, vtail_g, vrim_g, craw_g, crim_g, cw_g, ccw_g, small_g, skip_g,
     ) = refs[:9]
@@ -578,7 +610,7 @@
 
 def backward_ssd(
     marks, micros, raw, rims, inner, twice, tokens, grad, mixer, states, fin, entering, cd, pulled,
-    cw, cb, ccw, ccb, sbias, rate, skip, sel, selcol, selt, terms, collective_id,
+    cw, cb, ccw, ccb, sbias, rate, skip, sel, selcol, selt, terms, first, collective_id,
 ):
     width = twice // 2
     chunks = tokens // CHUNK
@@ -618,7 +650,7 @@
 
     hbm = pl.BlockSpec(memory_space=pl.ANY)
     return pl.pallas_call(
-        functools.partial(backward_kernel, heads, chunks, plan),
+        functools.partial(backward_kernel, heads, chunks, plan, len(first)),
         grid=(micros * chunks,),
         in_specs=[
             pl.BlockSpec(memory_space=pltpu.SMEM),
@@ -648,7 +680,7 @@
             whole(selcol.shape),
             whole(selt.shape),
         ]
-        + [hbm] * len(terms),
+        + [hbm] * (len(terms) + len(first)),
         out_specs=[
             part(lead, 0),
             each(8, inner),
@@ -699,152 +731,362 @@
     )(
         marks, raw, raw, rims, raw, raw, rims, raw, grad, mixer, states, states, fin, entering,
         cd, pulled, cw, cb, ccw, ccb, sbias, rate, skip, sel, selcol, selt,
-        *[term.reshape(pairs, 2, shard_rows, -1) for term in terms],
-    )
-
-
-def gather_kernel(arrays, shared, *refs):
+        *[term.reshape(pairs, 2, shard_rows, -1) for term in terms], *first,
+    )
+
+
+class Gathering:
+    def __init__(self, rows, pairs, arrays, shared):
+        self.rows, self.pairs, self.arrays, self.shared = rows, pairs, arrays, shared
+        self.moved = rows - shared
+        self.order = [(j, k) for k in range(pairs) for j in range(arrays)]
+        self.lag = max(arrays, 2)
+
+    def scratch(self):
+        dma, pairs, arrays = pltpu.SemaphoreType.DMA, self.pairs, self.arrays
+        return [
+            dma((arrays, max(pairs - 1, 1))),
+            dma((arrays, max(pairs - 1, 1))),
+            dma((arrays, pairs)),
+            dma((arrays, pairs)),
+            dma((arrays, 2 * pairs)),
+            dma((arrays, 2 * pairs)),
+            dma((arrays,)),
+        ]
+
+    def bind(self, weights, fulls, scratch):
+        self.weights, self.fulls = weights, fulls
+        (
+            self.ring_send, self.ring_recv, self.pair_send, self.pair_recv,
+            self.cross_send, self.cross_recv, self.local,
+        ) = scratch
+        self.own, self.place = lax.axis_index("fsdp"), lax.axis_index("context")
+        self.side = lax.axis_index("tensor")
+        self.pair, self.member = self.own // 2, lax.rem(self.own, 2)
+        pairs, pair, member = self.pairs, self.pair, self.member
+        self.ahead = (2 * lax.rem(pair + 1, pairs) + member, self.place, self.side)
+        self.behind = (2 * lax.rem(pair + pairs - 1, pairs) + member, self.place, self.side)
+        self.partner = (2 * pair + 1 - member, self.place, self.side)
+        self.across = (self.own, 1 - self.place, self.side)
+        self.beside = (self.own, self.place, 1 - self.side)
+        self.moved_start = pl.multiple_of(self.place * self.shared, 16)
+        self.shared_start = pl.multiple_of(self.place * self.moved, 16)
+
+    def greet(self, *others):
+        barrier = pltpu.get_barrier_semaphore()
+        devices = [self.ahead, self.behind, self.partner, self.across, *others]
+        for device in devices:
+            pl.semaphore_signal(barrier, inc=1, device_id=device, device_id_type=MESH)
+        pl.semaphore_wait(barrier, len(devices))
+
+    def part(self, j, k, which, start, size):
+        there = lax.rem(self.pair + self.pairs - k, self.pairs)
+        index = 2 * there + (self.member if which == 0 else 1 - self.member)
+        return self.fulls[j].at[pl.ds(pl.multiple_of(index * self.rows + start, 16), size), :]
+
+    def source(self, j, k):
+        if k == 0:
+            return self.weights[j].at[pl.ds(self.moved_start, self.moved), :]
+        return self.part(j, k, 0, self.moved_start, self.moved)
+
+    def ring_copy(self, j, k):
+        return pltpu.make_async_remote_copy(
+            src_ref=self.source(j, k), dst_ref=self.part(j, k, 0, self.moved_start, self.moved),
+            send_sem=self.ring_send.at[j, k], recv_sem=self.ring_recv.at[j, k],
+            device_id=self.ahead, device_id_type=MESH,
+        )
+
+    def pair_copy(self, j, k):
+        return pltpu.make_async_remote_copy(
+            src_ref=self.source(j, k), dst_ref=self.part(j, k, 0, self.moved_start, self.moved),
+            send_sem=self.pair_send.at[j, k], recv_sem=self.pair_recv.at[j, k],
+            device_id=self.partner, device_id_type=MESH,
+        )
+
+    def cross_copy(self, j, k, which):
+        here = self.part(j, k, which, self.shared_start, self.shared)
+        return pltpu.make_async_remote_copy(
+            src_ref=here, dst_ref=here,
+            send_sem=self.cross_send.at[j, 2 * k + which], recv_sem=self.cross_recv.at[j, 2 * k + which],
+            device_id=self.across, device_id_type=MESH,
+        )
+
+    def keep_copy(self, j):
+        rows = pl.ds(pl.multiple_of(self.own * self.rows, 16), self.rows)
+        return pltpu.make_async_copy(self.weights[j], self.fulls[j].at[rows, :], self.local.at[j])
+
+    def event(self, number):
+        j, k = self.order[number]
+        if k > 0:
+            self.ring_copy(j, k - 1).wait_recv()
+        else:
+            self.keep_copy(j).start()
+        if k < self.pairs - 1:
+            self.ring_copy(j, k).start()
+        self.pair_copy(j, k).start()
+        if k > 0:
+            self.cross_copy(j, k, 0).start()
+        if number >= self.lag:
+            self.share(number - self.lag)
+
+    def share(self, number):
+        j, k = self.order[number]
+        self.pair_copy(j, k).wait_recv()
+        self.cross_copy(j, k, 1).start()
+
+    def finish(self):
+        for number in range(max(len(self.order) - self.lag, 0), len(self.order)):
+            self.share(number)
+        crossed = [(j, k, which) for j, k in self.order for which in range(2) if k or which]
+        for item in crossed:
+            self.cross_copy(*item).wait_recv()
+        for j, k in self.order:
+            if k < self.pairs - 1:
+                self.ring_copy(j, k).wait_send()
+            self.pair_copy(j, k).wait_send()
+        for item in crossed:
+            self.cross_copy(*item).wait_send()
+        for j in range(self.arrays):
+            self.keep_copy(j).wait()
+
+
+def gather_kernel(plan, *refs):
+    arrays = plan.arrays
     weights, tokens = refs[:arrays], refs[arrays]
     fulls, far = refs[arrays + 1 : 2 * arrays + 1], refs[2 * arrays + 1]
-    refs = refs[2 * arrays + 2 :]
-    ring_send, ring_recv, pair_send, pair_recv, cross_send, cross_recv, extra_send, extra_recv, local_sem = refs
-    count = lax.axis_size("fsdp")
-    pairs = count // 2
-    own, place, side = lax.axis_index("fsdp"), lax.axis_index("context"), lax.axis_index("tensor")
-    pair, member = own // 2, lax.rem(own, 2)
-    rows = weights[0].shape[0]
-    moved = rows - shared
-
-    def at(offset, which):
-        there = lax.rem(pair + pairs - offset, pairs)
-        return 2 * there + (member if which == 0 else 1 - member)
-
-    ahead = (2 * lax.rem(pair + 1, pairs) + member, place, side)
-    behind = (2 * lax.rem(pair + pairs - 1, pairs) + member, place, side)
-    partner = (2 * pair + 1 - member, place, side)
-    across = (own, 1 - place, side)
-    beside = (own, place, 1 - side)
-    barrier = pltpu.get_barrier_semaphore()
-    greeted = [ahead, behind, partner, across, beside]
-    for device in greeted:
-        pl.semaphore_signal(barrier, inc=1, device_id=device, device_id_type=MESH)
-    pl.semaphore_wait(barrier, len(greeted))
-
-    def part(index, j, start, size):
-        return fulls[j].at[pl.ds(pl.multiple_of(index * rows + start, 16), size), :]
-
-    moved_start = pl.multiple_of(place * shared, 16)
-    shared_start = pl.multiple_of(place * moved, 16)
-
-    started = []
-
-    def send(src, dst, send_sem, recv_sem, device):
-        copy = pltpu.make_async_remote_copy(
-            src_ref=src, dst_ref=dst, send_sem=send_sem, recv_sem=recv_sem,
+    extra_send, extra_recv = refs[2 * arrays + 2 : 2 * arrays + 4]
+    plan.bind(weights, fulls, refs[2 * arrays + 4 :])
+    plan.greet(plan.beside)
+    half = tokens.shape[2] // 2
+    lanes = pl.ds(pl.multiple_of(plan.side * half, 128), half)
+
+    def token_copy(src, number, device):
+        return pltpu.make_async_remote_copy(
+            src_ref=src.at[:, :, lanes], dst_ref=far.at[:, :, lanes],
+            send_sem=extra_send.at[number], recv_sem=extra_recv.at[number],
             device_id=device, device_id_type=MESH,
         )
-        copy.start()
-        started.append(copy)
-        return copy
-
-    kept = []
-    for j in range(arrays):
-        kept.append(
-            pltpu.make_async_copy(
-                weights[j], fulls[j].at[pl.ds(pl.multiple_of(own * rows, 16), rows), :], local_sem.at[j]
-            )
-        )
-        kept[-1].start()
-
-    def from_own(j):
-        return weights[j].at[pl.ds(moved_start, moved), :]
-
-    ring, within, crossed = {}, {}, []
-
-    def start_ring(j, k):
-        dst = part(at(k, 0), j, moved_start, moved)
-        ring[j, k] = send(
-            from_own(j) if k == 0 else dst, dst, ring_send.at[j, k], ring_recv.at[j, k], ahead
-        )
-
-    def start_pair(j, k):
-        dst = part(at(k, 0), j, moved_start, moved)
-        within[j, k] = send(
-            from_own(j) if k == 0 else dst, dst, pair_send.at[j, k], pair_recv.at[j, k], partner
-        )
-
-    def start_cross(j, k, which):
-        here = part(at(k, which), j, shared_start, shared)
-        slot = 2 * k + which
-        crossed.append(
-            send(here, here, cross_send.at[j, slot], cross_recv.at[j, slot], across)
-        )
-
-    half = tokens.shape[2] // 2
-    lanes = pl.ds(pl.multiple_of(side * half, 128), half)
-    token_copy = send(
-        tokens.at[:, :, lanes], far.at[:, :, lanes], extra_send.at[0], extra_recv.at[0], across
-    )
-    steps = [(j, k) for j in range(arrays) for k in range(pairs)]
-    waiting = []
-    forwarded = None
-    for number, (j, k) in enumerate(steps):
-        if k > 0:
-            ring[j, k - 1].wait_recv()
-        if k < pairs - 1:
-            start_ring(j, k)
-        start_pair(j, k)
-        if k > 0:
-            start_cross(j, k, 0)
-        waiting.append((j, k))
-        if len(waiting) > 2:
-            wj, wk = waiting.pop(0)
-            within[wj, wk].wait_recv()
-            start_cross(wj, wk, 1)
-        if number == min(pairs, len(steps) - 1):
-            token_copy.wait_recv()
-            forwarded = send(
-                far.at[:, :, lanes], far.at[:, :, lanes], extra_send.at[1], extra_recv.at[1], beside
-            )
-    for wj, wk in waiting:
-        within[wj, wk].wait_recv()
-        start_cross(wj, wk, 1)
-    forwarded.wait_recv()
-    for copy in crossed:
-        copy.wait_recv()
-    for copy in started:
-        copy.wait_send()
-    for copy in kept:
-        copy.wait()
+
+    first, second = token_copy(tokens, 0, plan.across), token_copy(far, 1, plan.beside)
+    first.start()
+    for number in range(len(plan.order)):
+        plan.event(number)
+        if number == min(2, len(plan.order) - 1):
+            first.wait_recv()
+            second.start()
+    second.wait_recv()
+    plan.finish()
+    first.wait_send()
+    second.wait_send()
 
 
 def gather_weights(shards, tokens, shared, collective_id):
     rows = shards[0].shape[0]
     pairs = lax.axis_size("fsdp") // 2
     count = len(shards)
+    plan = Gathering(rows, pairs, count, shared)
     hbm = pl.BlockSpec(memory_space=pl.ANY)
     dma = pltpu.SemaphoreType.DMA
     return pl.pallas_call(
-        functools.partial(gather_kernel, count, shared),
+        functools.partial(gather_kernel, plan),
         out_shape=[
             jax.ShapeDtypeStruct((2 * pairs * rows, shard.shape[1]), shard.dtype) for shard in shards
         ]
         + [jax.ShapeDtypeStruct(tokens.shape, tokens.dtype)],
         in_specs=[hbm] * (count + 1),
         out_specs=[hbm] * (count + 1),
-        scratch_shapes=[
-            dma((count, max(pairs - 1, 1))),
-            dma((count, max(pairs - 1, 1))),
-            dma((count, pairs)),
-            dma((count, pairs)),
-            dma((count, 2 * pairs)),
-            dma((count, 2 * pairs)),
-            dma((2,)),
-            dma((2,)),
-            dma((count,)),
-        ],
+        scratch_shapes=[dma((2,)), dma((2,))] + plan.scratch(),
         compiler_params=pltpu.CompilerParams(collective_id=collective_id, has_side_effects=True),
     )(*shards, tokens)
+
+
+def order_kernel(near_index, far_index, is_near, near, far, gain, x_out, normed_out, scale_out):
+    step = pl.program_id(0)
+    near_now = is_near[step] == 1
+    x = jnp.where(near_now, near[...], far[...])
+    x_out[...] = x
+    value = x.astype(f32)
+    mean = jnp.sum(value * value, axis=-1, keepdims=True) * (1.0 / value.shape[-1])
+    scale = lax.rsqrt(mean + epsilon)
+    normed_out[...] = (value * scale * gain[...]).astype(bf16)
+    scale_out[...] = jnp.broadcast_to(scale, scale_out.shape)
+
+
+def ordered(near, far, near_index, far_index, is_near, gain):
+    micros, count, length, model = near.shape
+    blocks = micros * count
+
+    def block(spec_index):
+        return pl.BlockSpec((None, None, length, model), spec_index)
+
+    def rows(lanes):
+        return pl.BlockSpec((length, lanes), lambda step, *_: (step, 0))
+
+    return pl.pallas_call(
+        order_kernel,
+        grid_spec=pltpu.PrefetchScalarGridSpec(
+            num_scalar_prefetch=3,
+            grid=(blocks,),
+            in_specs=[
+                block(lambda step, near_at, far_at, flags: (step // count, near_at[step], 0, 0)),
+                block(lambda step, near_at, far_at, flags: (step // count, far_at[step], 0, 0)),
+                pl.BlockSpec((1, model), lambda *_: (0, 0)),
+            ],
+            out_specs=[rows(model), rows(model), rows(LANES)],
+        ),
+        out_shape=[
+            jax.ShapeDtypeStruct((blocks * length, model), bf16),
+            jax.ShapeDtypeStruct((blocks * length, model), bf16),
+            jax.ShapeDtypeStruct((blocks * length, LANES), f32),
+        ],
+        compiler_params=pltpu.CompilerParams(vmem_limit_bytes=32 * 1024 * 1024),
+    )(near_index, far_index, is_near, near, far, gain)
+
+
+def gate_kernel(
+    normed, out_grad, gate_weight, out_weight, y_own, carry, coupled, entering, gain,
+    mixer_out, gate_out, grad_out, sums_out,
+):
+    gate_in = mm(normed[...], gate_weight[...])
+    grads = mm(out_grad[...], out_weight[...])
+    width = entering.shape[0]
+    arrived = mm_three(split_two(coupled[:, width:]), split_two(entering[...]))
+    mixer = y_own[...] + carry[...] * arrived
+    gated = mixer * (gate_in * logistic(gate_in))
+    mixer_out[...] = mixer
+    gate_out[...] = gate_in
+    grad_out[...] = grads
+    square = jnp.sum(gated * gated, axis=-1, keepdims=True)
+    product = jnp.sum(grads * gain[...] * gated, axis=-1, keepdims=True)
+    lane = lax.broadcasted_iota(jnp.int32, sums_out.shape, 1)
+    sums_out[...] = jnp.where(lane == 0, square, jnp.where(lane == 1, product, 0.0))
+
+
+def gate_stage(normed, out_grad, gate_weight, out_weight, y_own, carry, coupled, entering, gain):
+    rows, model = normed.shape
+    inner = y_own.shape[1]
+    twice = coupled.shape[1]
+    micros, width, _ = entering.shape
+    size = 2 * CHUNK
+    per_micro = rows // micros // size
+
+    def block(lanes):
+        return pl.BlockSpec((size, lanes), lambda step: (step, 0))
+
+    return pl.pallas_call(
+        gate_kernel,
+        grid=(rows // size,),
+        in_specs=[
+            block(model),
+            block(model),
+            pl.BlockSpec((model, inner), lambda step: (0, 0), pipeline_mode=pl.Buffered(1)),
+            pl.BlockSpec((model, inner), lambda step: (0, 0), pipeline_mode=pl.Buffered(1)),
+            block(inner),
+            block(inner),
+            block(twice),
+            pl.BlockSpec((None, width, inner), lambda step: (step // per_micro, 0, 0)),
+            pl.BlockSpec((1, inner), lambda step: (0, 0)),
+        ],
+        out_specs=[block(inner), block(inner), block(inner), block(LANES)],
+        out_shape=[jax.ShapeDtypeStruct((rows, inner), f32)] * 3
+        + [jax.ShapeDtypeStruct((rows, LANES), f32)],
+        compiler_params=pltpu.CompilerParams(vmem_limit_bytes=60 * 1024 * 1024),
+        cost_estimate=pl.CostEstimate(
+            flops=4 * rows * model * inner, bytes_accessed=24 * rows * inner, transcendentals=0
+        ),
+    )(normed, out_grad, gate_weight, out_weight, y_own, carry, coupled, entering, gain)
+
+
+def gate_back_kernel(
+    inner_total, per_micro, mixer, gate_in, grads, carry, coupled, sums, gain,
+    norm_out, gate_out, mixer_out, pull_out, gain_out,
+):
+    step = pl.program_id(0)
+    width = pull_out.shape[0]
+    inv_norm = lax.rsqrt(sums[:, 0:1] / inner_total + epsilon)
+    inner_dot = sums[:, 1:2] * (inv_norm * inv_norm * inv_norm) / inner_total
+    mixer_now, gate_now, grad_now = mixer[...], gate_in[...], grads[...]
+    sig = logistic(gate_now)
+    act = gate_now * sig
+    gated = mixer_now * act
+    norm_out[...] = (gated * inv_norm * gain[...]).astype(bf16)
+    gated_grad = grad_now * gain[...] * inv_norm - gated * inner_dot
+    gate_out[...] = (gated_grad * mixer_now * sig * (1.0 + gate_now * (1.0 - sig))).astype(bf16)
+    mixer_grad = gated_grad * act
+    mixer_out[...] = mixer_grad
+
+    @pl.when(step == 0)
+    def _():
+        gain_out[...] = jnp.zeros_like(gain_out)
+
+    gain_out[0:1, :] += jnp.sum(grad_now * gated * inv_norm, axis=0, keepdims=True)
+
+    @pl.when(lax.rem(step, per_micro) == 0)
+    def _():
+        pull_out[...] = jnp.zeros_like(pull_out)
+
+    turned = split_two(jnp.transpose(coupled[:, width:]))
+    pull_out[...] += mm_three(turned, split_two(carry[...] * mixer_grad))
+
+
+def gate_back_stage(mixer, gate_in, grads, carry, coupled, sums, gain, micros, inner_total):
+    rows, inner = mixer.shape
+    twice = coupled.shape[1]
+    width = twice // 2
+    per_micro = rows // micros // CHUNK
+
+    def block(lanes):
+        return pl.BlockSpec((CHUNK, lanes), lambda step: (step, 0))
+
+    return pl.pallas_call(
+        functools.partial(gate_back_kernel, inner_total, per_micro),
+        grid=(rows // CHUNK,),
+        in_specs=[
+            block(inner),
+            block(inner),
+            block(inner),
+            block(inner),
+            block(twice),
+            block(LANES),
+            pl.BlockSpec((1, inner), lambda step: (0, 0)),
+        ],
+        out_specs=[
+            block(inner),
+            block(inner),
+            block(inner),
+            pl.BlockSpec((None, width, inner), lambda step: (step // per_micro, 0, 0)),
+            pl.BlockSpec((8, inner), lambda step: (0, 0)),
+        ],
+        out_shape=[
+            jax.ShapeDtypeStruct((rows, inner), bf16),
+            jax.ShapeDtypeStruct((rows, inner), bf16),
+            jax.ShapeDtypeStruct((rows, inner), f32),
+            jax.ShapeDtypeStruct((micros, width, inner), f32),
+            jax.ShapeDtypeStruct((8, inner), f32),
+        ],
+        compiler_params=pltpu.CompilerParams(vmem_limit_bytes=48 * 1024 * 1024),
+        cost_estimate=pl.CostEstimate(
+            flops=8 * rows * width * inner, bytes_accessed=24 * rows * inner, transcendentals=0
+        ),
+    )(mixer, gate_in, grads, carry, coupled, sums, gain)
+
+
+def weave_kernel(first, second, out):
+    out[:, 0, :] = first[...]
+    out[:, 1, :] = second[...]
+
+
+def woven(first, second, columns):
+    rows = first.shape[0]
+    size = 32
+    block = pl.BlockSpec((size, columns), lambda step: (step, 0))
+    return pl.pallas_call(
+        weave_kernel,
+        grid=(rows // size,),
+        in_specs=[block, block],
+        out_specs=pl.BlockSpec((size, 2, columns), lambda step: (step, 0, 0)),
+        out_shape=jax.ShapeDtypeStruct((rows, 2, columns), first.dtype),
+    )(first, second)
 
 
 class Reduction:
@@ -994,7 +1236,7 @@
         exponent = jnp.ceil(jnp.log(peak) * 1.4426950408889634)
         factor = jnp.exp(exponent * -0.6931471805599453) * 32000.0
         out[place + (pl.ds(0, count), slice(None))] = (
-            jnp.round(value * factor).astype(jnp.int32).astype(jnp.int16)
+            (value * factor + 12582912.0 - 12582912.0).astype(jnp.int32).astype(jnp.int16)
         )
         out[place + (pl.ds(count, 16), slice(None))] = (
             jnp.broadcast_to(exponent, (16, LANES)).astype(jnp.int32).astype(jnp.int16)
@@ -1215,13 +1457,6 @@
     return results
 
 
-def chained(own, factor, steps):
-    arriving = passed_along(own, "context", steps)
-    for _ in range(lax.axis_size("context") - 2):
-        arriving = passed_along(factor * arriving + own, "context", steps)
-    return arriving
-
-
 def shards(
     tokens,
     lengths,
@@ -1241,7 +1476,6 @@
     skip_gain,
     inner_gain,
 ):
-    highest = lax.Precision.HIGHEST
     micros = tokens.shape[0]
     count = tokens.shape[2]
     model = tokens.shape[3]
@@ -1273,31 +1507,24 @@
         ],
         axis=1,
     )
-    shared_rows = max(shard_rows * 5 // 16 // 16 * 16, 16)
-    lead_full, gate_full, out_full, far = gather_weights(
-        [lead, in_weight[:, 0, :], jnp.transpose(out_weight)], tokens[:, 0], shared_rows, 1
-    )
+    def sharing(parts):
+        return max(shard_rows * parts // 16 // 16 * 16, 16)
+
+    lead_full, far = gather_weights([lead], tokens[:, 0], sharing(3), 1)
 
     near = tokens[:, 0].reshape(micros, own_blocks, block_len, model)
     far = far.reshape(micros, own_blocks, block_len, model)
-    everything = jnp.where(
-        place == 0, jnp.concatenate([near, far], 1), jnp.concatenate([far, near], 1)
-    )
     slots = jnp.arange(blocks_row, dtype=jnp.int32)
-    picked = []
-    for micro in range(micros):
-        for own in range(own_blocks):
-            wanted = place * own_blocks + own
-            slot = jnp.sum(jnp.where(block_order[micro, 0] == wanted, slots, 0))
-            picked.append(
-                lax.dynamic_slice(
-                    everything, (micro, slot, 0, 0), (1, 1, block_len, model)
-                ).reshape(block_len, model)
-            )
-    x_input = jnp.concatenate(picked, axis=0)
+    wanted = place * own_blocks + jnp.arange(own_blocks, dtype=jnp.int32)
+    found = block_order[:, 0, None, :] == wanted[None, :, None]
+    slot = jnp.sum(jnp.where(found, slots, 0), axis=2).reshape(-1)
+    is_near = (slot // own_blocks == place).astype(jnp.int32)
+    inside = slot % own_blocks
+    x_input, normed, scales = ordered(
+        near, far, inside * is_near, inside * (1 - is_near), is_near, norm_gain.reshape(1, model)
+    )
     x_float = x_input.astype(f32)
-    inv_rms = lax.rsqrt(jnp.mean(x_float * x_float, axis=-1, keepdims=True) + epsilon)
-    normed = (x_float * inv_rms * norm_gain).astype(bf16)
+    inv_rms = scales[:, :1]
 
     first_end = lengths[:, 0, 0]
     second_end = first_end + lengths[:, 0, 1]
@@ -1313,7 +1540,9 @@
     ccw, ccb = coupling_conv, coupling_bias.reshape(1, twice)
     sbias = jnp.pad(step_bias, (0, LANES - heads)).reshape(1, LANES)
     rate = jnp.pad(decay_rate, (0, LANES - heads)).reshape(1, LANES)
-    skip = jnp.repeat(skip_gain, head_size).reshape(1, inner)
+    skip = jnp.dot(
+        skip_gain.reshape(1, heads), jnp.asarray(narrow[:heads], f32), precision=lax.Precision.HIGHEST
+    )
 
     raw = jnp.dot(normed, lead_full, preferred_element_type=f32)
     rims = passed_along(
@@ -1321,66 +1550,36 @@
         "context",
         1,
     )
-    chunk_count = count // CHUNK
-    written, finals, entering = (), [], []
-    for micro in range(micros):
-        y_own, states, final, coupled, carry, reach = forward_ssd(
-            marks[micro], micro, micros, written, raw, rims[micro], inner, twice, count,
-            cw, cb, ccw, ccb, sbias, rate, skip, sel, selcol,
-        )
-        written = (y_own, states, coupled, carry, reach)
-        finals.append(final)
-        entering.append(chained(final, reach[micro, chunk_count], 1))
-    entering = jnp.stack(entering)
-    coupled_c = coupled[:, width:].reshape(micros, count, width)
-    gate_in = jnp.dot(normed, gate_full, preferred_element_type=f32)
+    (y_own, states, finals, coupled, carry, reach, entering, gate_full, out_full) = forward_ssd(
+        jnp.stack(marks), micros, raw, rims, inner, twice, count,
+        cw, cb, ccw, ccb, sbias, rate, skip, sel, selcol,
+        [in_weight[:, 0, :], jnp.transpose(out_weight)], sharing(4), 3,
+    )
+    entering = jnp.where(place == 0, 0.0, entering)
     cot = cotangent[:, 0].reshape(micros * count, model)
     out_grad = cot * keep.astype(bf16)
-    norm_grad = jnp.dot(out_grad, out_full, preferred_element_type=f32)
-
-    arrived = jnp.concatenate(
-        [jnp.dot(coupled_c[micro], entering[micro], precision=highest) for micro in range(micros)],
-        axis=0,
-    )
-    mixer = y_own + carry * arrived
-    gate_sig = jax.nn.sigmoid(gate_in)
-    gate_act = gate_in * gate_sig
-    gated = mixer * gate_act
-    scaled_grad = norm_grad * inner_gain
-    row_sums = jnp.stack([jnp.sum(gated * gated, axis=-1), jnp.sum(scaled_grad * gated, axis=-1)])
+    gain_row = inner_gain.reshape(1, inner)
+    mixer, gate_in, norm_grad, row_sums = gate_stage(
+        normed, out_grad, gate_full, out_full, y_own, carry, coupled, entering, gain_row
+    )
     row_sums = row_sums + paired(row_sums, "tensor")
-    inv_norm = lax.rsqrt(row_sums[0] / inner_total + epsilon)[:, None]
-    inner_dot = row_sums[1][:, None]
-    gated_norm = (gated * inv_norm * inner_gain).astype(bf16)
-    inner_gain_grad = jnp.sum(norm_grad * gated * inv_norm, axis=0)
-    gated_grad = scaled_grad * inv_norm - gated * (inner_dot * inv_norm**3 / inner_total)
-    gate_grad = (gated_grad * mixer * gate_sig * (1.0 + gate_in * (1.0 - gate_sig))).astype(bf16)
-    mixer_grad = gated_grad * gate_act
-
+    gated_norm, gate_grad, mixer_grad, own_pulls, inner_gain_rows = gate_back_stage(
+        mixer, gate_in, norm_grad, carry, coupled, row_sums, gain_row, micros, inner_total
+    )
+    pulled = passed_along(own_pulls, "context", -1)
     out_term = contract_rows(out_grad, gated_norm)
     gate_term = contract_rows(normed, gate_grad)
-    pulled = []
-    for micro in range(micros):
-        part = slice(micro * count, (micro + 1) * count)
-        own_pull = lax.dot_general(
-            coupled_c[micro],
-            carry[part] * mixer_grad[part],
-            (((0,), (0,)), ((), ())),
-            precision=highest,
-        )
-        pulled.append(chained(own_pull, reach[micro, chunk_count], -1))
-
     branch = contract_cols(gated_norm, out_full)
-    branch = branch + paired(branch, "tensor")
-    block_out = (x_float + keep * branch).astype(bf16)
+    gate_part = contract_cols(gate_grad, gate_full)
+    branch_other = paired(branch, "tensor")
 
     (
         lead_grad, tails, rims_grad, coupling_raw_grad, coupling_rims_grad,
         value_sums, coupling_sums, small_sums, skip_sums, out_shard, gate_shard,
     ) = backward_ssd(
         jnp.stack(marks), micros, raw, rims, inner, twice, count, mixer_grad, mixer, states,
-        jnp.stack(finals), entering, reach, jnp.stack(pulled),
-        cw, cb, ccw, ccb, sbias, rate, skip, sel, selcol, selt, [out_term, gate_term], 2,
+        finals, entering, reach, pulled,
+        cw, cb, ccw, ccb, sbias, rate, skip, sel, selcol, selt, [out_term, gate_term], [branch, gate_part], 2,
     )
     edges = passed_along(jnp.concatenate([rims_grad, coupling_rims_grad], axis=2), "context", -1)
     coupling_raw_grad = coupling_raw_grad.reshape(micros, count, twice) + jnp.pad(
@@ -1396,8 +1595,9 @@
         lead_grad = lax.dynamic_update_slice(
             lead_grad, tails[micro], ((micro + 1) * count - 8, 0)
         )
-    (lead_shard,) = reduce_terms([contract_rows(normed, lead_grad)], 2, 3)
-    normed_part = contract_cols(gate_grad, gate_full) + contract_cols(lead_grad, lead_full)
+    (lead_shard,) = reduce_terms([contract_rows(normed, lead_grad)], 2, 4)
+    normed_part = gate_part + contract_cols(lead_grad, lead_full)
+    block_out = (x_float + keep * (branch + branch_other)).astype(bf16)
     normed_grad = normed_part + paired(normed_part, "tensor")
     x_hat = x_float * inv_rms
     hat_grad = normed_grad * norm_gain
@@ -1410,7 +1610,7 @@
     skip_sums = skip_sums[0].reshape(heads, head_size).sum(axis=1)
     coupling_sums = coupling_sums + paired(coupling_sums, "tensor")
     (value_all, coupling_all, small_all, skip_all, inner_all, norm_all) = summed_everywhere(
-        [value_sums[:5], coupling_sums[:5], small_sums[:2], skip_sums, inner_gain_grad, norm_gain_grad]
+        [value_sums[:5], coupling_sums[:5], small_sums[:2], skip_sums, inner_gain_rows[0], norm_gain_grad]
     )
     coupling_shard = lead_shard[:, inner : inner + twice]
     coupling_shard = coupling_shard + paired(coupling_shard, "tensor")
@@ -1418,7 +1618,7 @@
         block_out.reshape(micros, 1, count, model),
         input_grad.reshape(micros, 1, count, model),
         norm_all,
-        jnp.stack([gate_shard, lead_shard[:, :inner]], axis=1),
+        woven(gate_shard, lead_shard, inner),
         coupling_shard,
         lead_shard[:, inner + twice : inner + twice + heads],
         jnp.transpose(out_shard),

time: 931 us -> 861 us (0.925)
  Pallas kernels: 553 us -> 602 us
  other arithmetic: 92.2 us -> 44.3 us
  matrix products: 148 us -> 116 us
  between operations: 17.2 us -> 1.83 us
  waiting for transfers between devices: 46.7 us -> 37.3 us
    pallas_call x4 -> x7, Pallas kernels: 444 us -> 492 us  [the longest x1 176 us: backward_ssd(): pl.pallas_call(functools.partial(backward_kernel, heads, chunks, plan, le...]
    dot_general x6 -> x1, matrix products: 41.7 us -> 0.26 us  [shards(): jnp.dot(skip_gain.reshape(1, heads), jnp.asarray(narrow[:heads], f32), pr...]
    ppermute x6 -> x3, waiting for transfers between devices: 39.1 us -> 18.4 us  [passed_along(): lax.ppermute(value, axis, [(source, source + steps) for source in range(i...]
    mul x1 -> x2, other arithmetic: 16.3 us -> 0.02 us  [the longest x1 0.02 us: shards(): inside * (1 - is_near)]
    reduce_sum x3 -> x1, other arithmetic: 16.8 us -> 0.86 us  [shards(): slot = jnp.sum(jnp.where(found, slots, 0), axis=2).reshape(-1)]
    another operation x6 -> x0, other arithmetic: 15.4 us -> none  [the longest x1 4.88 us: shards(): jnp.stack([gate_shard, lead_shard[:, :inner]], axis=1)]
    ppermute x6, waiting for transfers between devices: 1.43 us -> 12.5 us  [paired(): lax.ppermute(value, axis, [(source, source ^ 1) for source in range(count)])]
    dot_general x3, matrix products: 47.3 us -> 57 us  [contract_cols(): lax.dot_general(left, right, (((1,), (1,)), ((), ())), preferred_element_...]
  transfers between devices with their start and end apart: 16 -> 13, of which waited for: 6 -> 7; matrix products, arithmetic and copies ran while one was open for 20% -> 13% of each run, Pallas kernels for 12% -> 14%
where the time goes in v4:
time: 861 us; the launch traced here: 854 us
  Pallas kernels  602 us (70%)
  matrix products  116 us (13%)
  other arithmetic  44.3 us (5%)
  local copies, waits for them, and re-layouts  43.3 us (5%)
  waiting for transfers between devices  37.3 us (4%)
  starting transfers between devices  9.82 us (1%)
    pallas_call x1, Pallas kernels, backward_ssd(): pl.pallas_call(functools.partial(backward_kernel, heads, chunks, plan, le...  176 us
    pallas_call x1, Pallas kernels, forward_ssd(): pl.pallas_call(functools.partial(forward_kernel, heads, chunks, plan), gr...  145 us
    pallas_call x1, Pallas kernels, reduce_terms(): pl.pallas_call(functools.partial(reduce_kernel, plan, arrays), out_shape=...  110 us
    pallas_call x1, Pallas kernels, gather_weights(): pl.pallas_call(functools.partial(gather_kernel, plan), out_shape=[jax.Sha...  102 us
    dot_general x3, matrix products, contract_cols(): lax.dot_general(left, right, (((1,), (1,)), ((), ())), preferred_element_...  57 us
    dot_general x3, matrix products, contract_rows(): lax.dot_general(left, right, (((0,), (0,)), ((), ())), preferred_element_...  41.3 us
    pallas_call x1, Pallas kernels, gate_stage(): pl.pallas_call(gate_kernel, grid=(rows // size,), in_specs=[block(model),...  35.2 us
    pallas_call x1, Pallas kernels, gate_back_stage(): pl.pallas_call(functools.partial(gate_back_kernel, inner_total, per_micro...  23.8 us
  transfers between devices with their start and end apart: 13, of which 7 were waited for; matrix products, arithmetic and copies ran while one was open for 13% of the time, Pallas kernels for 14%

profile of v4, /device:TPU:0, one launch (start us, length us, event | category | flops | bytes accessed | tf_op | source)
XLA Modules:
  0.0 854.3 jit_solution(2959271231627180285)
XLA Ops:
  2.5 6.6 fusion.24
  9.7 1.1 fusion.13.refs_0_
  10.8 101.9 %shard_map.316 = (bf16[2048,2432]{1,0:T(8,128)(2,1)}, bf16[2,512,2048]{2,1,0:T(8,128)(2,1)}) custom-call(bf16[256,2432]{1,0:T(8,128)(2,1)} %fusion.13.refs_0_, bf16[2,512,2048]{2,1,0:T(8,128)(2,1)} %bitcast.100), custom_call_target="tpu_custom_call" | custom-call | tf_op jit(solution)/shard_map/pallas_call | solution.py:890
  112.7 2.2 copy-done.3
  114.9 2.2 copy-done.5
  117.1 3.2 shard_map.317
  120.3 17.2 %fusion.28.refs_1_.refs_2_.refs_4_.refs_5_.refs_7_ = f32[1024,2432]{1,0:T(8,128)S(1)} fusion(bf16[1024,2048]{1,0:T(8,128)(2,1)S(1)} %get-tuple-element.51.normed, bf16[2048,2432]{1,0:T(8,128)(2,1)} %get-tuple-element.52), kind=kOutput, calls=%fused_computation.80 | convolution fusion | flops 10200547328 | bytes 24117248 | tf_op jit(solution)/shard_map/dot_general | solution.py:1547
  137.6 3.7 copy-done.26
  141.3 2.7 collective-permute-start
  145.1 1.3 fusion.18
  147.1 4.6 bitcast_multiply_fusion.out_grad
  152.0 2.7 add_bitcast_fusion
  154.7 2.2 copy.69
  156.9 1.5 copy.57
  158.5 1.0 copy-done.7
  159.6 144.9 %shard_map.318 = (f32[1024,2048]{1,0:T(8,128)}, f32[8,128,2048]{2,1,0:T(8,128)}, f32[2,128,2048]{2,1,0:T(8,128)}, f32[1024,256]{1,0:T(8,128)S(1)}, f32[1024,2048...) custom-call(s32[2,3]{1,0:T(2,128)S(1)} %pad_add_fusion.1.refs_0_, ...), custom_call_target="tpu_custom_call" | custom-call | tf_op jit(solution)/shard_map/pallas_call | solution.py:308
  304.5 1.0 copy-done.8
  306.1 1.5 broadcast_select_fusion.entering.refs_13_
  307.7 35.2 %shard_map.319 = (f32[1024,2048]{1,0:T(8,128)}, f32[1024,2048]{1,0:T(8,128)}, f32[1024,2048]{1,0:T(8,128)}, f32[1024,128]{1,0:T(8,128)}) custom-call(bf16[1024,2048]{1,0:T(8,128)(2,1)} %copy-done.24, bf16[1024,2048]{1,0:T(8,128)(2,1)} %bitcast_multiply_fusion.out_grad, bf16[2048,2048]{1,0:T(8,128)(2,1)} %get-tuple-element.53.gate_weight, ...), custom_call_target="tpu_custom_call" | custom-call | flops 17179869184 | bytes 50331648 | tf_op jit(solution)/shard_map/pallas_call | solution.py:976
  343.0 6.6 copy.64
  349.6 23.8 %shard_map.320 = (bf16[1024,2048]{1,0:T(8,128)(2,1)}, bf16[1024,2048]{1,0:T(8,128)(2,1)}, f32[1024,2048]{1,0:T(8,128)}, f32[2,128,2048]{2,1,0:T(8,128)S(1)}, f32[8,2048]{1,0:T(8,128)S(1)}) custom-call(f32[1024,2048]{1,0:T(8,128)} %get-tuple-element.59.mixer.refs_9_, f32[1024,2048]{1,0:T(8,128)} %get-tuple-element.60.gate_in, ...), custom_call_target="tpu_custom_call" | custom-call | flops 2147483648 | bytes 50331648 | tf_op jit(solution)/shard_map/pallas_call | solution.py:1041
  373.5 24.9 %fusion.30.refs_29_ = f32[1024,2048]{1,0:T(8,128)} fusion(bf16[1024,2048]{1,0:T(8,128)(2,1)} %get-tuple-element.65, bf16[2048,2048]{1,0:T(8,128)(2,1)S(1)} %bitcast.128), kind=kOutput, calls=%fused_computation.82 | convolution fusion | flops 8589934592 | bytes 20971520 | tf_op jit(solution)/shard_map/dot_general | solution.py:1643
  398.4 1.3 collective-permute-start.3
  399.7 13.5 %fusion.29.refs_28_ = f32[1024,2048]{1,0:T(8,128)} fusion(bf16[1024,2048]{1,0:T(8,128)(2,1)S(1)} %copy-done.41, bf16[2048,2048]{1,0:T(8,128)(2,1)} %get-tuple-element.54.out_weight), kind=kOutput, calls=%fused_computation.81 | convolution fusion | flops 8589934592 | bytes 20971520 | tf_op jit(solution)/shard_map/dot_general | solution.py:1643
  413.2 11.4 %fusion.10.refs_26_ = f32[4,2,256,2048]{3,2,1,0:T(8,128)} fusion(bf16[4,2,256,1024]{3,2,1,0:T(8,128)(2,1)S(1)} %bitcast.118, bf16[1024,2048]{1,0:T(8,128)(2,1)S(1)} %copy-done.41), kind=kOutput, calls=%fused_computation.12 | convolution fusion | flops 8589934592 | bytes 25165824 | tf_op jit(solution)/shard_map/dot_general | solution.py:1637
  424.7 11.8 %fusion.31 = f32[2048,2048]{1,0:T(8,128)} fusion(bf16[1024,2048]{1,0:T(8,128)(2,1)S(1)} %copy-done.25, bf16[1024,2048]{1,0:T(8,128)(2,1)S(1)} %copy-done.40), kind=kOutput, calls=%fused_computation.83 | convolution fusion | flops 8589934592 | bytes 25165824 | tf_op jit(solution)/shard_map/dot_general | solution.py:1637
  436.5 12.7 %collective-permute-done.3.refs_15_ = f32[2,128,2048]{2,1,0:T(8,128)S(1)} collective-permute-done((f32[2,128,2048]{2,1,0:T(8,128)S(1)}, f32[2,128,2048]{2,1,0:T(8,128)S(1)}, u32[]{:S(2)}, u32[]{:S(2)}) %collective-permute-start.3) | collective-permute-done | bytes 2097184 | tf_op jit(solution)/shard_map/ppermute | solution.py:1423
  449.2 1.3 copy-done.29
  450.5 176.4 %shard_map.321 = (bf16[1024,2432]{1,0:T(8,128)(2,1)}, f32[2,8,2048]{2,1,0:T(8,128)}, f32[2,8,2048]{2,1,0:T(8,128)}, f32[1024,256]{1,0:T(8,128)}, f32[2,8,256]{2,...) custom-call(s32[2,3]{1,0:T(2,128)} %copy-done.19, ...), custom_call_target="tpu_custom_call" | custom-call | tf_op jit(solution)/shard_map/pallas_call | solution.py:652
  626.9 0.9 pad_maximum_fusion.1
  627.9 1.3 collective-permute-start.4
  629.2 5.7 collective-permute-done.4
  634.9 1.3 pad_add_fusion
  637.2 1.7 collective-permute-done.5
  641.2 18.6 %convolution_add_fusion = f32[1024,2048]{1,0:T(8,128)} fusion(f32[1024,2048]{1,0:T(8,128)} %fusion.30.refs_29_, bf16[1024,2432]{1,0:T(8,128)(2,1)} %fusion.16, bf16[2048,2432]{1,0:T(8,128)(2,1)} %get-tuple-element.52), kind=kOutput, calls=%fused_computation.15 | convolution fusion | flops 10202644480 | bytes 31719424 | tf_op jit(solution)/shard_map/dot_general | solution.py:1643
  662.5 6.6 collective-permute-done.7
  669.1 4.2 collective-permute-done.6
  673.3 8.5 fusion.8
  682.0 18.1 %fusion.32 = f32[2048,2432]{1,0:T(8,128)} fusion(bf16[1024,2048]{1,0:T(8,128)(2,1)} %copy-done.24, bf16[1024,2432]{1,0:T(8,128)(2,1)} %fusion.16), kind=kOutput, calls=%fused_computation.84 | convolution fusion | flops 10200547328 | bytes 29097984 | tf_op jit(solution)/shard_map/dot_general | solution.py:1637
  700.0 109.6 %shard_map.322.second = f32[256,2432]{1,0:T(8,128)} custom-call(f32[4,2,256,2432]{3,2,1,0:T(8,128)} %bitcast.112), custom_call_target="tpu_custom_call" | custom-call | tf_op jit(solution)/shard_map/pallas_call | solution.py:1408
  809.6 1.0 slice.154
  810.7 1.8 copy.62
  812.5 7.1 shard_map.323
  821.7 3.2 collective-permute-done.9
  824.9 1.2 collective-permute-start.10
  826.1 3.1 collective-permute-done.10
  829.2 1.8 collective-permute-start.11
  831.0 18.7 %fusion.7 = (bf16[1024,2048]{1,0:T(8,128)(2,1)}, bf16[1024,2048]{1,0:T(8,128)(2,1)}) fusion(bf16[1024,2048]{1,0:T(8,128)(2,1)} %copy-done.2, bf16[2,1,512,2048]{3,2,1,0:T(8,128)(2,1)} %param.24, f32[1024]{0:T(1024)S(1)} %broadcast_multiply_fusion, f32[2048]{0:T(1024)S(1)} %copy-done.15, f32[1024]{0:T(1024)S(1)} %slice_reduce_fusion, ...), kind=kLoop, calls=%fused_computation.9 | loop fusion | flops 29360128 | bytes 50352128 | tf_op jit(solution)/shard_map/convert_element_type | solution.py:1607
  (150 shorter events, 17.7 us)
Async XLA Ops:
  0.6 151.1 %copy-start = (f32[32]{0:T(128)S(1)}, f32[32]{0:T(128)}, u32[]{:S(2)}) copy-start(f32[32]{0:T(128)} %param.36) | copy-start | bytes 388
  2.5 7.2 copy-start.33
  9.1 103.6 %copy-start.14 = (f32[2048]{0:T(1024)S(1)}, f32[2048]{0:T(1024)}, u32[]{:S(2)}) copy-start(f32[2048]{0:T(1024)} %param.25) | copy-start | bytes 24580
  120.2 17.3 %copy-start.2 = (bf16[1024,2048]{1,0:T(8,128)(2,1)}, bf16[1024,2048]{1,0:T(8,128)(2,1)S(1)}, u32[]{:S(2)}) copy-start(bf16[1024,2048]{1,0:T(8,128)(2,1)S(1)} %get-tuple-element.50) | copy-start | bytes 12582916
  120.3 17.3 %copy-start.10 = (f32[1024,128]{1,0:T(8,128)}, f32[1024,128]{1,0:T(8,128)S(1)}, u32[]{:S(2)}) copy-start(f32[1024,128]{1,0:T(8,128)S(1)} %get-tuple-element.64) | copy-start | bytes 1572868
  120.3 17.3 %copy-start.24 = (bf16[1024,2048]{1,0:T(8,128)(2,1)}, bf16[1024,2048]{1,0:T(8,128)(2,1)S(1)}, u32[]{:S(2)}) copy-start(bf16[1024,2048]{1,0:T(8,128)(2,1)S(1)} %get-tuple-element.51.normed) | copy-start | bytes 12582916
  120.3 23.7 %copy-start.36 = (s32[2,1,2]{2,1,0:T(1,128)S(1)}, s32[2,1,2]{2,1,0:T(1,128)}, u32[]{:S(2)}) copy-start(s32[2,1,2]{2,1,0:T(1,128)} %param.22) | copy-start | bytes 52
  137.5 14.2 %copy-start.32 = (f32[32,2048]{1,0:T(8,128)S(1)}, f32[32,2048]{1,0:T(8,128)}, u32[]{:S(2)}) copy-start(f32[32,2048]{1,0:T(8,128)} %constant.79.clone) | copy-start | bytes 786436
  141.3 17.1 %collective-permute-start = (f32[2,8,2432]{2,1,0:T(8,128)S(1)}, f32[2,8,2432]{2,1,0:T(8,128)S(1)}, u32[]{:S(2)}, u32[]{:S(2)}) collective-permute-start(f32[2,8,2432]{2,1,0:T(8,128)S(1)} %pad_maximum_fusion), channel_id=1, source_target_pairs={{0,2},{1,3},{4,6},{5,7},{8,10},{9,11},{12,14},{13,15},{16,18},{17,... | collective-permute-start | bytes 466952 | tf_op jit(solution)/shard_map/ppermute | solution.py:1423
  147.0 11.3 %copy-start.38 = (f32[32]{0:T(128)S(1)}, f32[32]{0:T(128)}, u32[]{:S(2)}) copy-start(f32[32]{0:T(128)} %param.35) | copy-start | bytes 388
  147.0 11.4 %copy-start.39 = (f32[32]{0:T(128)S(1)}, f32[32]{0:T(128)}, u32[]{:S(2)}) copy-start(f32[32]{0:T(128)} %param.34) | copy-start | bytes 388
  147.0 11.4 %copy-start.4 = (bf16[128,4096]{1,0:T(8,128)(2,1)S(1)}, bf16[128,4096]{1,0:T(8,128)(2,1)}, u32[]{:S(2)}) copy-start(bf16[128,4096]{1,0:T(8,128)(2,1)} %constant.77.clone.refs_16_.refs_24_) | copy-start | bytes 3145732
  147.0 11.4 %copy-start.13 = (f32[4,2048]{1,0:T(4,128)S(1)}, f32[4,2048]{1,0:T(4,128)}, u32[]{:S(2)}) copy-start(f32[4,2048]{1,0:T(4,128)} %refs_16_.2) | copy-start | bytes 98308
  147.0 11.4 %copy-start.17 = (f32[2048]{0:T(1024)S(1)}, f32[2048]{0:T(1024)}, u32[]{:S(2)}) copy-start(f32[2048]{0:T(1024)} %param.31) | copy-start | bytes 24580
  147.0 11.4 %copy-start.18 = (f32[4,256]{1,0:T(4,128)S(1)}, f32[4,256]{1,0:T(4,128)}, u32[]{:S(2)}) copy-start(f32[4,256]{1,0:T(4,128)} %refs_18_.1) | copy-start | bytes 12292
  147.1 11.4 %copy-start.23 = (f32[256]{0:T(256)S(1)}, f32[256]{0:T(256)}, u32[]{:S(2)}) copy-start(f32[256]{0:T(256)} %param.33) | copy-start | bytes 3076
  152.0 152.5 %copy-start.16 = (f32[1,2048]{1,0:T(1,128)}, f32[1,2048]{1,0:T(1,128)S(1)}, u32[]{:S(2)}) copy-start(f32[1,2048]{1,0:T(1,128)S(1)} %fusion.21.refs_14_.refs_22_) | copy-start | bytes 24580
  154.7 149.8 %copy-start.19 = (s32[2,3]{1,0:T(2,128)}, s32[2,3]{1,0:T(2,128)S(1)}, u32[]{:S(2)}) copy-start(s32[2,3]{1,0:T(2,128)S(1)} %pad_add_fusion.1.refs_0_) | copy-start | bytes 76
  158.4 146.1 %copy-start.21 = (f32[1,128]{1,0:T(1,128)}, f32[1,128]{1,0:T(1,128)S(1)}, u32[]{:S(2)}) copy-start(f32[1,128]{1,0:T(1,128)S(1)} %get-tuple-element.154.refs_13_.refs_21_) | copy-start | bytes 1540
  158.4 146.1 %copy-start.22 = (f32[1,128]{1,0:T(1,128)}, f32[1,128]{1,0:T(1,128)S(1)}, u32[]{:S(2)}) copy-start(f32[1,128]{1,0:T(1,128)S(1)} %get-tuple-element.155.refs_12_.refs_20_) | copy-start | bytes 1540
  158.4 146.1 %copy-start.6 = (f32[2,8,2432]{2,1,0:T(8,128)}, f32[2,8,2432]{2,1,0:T(8,128)S(1)}, u32[]{:S(2)}) copy-start(f32[2,8,2432]{2,1,0:T(8,128)S(1)} %collective-permute-done.refs_3_.refs_6_) | copy-start | bytes 466948
  342.9 6.7 collective-permute-start.1
  349.5 24.0 %slice-start.1 = ((s8[8388608]{0:T(1024)(128)(4,1)}), s8[4194304]{0:T(1024)(128)(4,1)S(1)}, s32[]{:S(2)}) async-start(s8[8388608]{0:T(1024)(128)(4,1)} %bitcast.127), calls=%async_computation.1 | async-start | bytes 8388608
  349.6 23.9 %slice-start.2 = ((s8[8388608]{0:T(1024)(128)(4,1)}), s8[4194304]{0:T(1024)(128)(4,1)S(1)}, s32[]{:S(2)}) async-start(s8[8388608]{0:T(1024)(128)(4,1)} %bitcast.127), calls=%async_computation.2 | async-start | bytes 8388608
  373.5 26.2 %copy-start.41 = (bf16[1024,2048]{1,0:T(8,128)(2,1)S(1)}, bf16[1024,2048]{1,0:T(8,128)(2,1)}, u32[]{:S(2)}) copy-start(bf16[1024,2048]{1,0:T(8,128)(2,1)} %get-tuple-element.63) | copy-start | bytes 12582916
  398.4 50.7 %collective-permute-start.3 = (f32[2,128,2048]{2,1,0:T(8,128)S(1)}, f32[2,128,2048]{2,1,0:T(8,128)S(1)}, u32[]{:S(2)}, u32[]{:S(2)}) collective-permute-start(f32[2,128,2048]{2,1,0:T(8,128)S(1)} %get-tuple-element.70), channel_id=1, source_target_pairs={{2,0},{3,1},{6,4},{7,5},{10,8},{11,9},{14,12},{15,13},{18,16},{19,... | collective-permute-start | bytes 6291464 | tf_op jit(solution)/shard_map/ppermute | solution.py:1423
  399.7 13.5 %copy-start.28 = (bf16[2048,1024]{1,0:T(8,128)(2,1)S(1)}, bf16[2048,1024]{1,0:T(8,128)(2,1)}, u32[]{:S(2)}) copy-start(bf16[2048,1024]{1,0:T(8,128)(2,1)} %copy.64) | copy-start | bytes 12582916
  413.2 11.4 %copy-start.25 = (bf16[1024,2048]{1,0:T(8,128)(2,1)S(1)}, bf16[1024,2048]{1,0:T(8,128)(2,1)}, u32[]{:S(2)}) copy-start(bf16[1024,2048]{1,0:T(8,128)(2,1)} %copy-done.24) | copy-start | bytes 12582916
  413.2 11.4 %copy-start.40 = (bf16[1024,2048]{1,0:T(8,128)(2,1)S(1)}, bf16[1024,2048]{1,0:T(8,128)(2,1)}, u32[]{:S(2)}) copy-start(bf16[1024,2048]{1,0:T(8,128)(2,1)} %get-tuple-element.65) | copy-start | bytes 12582916
  627.9 7.0 collective-permute-start.4
  636.2 2.7 collective-permute-start.5
  641.2 19.1 %copy-start.11 = (f32[1024,128]{1,0:T(8,128)S(1)}, f32[1024,128]{1,0:T(8,128)}, u32[]{:S(2)}) copy-start(f32[1024,128]{1,0:T(8,128)} %copy-done.10) | copy-start | bytes 1572868
  641.2 19.3 %copy-start.37 = (f32[8,256]{1,0:T(8,128)S(1)}, f32[8,256]{1,0:T(8,128)}, u32[]{:S(2)}) copy-start(f32[8,256]{1,0:T(8,128)} %get-tuple-element.77) | copy-start | bytes 24580
  641.2 21.1 %copy-start.34 = (f32[8,2048]{1,0:T(8,128)S(1)}, f32[8,2048]{1,0:T(8,128)}, u32[]{:S(2)}) copy-start(f32[8,2048]{1,0:T(8,128)} %get-tuple-element.76) | copy-start | bytes 196612
  641.2 32.1 %copy-start.15 = (f32[2048]{0:T(1024)S(1)}, f32[2048]{0:T(1024)}, u32[]{:S(2)}) copy-start(f32[2048]{0:T(1024)} %param.25) | copy-start | bytes 24580
  659.8 13.5 %collective-permute-start.6 = (f32[1024,2048]{1,0:T(8,128)}, f32[1024,2048]{1,0:T(8,128)}, u32[]{:S(2)}, u32[]{:S(2)}) collective-permute-start(f32[1024,2048]{1,0:T(8,128)} %convolution_add_fusion), channel_id=1, source_target_pairs={{0,1},{1,0},{2,3},{3,2},{4,5},{5,4},{6,7},{7,6},{8,9},{9,8},{10,11... | collective-permute-start | bytes 25165832 | tf_op jit(solution)/shard_map/ppermute | solution.py:1428
  659.9 171.1 %collective-permute-start.2 = (f32[1024,2048]{1,0:T(8,128)}, f32[1024,2048]{1,0:T(8,128)}, u32[]{:S(2)}, u32[]{:S(2)}) collective-permute-start(f32[1024,2048]{1,0:T(8,128)} %fusion.29.refs_28_), channel_id=1, source_target_pairs={{0,1},{1,0},{2,3},{3,2},{4,5},{5,4},{6,7},{7,6},{8,9},{9,8},{10,11... | collective-permute-start | bytes 25165832 | tf_op jit(solution)/shard_map/ppermute | solution.py:1428
  660.5 8.5 collective-permute-start.7
  681.9 138.4 %collective-permute-start.8 = (f32[128,128]{1,0:T(8,128)S(1)}, f32[128,128]{1,0:T(8,128)S(1)}, u32[]{:S(2)}, u32[]{:S(2)}) collective-permute-start(f32[128,128]{1,0:T(8,128)S(1)} %pad_bitcast_fusion), channel_id=1, source_target_pairs={{0,2},{2,0},{1,3},{3,1},{4,6},{6,4},{5,7},{7,5},{8,10},{10,8},{9,1... | collective-permute-start | bytes 196616 | tf_op jit(solution)/shard_map/ppermute | solution.py:1448
  700.0 110.6 %copy-start.30 = (f32[256,2048]{1,0:T(8,128)S(1)}, f32[256,2048]{1,0:T(8,128)}, u32[]{:S(2)}) copy-start(f32[256,2048]{1,0:T(8,128)} %get-tuple-element.82) | copy-start | bytes 6291460
  810.6 10.3 %collective-permute-start.12 = (f32[256,256]{1,0:T(8,128)S(1)}, f32[256,256]{1,0:T(8,128)S(1)}, u32[]{:S(2)}, u32[]{:S(2)}) collective-permute-start(f32[256,256]{1,0:T(8,128)S(1)} %slice.154), channel_id=1, source_target_pairs={{0,1},{1,0},{2,3},{3,2},{4,5},{5,4},{6,7},{7,6},{8,9},{9,8},{10,11... | collective-permute-start | bytes 786440 | tf_op jit(solution)/shard_map/ppermute | solution.py:1428
  812.5 7.1 slice-start
  812.5 8.4 copy-start.27
  812.5 18.5 %copy-start.35 = (f32[1024]{0:T(1024)S(1)}, f32[1024]{0:T(1024)}, u32[]{:S(2)}) copy-start(f32[1024]{0:T(1024)} %get-tuple-element.144) | copy-start | bytes 12292
  820.3 4.5 collective-permute-start.9
  824.9 4.3 collective-permute-start.10
  829.2 20.5 %collective-permute-start.11 = (f32[128,128]{1,0:T(8,128)S(1)}, f32[128,128]{1,0:T(8,128)S(1)}, u32[]{:S(2)}, u32[]{:S(2)}) collective-permute-start(f32[128,128]{1,0:T(8,128)S(1)} %add.111), channel_id=1, source_target_pairs={{0,16},{4,20},{8,24},{12,28},{16,0},{20,4},{24,8},{28,12},{1,17},{... | collective-permute-start | bytes 196616 | tf_op jit(solution)/shard_map/ppermute | solution.py:1448
  831.0 22.8 %copy-start.1 = (f32[32]{0:T(128)S(1)}, f32[32]{0:T(128)}, u32[]{:S(2)}) copy-start(f32[32]{0:T(128)} %param.36) | copy-start | bytes 388
  (10 other events, 32.2 us)

commit v5 on v4

--- a/solution.py
+++ b/solution.py
@@ -135,8 +135,10 @@
     chunk = lax.rem(grid_step, chunks)
     micro = grid_step // chunks
     width = state.shape[0]
-    early = {0: range(0, arrays), 3: range(arrays, arrays + 1), 5: range(arrays + 1, arrays + 2)}
-    placed = max(early[5])
+    early = {0: range(2)}
+    for when in range(1, min(2 * chunks - 1, len(plan.order) - 1)):
+        early[when] = [when + 1]
+    placed = len(early)
 
     def leave_copy(which):
         return pltpu.make_async_remote_copy(
@@ -287,7 +289,7 @@
     eighth = CHUNK // 8
     pairs = lax.axis_size("fsdp") // 2
     shard_rows = shards[0].shape[0]
-    plan = Gathering(shard_rows, pairs, len(shards), shared)
+    plan = Gathering(shard_rows, pairs, [shard.shape[1] for shard in shards], 2, shared)
 
     def part(count, start):
         return pl.BlockSpec((CHUNK, count), lambda step: (step, start // count))
@@ -736,14 +738,25 @@
 
 
 class Gathering:
-    def __init__(self, rows, pairs, arrays, shared):
-        self.rows, self.pairs, self.arrays, self.shared = rows, pairs, arrays, shared
+    def __init__(self, rows, pairs, widths, cuts, shared):
+        self.rows, self.pairs, self.shared = rows, pairs, shared
+        self.arrays = len(widths)
+        self.pieces = []
+        for array, width in enumerate(widths):
+            size = -(-width // LANES // cuts) * LANES
+            self.pieces += [
+                (array, start, min(size, width - start)) for start in range(0, width, size)
+            ]
         self.moved = rows - shared
-        self.order = [(j, k) for k in range(pairs) for j in range(arrays)]
-        self.lag = max(arrays, 2)
+        self.early = min(rows // 8, self.moved - shared) // 16 * 16
+        self.late = self.moved - self.early
+        self.order = [(j, k) for j in range(len(self.pieces)) for k in range(pairs)]
+        if pairs > 1:
+            self.order.sort(key=lambda item: (item[0] * pairs + (item[1] or -0.5 - (item[0] > 0))))
+        self.lag = 2
 
     def scratch(self):
-        dma, pairs, arrays = pltpu.SemaphoreType.DMA, self.pairs, self.arrays
+        dma, pairs, arrays = pltpu.SemaphoreType.DMA, self.pairs, len(self.pieces)
         return [
             dma((arrays, max(pairs - 1, 1))),
             dma((arrays, max(pairs - 1, 1))),
@@ -751,6 +764,8 @@
             dma((arrays, pairs)),
             dma((arrays, 2 * pairs)),
             dma((arrays, 2 * pairs)),
+            dma((arrays, 2 * pairs)),
+            dma((arrays, 2 * pairs)),
             dma((arrays,)),
         ]
 
@@ -758,7 +773,7 @@
         self.weights, self.fulls = weights, fulls
         (
             self.ring_send, self.ring_recv, self.pair_send, self.pair_recv,
-            self.cross_send, self.cross_recv, self.local,
+            self.cross_send, self.cross_recv, self.early_send, self.early_recv, self.local,
         ) = scratch
         self.own, self.place = lax.axis_index("fsdp"), lax.axis_index("context")
         self.side = lax.axis_index("tensor")
@@ -769,7 +784,10 @@
         self.partner = (2 * pair + 1 - member, self.place, self.side)
         self.across = (self.own, 1 - self.place, self.side)
         self.beside = (self.own, self.place, 1 - self.side)
-        self.moved_start = pl.multiple_of(self.place * self.shared, 16)
+        self.late_start = pl.multiple_of(self.place * (self.shared + self.early), 16)
+        self.early_start = pl.multiple_of(
+            self.place * self.shared + (1 - self.place) * self.late, 16
+        )
         self.shared_start = pl.multiple_of(self.place * self.moved, 16)
 
     def greet(self, *others):
@@ -782,26 +800,57 @@
     def part(self, j, k, which, start, size):
         there = lax.rem(self.pair + self.pairs - k, self.pairs)
         index = 2 * there + (self.member if which == 0 else 1 - self.member)
-        return self.fulls[j].at[pl.ds(pl.multiple_of(index * self.rows + start, 16), size), :]
-
-    def source(self, j, k):
-        if k == 0:
-            return self.weights[j].at[pl.ds(self.moved_start, self.moved), :]
-        return self.part(j, k, 0, self.moved_start, self.moved)
+        array, first, width = self.pieces[j]
+        rows = pl.ds(pl.multiple_of(index * self.rows + start, 16), size)
+        return self.fulls[array].at[rows, pl.ds(first, width)]
+
+    def source(self, j, k, which, start, size):
+        if k == 0 and which == 0:
+            array, first, width = self.pieces[j]
+            return self.weights[array].at[pl.ds(start, size), pl.ds(first, width)]
+        return self.part(j, k, which, start, size)
 
     def ring_copy(self, j, k):
         return pltpu.make_async_remote_copy(
-            src_ref=self.source(j, k), dst_ref=self.part(j, k, 0, self.moved_start, self.moved),
+            src_ref=self.source(j, k, 0, self.late_start, self.late),
+            dst_ref=self.part(j, k, 0, self.late_start, self.late),
             send_sem=self.ring_send.at[j, k], recv_sem=self.ring_recv.at[j, k],
             device_id=self.ahead, device_id_type=MESH,
         )
 
     def pair_copy(self, j, k):
         return pltpu.make_async_remote_copy(
-            src_ref=self.source(j, k), dst_ref=self.part(j, k, 0, self.moved_start, self.moved),
+            src_ref=self.source(j, k, 0, self.late_start, self.late),
+            dst_ref=self.part(j, k, 0, self.late_start, self.late),
             send_sem=self.pair_send.at[j, k], recv_sem=self.pair_recv.at[j, k],
             device_id=self.partner, device_id_type=MESH,
         )
+
+    def early_copy(self, j, k, which):
+        own = k == self.pairs - 1
+        k = 0 if own else k
+        slot = 2 * self.pairs - 2 if own else 2 * k + which
+        return pltpu.make_async_remote_copy(
+            src_ref=self.source(j, k, which, self.early_start, self.early),
+            dst_ref=self.part(j, k, which, self.early_start, self.early),
+            send_sem=self.early_send.at[j, slot], recv_sem=self.early_recv.at[j, slot],
+            device_id=self.partner if own else self.ahead, device_id_type=MESH,
+        )
+
+    def early_event(self, j, k):
+        last = self.pairs - 1
+        if k == 0:
+            self.early_copy(j, last, 0).start()
+        else:
+            self.early_copy(j, k - 1, 0).wait_recv()
+        if k < last:
+            self.early_copy(j, k, 0).start()
+        if k == 1:
+            self.early_copy(j, last, 0).wait_recv()
+        elif k > 1:
+            self.early_copy(j, k - 2, 1).wait_recv()
+        if k > 0:
+            self.early_copy(j, k - 1, 1).start()
 
     def cross_copy(self, j, k, which):
         here = self.part(j, k, which, self.shared_start, self.shared)
@@ -819,13 +868,16 @@
         j, k = self.order[number]
         if k > 0:
             self.ring_copy(j, k - 1).wait_recv()
-        else:
-            self.keep_copy(j).start()
+        if number == 0:
+            for array in range(self.arrays):
+                self.keep_copy(array).start()
         if k < self.pairs - 1:
             self.ring_copy(j, k).start()
         self.pair_copy(j, k).start()
         if k > 0:
             self.cross_copy(j, k, 0).start()
+        if self.early:
+            self.early_event(j, k)
         if number >= self.lag:
             self.share(number - self.lag)
 
@@ -846,8 +898,19 @@
             self.pair_copy(j, k).wait_send()
         for item in crossed:
             self.cross_copy(*item).wait_send()
-        for j in range(self.arrays):
-            self.keep_copy(j).wait()
+        for j in range(len(self.pieces)):
+            if self.early:
+                last = self.pairs - 1
+                if last:
+                    self.early_copy(j, last - 1, 1).wait_recv()
+                else:
+                    self.early_copy(j, last, 0).wait_recv()
+                self.early_copy(j, last, 0).wait_send()
+                for k in range(last):
+                    for which in range(2):
+                        self.early_copy(j, k, which).wait_send()
+        for array in range(self.arrays):
+            self.keep_copy(array).wait()
 
 
 def gather_kernel(plan, *refs):
@@ -871,7 +934,7 @@
     first.start()
     for number in range(len(plan.order)):
         plan.event(number)
-        if number == min(2, len(plan.order) - 1):
+        if number == min(5, len(plan.order) - 1):
             first.wait_recv()
             second.start()
     second.wait_recv()
@@ -884,7 +947,7 @@
     rows = shards[0].shape[0]
     pairs = lax.axis_size("fsdp") // 2
     count = len(shards)
-    plan = Gathering(rows, pairs, count, shared)
+    plan = Gathering(rows, pairs, [shard.shape[1] for shard in shards], 2, shared)
     hbm = pl.BlockSpec(memory_space=pl.ANY)
     dma = pltpu.SemaphoreType.DMA
     return pl.pallas_call(

time: 861 us -> 856 us (level)
    pallas_call x1, Pallas kernels: 102 us -> 91.8 us  [gather_weights(): pl.pallas_call(functools.partial(gather_kernel, plan), out_shape=[jax.Sha...]
where the time goes in v5:
time: 856 us; the launch traced here: 849 us
  Pallas kernels  595 us (70%)
  matrix products  116 us (14%)
  other arithmetic  44.3 us (5%)
  local copies, waits for them, and re-layouts  43.5 us (5%)
  waiting for transfers between devices  37.5 us (4%)
  starting transfers between devices  10.6 us (1%)
    pallas_call x1, Pallas kernels, backward_ssd(): pl.pallas_call(functools.partial(backward_kernel, heads, chunks, plan, le...  177 us
    pallas_call x1, Pallas kernels, forward_ssd(): pl.pallas_call(functools.partial(forward_kernel, heads, chunks, plan), gr...  148 us
    pallas_call x1, Pallas kernels, reduce_terms(): pl.pallas_call(functools.partial(reduce_kernel, plan, arrays), out_shape=...  109 us
    pallas_call x1, Pallas kernels, gather_weights(): pl.pallas_call(functools.partial(gather_kernel, plan), out_shape=[jax.Sha...  91.8 us
    dot_general x3, matrix products, contract_cols(): lax.dot_general(left, right, (((1,), (1,)), ((), ())), preferred_element_...  57 us
    dot_general x3, matrix products, contract_rows(): lax.dot_general(left, right, (((0,), (0,)), ((), ())), preferred_element_...  41.3 us
    pallas_call x1, Pallas kernels, gate_stage(): pl.pallas_call(gate_kernel, grid=(rows // size,), in_specs=[block(model),...  35.2 us
    pallas_call x1, Pallas kernels, gate_back_stage(): pl.pallas_call(functools.partial(gate_back_kernel, inner_total, per_micro...  23.8 us
  transfers between devices with their start and end apart: 13, of which 7 were waited for; matrix products, arithmetic and copies ran while one was open for 13% of the time, Pallas kernels for 14%

profile of v5, /device:TPU:0, one launch (start us, length us, event | category | flops | bytes accessed | tf_op | source)
XLA Modules:
  0.0 848.9 jit_solution(8732630149427623640)
XLA Ops:
  2.5 6.6 fusion.24
  9.7 1.1 fusion.13.refs_0_
  10.8 91.8 %shard_map.316 = (bf16[2048,2432]{1,0:T(8,128)(2,1)}, bf16[2,512,2048]{2,1,0:T(8,128)(2,1)}) custom-call(bf16[256,2432]{1,0:T(8,128)(2,1)} %fusion.13.refs_0_, bf16[2,512,2048]{2,1,0:T(8,128)(2,1)} %bitcast.100), custom_call_target="tpu_custom_call" | custom-call | tf_op jit(solution)/shard_map/pallas_call | solution.py:953
  102.7 2.2 copy-done.3
  104.8 2.2 copy-done.5
  107.0 3.2 shard_map.317
  110.2 17.2 %fusion.28.refs_1_.refs_2_.refs_4_.refs_5_.refs_7_ = f32[1024,2432]{1,0:T(8,128)S(1)} fusion(bf16[1024,2048]{1,0:T(8,128)(2,1)S(1)} %get-tuple-element.51.normed, bf16[2048,2432]{1,0:T(8,128)(2,1)} %get-tuple-element.52), kind=kOutput, calls=%fused_computation.80 | convolution fusion | flops 10200547328 | bytes 24117248 | tf_op jit(solution)/shard_map/dot_general | solution.py:1610
  127.5 3.7 copy-done.26
  131.2 3.3 collective-permute-start
  135.7 1.3 fusion.18
  137.6 4.6 bitcast_multiply_fusion.out_grad
  142.5 2.7 add_bitcast_fusion
  145.2 2.2 copy.69
  147.4 1.7 copy.57
  149.3 1.0 copy-done.7
  150.4 148.1 %shard_map.318 = (f32[1024,2048]{1,0:T(8,128)}, f32[8,128,2048]{2,1,0:T(8,128)}, f32[2,128,2048]{2,1,0:T(8,128)}, f32[1024,256]{1,0:T(8,128)S(1)}, f32[1024,2048...) custom-call(s32[2,3]{1,0:T(2,128)S(1)} %pad_add_fusion.1.refs_0_, ...), custom_call_target="tpu_custom_call" | custom-call | tf_op jit(solution)/shard_map/pallas_call | solution.py:310
  298.5 1.0 copy-done.8
  300.2 1.5 broadcast_select_fusion.entering.refs_13_
  301.7 35.2 %shard_map.319 = (f32[1024,2048]{1,0:T(8,128)}, f32[1024,2048]{1,0:T(8,128)}, f32[1024,2048]{1,0:T(8,128)}, f32[1024,128]{1,0:T(8,128)}) custom-call(bf16[1024,2048]{1,0:T(8,128)(2,1)} %copy-done.24, bf16[1024,2048]{1,0:T(8,128)(2,1)} %bitcast_multiply_fusion.out_grad, bf16[2048,2048]{1,0:T(8,128)(2,1)} %get-tuple-element.53.gate_weight, ...), custom_call_target="tpu_custom_call" | custom-call | flops 17179869184 | bytes 50331648 | tf_op jit(solution)/shard_map/pallas_call | solution.py:1039
  337.0 6.6 copy.64
  343.7 23.8 %shard_map.320 = (bf16[1024,2048]{1,0:T(8,128)(2,1)}, bf16[1024,2048]{1,0:T(8,128)(2,1)}, f32[1024,2048]{1,0:T(8,128)}, f32[2,128,2048]{2,1,0:T(8,128)S(1)}, f32[8,2048]{1,0:T(8,128)S(1)}) custom-call(f32[1024,2048]{1,0:T(8,128)} %get-tuple-element.59.mixer.refs_9_, f32[1024,2048]{1,0:T(8,128)} %get-tuple-element.60.gate_in, ...), custom_call_target="tpu_custom_call" | custom-call | flops 2147483648 | bytes 50331648 | tf_op jit(solution)/shard_map/pallas_call | solution.py:1104
  367.5 24.9 %fusion.30.refs_29_ = f32[1024,2048]{1,0:T(8,128)} fusion(bf16[1024,2048]{1,0:T(8,128)(2,1)} %get-tuple-element.65, bf16[2048,2048]{1,0:T(8,128)(2,1)S(1)} %bitcast.128), kind=kOutput, calls=%fused_computation.82 | convolution fusion | flops 8589934592 | bytes 20971520 | tf_op jit(solution)/shard_map/dot_general | solution.py:1706
  392.5 1.3 collective-permute-start.3
  393.8 13.5 %fusion.29.refs_28_ = f32[1024,2048]{1,0:T(8,128)} fusion(bf16[1024,2048]{1,0:T(8,128)(2,1)S(1)} %copy-done.41, bf16[2048,2048]{1,0:T(8,128)(2,1)} %get-tuple-element.54.out_weight), kind=kOutput, calls=%fused_computation.81 | convolution fusion | flops 8589934592 | bytes 20971520 | tf_op jit(solution)/shard_map/dot_general | solution.py:1706
  407.3 11.4 %fusion.10.refs_26_ = f32[4,2,256,2048]{3,2,1,0:T(8,128)} fusion(bf16[4,2,256,1024]{3,2,1,0:T(8,128)(2,1)S(1)} %bitcast.118, bf16[1024,2048]{1,0:T(8,128)(2,1)S(1)} %copy-done.41), kind=kOutput, calls=%fused_computation.12 | convolution fusion | flops 8589934592 | bytes 25165824 | tf_op jit(solution)/shard_map/dot_general | solution.py:1700
  418.7 11.8 %fusion.31 = f32[2048,2048]{1,0:T(8,128)} fusion(bf16[1024,2048]{1,0:T(8,128)(2,1)S(1)} %copy-done.25, bf16[1024,2048]{1,0:T(8,128)(2,1)S(1)} %copy-done.40), kind=kOutput, calls=%fused_computation.83 | convolution fusion | flops 8589934592 | bytes 25165824 | tf_op jit(solution)/shard_map/dot_general | solution.py:1700
  430.5 13.1 %collective-permute-done.3.refs_15_ = f32[2,128,2048]{2,1,0:T(8,128)S(1)} collective-permute-done((f32[2,128,2048]{2,1,0:T(8,128)S(1)}, f32[2,128,2048]{2,1,0:T(8,128)S(1)}, u32[]{:S(2)}, u32[]{:S(2)}) %collective-permute-start.3) | collective-permute-done | bytes 2097184 | tf_op jit(solution)/shard_map/ppermute | solution.py:1486
  443.7 1.3 copy-done.29
  445.0 177.1 %shard_map.321 = (bf16[1024,2432]{1,0:T(8,128)(2,1)}, f32[2,8,2048]{2,1,0:T(8,128)}, f32[2,8,2048]{2,1,0:T(8,128)}, f32[1024,256]{1,0:T(8,128)}, f32[2,8,256]{2,...) custom-call(s32[2,3]{1,0:T(2,128)} %copy-done.19, ...), custom_call_target="tpu_custom_call" | custom-call | tf_op jit(solution)/shard_map/pallas_call | solution.py:654
  622.1 0.9 pad_maximum_fusion.1
  623.0 1.3 collective-permute-start.4
  624.3 5.7 collective-permute-done.4
  630.1 1.3 pad_add_fusion
  632.4 1.7 collective-permute-done.5
  636.4 18.6 %convolution_add_fusion = f32[1024,2048]{1,0:T(8,128)} fusion(f32[1024,2048]{1,0:T(8,128)} %fusion.30.refs_29_, bf16[1024,2432]{1,0:T(8,128)(2,1)} %fusion.16, bf16[2048,2432]{1,0:T(8,128)(2,1)} %get-tuple-element.52), kind=kOutput, calls=%fused_computation.15 | convolution fusion | flops 10202644480 | bytes 31719424 | tf_op jit(solution)/shard_map/dot_general | solution.py:1706
  657.7 6.6 collective-permute-done.7
  664.3 4.2 collective-permute-done.6
  668.5 8.5 fusion.8
  677.1 18.1 %fusion.32 = f32[2048,2432]{1,0:T(8,128)} fusion(bf16[1024,2048]{1,0:T(8,128)(2,1)} %copy-done.24, bf16[1024,2432]{1,0:T(8,128)(2,1)} %fusion.16), kind=kOutput, calls=%fused_computation.84 | convolution fusion | flops 10200547328 | bytes 29097984 | tf_op jit(solution)/shard_map/dot_general | solution.py:1700
  695.2 109.0 %shard_map.322.second = f32[256,2432]{1,0:T(8,128)} custom-call(f32[4,2,256,2432]{3,2,1,0:T(8,128)} %bitcast.112), custom_call_target="tpu_custom_call" | custom-call | tf_op jit(solution)/shard_map/pallas_call | solution.py:1471
  804.2 1.0 slice.154
  805.3 1.8 copy.62
  807.1 7.1 shard_map.323
  816.4 3.0 collective-permute-done.9
  819.5 1.2 collective-permute-start.10
  820.7 3.1 collective-permute-done.10
  823.8 1.8 collective-permute-start.11
  825.6 18.7 %fusion.7 = (bf16[1024,2048]{1,0:T(8,128)(2,1)}, bf16[1024,2048]{1,0:T(8,128)(2,1)}) fusion(bf16[1024,2048]{1,0:T(8,128)(2,1)} %copy-done.2, bf16[2,1,512,2048]{3,2,1,0:T(8,128)(2,1)} %param.24, f32[1024]{0:T(1024)S(1)} %broadcast_multiply_fusion, f32[2048]{0:T(1024)S(1)} %copy-done.15, f32[1024]{0:T(1024)S(1)} %slice_reduce_fusion, ...), kind=kLoop, calls=%fused_computation.9 | loop fusion | flops 29360128 | bytes 50352128 | tf_op jit(solution)/shard_map/convert_element_type | solution.py:1670
  (150 shorter events, 17.9 us)
Async XLA Ops:
  0.6 141.6 %copy-start = (f32[32]{0:T(128)S(1)}, f32[32]{0:T(128)}, u32[]{:S(2)}) copy-start(f32[32]{0:T(128)} %param.36) | copy-start | bytes 388
  2.5 7.2 copy-start.33
  9.1 93.6 %copy-start.14 = (f32[2048]{0:T(1024)S(1)}, f32[2048]{0:T(1024)}, u32[]{:S(2)}) copy-start(f32[2048]{0:T(1024)} %param.25) | copy-start | bytes 24580
  110.2 17.2 %copy-start.2 = (bf16[1024,2048]{1,0:T(8,128)(2,1)}, bf16[1024,2048]{1,0:T(8,128)(2,1)S(1)}, u32[]{:S(2)}) copy-start(bf16[1024,2048]{1,0:T(8,128)(2,1)S(1)} %get-tuple-element.50) | copy-start | bytes 12582916
  110.2 17.2 %copy-start.10 = (f32[1024,128]{1,0:T(8,128)}, f32[1024,128]{1,0:T(8,128)S(1)}, u32[]{:S(2)}) copy-start(f32[1024,128]{1,0:T(8,128)S(1)} %get-tuple-element.64) | copy-start | bytes 1572868
  110.2 17.2 %copy-start.24 = (bf16[1024,2048]{1,0:T(8,128)(2,1)}, bf16[1024,2048]{1,0:T(8,128)(2,1)S(1)}, u32[]{:S(2)}) copy-start(bf16[1024,2048]{1,0:T(8,128)(2,1)S(1)} %get-tuple-element.51.normed) | copy-start | bytes 12582916
  110.2 24.3 %copy-start.36 = (s32[2,1,2]{2,1,0:T(1,128)S(1)}, s32[2,1,2]{2,1,0:T(1,128)}, u32[]{:S(2)}) copy-start(s32[2,1,2]{2,1,0:T(1,128)} %param.22) | copy-start | bytes 52
  127.5 14.8 %copy-start.32 = (f32[32,2048]{1,0:T(8,128)S(1)}, f32[32,2048]{1,0:T(8,128)}, u32[]{:S(2)}) copy-start(f32[32,2048]{1,0:T(8,128)} %constant.79.clone) | copy-start | bytes 786436
  131.2 18.0 %collective-permute-start = (f32[2,8,2432]{2,1,0:T(8,128)S(1)}, f32[2,8,2432]{2,1,0:T(8,128)S(1)}, u32[]{:S(2)}, u32[]{:S(2)}) collective-permute-start(f32[2,8,2432]{2,1,0:T(8,128)S(1)} %pad_maximum_fusion), channel_id=1, source_target_pairs={{0,2},{1,3},{4,6},{5,7},{8,10},{9,11},{12,14},{13,15},{16,18},{17,... | collective-permute-start | bytes 466952 | tf_op jit(solution)/shard_map/ppermute | solution.py:1486
  137.6 11.6 %copy-start.38 = (f32[32]{0:T(128)S(1)}, f32[32]{0:T(128)}, u32[]{:S(2)}) copy-start(f32[32]{0:T(128)} %param.35) | copy-start | bytes 388
  137.6 11.6 %copy-start.39 = (f32[32]{0:T(128)S(1)}, f32[32]{0:T(128)}, u32[]{:S(2)}) copy-start(f32[32]{0:T(128)} %param.34) | copy-start | bytes 388
  137.6 11.7 %copy-start.4 = (bf16[128,4096]{1,0:T(8,128)(2,1)S(1)}, bf16[128,4096]{1,0:T(8,128)(2,1)}, u32[]{:S(2)}) copy-start(bf16[128,4096]{1,0:T(8,128)(2,1)} %constant.77.clone.refs_16_.refs_24_) | copy-start | bytes 3145732
  137.6 11.7 %copy-start.13 = (f32[4,2048]{1,0:T(4,128)S(1)}, f32[4,2048]{1,0:T(4,128)}, u32[]{:S(2)}) copy-start(f32[4,2048]{1,0:T(4,128)} %refs_16_.2) | copy-start | bytes 98308
  137.6 11.7 %copy-start.17 = (f32[2048]{0:T(1024)S(1)}, f32[2048]{0:T(1024)}, u32[]{:S(2)}) copy-start(f32[2048]{0:T(1024)} %param.31) | copy-start | bytes 24580
  137.6 11.7 %copy-start.18 = (f32[4,256]{1,0:T(4,128)S(1)}, f32[4,256]{1,0:T(4,128)}, u32[]{:S(2)}) copy-start(f32[4,256]{1,0:T(4,128)} %refs_18_.1) | copy-start | bytes 12292
  137.6 11.7 %copy-start.23 = (f32[256]{0:T(256)S(1)}, f32[256]{0:T(256)}, u32[]{:S(2)}) copy-start(f32[256]{0:T(256)} %param.33) | copy-start | bytes 3076
  142.5 155.9 %copy-start.16 = (f32[1,2048]{1,0:T(1,128)}, f32[1,2048]{1,0:T(1,128)S(1)}, u32[]{:S(2)}) copy-start(f32[1,2048]{1,0:T(1,128)S(1)} %fusion.21.refs_14_.refs_22_) | copy-start | bytes 24580
  145.2 153.3 %copy-start.19 = (s32[2,3]{1,0:T(2,128)}, s32[2,3]{1,0:T(2,128)S(1)}, u32[]{:S(2)}) copy-start(s32[2,3]{1,0:T(2,128)S(1)} %pad_add_fusion.1.refs_0_) | copy-start | bytes 76
  149.2 149.3 %copy-start.21 = (f32[1,128]{1,0:T(1,128)}, f32[1,128]{1,0:T(1,128)S(1)}, u32[]{:S(2)}) copy-start(f32[1,128]{1,0:T(1,128)S(1)} %get-tuple-element.154.refs_13_.refs_21_) | copy-start | bytes 1540
  149.2 149.3 %copy-start.22 = (f32[1,128]{1,0:T(1,128)}, f32[1,128]{1,0:T(1,128)S(1)}, u32[]{:S(2)}) copy-start(f32[1,128]{1,0:T(1,128)S(1)} %get-tuple-element.155.refs_12_.refs_20_) | copy-start | bytes 1540
  149.3 149.3 %copy-start.6 = (f32[2,8,2432]{2,1,0:T(8,128)}, f32[2,8,2432]{2,1,0:T(8,128)S(1)}, u32[]{:S(2)}) copy-start(f32[2,8,2432]{2,1,0:T(8,128)S(1)} %collective-permute-done.refs_3_.refs_6_) | copy-start | bytes 466948
  336.9 6.7 collective-permute-start.1
  343.6 24.0 %slice-start.1 = ((s8[8388608]{0:T(1024)(128)(4,1)}), s8[4194304]{0:T(1024)(128)(4,1)S(1)}, s32[]{:S(2)}) async-start(s8[8388608]{0:T(1024)(128)(4,1)} %bitcast.127), calls=%async_computation.1 | async-start | bytes 8388608
  343.7 23.9 %slice-start.2 = ((s8[8388608]{0:T(1024)(128)(4,1)}), s8[4194304]{0:T(1024)(128)(4,1)S(1)}, s32[]{:S(2)}) async-start(s8[8388608]{0:T(1024)(128)(4,1)} %bitcast.127), calls=%async_computation.2 | async-start | bytes 8388608
  367.5 26.2 %copy-start.41 = (bf16[1024,2048]{1,0:T(8,128)(2,1)S(1)}, bf16[1024,2048]{1,0:T(8,128)(2,1)}, u32[]{:S(2)}) copy-start(bf16[1024,2048]{1,0:T(8,128)(2,1)} %get-tuple-element.63) | copy-start | bytes 12582916
  392.5 51.2 %collective-permute-start.3 = (f32[2,128,2048]{2,1,0:T(8,128)S(1)}, f32[2,128,2048]{2,1,0:T(8,128)S(1)}, u32[]{:S(2)}, u32[]{:S(2)}) collective-permute-start(f32[2,128,2048]{2,1,0:T(8,128)S(1)} %get-tuple-element.70), channel_id=1, source_target_pairs={{2,0},{3,1},{6,4},{7,5},{10,8},{11,9},{14,12},{15,13},{18,16},{19,... | collective-permute-start | bytes 6291464 | tf_op jit(solution)/shard_map/ppermute | solution.py:1486
  393.8 13.5 %copy-start.28 = (bf16[2048,1024]{1,0:T(8,128)(2,1)S(1)}, bf16[2048,1024]{1,0:T(8,128)(2,1)}, u32[]{:S(2)}) copy-start(bf16[2048,1024]{1,0:T(8,128)(2,1)} %copy.64) | copy-start | bytes 12582916
  407.3 11.4 %copy-start.25 = (bf16[1024,2048]{1,0:T(8,128)(2,1)S(1)}, bf16[1024,2048]{1,0:T(8,128)(2,1)}, u32[]{:S(2)}) copy-start(bf16[1024,2048]{1,0:T(8,128)(2,1)} %copy-done.24) | copy-start | bytes 12582916
  407.3 11.4 %copy-start.40 = (bf16[1024,2048]{1,0:T(8,128)(2,1)S(1)}, bf16[1024,2048]{1,0:T(8,128)(2,1)}, u32[]{:S(2)}) copy-start(bf16[1024,2048]{1,0:T(8,128)(2,1)} %get-tuple-element.65) | copy-start | bytes 12582916
  623.0 7.0 collective-permute-start.4
  631.4 2.7 collective-permute-start.5
  636.3 19.1 %copy-start.11 = (f32[1024,128]{1,0:T(8,128)S(1)}, f32[1024,128]{1,0:T(8,128)}, u32[]{:S(2)}) copy-start(f32[1024,128]{1,0:T(8,128)} %copy-done.10) | copy-start | bytes 1572868
  636.3 19.3 %copy-start.37 = (f32[8,256]{1,0:T(8,128)S(1)}, f32[8,256]{1,0:T(8,128)}, u32[]{:S(2)}) copy-start(f32[8,256]{1,0:T(8,128)} %get-tuple-element.77) | copy-start | bytes 24580
  636.4 21.1 %copy-start.34 = (f32[8,2048]{1,0:T(8,128)S(1)}, f32[8,2048]{1,0:T(8,128)}, u32[]{:S(2)}) copy-start(f32[8,2048]{1,0:T(8,128)} %get-tuple-element.76) | copy-start | bytes 196612
  636.4 32.1 %copy-start.15 = (f32[2048]{0:T(1024)S(1)}, f32[2048]{0:T(1024)}, u32[]{:S(2)}) copy-start(f32[2048]{0:T(1024)} %param.25) | copy-start | bytes 24580
  655.0 13.5 %collective-permute-start.6 = (f32[1024,2048]{1,0:T(8,128)}, f32[1024,2048]{1,0:T(8,128)}, u32[]{:S(2)}, u32[]{:S(2)}) collective-permute-start(f32[1024,2048]{1,0:T(8,128)} %convolution_add_fusion), channel_id=1, source_target_pairs={{0,1},{1,0},{2,3},{3,2},{4,5},{5,4},{6,7},{7,6},{8,9},{9,8},{10,11... | collective-permute-start | bytes 25165832 | tf_op jit(solution)/shard_map/ppermute | solution.py:1491
  655.1 170.5 %collective-permute-start.2 = (f32[1024,2048]{1,0:T(8,128)}, f32[1024,2048]{1,0:T(8,128)}, u32[]{:S(2)}, u32[]{:S(2)}) collective-permute-start(f32[1024,2048]{1,0:T(8,128)} %fusion.29.refs_28_), channel_id=1, source_target_pairs={{0,1},{1,0},{2,3},{3,2},{4,5},{5,4},{6,7},{7,6},{8,9},{9,8},{10,11... | collective-permute-start | bytes 25165832 | tf_op jit(solution)/shard_map/ppermute | solution.py:1491
  655.7 8.5 %collective-permute-start.7 = (f32[8,256]{1,0:T(8,128)S(1)}, f32[8,256]{1,0:T(8,128)S(1)}, u32[]{:S(2)}, u32[]{:S(2)}) collective-permute-start(f32[8,256]{1,0:T(8,128)S(1)} %copy-done.37), channel_id=1, source_target_pairs={{0,1},{1,0},{2,3},{3,2},{4,5},{5,4},{6,7},{7,6},{8,9},{9,8},{10,11... | collective-permute-start | bytes 24584 | tf_op jit(solution)/shard_map/ppermute | solution.py:1491
  677.0 137.8 %collective-permute-start.8 = (f32[128,128]{1,0:T(8,128)S(1)}, f32[128,128]{1,0:T(8,128)S(1)}, u32[]{:S(2)}, u32[]{:S(2)}) collective-permute-start(f32[128,128]{1,0:T(8,128)S(1)} %pad_bitcast_fusion), channel_id=1, source_target_pairs={{0,2},{2,0},{1,3},{3,1},{4,6},{6,4},{5,7},{7,5},{8,10},{10,8},{9,1... | collective-permute-start | bytes 196616 | tf_op jit(solution)/shard_map/ppermute | solution.py:1511
  695.2 110.0 %copy-start.30 = (f32[256,2048]{1,0:T(8,128)S(1)}, f32[256,2048]{1,0:T(8,128)}, u32[]{:S(2)}) copy-start(f32[256,2048]{1,0:T(8,128)} %get-tuple-element.82) | copy-start | bytes 6291460
  805.2 10.5 %collective-permute-start.12 = (f32[256,256]{1,0:T(8,128)S(1)}, f32[256,256]{1,0:T(8,128)S(1)}, u32[]{:S(2)}, u32[]{:S(2)}) collective-permute-start(f32[256,256]{1,0:T(8,128)S(1)} %slice.154), channel_id=1, source_target_pairs={{0,1},{1,0},{2,3},{3,2},{4,5},{5,4},{6,7},{7,6},{8,9},{9,8},{10,11... | collective-permute-start | bytes 786440 | tf_op jit(solution)/shard_map/ppermute | solution.py:1491
  807.1 7.1 slice-start
  807.1 8.6 %copy-start.27 = (f32[256,2432]{1,0:T(8,128)S(1)}, f32[256,2432]{1,0:T(8,128)}, u32[]{:S(2)}) copy-start(f32[256,2432]{1,0:T(8,128)} %shard_map.322.second) | copy-start | bytes 7471108
  807.1 18.5 %copy-start.35 = (f32[1024]{0:T(1024)S(1)}, f32[1024]{0:T(1024)}, u32[]{:S(2)}) copy-start(f32[1024]{0:T(1024)} %get-tuple-element.144) | copy-start | bytes 12292
  814.9 4.5 collective-permute-start.9
  819.5 4.3 collective-permute-start.10
  823.8 20.5 %collective-permute-start.11 = (f32[128,128]{1,0:T(8,128)S(1)}, f32[128,128]{1,0:T(8,128)S(1)}, u32[]{:S(2)}, u32[]{:S(2)}) collective-permute-start(f32[128,128]{1,0:T(8,128)S(1)} %add.111), channel_id=1, source_target_pairs={{0,16},{4,20},{8,24},{12,28},{16,0},{20,4},{24,8},{28,12},{1,17},{... | collective-permute-start | bytes 196616 | tf_op jit(solution)/shard_map/ppermute | solution.py:1511
  825.6 22.8 %copy-start.1 = (f32[32]{0:T(128)S(1)}, f32[32]{0:T(128)}, u32[]{:S(2)}) copy-start(f32[32]{0:T(128)} %param.36) | copy-start | bytes 388
  (10 other events, 32.2 us)

commit v6 on v5

--- a/solution.py
+++ b/solution.py
@@ -1450,34 +1450,147 @@
                     self.ring_copy(jnp.int32(self.count - 2 + slot), offset).wait_send()
 
 
-def reduce_kernel(plan, arrays, *refs):
-    plan.bind(refs[:arrays], refs[arrays : 2 * arrays], refs[2 * arrays :])
-    plan.greet()
-
-    def body(number, carried):
-        plan.step(number)
-        return carried
-
-    lax.fori_loop(0, plan.steps, body, 0)
-
-
-def reduce_terms(terms, lag, collective_id):
+def finish_kernel(plan, blocks, *refs):
+    (
+        term, x, cot, scale, keep, branch, branch_other, part, part_other, gain, small,
+        out, block_out, input_out, small_out,
+        gain_sum, cross_in, pair_out, pair_in, ring_in,
+        cross_send, cross_recv, pair_send, pair_recv, ring_send, ring_recv, final_sem,
+    ) = refs[:27]
+    plan.bind([term], [out], refs[27:])
+    step = pl.program_id(0)
+
+    @pl.when(step == 0)
+    def _():
+        plan.greet()
+        gain_sum[...] = jnp.zeros_like(gain_sum)
+
+    @pl.when(step < plan.steps)
+    def _():
+        plan.step(step)
+
+    @pl.when(step < blocks)
+    def _():
+        x_float = x[...].astype(f32)
+        block_out[...] = (x_float + keep[:, 0:1] * (branch[...] + branch_other[...])).astype(bf16)
+        inv_rms = scale[:, 0:1]
+        x_hat = x_float * inv_rms
+        normed_grad = part[...] + part_other[...]
+        hat_grad = normed_grad * gain[...]
+        mean = jnp.sum(hat_grad * x_hat, axis=-1, keepdims=True) * (1.0 / x_float.shape[-1])
+        input_out[...] = (cot[...].astype(f32) + inv_rms * (hat_grad - x_hat * mean)).astype(bf16)
+        gain_sum[0:1, :] += jnp.sum(normed_grad * x_hat, axis=0, keepdims=True)
+
+    rows = small.shape[0]
+    lines = gain_sum.shape[1] // LANES
+
+    def cross_copy():
+        return pltpu.make_async_remote_copy(
+            src_ref=pair_out, dst_ref=cross_in, send_sem=cross_send.at[0], recv_sem=cross_recv.at[0],
+            device_id=plan.across, device_id_type=MESH,
+        )
+
+    def pair_copy():
+        return pltpu.make_async_remote_copy(
+            src_ref=pair_out, dst_ref=pair_in, send_sem=pair_send.at[0], recv_sem=pair_recv.at[0],
+            device_id=plan.partner, device_id_type=MESH,
+        )
+
+    def ring_copy(offset):
+        return pltpu.make_async_remote_copy(
+            src_ref=ring_in.at[0], dst_ref=ring_in.at[plan.pairs - offset],
+            send_sem=ring_send.at[offset - 1], recv_sem=ring_recv.at[offset - 1],
+            device_id=plan.peer(offset), device_id_type=MESH,
+        )
+
+    @pl.when(step == blocks)
+    def _():
+        pair_out[pl.ds(0, rows), :] = small[...]
+        for line in range(lines):
+            pair_out[rows + line : rows + line + 1, :] = gain_sum[
+                0:1, line * LANES : (line + 1) * LANES
+            ]
+        cross_copy().start()
+
+    @pl.when(step == blocks + 2)
+    def _():
+        cross_copy().wait()
+        pair_out[...] += cross_in[...]
+        pair_copy().start()
+
+    @pl.when(step == blocks + 4)
+    def _():
+        pair_copy().wait()
+        ring_in[0] = pair_out[...] + pair_in[...]
+        for offset in range(1, plan.pairs):
+            ring_copy(offset).start()
+
+    @pl.when(step == blocks + 6)
+    def _():
+        for offset in range(1, plan.pairs):
+            ring_copy(offset).wait()
+        total = jnp.zeros_like(pair_out)
+        for index in range(plan.pairs):
+            total = total + ring_in[lax.rem(index + plan.pairs - plan.pair, plan.pairs)]
+        pair_in[...] = total
+        copy = pltpu.make_async_copy(pair_in, small_out, final_sem.at[0])
+        copy.start()
+        copy.wait()
+
+
+def finish(term, x, cot, scale, keep, branch, branch_other, part, part_other, gain, small, collective_id):
     pairs = lax.axis_size("fsdp") // 2
-    rows = terms[0].shape[0] // (2 * pairs)
-    columns = [term.shape[1] for term in terms]
-    plan = Reduction(rows, pairs, columns, lag)
+    shard_rows = term.shape[0] // (2 * pairs)
+    plan = Reduction(shard_rows, pairs, [term.shape[1]], 2)
+    rows, model = x.shape
+    size = 64
+    blocks = rows // size
+    steps = max(plan.steps, blocks + 7)
+    total_rows = small.shape[0] + model // LANES
     hbm = pl.BlockSpec(memory_space=pl.ANY)
-    arrays = len(terms)
+    dma = pltpu.SemaphoreType.DMA
+
+    def block(lanes):
+        return pl.BlockSpec((size, lanes), lambda step: (jnp.minimum(step, blocks - 1), 0))
+
+    def constant(shape):
+        return pl.BlockSpec(shape, lambda step: (0, 0))
+
     return pl.pallas_call(
-        functools.partial(reduce_kernel, plan, arrays),
-        out_shape=[jax.ShapeDtypeStruct((rows, count), f32) for count in columns],
-        in_specs=[hbm] * arrays,
-        out_specs=[hbm] * arrays,
-        scratch_shapes=plan.scratch(),
+        functools.partial(finish_kernel, plan, blocks),
+        grid=(steps,),
+        in_specs=[hbm]
+        + [block(lanes) for lanes in (model, model, LANES, LANES, model, model, model, model)]
+        + [constant((1, model)), constant(small.shape)],
+        out_specs=[hbm, block(model), block(model), hbm],
+        out_shape=[
+            jax.ShapeDtypeStruct((shard_rows, term.shape[1]), f32),
+            jax.ShapeDtypeStruct((rows, model), bf16),
+            jax.ShapeDtypeStruct((rows, model), bf16),
+            jax.ShapeDtypeStruct((total_rows, LANES), f32),
+        ],
+        scratch_shapes=[
+            pltpu.VMEM((8, model), f32),
+            pltpu.VMEM((total_rows, LANES), f32),
+            pltpu.VMEM((total_rows, LANES), f32),
+            pltpu.VMEM((total_rows, LANES), f32),
+            pltpu.VMEM((pairs, total_rows, LANES), f32),
+            dma((1,)),
+            dma((1,)),
+            dma((1,)),
+            dma((1,)),
+            dma((max(pairs - 1, 1),)),
+            dma((max(pairs - 1, 1),)),
+            dma((1,)),
+        ]
+        + plan.scratch(),
         compiler_params=pltpu.CompilerParams(
-            collective_id=collective_id, has_side_effects=True, vmem_limit_bytes=58 * 1024 * 1024
+            collective_id=collective_id, has_side_effects=True, vmem_limit_bytes=56 * 1024 * 1024
         ),
-    )(*[term.reshape(pairs, 2, rows, -1) for term in terms])
+    )(
+        term.reshape(pairs, 2, shard_rows, -1), x, cot, scale, keep, branch, branch_other, part,
+        part_other, gain, small,
+    )
 
 
 def passed_along(value, axis, steps):
@@ -1498,25 +1611,16 @@
     )
 
 
-def summed_everywhere(values):
-    sizes = [value.size for value in values]
-    shapes = [value.shape for value in values]
+def packed_rows(values):
     flat = jnp.concatenate([value.reshape(-1) for value in values])
-    count = flat.shape[0]
-    flat = jnp.pad(flat, (0, -count % 1024)).reshape(-1, 128)
-    for axis in ("context", "fsdp"):
-        members = lax.axis_size(axis)
-        reach = 1
-        while reach < members:
-            flat = flat + lax.ppermute(
-                flat, axis, [(source, source ^ reach) for source in range(members)]
-            )
-            reach *= 2
-    flat = flat.reshape(-1)
+    return jnp.pad(flat, (0, -flat.shape[0] % 1024)).reshape(-1, LANES)
+
+
+def unpacked(flat, values):
     results, start = [], 0
-    for size, shape in zip(sizes, shapes):
-        results.append(flat[start : start + size].reshape(shape))
-        start += size
+    for value in values:
+        results.append(flat[start : start + value.size].reshape(value.shape))
+        start += value.size
     return results
 
 
@@ -1586,8 +1690,6 @@
     x_input, normed, scales = ordered(
         near, far, inside * is_near, inside * (1 - is_near), is_near, norm_gain.reshape(1, model)
     )
-    x_float = x_input.astype(f32)
-    inv_rms = scales[:, :1]
 
     first_end = lengths[:, 0, 0]
     second_end = first_end + lengths[:, 0, 1]
@@ -1658,23 +1760,19 @@
         lead_grad = lax.dynamic_update_slice(
             lead_grad, tails[micro], ((micro + 1) * count - 8, 0)
         )
-    (lead_shard,) = reduce_terms([contract_rows(normed, lead_grad)], 2, 4)
     normed_part = gate_part + contract_cols(lead_grad, lead_full)
-    block_out = (x_float + keep * (branch + branch_other)).astype(bf16)
-    normed_grad = normed_part + paired(normed_part, "tensor")
-    x_hat = x_float * inv_rms
-    hat_grad = normed_grad * norm_gain
-    input_grad = (
-        cot.astype(f32)
-        + inv_rms * (hat_grad - x_hat * jnp.mean(hat_grad * x_hat, axis=-1, keepdims=True))
-    ).astype(bf16)
-    norm_gain_grad = jnp.sum(normed_grad * x_hat, axis=0)
-
     skip_sums = skip_sums[0].reshape(heads, head_size).sum(axis=1)
     coupling_sums = coupling_sums + paired(coupling_sums, "tensor")
-    (value_all, coupling_all, small_all, skip_all, inner_all, norm_all) = summed_everywhere(
-        [value_sums[:5], coupling_sums[:5], small_sums[:2], skip_sums, inner_gain_rows[0], norm_gain_grad]
-    )
+    small = [value_sums[:5], coupling_sums[:5], small_sums[:2], skip_sums, inner_gain_rows[0]]
+    small_rows = packed_rows(small)
+    lead_shard, block_out, input_grad, summed = finish(
+        contract_rows(normed, lead_grad), x_input, cot, scales,
+        jnp.broadcast_to(keep, (micros * count, LANES)), branch, branch_other,
+        normed_part, paired(normed_part, "tensor"), norm_gain.reshape(1, model), small_rows, 4,
+    )
+    flat = summed.reshape(-1)
+    value_all, coupling_all, small_all, skip_all, inner_all = unpacked(flat, small)
+    norm_all = flat[small_rows.size :]
     coupling_shard = lead_shard[:, inner : inner + twice]
     coupling_shard = coupling_shard + paired(coupling_shard, "tensor")
     return (

time: 856 us -> 832 us (0.972)
  other arithmetic: 44.3 us -> 18.2 us
  local copies, waits for them, and re-layouts: 43.5 us -> 55.6 us
  matrix products: 116 us -> 104 us
    convert_element_type x1 -> x0, other arithmetic: 18.7 us -> none  [shards(): input_grad = (cot.astype(f32) + inv_rms * (hat_grad - x_hat * jnp.mean(ha...]
    ppermute x3, waiting for transfers between devices: 18.9 us -> 32.1 us  [passed_along(): lax.ppermute(value, axis, [(source, source + steps) for source in range(i...]
    dot_general x3, matrix products: 57 us -> 45.4 us  [contract_cols(): lax.dot_general(left, right, (((1,), (1,)), ((), ())), preferred_element_...]
    ppermute x6, waiting for transfers between devices: 12.5 us -> 3.1 us  [paired(): lax.ppermute(value, axis, [(source, source ^ 1) for source in range(count)])]
    unnamed x94 -> x96, local copies, waits for them, and re-layouts: 20.2 us -> 25 us
  transfers between devices with their start and end apart: 13 -> 9, of which waited for: 7 -> 4; matrix products, arithmetic and copies ran while one was open for 13% -> 12% of each run, Pallas kernels for 14% -> 1%
where the time goes in v6:
time: 832 us; the launch traced here: 825 us
  Pallas kernels  602 us (72%)
  matrix products  104 us (12%)
  local copies, waits for them, and re-layouts  55.6 us (7%)
  waiting for transfers between devices  35.2 us (4%)
  other arithmetic  18.2 us (2%)
    pallas_call x1, Pallas kernels, backward_ssd(): pl.pallas_call(functools.partial(backward_kernel, heads, chunks, plan, le...  177 us
    pallas_call x1, Pallas kernels, forward_ssd(): pl.pallas_call(functools.partial(forward_kernel, heads, chunks, plan), gr...  148 us
    pallas_call x1, Pallas kernels, finish(): pl.pallas_call(functools.partial(finish_kernel, plan, blocks), grid=(step...  116 us
    pallas_call x1, Pallas kernels, gather_weights(): pl.pallas_call(functools.partial(gather_kernel, plan), out_shape=[jax.Sha...  91.8 us
    dot_general x3, matrix products, contract_cols(): lax.dot_general(left, right, (((1,), (1,)), ((), ())), preferred_element_...  45.4 us
    dot_general x3, matrix products, contract_rows(): lax.dot_general(left, right, (((0,), (0,)), ((), ())), preferred_element_...  41.6 us
    pallas_call x1, Pallas kernels, gate_stage(): pl.pallas_call(gate_kernel, grid=(rows // size,), in_specs=[block(model),...  35.1 us
    ppermute x3, waiting for transfers between devices, passed_along(): lax.ppermute(value, axis, [(source, source + steps) for source in range(i...  32.1 us
  transfers between devices with their start and end apart: 9, of which 4 were waited for; matrix products, arithmetic and copies ran while one was open for 12% of the time, Pallas kernels for 1%

profile of v6, /device:TPU:0, one launch (start us, length us, event | category | flops | bytes accessed | tf_op | source)
XLA Modules:
  0.0 824.7 jit_solution(4625165179859296610)
XLA Ops:
  1.7 6.5 fusion.13
  9.0 1.1 fusion.3.refs_0_
  10.1 91.8 %shard_map.316 = (bf16[2048,2432]{1,0:T(8,128)(2,1)}, bf16[2,512,2048]{2,1,0:T(8,128)(2,1)}) custom-call(bf16[256,2432]{1,0:T(8,128)(2,1)} %fusion.3.refs_0_, bf16[2,512,2048]{2,1,0:T(8,128)(2,1)} %bitcast.97), custom_call_target="tpu_custom_call" | custom-call | tf_op jit(solution)/shard_map/pallas_call | solution.py:953
  102.0 2.2 copy-done.2
  104.1 2.2 copy-done.5
  106.3 3.2 shard_map.317
  109.5 17.2 %fusion.16.refs_1_.refs_2_.refs_4_.refs_5_.refs_7_ = f32[1024,2432]{1,0:T(8,128)S(1)} fusion(bf16[1024,2048]{1,0:T(8,128)(2,1)S(1)} %get-tuple-element.54.normed, bf16[2048,2432]{1,0:T(8,128)(2,1)} %get-tuple-element.55), kind=kOutput, calls=%fused_computation.65 | convolution fusion | flops 10200547328 | bytes 24117248 | tf_op jit(solution)/shard_map/dot_general | solution.py:1712
  126.8 3.7 copy-done.24
  130.5 3.3 collective-permute-start
  135.3 1.3 fusion.8
  137.2 4.7 broadcast_multiply_fusion.out_grad
  141.9 2.7 add_bitcast_fusion
  145.3 2.0 copy.48
  147.4 1.0 copy-done.7
  148.5 148.0 %shard_map.318 = (f32[1024,2048]{1,0:T(8,128)}, f32[8,128,2048]{2,1,0:T(8,128)}, f32[2,128,2048]{2,1,0:T(8,128)}, f32[1024,256]{1,0:T(8,128)S(1)}, f32[1024,2048...) custom-call(s32[2,3]{1,0:T(2,128)S(1)} %pad_add_fusion.1.refs_0_, ...), custom_call_target="tpu_custom_call" | custom-call | tf_op jit(solution)/shard_map/pallas_call | solution.py:310
  296.5 1.0 copy-done.8
  298.1 1.5 broadcast_select_fusion.entering.refs_13_
  299.7 35.1 %shard_map.319 = (f32[1024,2048]{1,0:T(8,128)}, f32[1024,2048]{1,0:T(8,128)}, f32[1024,2048]{1,0:T(8,128)}, f32[1024,128]{1,0:T(8,128)}) custom-call(bf16[1024,2048]{1,0:T(8,128)(2,1)} %copy-done.22, bf16[1024,2048]{1,0:T(8,128)(2,1)} %broadcast_multiply_fusion.out_grad, bf16[2048,2048]{1,0:T(8,128)(2,1)} %get-tuple-element.56.gate_weight, ...), custom_call_target="tpu_custom_call" | custom-call | flops 17179869184 | bytes 50331648 | tf_op jit(solution)/shard_map/pallas_call | solution.py:1039
  334.9 6.5 copy.55
  341.6 23.9 %shard_map.320 = (bf16[1024,2048]{1,0:T(8,128)(2,1)}, bf16[1024,2048]{1,0:T(8,128)(2,1)}, f32[1024,2048]{1,0:T(8,128)}, f32[2,128,2048]{2,1,0:T(8,128)S(1)}, f32[8,2048]{1,0:T(8,128)S(1)}) custom-call(f32[1024,2048]{1,0:T(8,128)} %get-tuple-element.62.mixer.refs_9_, f32[1024,2048]{1,0:T(8,128)} %get-tuple-element.63.gate_in, ...), custom_call_target="tpu_custom_call" | custom-call | flops 2147483648 | bytes 50331648 | tf_op jit(solution)/shard_map/pallas_call | solution.py:1104
  365.5 13.0 %fusion.19.refs_29_ = f32[1024,2048]{1,0:T(8,128)} fusion(bf16[1024,2048]{1,0:T(8,128)(2,1)} %get-tuple-element.72, bf16[2048,2048]{1,0:T(8,128)(2,1)S(1)} %bitcast.127), kind=kOutput, calls=%fused_computation.68 | convolution fusion | flops 8589934592 | bytes 20971520 | tf_op jit(solution)/shard_map/dot_general | solution.py:1804
  378.5 13.4 %fusion.18.refs_28_.refs_5_ = f32[1024,2048]{1,0:T(8,128)} fusion(bf16[1024,2048]{1,0:T(8,128)(2,1)S(1)} %copy-done.41, bf16[2048,2048]{1,0:T(8,128)(2,1)} %get-tuple-element.57.out_weight), kind=kOutput, calls=%fused_computation.67 | convolution fusion | flops 8589934592 | bytes 20971520 | tf_op jit(solution)/shard_map/dot_general | solution.py:1804
  391.9 1.3 collective-permute-start.2
  393.2 11.6 %fusion.refs_26_ = f32[4,2,256,2048]{3,2,1,0:T(8,128)} fusion(bf16[4,2,256,1024]{3,2,1,0:T(8,128)(2,1)S(1)} %bitcast.117, bf16[1024,2048]{1,0:T(8,128)(2,1)S(1)} %copy-done.41), kind=kOutput, calls=%fused_computation | convolution fusion | flops 8589934592 | bytes 25165824 | tf_op jit(solution)/shard_map/dot_general | solution.py:1798
  404.9 11.9 %fusion.17 = f32[2048,2048]{1,0:T(8,128)} fusion(bf16[1024,2048]{1,0:T(8,128)(2,1)S(1)} %copy-done.23, bf16[1024,2048]{1,0:T(8,128)(2,1)S(1)} %copy-done.40), kind=kOutput, calls=%fused_computation.66 | convolution fusion | flops 8589934592 | bytes 25165824 | tf_op jit(solution)/shard_map/dot_general | solution.py:1798
  416.8 26.3 %collective-permute-done.2.refs_15_ = f32[2,128,2048]{2,1,0:T(8,128)S(1)} collective-permute-done((f32[2,128,2048]{2,1,0:T(8,128)S(1)}, f32[2,128,2048]{2,1,0:T(8,128)S(1)}, u32[]{:S(2)}, u32[]{:S(2)}) %collective-permute-start.2) | collective-permute-done | bytes 2097184 | tf_op jit(solution)/shard_map/ppermute | solution.py:1599
  443.1 1.3 copy-done.28
  444.4 177.2 %shard_map.321 = (bf16[1024,2432]{1,0:T(8,128)(2,1)}, f32[2,8,2048]{2,1,0:T(8,128)}, f32[2,8,2048]{2,1,0:T(8,128)}, f32[1024,256]{1,0:T(8,128)}, f32[2,8,256]{2,...) custom-call(s32[2,3]{1,0:T(2,128)} %copy-done.17, ...), custom_call_target="tpu_custom_call" | custom-call | tf_op jit(solution)/shard_map/pallas_call | solution.py:654
  622.6 1.3 collective-permute-start.3
  623.9 5.7 collective-permute-done.3
  629.7 1.3 pad_add_fusion
  632.5 1.8 collective-permute-done.4
  636.5 18.9 %convolution_add_fusion.refs_7_ = f32[1024,2048]{1,0:T(8,128)} fusion(f32[1024,2048]{1,0:T(8,128)} %fusion.19.refs_29_, bf16[1024,2432]{1,0:T(8,128)(2,1)} %fusion.6, bf16[2048,2432]{1,0:T(8,128)(2,1)} %get-tuple-element.55), kind=kOutput, calls=%fused_computation.2 | convolution fusion | flops 10202644480 | bytes 31719424 | tf_op jit(solution)/shard_map/dot_general | solution.py:1804
  657.7 1.8 copy.53
  659.6 1.3 collective-permute-done.7
  661.6 18.1 %fusion.20 = f32[2048,2432]{1,0:T(8,128)} fusion(bf16[1024,2048]{1,0:T(8,128)(2,1)} %copy-done.22, bf16[1024,2432]{1,0:T(8,128)(2,1)} %fusion.6), kind=kOutput, calls=%fused_computation.69 | convolution fusion | flops 10200547328 | bytes 29097984 | tf_op jit(solution)/shard_map/dot_general | solution.py:1798
  679.7 1.0 broadcast_in_dim.23.refs_4_
  680.7 116.4 %shard_map.322 = (f32[256,2432]{1,0:T(8,128)}, bf16[1024,2048]{1,0:T(8,128)(2,1)}, bf16[1024,2048]{1,0:T(8,128)(2,1)}, f32[128,128]{1,0:T(8,128)}) custom-call(f32[4,2,256,2432]{3,2,1,0:T(8,128)} %bitcast.110, bf16[1024,2048]{1,0:T(8,128)(2,1)} %copy-done.4, bf16[1024,2048]{1,0:T(8,128)(2,1)} %bitcast.112, f32[1024,128]{1,0:T(8,128)} %copy-done.10, ...), custom_call_target="tpu_custom_call" | custom-call | tf_op jit(solution)/shard_map/pallas_call | solution.py:1559
  797.2 1.0 slice.154
  798.2 1.3 slice_bitcast_fusion.8
  799.5 1.2 slice_bitcast_fusion.6
  803.1 1.4 slice.177
  804.4 1.2 slice.176
  805.6 6.7 shard_map.323
  814.3 1.3 slice_bitcast_fusion.4
  815.6 1.7 slice_add_fusion.3
  817.3 4.9 copy.67
  822.2 2.0 copy.68
  (136 shorter events, 17.4 us)
Async XLA Ops:
  0.6 134.3 %copy-start = (f32[32]{0:T(128)S(1)}, f32[32]{0:T(128)}, u32[]{:S(2)}) copy-start(f32[32]{0:T(128)} %param.36) | copy-start | bytes 388
  1.6 7.2 copy-start.35
  1.7 7.3 copy-start.32
  8.8 93.1 %copy-start.14 = (f32[2048]{0:T(1024)S(1)}, f32[2048]{0:T(1024)}, u32[]{:S(2)}) copy-start(f32[2048]{0:T(1024)} %param.25) | copy-start | bytes 24580
  101.9 2.2 copy-start.2
  109.5 17.2 %copy-start.4 = (bf16[1024,2048]{1,0:T(8,128)(2,1)}, bf16[1024,2048]{1,0:T(8,128)(2,1)S(1)}, u32[]{:S(2)}) copy-start(bf16[1024,2048]{1,0:T(8,128)(2,1)S(1)} %get-tuple-element.78.refs_1_) | copy-start | bytes 12582916
  109.5 17.2 %copy-start.10 = (f32[1024,128]{1,0:T(8,128)}, f32[1024,128]{1,0:T(8,128)S(1)}, u32[]{:S(2)}) copy-start(f32[1024,128]{1,0:T(8,128)S(1)} %get-tuple-element.79.refs_3_) | copy-start | bytes 1572868
  109.5 17.2 %copy-start.22 = (bf16[1024,2048]{1,0:T(8,128)(2,1)}, bf16[1024,2048]{1,0:T(8,128)(2,1)S(1)}, u32[]{:S(2)}) copy-start(bf16[1024,2048]{1,0:T(8,128)(2,1)S(1)} %get-tuple-element.54.normed) | copy-start | bytes 12582916
  109.5 24.3 %copy-start.36 = (s32[2,1,2]{2,1,0:T(1,128)S(1)}, s32[2,1,2]{2,1,0:T(1,128)}, u32[]{:S(2)}) copy-start(s32[2,1,2]{2,1,0:T(1,128)} %param.22) | copy-start | bytes 52
  109.5 25.5 %copy-start.31 = (f32[32,2048]{1,0:T(8,128)S(1)}, f32[32,2048]{1,0:T(8,128)}, u32[]{:S(2)}) copy-start(f32[32,2048]{1,0:T(8,128)} %constant.76.clone) | copy-start | bytes 786436
  126.8 3.8 copy-start.24
  130.5 16.8 %collective-permute-start = (f32[2,8,2432]{2,1,0:T(8,128)S(1)}, f32[2,8,2432]{2,1,0:T(8,128)S(1)}, u32[]{:S(2)}, u32[]{:S(2)}) collective-permute-start(f32[2,8,2432]{2,1,0:T(8,128)S(1)} %pad_maximum_fusion), channel_id=1, source_target_pairs={{0,2},{1,3},{4,6},{5,7},{8,10},{9,11},{12,14},{13,15},{16,18},{17,... | collective-permute-start | bytes 466952 | tf_op jit(solution)/shard_map/ppermute | solution.py:1599
  135.3 12.1 %copy-start.13 = (f32[1,2048]{1,0:T(1,128)}, f32[1,2048]{1,0:T(1,128)S(1)}, u32[]{:S(2)}) copy-start(f32[1,2048]{1,0:T(1,128)S(1)} %fusion.11.refs_14_.refs_22_) | copy-start | bytes 24580
  137.2 7.5 copy-start.25
  141.9 5.4 copy-start.38
  141.9 5.4 copy-start.39
  141.9 5.5 copy-start.3
  141.9 5.5 copy-start.12
  141.9 5.5 copy-start.15
  141.9 5.5 copy-start.16
  141.9 5.5 copy-start.21
  144.7 151.8 %copy-start.17 = (s32[2,3]{1,0:T(2,128)}, s32[2,3]{1,0:T(2,128)S(1)}, u32[]{:S(2)}) copy-start(s32[2,3]{1,0:T(2,128)S(1)} %pad_add_fusion.1.refs_0_) | copy-start | bytes 76
  147.3 149.2 %copy-start.19 = (f32[1,128]{1,0:T(1,128)}, f32[1,128]{1,0:T(1,128)S(1)}, u32[]{:S(2)}) copy-start(f32[1,128]{1,0:T(1,128)S(1)} %get-tuple-element.143.refs_13_.refs_21_) | copy-start | bytes 1540
  147.3 149.2 %copy-start.20 = (f32[1,128]{1,0:T(1,128)}, f32[1,128]{1,0:T(1,128)S(1)}, u32[]{:S(2)}) copy-start(f32[1,128]{1,0:T(1,128)S(1)} %get-tuple-element.144.refs_12_.refs_20_) | copy-start | bytes 1540
  147.3 149.2 %copy-start.6 = (f32[2,8,2432]{2,1,0:T(8,128)}, f32[2,8,2432]{2,1,0:T(8,128)S(1)}, u32[]{:S(2)}) copy-start(f32[2,8,2432]{2,1,0:T(8,128)S(1)} %collective-permute-done.refs_3_.refs_6_) | copy-start | bytes 466948
  334.8 6.6 collective-permute-start.1
  334.9 6.6 copy-start.30
  334.9 6.6 copy-start.9
  334.9 6.6 copy-start.18
  341.5 24.0 %slice-start = ((s8[8388608]{0:T(1024)(128)(4,1)}), s8[4194304]{0:T(1024)(128)(4,1)S(1)}, s32[]{:S(2)}) async-start(s8[8388608]{0:T(1024)(128)(4,1)} %bitcast.126), calls=%async_computation | async-start | bytes 8388608
  341.6 23.9 %slice-start.1 = ((s8[8388608]{0:T(1024)(128)(4,1)}), s8[4194304]{0:T(1024)(128)(4,1)S(1)}, s32[]{:S(2)}) async-start(s8[8388608]{0:T(1024)(128)(4,1)} %bitcast.126), calls=%async_computation.1 | async-start | bytes 8388608
  365.4 13.0 %copy-start.41 = (bf16[1024,2048]{1,0:T(8,128)(2,1)S(1)}, bf16[1024,2048]{1,0:T(8,128)(2,1)}, u32[]{:S(2)}) copy-start(bf16[1024,2048]{1,0:T(8,128)(2,1)} %get-tuple-element.71) | copy-start | bytes 12582916
  378.5 14.7 %copy-start.27 = (bf16[2048,1024]{1,0:T(8,128)(2,1)S(1)}, bf16[2048,1024]{1,0:T(8,128)(2,1)}, u32[]{:S(2)}) copy-start(bf16[2048,1024]{1,0:T(8,128)(2,1)} %copy.55) | copy-start | bytes 12582916
  391.9 51.2 %collective-permute-start.2 = (f32[2,128,2048]{2,1,0:T(8,128)S(1)}, f32[2,128,2048]{2,1,0:T(8,128)S(1)}, u32[]{:S(2)}, u32[]{:S(2)}) collective-permute-start(f32[2,128,2048]{2,1,0:T(8,128)S(1)} %get-tuple-element.70), channel_id=1, source_target_pairs={{2,0},{3,1},{6,4},{7,5},{10,8},{11,9},{14,12},{15,13},{18,16},{19,... | collective-permute-start | bytes 6291464 | tf_op jit(solution)/shard_map/ppermute | solution.py:1599
  393.2 11.7 %copy-start.23 = (bf16[1024,2048]{1,0:T(8,128)(2,1)S(1)}, bf16[1024,2048]{1,0:T(8,128)(2,1)}, u32[]{:S(2)}) copy-start(bf16[1024,2048]{1,0:T(8,128)(2,1)} %copy-done.22) | copy-start | bytes 12582916
  393.2 11.7 %copy-start.40 = (bf16[1024,2048]{1,0:T(8,128)(2,1)S(1)}, bf16[1024,2048]{1,0:T(8,128)(2,1)}, u32[]{:S(2)}) copy-start(bf16[1024,2048]{1,0:T(8,128)(2,1)} %get-tuple-element.72) | copy-start | bytes 12582916
  622.6 7.0 collective-permute-start.3
  631.0 3.3 collective-permute-start.4
  631.1 48.6 %collective-permute-start.5 = (f32[1024,2048]{1,0:T(8,128)}, f32[1024,2048]{1,0:T(8,128)}, u32[]{:S(2)}, u32[]{:S(2)}) collective-permute-start(f32[1024,2048]{1,0:T(8,128)} %fusion.18.refs_28_.refs_5_), channel_id=1, source_target_pairs={{0,1},{1,0},{2,3},{3,2},{4,5},{5,4},{6,7},{7,6},{8,9},{9,8},{10,11... | collective-permute-start | bytes 25165832 | tf_op jit(solution)/shard_map/ppermute | solution.py:1604
  636.5 19.1 %copy-start.37 = (f32[8,256]{1,0:T(8,128)S(1)}, f32[8,256]{1,0:T(8,128)}, u32[]{:S(2)}) copy-start(f32[8,256]{1,0:T(8,128)} %get-tuple-element.81) | copy-start | bytes 24580
  636.5 21.0 %copy-start.33 = (f32[8,2048]{1,0:T(8,128)S(1)}, f32[8,2048]{1,0:T(8,128)}, u32[]{:S(2)}) copy-start(f32[8,2048]{1,0:T(8,128)} %get-tuple-element.80) | copy-start | bytes 196612
  636.5 21.2 %copy-start.29 = (f32[256,2048]{1,0:T(8,128)S(1)}, f32[256,2048]{1,0:T(8,128)}, u32[]{:S(2)}) copy-start(f32[256,2048]{1,0:T(8,128)} %get-tuple-element.90) | copy-start | bytes 6291460
  655.4 24.3 %collective-permute-start.6 = (f32[1024,2048]{1,0:T(8,128)}, f32[1024,2048]{1,0:T(8,128)}, u32[]{:S(2)}, u32[]{:S(2)}) collective-permute-start(f32[1024,2048]{1,0:T(8,128)} %convolution_add_fusion.refs_7_), channel_id=1, source_target_pairs={{0,1},{1,0},{2,3},{3,2},{4,5},{5,4},{6,7},{7,6},{8,9},{9,8},{10,11... | collective-permute-start | bytes 25165832 | tf_op jit(solution)/shard_map/ppermute | solution.py:1604
  655.6 5.3 collective-permute-start.7
  661.6 18.1 %copy-start.34 = (f32[1024]{0:T(1024)S(1)}, f32[1024]{0:T(1024)}, u32[]{:S(2)}) copy-start(f32[1024]{0:T(1024)} %get-tuple-element.133) | copy-start | bytes 12292
  798.1 17.4 %collective-permute-start.8 = (f32[256,256]{1,0:T(8,128)S(1)}, f32[256,256]{1,0:T(8,128)S(1)}, u32[]{:S(2)}, u32[]{:S(2)}) collective-permute-start(f32[256,256]{1,0:T(8,128)S(1)} %slice.154), channel_id=1, source_target_pairs={{0,1},{1,0},{2,3},{3,2},{4,5},{5,4},{6,7},{7,6},{8,9},{9,8},{10,11... | collective-permute-start | bytes 786440 | tf_op jit(solution)/shard_map/ppermute | solution.py:1604
  817.3 4.9 copy-start.26
  817.3 7.0 copy-start.1
  (5 other events, 6.2 us)

commit v7 on v6

--- a/solution.py
+++ b/solution.py
@@ -1718,7 +1718,7 @@
     (y_own, states, finals, coupled, carry, reach, entering, gate_full, out_full) = forward_ssd(
         jnp.stack(marks), micros, raw, rims, inner, twice, count,
         cw, cb, ccw, ccb, sbias, rate, skip, sel, selcol,
-        [in_weight[:, 0, :], jnp.transpose(out_weight)], sharing(4), 3,
+        [in_weight[:, 0, :], jnp.transpose(out_weight)], sharing(3), 3,
     )
     entering = jnp.where(place == 0, 0.0, entering)
     cot = cotangent[:, 0].reshape(micros * count, model)
@@ -1732,7 +1732,7 @@
         mixer, gate_in, norm_grad, carry, coupled, row_sums, gain_row, micros, inner_total
     )
     pulled = passed_along(own_pulls, "context", -1)
-    out_term = contract_rows(out_grad, gated_norm)
+    out_term = lax.optimization_barrier(contract_rows(out_grad, gated_norm))
     gate_term = contract_rows(normed, gate_grad)
     branch = contract_cols(gated_norm, out_full)
     gate_part = contract_cols(gate_grad, gate_full)

time: 832 us -> 822 us (0.988)
    unnamed x96 -> x92, local copies, waits for them, and re-layouts: 25 us -> 23.8 us
  transfers between devices with their start and end apart: 9 -> 9, of which waited for: 4 -> 5; matrix products, arithmetic and copies ran while one was open for 12% -> 11% of each run, Pallas kernels for 1% -> 1%
where the time goes in v7:
time: 822 us; the launch traced here: 816 us
  Pallas kernels  595 us (72%)
  matrix products  107 us (13%)
  local copies, waits for them, and re-layouts  47.9 us (6%)
  waiting for transfers between devices  37.5 us (5%)
  other arithmetic  19.3 us (2%)
    pallas_call x1, Pallas kernels, backward_ssd(): pl.pallas_call(functools.partial(backward_kernel, heads, chunks, plan, le...  177 us
    pallas_call x1, Pallas kernels, forward_ssd(): pl.pallas_call(functools.partial(forward_kernel, heads, chunks, plan), gr...  141 us
    pallas_call x1, Pallas kernels, finish(): pl.pallas_call(functools.partial(finish_kernel, plan, blocks), grid=(step...  117 us
    pallas_call x1, Pallas kernels, gather_weights(): pl.pallas_call(functools.partial(gather_kernel, plan), out_shape=[jax.Sha...  91.8 us
    dot_general x3, matrix products, contract_cols(): lax.dot_general(left, right, (((1,), (1,)), ((), ())), preferred_element_...  45 us
    dot_general x3, matrix products, contract_rows(): lax.dot_general(left, right, (((0,), (0,)), ((), ())), preferred_element_...  44.4 us
    pallas_call x1, Pallas kernels, gate_stage(): pl.pallas_call(gate_kernel, grid=(rows // size,), in_specs=[block(model),...  35.2 us
    ppermute x3, waiting for transfers between devices, passed_along(): lax.ppermute(value, axis, [(source, source + steps) for source in range(i...  32.3 us
  transfers between devices with their start and end apart: 9, of which 5 were waited for; matrix products, arithmetic and copies ran while one was open for 11% of the time, Pallas kernels for 1%

profile of v7, /device:TPU:0, one launch (start us, length us, event | category | flops | bytes accessed | tf_op | source)
XLA Modules:
  0.0 815.9 jit_solution(3719121085362447547)
XLA Ops:
  1.7 6.5 fusion.11
  9.0 1.1 fusion.1.refs_0_
  10.1 91.8 %shard_map.316 = (bf16[2048,2432]{1,0:T(8,128)(2,1)}, bf16[2,512,2048]{2,1,0:T(8,128)(2,1)}) custom-call(bf16[256,2432]{1,0:T(8,128)(2,1)} %fusion.1.refs_0_, bf16[2,512,2048]{2,1,0:T(8,128)(2,1)} %bitcast.92), custom_call_target="tpu_custom_call" | custom-call | tf_op jit(solution)/shard_map/pallas_call | solution.py:953
  102.0 2.2 copy-done.2
  104.1 2.2 copy-done.5
  106.3 3.2 shard_map.317
  109.5 17.2 %fusion.14.refs_1_.refs_2_.refs_4_.refs_5_.refs_7_ = f32[1024,2432]{1,0:T(8,128)S(1)} fusion(bf16[1024,2048]{1,0:T(8,128)(2,1)S(1)} %get-tuple-element.54.normed, bf16[2048,2432]{1,0:T(8,128)(2,1)} %get-tuple-element.55), kind=kOutput, calls=%fused_computation.63 | convolution fusion | flops 10200547328 | bytes 24117248 | tf_op jit(solution)/shard_map/dot_general | solution.py:1712
  126.8 3.7 copy-done.24
  130.5 3.8 collective-permute-start
  135.7 1.3 fusion.6
  137.6 4.7 broadcast_multiply_fusion.out_grad
  142.4 2.7 add_bitcast_fusion
  145.8 1.5 copy.47
  147.4 1.0 copy-done.7
  148.4 140.8 %shard_map.318 = (f32[1024,2048]{1,0:T(8,128)}, f32[8,128,2048]{2,1,0:T(8,128)}, f32[2,128,2048]{2,1,0:T(8,128)}, f32[1024,256]{1,0:T(8,128)S(1)}, f32[1024,2048...) custom-call(s32[2,3]{1,0:T(2,128)S(1)} %pad_add_fusion.1.refs_0_, ...), custom_call_target="tpu_custom_call" | custom-call | tf_op jit(solution)/shard_map/pallas_call | solution.py:310
  290.3 1.5 broadcast_select_fusion.entering.refs_13_
  291.9 35.2 %shard_map.319 = (f32[1024,2048]{1,0:T(8,128)}, f32[1024,2048]{1,0:T(8,128)}, f32[1024,2048]{1,0:T(8,128)}, f32[1024,128]{1,0:T(8,128)}) custom-call(bf16[1024,2048]{1,0:T(8,128)(2,1)} %copy-done.22, bf16[1024,2048]{1,0:T(8,128)(2,1)} %broadcast_multiply_fusion.out_grad, bf16[2048,2048]{1,0:T(8,128)(2,1)} %get-tuple-element.56.gate_weight, ...), custom_call_target="tpu_custom_call" | custom-call | flops 17179869184 | bytes 50331648 | tf_op jit(solution)/shard_map/pallas_call | solution.py:1039
  327.2 2.1 collective-permute-done.1
  329.3 1.1 add.75.sums
  330.4 23.6 %shard_map.320 = (bf16[1024,2048]{1,0:T(8,128)(2,1)}, bf16[1024,2048]{1,0:T(8,128)(2,1)}, f32[1024,2048]{1,0:T(8,128)}, f32[2,128,2048]{2,1,0:T(8,128)S(1)}, f32[8,2048]{1,0:T(8,128)S(1)}) custom-call(f32[1024,2048]{1,0:T(8,128)} %get-tuple-element.62.mixer.refs_9_, f32[1024,2048]{1,0:T(8,128)} %get-tuple-element.63.gate_in, ...), custom_call_target="tpu_custom_call" | custom-call | flops 2147483648 | bytes 50331648 | tf_op jit(solution)/shard_map/pallas_call | solution.py:1104
  354.0 14.9 %fusion.17.refs_28_.refs_5_ = f32[1024,2048]{1,0:T(8,128)} fusion(bf16[1024,2048]{1,0:T(8,128)(2,1)} %get-tuple-element.71, bf16[2048,2048]{1,0:T(8,128)(2,1)} %get-tuple-element.57.out_weight), kind=kOutput, calls=%fused_computation.66 | convolution fusion | flops 8589934592 | bytes 20971520 | tf_op jit(solution)/shard_map/dot_general | solution.py:1804
  368.9 14.5 %fusion.15 = f32[2048,2048]{1,0:T(8,128)} fusion(bf16[1024,2048]{1,0:T(8,128)(2,1)S(1)} %copy-done.26, bf16[1024,2048]{1,0:T(8,128)(2,1)} %get-tuple-element.71), kind=kOutput, calls=%fused_computation.64 | convolution fusion | flops 8589934592 | bytes 25165824 | tf_op jit(solution)/shard_map/dot_general | solution.py:1798
  383.4 1.3 collective-permute-start.2
  384.7 11.4 %fusion.18.refs_29_ = f32[1024,2048]{1,0:T(8,128)} fusion(bf16[1024,2048]{1,0:T(8,128)(2,1)S(1)} %copy-done.39, bf16[2048,2048]{1,0:T(8,128)(2,1)S(1)} %bitcast.121), kind=kOutput, calls=%fused_computation.67 | convolution fusion | flops 8589934592 | bytes 20971520 | tf_op jit(solution)/shard_map/dot_general | solution.py:1804
  396.1 11.9 %fusion.16 = f32[2048,2048]{1,0:T(8,128)} fusion(bf16[1024,2048]{1,0:T(8,128)(2,1)S(1)} %copy-done.23, bf16[1024,2048]{1,0:T(8,128)(2,1)S(1)} %copy-done.39), kind=kOutput, calls=%fused_computation.65 | convolution fusion | flops 8589934592 | bytes 25165824 | tf_op jit(solution)/shard_map/dot_general | solution.py:1798
  408.0 26.6 %collective-permute-done.2.refs_15_ = f32[2,128,2048]{2,1,0:T(8,128)S(1)} collective-permute-done((f32[2,128,2048]{2,1,0:T(8,128)S(1)}, f32[2,128,2048]{2,1,0:T(8,128)S(1)}, u32[]{:S(2)}, u32[]{:S(2)}) %collective-permute-start.2) | collective-permute-done | bytes 2097184 | tf_op jit(solution)/shard_map/ppermute | solution.py:1599
  434.6 1.3 copy-done.28
  435.9 177.1 %shard_map.321 = (bf16[1024,2432]{1,0:T(8,128)(2,1)}, f32[2,8,2048]{2,1,0:T(8,128)}, f32[2,8,2048]{2,1,0:T(8,128)}, f32[1024,256]{1,0:T(8,128)}, f32[2,8,256]{2,...) custom-call(s32[2,3]{1,0:T(2,128)} %copy-done.17, ...), custom_call_target="tpu_custom_call" | custom-call | tf_op jit(solution)/shard_map/pallas_call | solution.py:654
  613.9 1.3 collective-permute-start.3
  615.2 5.7 collective-permute-done.3
  621.0 1.3 pad_add_fusion
  623.8 1.8 collective-permute-done.4
  627.8 18.8 %convolution_add_fusion.refs_7_ = f32[1024,2048]{1,0:T(8,128)} fusion(f32[1024,2048]{1,0:T(8,128)} %fusion.18.refs_29_, bf16[1024,2432]{1,0:T(8,128)(2,1)} %fusion.4, bf16[2048,2432]{1,0:T(8,128)(2,1)} %get-tuple-element.55), kind=kOutput, calls=%fused_computation | convolution fusion | flops 10202644480 | bytes 31719424 | tf_op jit(solution)/shard_map/dot_general | solution.py:1804
  648.8 1.8 copy.51
  650.7 1.3 collective-permute-done.7
  652.7 18.1 %fusion.19 = f32[2048,2432]{1,0:T(8,128)} fusion(bf16[1024,2048]{1,0:T(8,128)(2,1)} %copy-done.22, bf16[1024,2432]{1,0:T(8,128)(2,1)} %fusion.4), kind=kOutput, calls=%fused_computation.68 | convolution fusion | flops 10200547328 | bytes 29097984 | tf_op jit(solution)/shard_map/dot_general | solution.py:1798
  670.8 1.0 broadcast_in_dim.23.refs_4_
  671.8 116.6 %shard_map.322 = (f32[256,2432]{1,0:T(8,128)}, bf16[1024,2048]{1,0:T(8,128)(2,1)}, bf16[1024,2048]{1,0:T(8,128)(2,1)}, f32[128,128]{1,0:T(8,128)}) custom-call(f32[4,2,256,2432]{3,2,1,0:T(8,128)} %bitcast.105, bf16[1024,2048]{1,0:T(8,128)(2,1)} %copy-done.4, bf16[1024,2048]{1,0:T(8,128)(2,1)} %bitcast.108, f32[1024,128]{1,0:T(8,128)} %copy-done.10, ...), custom_call_target="tpu_custom_call" | custom-call | tf_op jit(solution)/shard_map/pallas_call | solution.py:1559
  788.4 1.0 slice.154
  789.4 1.3 slice_bitcast_fusion.8
  790.7 1.2 slice_bitcast_fusion.6
  794.3 1.4 slice.177
  795.7 1.2 slice.176
  796.8 6.7 shard_map.323
  805.5 1.3 slice_bitcast_fusion.4
  806.8 1.7 slice_add_fusion.3
  808.5 4.9 copy.63
  813.5 2.0 copy.64
  (131 shorter events, 17.6 us)
Async XLA Ops:
  0.6 134.8 %copy-start = (f32[32]{0:T(128)S(1)}, f32[32]{0:T(128)}, u32[]{:S(2)}) copy-start(f32[32]{0:T(128)} %param.36) | copy-start | bytes 388
  1.6 7.2 copy-start.34
  1.7 7.3 copy-start.31
  8.8 93.1 %copy-start.14 = (f32[2048]{0:T(1024)S(1)}, f32[2048]{0:T(1024)}, u32[]{:S(2)}) copy-start(f32[2048]{0:T(1024)} %param.25) | copy-start | bytes 24580
  101.9 2.2 copy-start.2
  104.1 2.2 copy-start.5
  109.5 17.2 %copy-start.4 = (bf16[1024,2048]{1,0:T(8,128)(2,1)}, bf16[1024,2048]{1,0:T(8,128)(2,1)S(1)}, u32[]{:S(2)}) copy-start(bf16[1024,2048]{1,0:T(8,128)(2,1)S(1)} %get-tuple-element.78.refs_1_) | copy-start | bytes 12582916
  109.5 17.2 %copy-start.10 = (f32[1024,128]{1,0:T(8,128)}, f32[1024,128]{1,0:T(8,128)S(1)}, u32[]{:S(2)}) copy-start(f32[1024,128]{1,0:T(8,128)S(1)} %get-tuple-element.79.refs_3_) | copy-start | bytes 1572868
  109.5 17.2 %copy-start.22 = (bf16[1024,2048]{1,0:T(8,128)(2,1)}, bf16[1024,2048]{1,0:T(8,128)(2,1)S(1)}, u32[]{:S(2)}) copy-start(bf16[1024,2048]{1,0:T(8,128)(2,1)S(1)} %get-tuple-element.54.normed) | copy-start | bytes 12582916
  109.5 24.8 %copy-start.35 = (s32[2,1,2]{2,1,0:T(1,128)S(1)}, s32[2,1,2]{2,1,0:T(1,128)}, u32[]{:S(2)}) copy-start(s32[2,1,2]{2,1,0:T(1,128)} %param.22) | copy-start | bytes 52
  109.5 25.9 %copy-start.30 = (f32[32,2048]{1,0:T(8,128)S(1)}, f32[32,2048]{1,0:T(8,128)}, u32[]{:S(2)}) copy-start(f32[32,2048]{1,0:T(8,128)} %constant.76.clone) | copy-start | bytes 786436
  126.8 3.7 copy-start.24
  130.5 16.8 %collective-permute-start = (f32[2,8,2432]{2,1,0:T(8,128)S(1)}, f32[2,8,2432]{2,1,0:T(8,128)S(1)}, u32[]{:S(2)}, u32[]{:S(2)}) collective-permute-start(f32[2,8,2432]{2,1,0:T(8,128)S(1)} %pad_maximum_fusion), channel_id=1, source_target_pairs={{0,2},{1,3},{4,6},{5,7},{8,10},{9,11},{12,14},{13,15},{16,18},{17,... | collective-permute-start | bytes 466952 | tf_op jit(solution)/shard_map/ppermute | solution.py:1599
  135.7 11.6 %copy-start.13 = (f32[1,2048]{1,0:T(1,128)}, f32[1,2048]{1,0:T(1,128)S(1)}, u32[]{:S(2)}) copy-start(f32[1,2048]{1,0:T(1,128)S(1)} %fusion.9.refs_14_.refs_22_) | copy-start | bytes 24580
  137.6 7.5 copy-start.25
  142.3 4.9 copy-start.37
  142.3 5.0 copy-start.38
  142.3 5.0 copy-start.3
  142.3 5.0 copy-start.12
  142.3 5.0 copy-start.15
  142.3 5.0 copy-start.16
  142.4 5.0 copy-start.21
  145.1 144.2 %copy-start.17 = (s32[2,3]{1,0:T(2,128)}, s32[2,3]{1,0:T(2,128)S(1)}, u32[]{:S(2)}) copy-start(s32[2,3]{1,0:T(2,128)S(1)} %pad_add_fusion.1.refs_0_) | copy-start | bytes 76
  147.3 142.0 %copy-start.19 = (f32[1,128]{1,0:T(1,128)}, f32[1,128]{1,0:T(1,128)S(1)}, u32[]{:S(2)}) copy-start(f32[1,128]{1,0:T(1,128)S(1)} %get-tuple-element.143.refs_13_.refs_21_) | copy-start | bytes 1540
  147.3 142.0 %copy-start.20 = (f32[1,128]{1,0:T(1,128)}, f32[1,128]{1,0:T(1,128)S(1)}, u32[]{:S(2)}) copy-start(f32[1,128]{1,0:T(1,128)S(1)} %get-tuple-element.144.refs_12_.refs_20_) | copy-start | bytes 1540
  147.3 142.0 %copy-start.6 = (f32[2,8,2432]{2,1,0:T(8,128)}, f32[2,8,2432]{2,1,0:T(8,128)S(1)}, u32[]{:S(2)}) copy-start(f32[2,8,2432]{2,1,0:T(8,128)S(1)} %collective-permute-done.refs_3_.refs_6_) | copy-start | bytes 466948
  290.3 1.5 copy-start.11
  291.8 38.5 %copy-start.9 = (f32[1024,256]{1,0:T(8,128)S(1)}, f32[1024,256]{1,0:T(8,128)}, u32[]{:S(2)}) copy-start(f32[1024,256]{1,0:T(8,128)} %copy-done.8) | copy-start | bytes 3145732
  291.9 38.6 %copy-start.18 = (f32[2048]{0:T(1024)S(1)}, f32[2048]{0:T(1024)}, u32[]{:S(2)}) copy-start(f32[2048]{0:T(1024)} %param.37) | copy-start | bytes 24580
  327.1 2.2 collective-permute-start.1
  330.4 54.3 %slice-start = ((s8[8388608]{0:T(1024)(128)(4,1)}), s8[4194304]{0:T(1024)(128)(4,1)S(1)}, s32[]{:S(2)}) async-start(s8[8388608]{0:T(1024)(128)(4,1)} %bitcast.120), calls=%async_computation | async-start | bytes 8388608
  354.0 14.9 %copy-start.26 = (bf16[1024,2048]{1,0:T(8,128)(2,1)S(1)}, bf16[1024,2048]{1,0:T(8,128)(2,1)}, u32[]{:S(2)}) copy-start(bf16[1024,2048]{1,0:T(8,128)(2,1)} %broadcast_multiply_fusion.out_grad) | copy-start | bytes 12582916
  354.0 30.7 %slice-start.1 = ((s8[8388608]{0:T(1024)(128)(4,1)}), s8[4194304]{0:T(1024)(128)(4,1)S(1)}, s32[]{:S(2)}) async-start(s8[8388608]{0:T(1024)(128)(4,1)} %bitcast.120), calls=%async_computation.1 | async-start | bytes 8388608
  368.9 15.8 %copy-start.39 = (bf16[1024,2048]{1,0:T(8,128)(2,1)S(1)}, bf16[1024,2048]{1,0:T(8,128)(2,1)}, u32[]{:S(2)}) copy-start(bf16[1024,2048]{1,0:T(8,128)(2,1)} %get-tuple-element.72) | copy-start | bytes 12582916
  383.4 51.2 %collective-permute-start.2 = (f32[2,128,2048]{2,1,0:T(8,128)S(1)}, f32[2,128,2048]{2,1,0:T(8,128)S(1)}, u32[]{:S(2)}, u32[]{:S(2)}) collective-permute-start(f32[2,128,2048]{2,1,0:T(8,128)S(1)} %get-tuple-element.70), channel_id=1, source_target_pairs={{2,0},{3,1},{6,4},{7,5},{10,8},{11,9},{14,12},{15,13},{18,16},{19,... | collective-permute-start | bytes 6291464 | tf_op jit(solution)/shard_map/ppermute | solution.py:1599
  384.7 11.4 %copy-start.23 = (bf16[1024,2048]{1,0:T(8,128)(2,1)S(1)}, bf16[1024,2048]{1,0:T(8,128)(2,1)}, u32[]{:S(2)}) copy-start(bf16[1024,2048]{1,0:T(8,128)(2,1)} %copy-done.22) | copy-start | bytes 12582916
  613.9 7.0 collective-permute-start.3
  622.3 3.3 collective-permute-start.4
  622.4 48.4 %collective-permute-start.5 = (f32[1024,2048]{1,0:T(8,128)}, f32[1024,2048]{1,0:T(8,128)}, u32[]{:S(2)}, u32[]{:S(2)}) collective-permute-start(f32[1024,2048]{1,0:T(8,128)} %fusion.17.refs_28_.refs_5_), channel_id=1, source_target_pairs={{0,1},{1,0},{2,3},{3,2},{4,5},{5,4},{6,7},{7,6},{8,9},{9,8},{10,11... | collective-permute-start | bytes 25165832 | tf_op jit(solution)/shard_map/ppermute | solution.py:1604
  627.8 18.9 %copy-start.36 = (f32[8,256]{1,0:T(8,128)S(1)}, f32[8,256]{1,0:T(8,128)}, u32[]{:S(2)}) copy-start(f32[8,256]{1,0:T(8,128)} %get-tuple-element.81) | copy-start | bytes 24580
  627.8 20.9 %copy-start.32 = (f32[8,2048]{1,0:T(8,128)S(1)}, f32[8,2048]{1,0:T(8,128)}, u32[]{:S(2)}) copy-start(f32[8,2048]{1,0:T(8,128)} %get-tuple-element.80) | copy-start | bytes 196612
  627.8 21.0 %copy-start.29 = (f32[256,2048]{1,0:T(8,128)S(1)}, f32[256,2048]{1,0:T(8,128)}, u32[]{:S(2)}) copy-start(f32[256,2048]{1,0:T(8,128)} %get-tuple-element.90) | copy-start | bytes 6291460
  646.6 24.2 %collective-permute-start.6 = (f32[1024,2048]{1,0:T(8,128)}, f32[1024,2048]{1,0:T(8,128)}, u32[]{:S(2)}, u32[]{:S(2)}) collective-permute-start(f32[1024,2048]{1,0:T(8,128)} %convolution_add_fusion.refs_7_), channel_id=1, source_target_pairs={{0,1},{1,0},{2,3},{3,2},{4,5},{5,4},{6,7},{7,6},{8,9},{9,8},{10,11... | collective-permute-start | bytes 25165832 | tf_op jit(solution)/shard_map/ppermute | solution.py:1604
  646.7 5.3 collective-permute-start.7
  652.7 18.1 %copy-start.33 = (f32[1024]{0:T(1024)S(1)}, f32[1024]{0:T(1024)}, u32[]{:S(2)}) copy-start(f32[1024]{0:T(1024)} %get-tuple-element.133) | copy-start | bytes 12292
  789.4 17.5 %collective-permute-start.8 = (f32[256,256]{1,0:T(8,128)S(1)}, f32[256,256]{1,0:T(8,128)S(1)}, u32[]{:S(2)}, u32[]{:S(2)}) collective-permute-start(f32[256,256]{1,0:T(8,128)S(1)} %slice.154), channel_id=1, source_target_pairs={{0,1},{1,0},{2,3},{3,2},{4,5},{5,4},{6,7},{7,6},{8,9},{9,8},{10,11... | collective-permute-start | bytes 786440 | tf_op jit(solution)/shard_map/ppermute | solution.py:1604
  808.5 4.9 copy-start.27
  808.5 7.0 copy-start.1
  (3 other events, 3.3 us)

commit v8 on v7

--- a/solution.py
+++ b/solution.py
@@ -289,7 +289,7 @@
     eighth = CHUNK // 8
     pairs = lax.axis_size("fsdp") // 2
     shard_rows = shards[0].shape[0]
-    plan = Gathering(shard_rows, pairs, [shard.shape[1] for shard in shards], 2, shared)
+    plan = Gathering(shard_rows, pairs, [shard.shape[1] for shard in shards], 3, shared)
 
     def part(count, start):
         return pl.BlockSpec((CHUNK, count), lambda step: (step, start // count))
@@ -947,7 +947,7 @@
     rows = shards[0].shape[0]
     pairs = lax.axis_size("fsdp") // 2
     count = len(shards)
-    plan = Gathering(rows, pairs, [shard.shape[1] for shard in shards], 2, shared)
+    plan = Gathering(rows, pairs, [shard.shape[1] for shard in shards], 3, shared)
     hbm = pl.BlockSpec(memory_space=pl.ANY)
     dma = pltpu.SemaphoreType.DMA
     return pl.pallas_call(

time: 822 us -> 837 us (1.018)
  Pallas kernels: 595 us -> 610 us
    pallas_call x1, Pallas kernels: 141 us -> 155 us  [forward_ssd(): pl.pallas_call(functools.partial(forward_kernel, heads, chunks, plan), gr...]
where the time goes in v8:
time: 837 us; the launch traced here: 829 us
  Pallas kernels  610 us (73%)
  matrix products  107 us (13%)
  local copies, waits for them, and re-layouts  48.4 us (6%)
  waiting for transfers between devices  35.9 us (4%)
  other arithmetic  19.3 us (2%)
    pallas_call x1, Pallas kernels, backward_ssd(): pl.pallas_call(functools.partial(backward_kernel, heads, chunks, plan, le...  178 us
    pallas_call x1, Pallas kernels, forward_ssd(): pl.pallas_call(functools.partial(forward_kernel, heads, chunks, plan), gr...  155 us
    pallas_call x1, Pallas kernels, finish(): pl.pallas_call(functools.partial(finish_kernel, plan, blocks), grid=(step...  116 us
    pallas_call x1, Pallas kernels, gather_weights(): pl.pallas_call(functools.partial(gather_kernel, plan), out_shape=[jax.Sha...  92.9 us
    dot_general x3, matrix products, contract_cols(): lax.dot_general(left, right, (((1,), (1,)), ((), ())), preferred_element_...  45 us
    dot_general x3, matrix products, contract_rows(): lax.dot_general(left, right, (((0,), (0,)), ((), ())), preferred_element_...  44.4 us
    pallas_call x1, Pallas kernels, gate_stage(): pl.pallas_call(gate_kernel, grid=(rows // size,), in_specs=[block(model),...  35.2 us
    ppermute x3, waiting for transfers between devices, passed_along(): lax.ppermute(value, axis, [(source, source + steps) for source in range(i...  30.7 us
  transfers between devices with their start and end apart: 9, of which 5 were waited for; matrix products, arithmetic and copies ran while one was open for 11% of the time, Pallas kernels for 1%

profile of v8, /device:TPU:0, one launch (start us, length us, event | category | flops | bytes accessed | tf_op | source)
XLA Modules:
  0.0 829.5 jit_solution(10082015133010250646)
XLA Ops:
  1.7 6.5 fusion.11
  9.0 1.1 fusion.1.refs_0_
  10.1 92.9 %shard_map.316 = (bf16[2048,2432]{1,0:T(8,128)(2,1)}, bf16[2,512,2048]{2,1,0:T(8,128)(2,1)}) custom-call(bf16[256,2432]{1,0:T(8,128)(2,1)} %fusion.1.refs_0_, bf16[2,512,2048]{2,1,0:T(8,128)(2,1)} %bitcast.92), custom_call_target="tpu_custom_call" | custom-call | tf_op jit(solution)/shard_map/pallas_call | solution.py:953
  103.1 2.2 copy-done.2
  105.3 2.2 copy-done.5
  107.4 3.2 shard_map.317
  110.7 17.2 %fusion.14.refs_1_.refs_2_.refs_4_.refs_5_.refs_7_ = f32[1024,2432]{1,0:T(8,128)S(1)} fusion(bf16[1024,2048]{1,0:T(8,128)(2,1)S(1)} %get-tuple-element.54.normed, bf16[2048,2432]{1,0:T(8,128)(2,1)} %get-tuple-element.55), kind=kOutput, calls=%fused_computation.63 | convolution fusion | flops 10200547328 | bytes 24117248 | tf_op jit(solution)/shard_map/dot_general | solution.py:1712
  127.9 3.7 copy-done.24
  131.6 3.2 collective-permute-start
  136.3 1.3 fusion.6
  138.2 4.7 broadcast_multiply_fusion.out_grad
  142.9 2.7 add_bitcast_fusion
  146.3 2.0 copy.47
  148.4 1.0 copy-done.7
  149.5 155.0 %shard_map.318 = (f32[1024,2048]{1,0:T(8,128)}, f32[8,128,2048]{2,1,0:T(8,128)}, f32[2,128,2048]{2,1,0:T(8,128)}, f32[1024,256]{1,0:T(8,128)S(1)}, f32[1024,2048...) custom-call(s32[2,3]{1,0:T(2,128)S(1)} %pad_add_fusion.1.refs_0_, ...), custom_call_target="tpu_custom_call" | custom-call | tf_op jit(solution)/shard_map/pallas_call | solution.py:310
  305.5 1.5 broadcast_select_fusion.entering.refs_13_
  307.0 35.2 %shard_map.319 = (f32[1024,2048]{1,0:T(8,128)}, f32[1024,2048]{1,0:T(8,128)}, f32[1024,2048]{1,0:T(8,128)}, f32[1024,128]{1,0:T(8,128)}) custom-call(bf16[1024,2048]{1,0:T(8,128)(2,1)} %copy-done.22, bf16[1024,2048]{1,0:T(8,128)(2,1)} %broadcast_multiply_fusion.out_grad, bf16[2048,2048]{1,0:T(8,128)(2,1)} %get-tuple-element.56.gate_weight, ...), custom_call_target="tpu_custom_call" | custom-call | flops 17179869184 | bytes 50331648 | tf_op jit(solution)/shard_map/pallas_call | solution.py:1039
  342.3 2.1 collective-permute-done.1
  344.5 1.1 add.75.sums
  345.6 23.6 %shard_map.320 = (bf16[1024,2048]{1,0:T(8,128)(2,1)}, bf16[1024,2048]{1,0:T(8,128)(2,1)}, f32[1024,2048]{1,0:T(8,128)}, f32[2,128,2048]{2,1,0:T(8,128)S(1)}, f32[8,2048]{1,0:T(8,128)S(1)}) custom-call(f32[1024,2048]{1,0:T(8,128)} %get-tuple-element.62.mixer.refs_9_, f32[1024,2048]{1,0:T(8,128)} %get-tuple-element.63.gate_in, ...), custom_call_target="tpu_custom_call" | custom-call | flops 2147483648 | bytes 50331648 | tf_op jit(solution)/shard_map/pallas_call | solution.py:1104
  369.2 14.9 %fusion.17.refs_28_.refs_5_ = f32[1024,2048]{1,0:T(8,128)} fusion(bf16[1024,2048]{1,0:T(8,128)(2,1)} %get-tuple-element.71, bf16[2048,2048]{1,0:T(8,128)(2,1)} %get-tuple-element.57.out_weight), kind=kOutput, calls=%fused_computation.66 | convolution fusion | flops 8589934592 | bytes 20971520 | tf_op jit(solution)/shard_map/dot_general | solution.py:1804
  384.1 14.5 %fusion.15 = f32[2048,2048]{1,0:T(8,128)} fusion(bf16[1024,2048]{1,0:T(8,128)(2,1)S(1)} %copy-done.26, bf16[1024,2048]{1,0:T(8,128)(2,1)} %get-tuple-element.71), kind=kOutput, calls=%fused_computation.64 | convolution fusion | flops 8589934592 | bytes 25165824 | tf_op jit(solution)/shard_map/dot_general | solution.py:1798
  398.6 1.3 collective-permute-start.2
  399.9 11.4 %fusion.18.refs_29_ = f32[1024,2048]{1,0:T(8,128)} fusion(bf16[1024,2048]{1,0:T(8,128)(2,1)S(1)} %copy-done.39, bf16[2048,2048]{1,0:T(8,128)(2,1)S(1)} %bitcast.121), kind=kOutput, calls=%fused_computation.67 | convolution fusion | flops 8589934592 | bytes 20971520 | tf_op jit(solution)/shard_map/dot_general | solution.py:1804
  411.3 11.9 %fusion.16 = f32[2048,2048]{1,0:T(8,128)} fusion(bf16[1024,2048]{1,0:T(8,128)(2,1)S(1)} %copy-done.23, bf16[1024,2048]{1,0:T(8,128)(2,1)S(1)} %copy-done.39), kind=kOutput, calls=%fused_computation.65 | convolution fusion | flops 8589934592 | bytes 25165824 | tf_op jit(solution)/shard_map/dot_general | solution.py:1798
  423.2 25.0 %collective-permute-done.2.refs_15_ = f32[2,128,2048]{2,1,0:T(8,128)S(1)} collective-permute-done((f32[2,128,2048]{2,1,0:T(8,128)S(1)}, f32[2,128,2048]{2,1,0:T(8,128)S(1)}, u32[]{:S(2)}, u32[]{:S(2)}) %collective-permute-start.2) | collective-permute-done | bytes 2097184 | tf_op jit(solution)/shard_map/ppermute | solution.py:1599
  448.2 1.3 copy-done.28
  449.5 177.8 %shard_map.321 = (bf16[1024,2432]{1,0:T(8,128)(2,1)}, f32[2,8,2048]{2,1,0:T(8,128)}, f32[2,8,2048]{2,1,0:T(8,128)}, f32[1024,256]{1,0:T(8,128)}, f32[2,8,256]{2,...) custom-call(s32[2,3]{1,0:T(2,128)} %copy-done.17, ...), custom_call_target="tpu_custom_call" | custom-call | tf_op jit(solution)/shard_map/pallas_call | solution.py:654
  628.3 1.3 collective-permute-start.3
  629.6 5.7 collective-permute-done.3
  635.3 1.3 pad_add_fusion
  638.1 1.8 collective-permute-done.4
  642.1 18.8 %convolution_add_fusion.refs_7_ = f32[1024,2048]{1,0:T(8,128)} fusion(f32[1024,2048]{1,0:T(8,128)} %fusion.18.refs_29_, bf16[1024,2432]{1,0:T(8,128)(2,1)} %fusion.4, bf16[2048,2432]{1,0:T(8,128)(2,1)} %get-tuple-element.55), kind=kOutput, calls=%fused_computation | convolution fusion | flops 10202644480 | bytes 31719424 | tf_op jit(solution)/shard_map/dot_general | solution.py:1804
  663.1 1.8 copy.51
  665.1 1.3 collective-permute-done.7
  667.1 18.1 %fusion.19 = f32[2048,2432]{1,0:T(8,128)} fusion(bf16[1024,2048]{1,0:T(8,128)(2,1)} %copy-done.22, bf16[1024,2432]{1,0:T(8,128)(2,1)} %fusion.4), kind=kOutput, calls=%fused_computation.68 | convolution fusion | flops 10200547328 | bytes 29097984 | tf_op jit(solution)/shard_map/dot_general | solution.py:1798
  685.1 1.0 broadcast_in_dim.23.refs_4_
  686.1 115.8 %shard_map.322 = (f32[256,2432]{1,0:T(8,128)}, bf16[1024,2048]{1,0:T(8,128)(2,1)}, bf16[1024,2048]{1,0:T(8,128)(2,1)}, f32[128,128]{1,0:T(8,128)}) custom-call(f32[4,2,256,2432]{3,2,1,0:T(8,128)} %bitcast.105, bf16[1024,2048]{1,0:T(8,128)(2,1)} %copy-done.4, bf16[1024,2048]{1,0:T(8,128)(2,1)} %bitcast.108, f32[1024,128]{1,0:T(8,128)} %copy-done.10, ...), custom_call_target="tpu_custom_call" | custom-call | tf_op jit(solution)/shard_map/pallas_call | solution.py:1559
  801.9 1.0 slice.154
  803.0 1.3 slice_bitcast_fusion.8
  804.3 1.2 slice_bitcast_fusion.6
  807.8 1.4 slice.177
  809.2 1.2 slice.176
  810.4 6.7 shard_map.323
  819.1 1.3 slice_bitcast_fusion.4
  820.4 1.7 slice_add_fusion.3
  822.1 4.9 copy.63
  827.0 2.0 copy.64
  (131 shorter events, 17.6 us)
Async XLA Ops:
  0.6 135.3 %copy-start = (f32[32]{0:T(128)S(1)}, f32[32]{0:T(128)}, u32[]{:S(2)}) copy-start(f32[32]{0:T(128)} %param.36) | copy-start | bytes 388
  1.6 7.2 copy-start.34
  1.7 7.3 copy-start.31
  8.8 94.2 %copy-start.14 = (f32[2048]{0:T(1024)S(1)}, f32[2048]{0:T(1024)}, u32[]{:S(2)}) copy-start(f32[2048]{0:T(1024)} %param.25) | copy-start | bytes 24580
  103.1 2.2 copy-start.2
  105.3 2.2 copy-start.5
  110.6 17.2 %copy-start.4 = (bf16[1024,2048]{1,0:T(8,128)(2,1)}, bf16[1024,2048]{1,0:T(8,128)(2,1)S(1)}, u32[]{:S(2)}) copy-start(bf16[1024,2048]{1,0:T(8,128)(2,1)S(1)} %get-tuple-element.78.refs_1_) | copy-start | bytes 12582916
  110.6 17.2 %copy-start.10 = (f32[1024,128]{1,0:T(8,128)}, f32[1024,128]{1,0:T(8,128)S(1)}, u32[]{:S(2)}) copy-start(f32[1024,128]{1,0:T(8,128)S(1)} %get-tuple-element.79.refs_3_) | copy-start | bytes 1572868
  110.6 17.2 %copy-start.22 = (bf16[1024,2048]{1,0:T(8,128)(2,1)}, bf16[1024,2048]{1,0:T(8,128)(2,1)S(1)}, u32[]{:S(2)}) copy-start(bf16[1024,2048]{1,0:T(8,128)(2,1)S(1)} %get-tuple-element.54.normed) | copy-start | bytes 12582916
  110.6 24.2 %copy-start.35 = (s32[2,1,2]{2,1,0:T(1,128)S(1)}, s32[2,1,2]{2,1,0:T(1,128)}, u32[]{:S(2)}) copy-start(s32[2,1,2]{2,1,0:T(1,128)} %param.22) | copy-start | bytes 52
  110.7 25.3 %copy-start.30 = (f32[32,2048]{1,0:T(8,128)S(1)}, f32[32,2048]{1,0:T(8,128)}, u32[]{:S(2)}) copy-start(f32[32,2048]{1,0:T(8,128)} %constant.76.clone) | copy-start | bytes 786436
  127.9 3.7 copy-start.24
  131.6 16.7 %collective-permute-start = (f32[2,8,2432]{2,1,0:T(8,128)S(1)}, f32[2,8,2432]{2,1,0:T(8,128)S(1)}, u32[]{:S(2)}, u32[]{:S(2)}) collective-permute-start(f32[2,8,2432]{2,1,0:T(8,128)S(1)} %pad_maximum_fusion), channel_id=1, source_target_pairs={{0,2},{1,3},{4,6},{5,7},{8,10},{9,11},{12,14},{13,15},{16,18},{17,... | collective-permute-start | bytes 466952 | tf_op jit(solution)/shard_map/ppermute | solution.py:1599
  136.3 12.1 %copy-start.13 = (f32[1,2048]{1,0:T(1,128)}, f32[1,2048]{1,0:T(1,128)S(1)}, u32[]{:S(2)}) copy-start(f32[1,2048]{1,0:T(1,128)S(1)} %fusion.9.refs_14_.refs_22_) | copy-start | bytes 24580
  138.2 7.5 copy-start.25
  142.9 5.4 copy-start.37
  142.9 5.4 copy-start.38
  142.9 5.5 copy-start.3
  142.9 5.5 copy-start.12
  142.9 5.5 copy-start.15
  142.9 5.5 copy-start.16
  142.9 5.5 copy-start.21
  145.7 158.8 %copy-start.17 = (s32[2,3]{1,0:T(2,128)}, s32[2,3]{1,0:T(2,128)S(1)}, u32[]{:S(2)}) copy-start(s32[2,3]{1,0:T(2,128)S(1)} %pad_add_fusion.1.refs_0_) | copy-start | bytes 76
  148.3 156.2 %copy-start.19 = (f32[1,128]{1,0:T(1,128)}, f32[1,128]{1,0:T(1,128)S(1)}, u32[]{:S(2)}) copy-start(f32[1,128]{1,0:T(1,128)S(1)} %get-tuple-element.143.refs_13_.refs_21_) | copy-start | bytes 1540
  148.3 156.2 %copy-start.20 = (f32[1,128]{1,0:T(1,128)}, f32[1,128]{1,0:T(1,128)S(1)}, u32[]{:S(2)}) copy-start(f32[1,128]{1,0:T(1,128)S(1)} %get-tuple-element.144.refs_12_.refs_20_) | copy-start | bytes 1540
  148.3 156.2 %copy-start.6 = (f32[2,8,2432]{2,1,0:T(8,128)}, f32[2,8,2432]{2,1,0:T(8,128)S(1)}, u32[]{:S(2)}) copy-start(f32[2,8,2432]{2,1,0:T(8,128)S(1)} %collective-permute-done.refs_3_.refs_6_) | copy-start | bytes 466948
  305.5 1.5 copy-start.11
  307.0 38.6 %copy-start.9 = (f32[1024,256]{1,0:T(8,128)S(1)}, f32[1024,256]{1,0:T(8,128)}, u32[]{:S(2)}) copy-start(f32[1024,256]{1,0:T(8,128)} %copy-done.8) | copy-start | bytes 3145732
  307.0 38.6 %copy-start.18 = (f32[2048]{0:T(1024)S(1)}, f32[2048]{0:T(1024)}, u32[]{:S(2)}) copy-start(f32[2048]{0:T(1024)} %param.37) | copy-start | bytes 24580
  342.3 2.2 collective-permute-start.1
  345.6 54.3 %slice-start = ((s8[8388608]{0:T(1024)(128)(4,1)}), s8[4194304]{0:T(1024)(128)(4,1)S(1)}, s32[]{:S(2)}) async-start(s8[8388608]{0:T(1024)(128)(4,1)} %bitcast.120), calls=%async_computation | async-start | bytes 8388608
  369.2 14.9 %copy-start.26 = (bf16[1024,2048]{1,0:T(8,128)(2,1)S(1)}, bf16[1024,2048]{1,0:T(8,128)(2,1)}, u32[]{:S(2)}) copy-start(bf16[1024,2048]{1,0:T(8,128)(2,1)} %broadcast_multiply_fusion.out_grad) | copy-start | bytes 12582916
  369.2 30.7 %slice-start.1 = ((s8[8388608]{0:T(1024)(128)(4,1)}), s8[4194304]{0:T(1024)(128)(4,1)S(1)}, s32[]{:S(2)}) async-start(s8[8388608]{0:T(1024)(128)(4,1)} %bitcast.120), calls=%async_computation.1 | async-start | bytes 8388608
  384.1 15.8 %copy-start.39 = (bf16[1024,2048]{1,0:T(8,128)(2,1)S(1)}, bf16[1024,2048]{1,0:T(8,128)(2,1)}, u32[]{:S(2)}) copy-start(bf16[1024,2048]{1,0:T(8,128)(2,1)} %get-tuple-element.72) | copy-start | bytes 12582916
  398.6 49.6 %collective-permute-start.2 = (f32[2,128,2048]{2,1,0:T(8,128)S(1)}, f32[2,128,2048]{2,1,0:T(8,128)S(1)}, u32[]{:S(2)}, u32[]{:S(2)}) collective-permute-start(f32[2,128,2048]{2,1,0:T(8,128)S(1)} %get-tuple-element.70), channel_id=1, source_target_pairs={{2,0},{3,1},{6,4},{7,5},{10,8},{11,9},{14,12},{15,13},{18,16},{19,... | collective-permute-start | bytes 6291464 | tf_op jit(solution)/shard_map/ppermute | solution.py:1599
  399.9 11.4 %copy-start.23 = (bf16[1024,2048]{1,0:T(8,128)(2,1)S(1)}, bf16[1024,2048]{1,0:T(8,128)(2,1)}, u32[]{:S(2)}) copy-start(bf16[1024,2048]{1,0:T(8,128)(2,1)} %copy-done.22) | copy-start | bytes 12582916
  628.3 7.0 collective-permute-start.3
  636.6 3.3 collective-permute-start.4
  636.7 48.4 %collective-permute-start.5 = (f32[1024,2048]{1,0:T(8,128)}, f32[1024,2048]{1,0:T(8,128)}, u32[]{:S(2)}, u32[]{:S(2)}) collective-permute-start(f32[1024,2048]{1,0:T(8,128)} %fusion.17.refs_28_.refs_5_), channel_id=1, source_target_pairs={{0,1},{1,0},{2,3},{3,2},{4,5},{5,4},{6,7},{7,6},{8,9},{9,8},{10,11... | collective-permute-start | bytes 25165832 | tf_op jit(solution)/shard_map/ppermute | solution.py:1604
  642.1 18.9 %copy-start.36 = (f32[8,256]{1,0:T(8,128)S(1)}, f32[8,256]{1,0:T(8,128)}, u32[]{:S(2)}) copy-start(f32[8,256]{1,0:T(8,128)} %get-tuple-element.81) | copy-start | bytes 24580
  642.1 20.9 %copy-start.32 = (f32[8,2048]{1,0:T(8,128)S(1)}, f32[8,2048]{1,0:T(8,128)}, u32[]{:S(2)}) copy-start(f32[8,2048]{1,0:T(8,128)} %get-tuple-element.80) | copy-start | bytes 196612
  642.1 21.0 %copy-start.29 = (f32[256,2048]{1,0:T(8,128)S(1)}, f32[256,2048]{1,0:T(8,128)}, u32[]{:S(2)}) copy-start(f32[256,2048]{1,0:T(8,128)} %get-tuple-element.90) | copy-start | bytes 6291460
  660.9 24.2 %collective-permute-start.6 = (f32[1024,2048]{1,0:T(8,128)}, f32[1024,2048]{1,0:T(8,128)}, u32[]{:S(2)}, u32[]{:S(2)}) collective-permute-start(f32[1024,2048]{1,0:T(8,128)} %convolution_add_fusion.refs_7_), channel_id=1, source_target_pairs={{0,1},{1,0},{2,3},{3,2},{4,5},{5,4},{6,7},{7,6},{8,9},{9,8},{10,11... | collective-permute-start | bytes 25165832 | tf_op jit(solution)/shard_map/ppermute | solution.py:1604
  661.1 5.3 collective-permute-start.7
  667.1 18.1 %copy-start.33 = (f32[1024]{0:T(1024)S(1)}, f32[1024]{0:T(1024)}, u32[]{:S(2)}) copy-start(f32[1024]{0:T(1024)} %get-tuple-element.133) | copy-start | bytes 12292
  802.9 17.5 %collective-permute-start.8 = (f32[256,256]{1,0:T(8,128)S(1)}, f32[256,256]{1,0:T(8,128)S(1)}, u32[]{:S(2)}, u32[]{:S(2)}) collective-permute-start(f32[256,256]{1,0:T(8,128)S(1)} %slice.154), channel_id=1, source_target_pairs={{0,1},{1,0},{2,3},{3,2},{4,5},{5,4},{6,7},{7,6},{8,9},{9,8},{10,11... | collective-permute-start | bytes 786440 | tf_op jit(solution)/shard_map/ppermute | solution.py:1604
  822.1 4.9 copy-start.27
  822.1 7.0 copy-start.1
  (3 other events, 3.3 us)

commit v9 on v7

--- a/solution.py
+++ b/solution.py
@@ -371,7 +371,7 @@
             for shard in shards
         ],
         compiler_params=pltpu.CompilerParams(
-            collective_id=collective_id, has_side_effects=True, vmem_limit_bytes=48 * 1024 * 1024
+            collective_id=collective_id, has_side_effects=True, vmem_limit_bytes=60 * 1024 * 1024
         ),
     )(
         marks, raw, raw, rims, raw, raw, rims, raw, cw, cb, ccw, ccb, sbias, rate, skip, sel, selcol,

time: 822 us -> 823 us (level)
    unnamed x92 -> x68, local copies, waits for them, and re-layouts: 23.8 us -> 23.4 us
where the time goes in v9:
time: 823 us; the launch traced here: 817 us
  Pallas kernels  596 us (72%)
  matrix products  107 us (13%)
  local copies, waits for them, and re-layouts  47 us (6%)
  waiting for transfers between devices  37.6 us (5%)
  other arithmetic  19.7 us (2%)
    pallas_call x1, Pallas kernels, backward_ssd(): pl.pallas_call(functools.partial(backward_kernel, heads, chunks, plan, le...  177 us
    pallas_call x1, Pallas kernels, forward_ssd(): pl.pallas_call(functools.partial(forward_kernel, heads, chunks, plan), gr...  142 us
    pallas_call x1, Pallas kernels, finish(): pl.pallas_call(functools.partial(finish_kernel, plan, blocks), grid=(step...  116 us
    pallas_call x1, Pallas kernels, gather_weights(): pl.pallas_call(functools.partial(gather_kernel, plan), out_shape=[jax.Sha...  91.8 us
    dot_general x3, matrix products, contract_cols(): lax.dot_general(left, right, (((1,), (1,)), ((), ())), preferred_element_...  45 us
    dot_general x3, matrix products, contract_rows(): lax.dot_general(left, right, (((0,), (0,)), ((), ())), preferred_element_...  44.4 us
    pallas_call x1, Pallas kernels, gate_stage(): pl.pallas_call(gate_kernel, grid=(rows // size,), in_specs=[block(model),...  35.3 us
    ppermute x3, waiting for transfers between devices, passed_along(): lax.ppermute(value, axis, [(source, source + steps) for source in range(i...  32.4 us
  transfers between devices with their start and end apart: 9, of which 5 were waited for; matrix products, arithmetic and copies ran while one was open for 11% of the time, Pallas kernels for 1%

profile of v9, /device:TPU:0, one launch (start us, length us, event | category | flops | bytes accessed | tf_op | source)
XLA Modules:
  0.0 817.0 jit_solution(11477274575022279728)
XLA Ops:
  1.7 5.6 fusion.11
  8.1 1.1 fusion.1.refs_0_
  9.2 91.8 %shard_map.316 = (bf16[2048,2432]{1,0:T(8,128)(2,1)}, bf16[2,512,2048]{2,1,0:T(8,128)(2,1)}) custom-call(bf16[256,2432]{1,0:T(8,128)(2,1)} %fusion.1.refs_0_, bf16[2,512,2048]{2,1,0:T(8,128)(2,1)} %bitcast.92), custom_call_target="tpu_custom_call" | custom-call | tf_op jit(solution)/shard_map/pallas_call | solution.py:953
  101.0 2.2 copy-done.2
  103.2 2.2 copy-done.4
  105.4 3.2 shard_map.317
  108.7 17.2 %fusion.14.refs_1_.refs_2_.refs_4_.refs_5_.refs_7_ = f32[1024,2432]{1,0:T(8,128)S(1)} fusion(bf16[1024,2048]{1,0:T(8,128)(2,1)S(1)} %get-tuple-element.54.normed, bf16[2048,2432]{1,0:T(8,128)(2,1)} %get-tuple-element.55), kind=kOutput, calls=%fused_computation.63 | convolution fusion | flops 10200547328 | bytes 24117248 | tf_op jit(solution)/shard_map/dot_general | solution.py:1712
  125.9 3.7 copy-done.11
  129.6 3.8 collective-permute-start
  135.4 1.3 fusion.6
  137.3 4.6 broadcast_multiply_fusion.out_grad
  142.0 2.7 add_bitcast_fusion
  145.2 1.6 copy.56
  146.8 1.4 copy.47
  149.4 142.0 %shard_map.318 = (f32[1024,2048]{1,0:T(8,128)}, f32[8,128,2048]{2,1,0:T(8,128)}, f32[2,128,2048]{2,1,0:T(8,128)}, f32[1024,256]{1,0:T(8,128)}, f32[1024,2048]{1,...) custom-call(s32[2,3]{1,0:T(2,128)} %pad_add_fusion.1.refs_0_, ...), custom_call_target="tpu_custom_call" | custom-call | tf_op jit(solution)/shard_map/pallas_call | solution.py:310
  291.4 1.6 broadcast_select_fusion.entering.refs_13_
  292.9 35.3 %shard_map.319 = (f32[1024,2048]{1,0:T(8,128)}, f32[1024,2048]{1,0:T(8,128)}, f32[1024,2048]{1,0:T(8,128)}, f32[1024,128]{1,0:T(8,128)}) custom-call(bf16[1024,2048]{1,0:T(8,128)(2,1)} %copy-done.9, bf16[1024,2048]{1,0:T(8,128)(2,1)} %broadcast_multiply_fusion.out_grad, bf16[2048,2048]{1,0:T(8,128)(2,1)} %get-tuple-element.56.gate_weight, ...), custom_call_target="tpu_custom_call" | custom-call | flops 17179869184 | bytes 50331648 | tf_op jit(solution)/shard_map/pallas_call | solution.py:1039
  328.3 2.1 collective-permute-done.1
  330.4 1.1 add.75.sums
  331.5 23.6 %shard_map.320 = (bf16[1024,2048]{1,0:T(8,128)(2,1)}, bf16[1024,2048]{1,0:T(8,128)(2,1)}, f32[1024,2048]{1,0:T(8,128)}, f32[2,128,2048]{2,1,0:T(8,128)S(1)}, f32[8,2048]{1,0:T(8,128)S(1)}) custom-call(f32[1024,2048]{1,0:T(8,128)} %get-tuple-element.62.mixer.refs_9_, f32[1024,2048]{1,0:T(8,128)} %get-tuple-element.63.gate_in, ...), custom_call_target="tpu_custom_call" | custom-call | flops 2147483648 | bytes 50331648 | tf_op jit(solution)/shard_map/pallas_call | solution.py:1104
  355.1 14.9 %fusion.17.refs_28_.refs_5_ = f32[1024,2048]{1,0:T(8,128)} fusion(bf16[1024,2048]{1,0:T(8,128)(2,1)} %get-tuple-element.71, bf16[2048,2048]{1,0:T(8,128)(2,1)} %get-tuple-element.57.out_weight), kind=kOutput, calls=%fused_computation.66 | convolution fusion | flops 8589934592 | bytes 20971520 | tf_op jit(solution)/shard_map/dot_general | solution.py:1804
  370.0 14.5 %fusion.15 = f32[2048,2048]{1,0:T(8,128)} fusion(bf16[1024,2048]{1,0:T(8,128)(2,1)S(1)} %copy-done.12, bf16[1024,2048]{1,0:T(8,128)(2,1)} %get-tuple-element.71), kind=kOutput, calls=%fused_computation.64 | convolution fusion | flops 8589934592 | bytes 25165824 | tf_op jit(solution)/shard_map/dot_general | solution.py:1798
  384.5 1.3 collective-permute-start.2
  385.8 11.4 %fusion.18.refs_29_ = f32[1024,2048]{1,0:T(8,128)} fusion(bf16[1024,2048]{1,0:T(8,128)(2,1)S(1)} %copy-done.27, bf16[2048,2048]{1,0:T(8,128)(2,1)S(1)} %bitcast.121), kind=kOutput, calls=%fused_computation.67 | convolution fusion | flops 8589934592 | bytes 20971520 | tf_op jit(solution)/shard_map/dot_general | solution.py:1804
  397.2 11.9 %fusion.16 = f32[2048,2048]{1,0:T(8,128)} fusion(bf16[1024,2048]{1,0:T(8,128)(2,1)S(1)} %copy-done.10, bf16[1024,2048]{1,0:T(8,128)(2,1)S(1)} %copy-done.27), kind=kOutput, calls=%fused_computation.65 | convolution fusion | flops 8589934592 | bytes 25165824 | tf_op jit(solution)/shard_map/dot_general | solution.py:1798
  409.1 26.7 %collective-permute-done.2.refs_15_ = f32[2,128,2048]{2,1,0:T(8,128)S(1)} collective-permute-done((f32[2,128,2048]{2,1,0:T(8,128)S(1)}, f32[2,128,2048]{2,1,0:T(8,128)S(1)}, u32[]{:S(2)}, u32[]{:S(2)}) %collective-permute-start.2) | collective-permute-done | bytes 2097184 | tf_op jit(solution)/shard_map/ppermute | solution.py:1599
  435.8 1.3 copy-done.15
  437.1 177.0 %shard_map.321 = (bf16[1024,2432]{1,0:T(8,128)(2,1)}, f32[2,8,2048]{2,1,0:T(8,128)}, f32[2,8,2048]{2,1,0:T(8,128)}, f32[1024,256]{1,0:T(8,128)}, f32[2,8,256]{2,...) custom-call(s32[2,3]{1,0:T(2,128)} %pad_add_fusion.1.refs_0_, ...), custom_call_target="tpu_custom_call" | custom-call | tf_op jit(solution)/shard_map/pallas_call | solution.py:654
  615.0 1.3 collective-permute-start.3
  616.3 5.7 collective-permute-done.3
  622.0 1.3 pad_add_fusion
  624.8 1.8 collective-permute-done.4
  628.9 18.8 %convolution_add_fusion.refs_7_ = f32[1024,2048]{1,0:T(8,128)} fusion(f32[1024,2048]{1,0:T(8,128)} %fusion.18.refs_29_, bf16[1024,2432]{1,0:T(8,128)(2,1)} %fusion.4, bf16[2048,2432]{1,0:T(8,128)(2,1)} %get-tuple-element.55), kind=kOutput, calls=%fused_computation | convolution fusion | flops 10202644480 | bytes 31719424 | tf_op jit(solution)/shard_map/dot_general | solution.py:1804
  649.9 1.8 copy.51
  651.8 1.3 collective-permute-done.7
  653.9 18.1 %fusion.19 = f32[2048,2432]{1,0:T(8,128)} fusion(bf16[1024,2048]{1,0:T(8,128)(2,1)} %copy-done.9, bf16[1024,2432]{1,0:T(8,128)(2,1)} %fusion.4), kind=kOutput, calls=%fused_computation.68 | convolution fusion | flops 10200547328 | bytes 29097984 | tf_op jit(solution)/shard_map/dot_general | solution.py:1798
  672.0 1.0 broadcast_in_dim.23.refs_4_
  673.0 116.5 %shard_map.322 = (f32[256,2432]{1,0:T(8,128)}, bf16[1024,2048]{1,0:T(8,128)(2,1)}, bf16[1024,2048]{1,0:T(8,128)(2,1)}, f32[128,128]{1,0:T(8,128)}) custom-call(f32[4,2,256,2432]{3,2,1,0:T(8,128)} %bitcast.99, bf16[1024,2048]{1,0:T(8,128)(2,1)} %copy-done.3, bf16[1024,2048]{1,0:T(8,128)(2,1)} %bitcast.102, f32[1024,128]{1,0:T(8,128)} %copy-done.6, ...), custom_call_target="tpu_custom_call" | custom-call | tf_op jit(solution)/shard_map/pallas_call | solution.py:1559
  789.4 1.0 slice.154
  790.5 1.3 slice_bitcast_fusion.8
  791.8 1.2 slice_bitcast_fusion.6
  795.4 1.4 slice.177
  796.7 1.2 slice.176
  797.9 6.7 shard_map.323
  806.6 1.3 slice_bitcast_fusion.4
  807.9 1.7 slice_add_fusion.3
  809.6 4.9 copy.63
  814.5 2.0 copy.64
  (107 shorter events, 18.4 us)
Async XLA Ops:
  0.6 133.9 %copy-start = (f32[32]{0:T(128)S(1)}, f32[32]{0:T(128)}, u32[]{:S(2)}) copy-start(f32[32]{0:T(128)} %param.36) | copy-start | bytes 388
  1.6 6.3 copy-start.22
  1.7 6.4 copy-start.19
  7.9 93.1 %copy-start.7 = (f32[2048]{0:T(1024)S(1)}, f32[2048]{0:T(1024)}, u32[]{:S(2)}) copy-start(f32[2048]{0:T(1024)} %param.25) | copy-start | bytes 24580
  101.0 2.2 copy-start.2
  103.2 2.2 copy-start.4
  108.6 17.2 %copy-start.3 = (bf16[1024,2048]{1,0:T(8,128)(2,1)}, bf16[1024,2048]{1,0:T(8,128)(2,1)S(1)}, u32[]{:S(2)}) copy-start(bf16[1024,2048]{1,0:T(8,128)(2,1)S(1)} %get-tuple-element.78.refs_1_) | copy-start | bytes 12582916
  108.6 17.2 %copy-start.6 = (f32[1024,128]{1,0:T(8,128)}, f32[1024,128]{1,0:T(8,128)S(1)}, u32[]{:S(2)}) copy-start(f32[1024,128]{1,0:T(8,128)S(1)} %get-tuple-element.79.refs_3_) | copy-start | bytes 1572868
  108.6 17.2 %copy-start.9 = (bf16[1024,2048]{1,0:T(8,128)(2,1)}, bf16[1024,2048]{1,0:T(8,128)(2,1)S(1)}, u32[]{:S(2)}) copy-start(bf16[1024,2048]{1,0:T(8,128)(2,1)S(1)} %get-tuple-element.54.normed) | copy-start | bytes 12582916
  108.6 24.8 %copy-start.23 = (s32[2,1,2]{2,1,0:T(1,128)S(1)}, s32[2,1,2]{2,1,0:T(1,128)}, u32[]{:S(2)}) copy-start(s32[2,1,2]{2,1,0:T(1,128)} %param.22) | copy-start | bytes 52
  108.6 25.9 %copy-start.18 = (f32[32,2048]{1,0:T(8,128)S(1)}, f32[32,2048]{1,0:T(8,128)}, u32[]{:S(2)}) copy-start(f32[32,2048]{1,0:T(8,128)} %constant.76.clone) | copy-start | bytes 786436
  125.9 3.8 copy-start.11
  129.6 19.1 %collective-permute-start = (f32[2,8,2432]{2,1,0:T(8,128)S(1)}, f32[2,8,2432]{2,1,0:T(8,128)S(1)}, u32[]{:S(2)}, u32[]{:S(2)}) collective-permute-start(f32[2,8,2432]{2,1,0:T(8,128)S(1)} %pad_maximum_fusion), channel_id=1, source_target_pairs={{0,2},{1,3},{4,6},{5,7},{8,10},{9,11},{12,14},{13,15},{16,18},{17,... | collective-permute-start | bytes 466952 | tf_op jit(solution)/shard_map/ppermute | solution.py:1599
  137.3 9.5 %copy-start.17 = (bf16[2048,256]{1,0:T(8,128)(2,1)S(1)}, bf16[2048,256]{1,0:T(8,128)(2,1)}, u32[]{:S(2)}) copy-start(bf16[2048,256]{1,0:T(8,128)(2,1)} %param.29) | copy-start | bytes 3145732
  142.0 6.3 copy-start.25
  142.0 6.3 copy-start.26
  148.8 0.7 copy-start.14
  292.9 38.6 %copy-start.5 = (f32[1024,256]{1,0:T(8,128)S(1)}, f32[1024,256]{1,0:T(8,128)}, u32[]{:S(2)}) copy-start(f32[1024,256]{1,0:T(8,128)} %get-tuple-element.60.coupled) | copy-start | bytes 3145732
  292.9 38.6 %copy-start.8 = (f32[2048]{0:T(1024)S(1)}, f32[2048]{0:T(1024)}, u32[]{:S(2)}) copy-start(f32[2048]{0:T(1024)} %param.37) | copy-start | bytes 24580
  328.2 2.2 collective-permute-start.1
  331.5 54.2 %slice-start = ((s8[8388608]{0:T(1024)(128)(4,1)}), s8[4194304]{0:T(1024)(128)(4,1)S(1)}, s32[]{:S(2)}) async-start(s8[8388608]{0:T(1024)(128)(4,1)} %bitcast.120), calls=%async_computation | async-start | bytes 8388608
  355.1 14.9 %copy-start.12 = (bf16[1024,2048]{1,0:T(8,128)(2,1)S(1)}, bf16[1024,2048]{1,0:T(8,128)(2,1)}, u32[]{:S(2)}) copy-start(bf16[1024,2048]{1,0:T(8,128)(2,1)} %broadcast_multiply_fusion.out_grad) | copy-start | bytes 12582916
  355.1 30.7 %slice-start.1 = ((s8[8388608]{0:T(1024)(128)(4,1)}), s8[4194304]{0:T(1024)(128)(4,1)S(1)}, s32[]{:S(2)}) async-start(s8[8388608]{0:T(1024)(128)(4,1)} %bitcast.120), calls=%async_computation.1 | async-start | bytes 8388608
  370.0 15.8 %copy-start.27 = (bf16[1024,2048]{1,0:T(8,128)(2,1)S(1)}, bf16[1024,2048]{1,0:T(8,128)(2,1)}, u32[]{:S(2)}) copy-start(bf16[1024,2048]{1,0:T(8,128)(2,1)} %get-tuple-element.72) | copy-start | bytes 12582916
  384.5 51.3 %collective-permute-start.2 = (f32[2,128,2048]{2,1,0:T(8,128)S(1)}, f32[2,128,2048]{2,1,0:T(8,128)S(1)}, u32[]{:S(2)}, u32[]{:S(2)}) collective-permute-start(f32[2,128,2048]{2,1,0:T(8,128)S(1)} %get-tuple-element.70), channel_id=1, source_target_pairs={{2,0},{3,1},{6,4},{7,5},{10,8},{11,9},{14,12},{15,13},{18,16},{19,... | collective-permute-start | bytes 6291464 | tf_op jit(solution)/shard_map/ppermute | solution.py:1599
  385.8 11.4 %copy-start.10 = (bf16[1024,2048]{1,0:T(8,128)(2,1)S(1)}, bf16[1024,2048]{1,0:T(8,128)(2,1)}, u32[]{:S(2)}) copy-start(bf16[1024,2048]{1,0:T(8,128)(2,1)} %copy-done.9) | copy-start | bytes 12582916
  435.8 1.3 copy-start.15
  615.0 7.0 collective-permute-start.3
  623.3 3.3 collective-permute-start.4
  623.4 48.5 %collective-permute-start.5 = (f32[1024,2048]{1,0:T(8,128)}, f32[1024,2048]{1,0:T(8,128)}, u32[]{:S(2)}, u32[]{:S(2)}) collective-permute-start(f32[1024,2048]{1,0:T(8,128)} %fusion.17.refs_28_.refs_5_), channel_id=1, source_target_pairs={{0,1},{1,0},{2,3},{3,2},{4,5},{5,4},{6,7},{7,6},{8,9},{9,8},{10,11... | collective-permute-start | bytes 25165832 | tf_op jit(solution)/shard_map/ppermute | solution.py:1604
  628.9 18.9 %copy-start.24 = (f32[8,256]{1,0:T(8,128)S(1)}, f32[8,256]{1,0:T(8,128)}, u32[]{:S(2)}) copy-start(f32[8,256]{1,0:T(8,128)} %get-tuple-element.81) | copy-start | bytes 24580
  628.9 20.9 %copy-start.20 = (f32[8,2048]{1,0:T(8,128)S(1)}, f32[8,2048]{1,0:T(8,128)}, u32[]{:S(2)}) copy-start(f32[8,2048]{1,0:T(8,128)} %get-tuple-element.80) | copy-start | bytes 196612
  628.9 21.0 %copy-start.16 = (f32[256,2048]{1,0:T(8,128)S(1)}, f32[256,2048]{1,0:T(8,128)}, u32[]{:S(2)}) copy-start(f32[256,2048]{1,0:T(8,128)} %get-tuple-element.90) | copy-start | bytes 6291460
  647.7 24.3 %collective-permute-start.6 = (f32[1024,2048]{1,0:T(8,128)}, f32[1024,2048]{1,0:T(8,128)}, u32[]{:S(2)}, u32[]{:S(2)}) collective-permute-start(f32[1024,2048]{1,0:T(8,128)} %convolution_add_fusion.refs_7_), channel_id=1, source_target_pairs={{0,1},{1,0},{2,3},{3,2},{4,5},{5,4},{6,7},{7,6},{8,9},{9,8},{10,11... | collective-permute-start | bytes 25165832 | tf_op jit(solution)/shard_map/ppermute | solution.py:1604
  647.8 5.3 collective-permute-start.7
  653.9 18.1 %copy-start.21 = (f32[1024]{0:T(1024)S(1)}, f32[1024]{0:T(1024)}, u32[]{:S(2)}) copy-start(f32[1024]{0:T(1024)} %get-tuple-element.133) | copy-start | bytes 12292
  790.4 17.5 %collective-permute-start.8 = (f32[256,256]{1,0:T(8,128)S(1)}, f32[256,256]{1,0:T(8,128)S(1)}, u32[]{:S(2)}, u32[]{:S(2)}) collective-permute-start(f32[256,256]{1,0:T(8,128)S(1)} %slice.154), channel_id=1, source_target_pairs={{0,1},{1,0},{2,3},{3,2},{4,5},{5,4},{6,7},{7,6},{8,9},{9,8},{10,11... | collective-permute-start | bytes 786440 | tf_op jit(solution)/shard_map/ppermute | solution.py:1604
  809.6 4.9 copy-start.13
  809.6 7.0 copy-start.1
